TPU v7x, 32 devices: a whole 2x2x4 slice. The times are simulated.
32 devices in a mesh: groups: 2 (over y), ctx: 8 (over z, x), tp: 2 (over core).
Axes of the slice: x: 2, y: 2, z: 4, core: 2. Of those that a mesh axis runs over, the one named last changes fastest.
Arguments:
- queries: bfloat16 [2048, 4096], P(('groups', 'ctx'), 'tp'), parts along dimension 0, may hold values from -10 to 10
- win_keys: bfloat16 [2048, 512], P(('groups', 'ctx'), 'tp'), parts along dimension 0, may hold values from -6 to 6
- win_values: bfloat16 [2048, 512], P(('groups', 'ctx'), 'tp'), parts along dimension 0, may hold values from -6 to 6
- cache_keys: bfloat16 [1024, 512], P(('groups', 'ctx'), 'tp'), parts along dimension 0, may hold values from -6 to 6
- cache_values: bfloat16 [1024, 512], P(('groups', 'ctx'), 'tp'), parts along dimension 0, may hold values from -6 to 6
- valid_counts: int32 [16], P('groups'), parts along dimension 0, may hold values from 1 to 128
- first_block: int32 [16], P('groups'), parts along dimension 0, may hold values from 0 to 3, as said below
Outputs:
- attended: bfloat16 [2048, 4096], P(('groups', 'ctx'), 'tp'), parts along dimension 0
There are 2 independent parts, one for each index of `groups`. A program takes and returns all parts, laid end to end along the dimension named above; each array names one. Nothing has to cross between parts.
Inputs may be any that keep to these rules, and one draw needn't show every extreme that they name: first_block[b] is at most b // 2.
All inputs are finite; a program needn't handle non-finite values.
Results may differ from a plain program's by a relative error of at most 0.005.
Values may be sent and summed in bfloat16 or wider, within the bound.
No kernel may reach another device: no remote copies, remote signals or barrier semaphores. Data moves between devices by JAX's collectives and lax.ppermute only.
A program may use at most 64 MiB of HBM per device.

v0:
```python
import jax
import jax.numpy as jnp
from jax import lax
from jax.sharding import PartitionSpec as P

HD = 128
TOK_DEV = 128


masked_score = -1e30


def table_pick(table, index):
    slots = lax.broadcasted_iota(jnp.int32, (index.shape[0], table.shape[0]), 1)
    return jnp.sum(jnp.where(slots == index[:, None], table[None, :], 0), axis=1)


def fold_ctx(key_stack, value_stack, combine, initial):
    return combine(
        initial,
        (
            lax.all_gather(key_stack, "ctx", axis=0, tiled=True),
            lax.all_gather(value_stack, "ctx", axis=0, tiled=True),
        ),
        jnp.int32(0),
    )


def absorb(carried, grouped, key_tile, value_tile, key_mask, score_scale):
    run_max, run_total, run_accum = carried
    score_tile = (
        jnp.einsum("rhgd,khd->rhgk", grouped, key_tile, preferred_element_type=jnp.float32)
        * score_scale
    )
    wide_mask = key_mask[:, None, None, :]
    score_tile = jnp.where(wide_mask, score_tile, masked_score)
    new_max = jnp.maximum(run_max, jnp.max(score_tile, axis=-1))
    exp_tile = jnp.where(wide_mask, jnp.exp(score_tile - new_max[..., None]), 0.0)
    factor = jnp.exp(run_max - new_max)
    run_total = run_total * factor + jnp.sum(exp_tile, axis=-1)
    run_accum = run_accum * factor[..., None] + jnp.einsum(
        "rhgk,khd->rhgd",
        exp_tile.astype(jnp.bfloat16),
        value_tile,
        preferred_element_type=jnp.float32,
    )
    return (new_max, run_total, run_accum)


def shards(queries, win_keys, win_values, cache_keys, cache_values, valid_counts, first_block):
    my_place = lax.axis_index("ctx")
    row_count = queries.shape[0]
    positions = my_place * row_count + jnp.arange(row_count, dtype=jnp.int32)
    kv_heads = win_keys.shape[1] // HD
    q_heads = queries.shape[1] // HD
    group_size = q_heads // kv_heads
    grouped = queries.reshape(row_count, kv_heads, group_size, HD)
    block_first = table_pick(first_block, positions // TOK_DEV)
    window_rows = win_keys.shape[0]
    cache_rows = cache_keys.shape[0]
    stride = window_rows + cache_rows
    key_stack = jnp.concatenate([win_keys, cache_keys], axis=0)
    value_stack = jnp.concatenate([win_values, cache_values], axis=0)
    score_scale = HD ** (-0.5)
    cache_mask = jnp.ones((row_count, cache_rows), dtype=bool)
    block_iota = jnp.arange(valid_counts.shape[0], dtype=jnp.int32)

    def combine(carried, arrived, first_row):
        key_piece, value_piece = arrived
        shard_total = key_piece.shape[0] // stride
        key_tiles = key_piece.reshape(shard_total, stride, kv_heads, HD)
        value_tiles = value_piece.reshape(shard_total, stride, kv_heads, HD)

        def one_shard(current, scan_items):
            key_tile, value_tile, offset = scan_items
            key_pos = offset * window_rows + jnp.arange(window_rows, dtype=jnp.int32)
            block_idx = offset * window_rows // TOK_DEV
            valid_limit = jnp.sum(jnp.where(block_iota == block_idx, valid_counts, 0))
            visible_win = (
                (key_pos[None, :] <= positions[:, None])
                & (block_idx >= block_first)[:, None]
                & (key_pos % TOK_DEV < valid_limit)[None, :]
            )
            full_mask = jnp.concatenate([visible_win, cache_mask], axis=1)
            current = lax.cond(
                jnp.any(visible_win),
                lambda inner_state: absorb(
                    inner_state, grouped, key_tile, value_tile, full_mask, score_scale
                ),
                lambda inner_state: absorb(
                    inner_state,
                    grouped,
                    key_tile[window_rows:],
                    value_tile[window_rows:],
                    cache_mask,
                    score_scale,
                ),
                current,
            )
            return (current, None)

        carried, _ = lax.scan(
            one_shard, carried, (key_tiles, value_tiles, jnp.arange(shard_total, dtype=jnp.int32))
        )
        return carried

    initial = (
        jnp.full((row_count, kv_heads, group_size), masked_score, jnp.float32),
        jnp.zeros((row_count, kv_heads, group_size), jnp.float32),
        jnp.zeros((row_count, kv_heads, group_size, HD), jnp.float32),
    )
    run_max, run_total, run_accum = fold_ctx(key_stack, value_stack, combine, initial)
    attended = (
        (run_accum / run_total[..., None]).reshape(row_count, q_heads * HD).astype(jnp.bfloat16)
    )
    return attended


def solution(mesh):
    in_specs = (
        P(("groups", "ctx"), "tp"),
        P(("groups", "ctx"), "tp"),
        P(("groups", "ctx"), "tp"),
        P(("groups", "ctx"), "tp"),
        P(("groups", "ctx"), "tp"),
        P("groups"),
        P("groups"),
    )
    out_specs = P(("groups", "ctx"), "tp")
    return jax.shard_map(shards, mesh=mesh, in_specs=in_specs, out_specs=out_specs, check_vma=False)
```

profile of v0, /device:TPU:0, one launch (start us, length us, event | category | flops | bytes accessed | tf_op | source)
XLA Modules:
  0.0 142.0 jit_solution(7771315581998130787)
XLA Ops:
  0.0 0.7 select_reduce_fusion
  0.8 0.9 pad_maximum_fusion
  1.6 0.9 pad_maximum_fusion.1
  2.5 1.3 copy.14
  4.1 33.8 %all_gather.7 = bf16[1536,256]{1,0:T(8,128)(2,1)S(1)} all-gather(bf16[192,256]{1,0:T(8,128)(2,1)S(1)} %pad_maximum_fusion.1), channel_id=1, replica_groups=mesh['groups'=2,'ctx'=8,'tp'=2] {'ctx'}, dimensions={0}, use_global_device_ids=true | all-gather | bytes 884736 | tf_op jit(solution)/shard_map/all_gather | solution.py:23
  38.1 32.1 %all_gather.6 = bf16[1536,256]{1,0:T(8,128)(2,1)S(1)} all-gather(bf16[192,256]{1,0:T(8,128)(2,1)S(1)} %pad_maximum_fusion), channel_id=1, replica_groups=mesh['groups'=2,'ctx'=8,'tp'=2] {'ctx'}, dimensions={0}, use_global_device_ids=true | all-gather | bytes 884736 | tf_op jit(solution)/shard_map/all_gather | solution.py:22
  70.6 69.8 %while.19 = (s32[]{:T(128)}, f32[128,2,8]{0,2,1:T(8,128)S(1)}, f32[128,2,8]{0,2,1:T(8,128)S(1)}, f32[128,2,8,128]{3,0,2,1:T(8,128)S(1)}, s32[8]{0:T(128)S(1)}, /...) while((s32[]{:T(128)}, f32[128,2,8]{0,2,1:T(8,128)S(1)}, ...), condition=%wide.region_10.11_spmd.clone.clone, body=%wide.region_1.10_spmd.clone.clone.sunk | while | flops 205461536 | bytes 8588858 | solution.py:102
  71.8 0.7 fusion.33
  73.2 0.7 fusion.35
  74.8 4.3 %conditional.4 = (f32[128,2,8]{0,2,1:T(8,128)}, f32[128,2,8]{0,2,1:T(8,128)S(1)}, f32[128,2,8,128]{3,0,2,1:T(8,128)S(1)}) conditional(s32[]{:T(128)} %convert_element_type.30, (bf16[192,2,128]{2,0,1:T(8,128)(2,1)S(1)}, bf16[128,2,8,128]{3,0,2,1:T(8,128)(2,1)S(1)}, f32[128,2,8]{0,2,1:T(8,128)S(1)}, f32[128,2,8]{0,2,1:T(8,128)S(1)}, ...), branch_computations={%region_4.6_spmd, %region_7.9_spmd} | conditional | flops 205393920 | bytes 7766041 | solution.py:85
  75.8 1.0 fusion.14
  76.8 0.7 multiply_add_fusion.1
  77.5 1.6 %fusion.12 = f32[128,2,8,128]{3,0,2,1:T(8,128)S(1)} fusion(f32[128,2,8,128]{3,0,2,1:T(8,128)S(1)} %get-tuple-element.221, f32[128,2,8,192]{0,3,2,1:T(8,128)S(1)} %get-tuple-element.353, f32[128,2,8]{0,2,1:T(8,128)} %max.6, pred[128,192]{0,1:T(8,128)(4,1)S(1)} %concatenate.7, f32[128,2,8]{0,2,1:T(8,128)S(1)} %get-tuple-element.347, ...), kind=kOutput, calls=%fused_computation.18 | convolution fusion | flops 102367232 | bytes 3809280 | tf_op jit(solution)/shard_map/while/body/eval_jaxpr/cond/branch_1_fun/rhgk,khd->rhgd/dot_general | solution.py:41
  79.1 0.7 copy.51
  81.0 0.7 fusion.33
  82.4 0.7 fusion.35
  83.9 3.8 %conditional.4 = (f32[128,2,8]{0,2,1:T(8,128)}, f32[128,2,8]{0,2,1:T(8,128)S(1)}, f32[128,2,8,128]{3,0,2,1:T(8,128)S(1)}) conditional(s32[]{:T(128)} %convert_element_type.30, (bf16[192,2,128]{2,0,1:T(8,128)(2,1)S(1)}, bf16[128,2,8,128]{3,0,2,1:T(8,128)(2,1)S(1)}, f32[128,2,8]{0,2,1:T(8,128)S(1)}, f32[128,2,8]{0,2,1:T(8,128)S(1)}, ...), branch_computations={%region_4.6_spmd, %region_7.9_spmd} | conditional | flops 205393920 | bytes 7766041 | solution.py:85
  84.9 0.8 fusion.5
  85.7 0.7 multiply_add_fusion
  86.4 1.3 fusion.2
  87.7 0.7 copy.51
  89.7 0.7 fusion.33
  91.0 0.7 fusion.35
  92.6 3.8 %conditional.4 = (f32[128,2,8]{0,2,1:T(8,128)}, f32[128,2,8]{0,2,1:T(8,128)S(1)}, f32[128,2,8,128]{3,0,2,1:T(8,128)S(1)}) conditional(s32[]{:T(128)} %convert_element_type.30, (bf16[192,2,128]{2,0,1:T(8,128)(2,1)S(1)}, bf16[128,2,8,128]{3,0,2,1:T(8,128)(2,1)S(1)}, f32[128,2,8]{0,2,1:T(8,128)S(1)}, f32[128,2,8]{0,2,1:T(8,128)S(1)}, ...), branch_computations={%region_4.6_spmd, %region_7.9_spmd} | conditional | flops 205393920 | bytes 7766041 | solution.py:85
  93.5 0.8 fusion.5
  94.3 0.7 multiply_add_fusion
  95.0 1.3 fusion.2
  96.4 0.7 copy.51
  98.4 0.7 fusion.33
  99.7 0.7 fusion.35
  101.3 3.8 %conditional.4 = (f32[128,2,8]{0,2,1:T(8,128)}, f32[128,2,8]{0,2,1:T(8,128)S(1)}, f32[128,2,8,128]{3,0,2,1:T(8,128)S(1)}) conditional(s32[]{:T(128)} %convert_element_type.30, (bf16[192,2,128]{2,0,1:T(8,128)(2,1)S(1)}, bf16[128,2,8,128]{3,0,2,1:T(8,128)(2,1)S(1)}, f32[128,2,8]{0,2,1:T(8,128)S(1)}, f32[128,2,8]{0,2,1:T(8,128)S(1)}, ...), branch_computations={%region_4.6_spmd, %region_7.9_spmd} | conditional | flops 205393920 | bytes 7766041 | solution.py:85
  102.2 0.8 fusion.5
  103.0 0.7 multiply_add_fusion
  103.7 1.3 fusion.2
  105.1 0.7 copy.51
  107.0 0.7 fusion.33
  108.3 0.7 fusion.35
  109.9 3.8 %conditional.4 = (f32[128,2,8]{0,2,1:T(8,128)}, f32[128,2,8]{0,2,1:T(8,128)S(1)}, f32[128,2,8,128]{3,0,2,1:T(8,128)S(1)}) conditional(s32[]{:T(128)} %convert_element_type.30, (bf16[192,2,128]{2,0,1:T(8,128)(2,1)S(1)}, bf16[128,2,8,128]{3,0,2,1:T(8,128)(2,1)S(1)}, f32[128,2,8]{0,2,1:T(8,128)S(1)}, f32[128,2,8]{0,2,1:T(8,128)S(1)}, ...), branch_computations={%region_4.6_spmd, %region_7.9_spmd} | conditional | flops 205393920 | bytes 7766041 | solution.py:85
  110.9 0.8 fusion.5
  111.7 0.7 multiply_add_fusion
  112.4 1.3 fusion.2
  113.7 0.7 copy.51
  115.7 0.7 fusion.33
  117.0 0.7 fusion.35
  118.6 3.8 %conditional.4 = (f32[128,2,8]{0,2,1:T(8,128)}, f32[128,2,8]{0,2,1:T(8,128)S(1)}, f32[128,2,8,128]{3,0,2,1:T(8,128)S(1)}) conditional(s32[]{:T(128)} %convert_element_type.30, (bf16[192,2,128]{2,0,1:T(8,128)(2,1)S(1)}, bf16[128,2,8,128]{3,0,2,1:T(8,128)(2,1)S(1)}, f32[128,2,8]{0,2,1:T(8,128)S(1)}, f32[128,2,8]{0,2,1:T(8,128)S(1)}, ...), branch_computations={%region_4.6_spmd, %region_7.9_spmd} | conditional | flops 205393920 | bytes 7766041 | solution.py:85
  119.5 0.8 fusion.5
  120.3 0.7 multiply_add_fusion
  121.0 1.3 fusion.2
  122.4 0.7 copy.51
  124.3 0.7 fusion.33
  125.7 0.7 fusion.35
  127.2 3.8 %conditional.4 = (f32[128,2,8]{0,2,1:T(8,128)}, f32[128,2,8]{0,2,1:T(8,128)S(1)}, f32[128,2,8,128]{3,0,2,1:T(8,128)S(1)}) conditional(s32[]{:T(128)} %convert_element_type.30, (bf16[192,2,128]{2,0,1:T(8,128)(2,1)S(1)}, bf16[128,2,8,128]{3,0,2,1:T(8,128)(2,1)S(1)}, f32[128,2,8]{0,2,1:T(8,128)S(1)}, f32[128,2,8]{0,2,1:T(8,128)S(1)}, ...), branch_computations={%region_4.6_spmd, %region_7.9_spmd} | conditional | flops 205393920 | bytes 7766041 | solution.py:85
  128.2 0.8 fusion.5
  129.0 0.7 multiply_add_fusion
  129.7 1.3 fusion.2
  131.0 0.7 copy.51
  133.0 0.7 fusion.33
  134.3 0.7 fusion.35
  135.9 3.8 %conditional.4 = (f32[128,2,8]{0,2,1:T(8,128)}, f32[128,2,8]{0,2,1:T(8,128)S(1)}, f32[128,2,8,128]{3,0,2,1:T(8,128)S(1)}) conditional(s32[]{:T(128)} %convert_element_type.30, (bf16[192,2,128]{2,0,1:T(8,128)(2,1)S(1)}, bf16[128,2,8,128]{3,0,2,1:T(8,128)(2,1)S(1)}, f32[128,2,8]{0,2,1:T(8,128)S(1)}, f32[128,2,8]{0,2,1:T(8,128)S(1)}, ...), branch_computations={%region_4.6_spmd, %region_7.9_spmd} | conditional | flops 205393920 | bytes 7766041 | solution.py:85
  136.8 0.8 fusion.5
  137.6 0.7 multiply_add_fusion
  138.3 1.3 fusion.2
  139.7 0.7 copy.51
  141.1 0.9 copy.31
  (77 shorter events, 20.1 us)
Async XLA Ops:
  38.1 32.5 %copy-start = (s32[8]{0:T(128)S(1)}, s32[8]{0:T(128)}, u32[]{:S(2)}) copy-start(s32[8]{0:T(128)} %param.16) | copy-start | bytes 100
where the time goes:
time: 145 us; the launch traced here: 142 us
  blocking collectives  66 us (46%)
  other arithmetic  36.2 us (25%)
  local copies, waits for them, and re-layouts  15 us (10%)
  matrix products  13.5 us (9%)
  loops' own time  11.3 us (8%)
    all_gather x1, blocking collectives, fold_ctx(): lax.all_gather(value_stack, 'ctx', axis=0, tiled=True)  33.8 us
    all_gather x1, blocking collectives, fold_ctx(): lax.all_gather(key_stack, 'ctx', axis=0, tiled=True)  32.1 us
    dot_general x8, matrix products, absorb(): jnp.einsum('rhgk,khd->rhgd', exp_tile.astype(jnp.bfloat16), value_tile, p...  11 us
    another operation x1, loops' own time, combine(): lax.scan(one_shard, carried, (key_tiles, value_tiles, jnp.arange(shard_to...  11 us
    reduce_sum x8, other arithmetic, absorb(): run_total = run_total * factor + jnp.sum(exp_tile, axis=-1)  6.5 us
    dynamic_slice x32, local copies, waits for them, and re-layouts, combine(): lax.scan(one_shard, carried, (key_tiles, value_tiles, jnp.arange(shard_to...  6.08 us
    reduce_or x8, other arithmetic, one_shard(): jnp.any(visible_win)  5.88 us
    add x8, other arithmetic, absorb(): run_total = run_total * factor + jnp.sum(exp_tile, axis=-1)  5.67 us

commit v1 on v0

v1 whole, which is shorter than its diff:
```python
import functools
import math

import jax
import jax.numpy as jnp
from jax import lax
from jax.experimental import pallas as pl
from jax.experimental.pallas import tpu as pltpu
from jax.sharding import PartitionSpec as P

HD = 128
EXP_SCALE = HD**-0.5 * math.log2(math.e)
HIDDEN = -1.0e30
CHUNK_HEADS = 4


def ring_width(count):
    width = round(count ** (1 / 3))
    if width > 1 and count % width == 0 and (count // width) % 2 == 0:
        return width
    return 1


def place_at(position, count):
    width = ring_width(count)
    if width == 1:
        return position
    rows = count // width
    row, step = position // (width - 1), position % (width - 1)
    forth = row * width + 1 + step
    back = row * width + width - 1 - step
    home = (rows - 1 - (position - rows * (width - 1))) * width
    if isinstance(position, int):
        return home if position >= rows * (width - 1) else (back if row % 2 else forth)
    return jnp.where(position >= rows * (width - 1), home, jnp.where(row % 2 == 1, back, forth))


def position_of(place, count):
    width = ring_width(count)
    if width == 1:
        return place
    rows = count // width
    row, column = place // width, place % width
    snake = row * (width - 1) + jnp.where(row % 2 == 1, width - 1 - column, column - 1)
    return jnp.where(column == 0, rows * (width - 1) + rows - 1 - row, snake)


def attend_kernel(offsets, own, last, count, window_rows, *refs):
    valid_ref, first_ref, q_ref = refs[:3]
    refs = refs[3:]
    key_refs, value_refs = refs[: len(offsets)], refs[len(offsets) : 2 * len(offsets)]
    refs = refs[2 * len(offsets) :]
    if not own:
        acc_in, top_in = refs[:2]
        refs = refs[2:]
    if last:
        (out_ref, keys, values) = refs
    else:
        (acc_out, top_out, keys, values) = refs

    me = lax.axis_index("ctx")
    position = position_of(me, count)
    first = first_ref[me]
    rows = q_ref.shape[0]
    kv_heads = key_refs[0].shape[1] // HD
    group = q_ref.shape[1] // HD // kv_heads
    cache_rows = key_refs[0].shape[0] - window_rows
    total_keys = keys.shape[1]
    cache_at = len(offsets) * window_rows
    row_iota = lax.broadcasted_iota(jnp.int32, (window_rows, HD), 0)

    for index, offset in enumerate(offsets):
        place = place_at(lax.rem(position + offset + 2 * count, count), count)
        if own:
            limit = window_rows
        else:
            limit = jnp.where((place >= first) & (place <= me), valid_ref[place], 0)
        shown = row_iota < limit
        for head in range(kv_heads):
            lanes = slice(head * HD, (head + 1) * HD)
            key, value = key_refs[index], value_refs[index]
            fill = key[window_rows : window_rows + 1, lanes].astype(jnp.float32)
            at = slice(index * window_rows, (index + 1) * window_rows)
            win_key = key[:window_rows, lanes]
            win_value = value[:window_rows, lanes]
            if own:
                keys[head, at, :] = win_key
                values[head, at, :HD] = win_value
                values[head, at, HD:] = jnp.ones((window_rows, HD), jnp.bfloat16)
            else:
                keys[head, at, :] = jnp.where(shown, win_key.astype(jnp.float32), fill).astype(jnp.bfloat16)
                values[head, at, :HD] = jnp.where(shown, win_value.astype(jnp.float32), 0.0).astype(jnp.bfloat16)
                values[head, at, HD:] = jnp.where(shown, 1.0, 0.0).astype(jnp.bfloat16)
            at = slice(cache_at + index * cache_rows, cache_at + (index + 1) * cache_rows)
            keys[head, at, :] = key[window_rows:, lanes]
            values[head, at, :HD] = value[window_rows:, lanes]
            values[head, at, HD:] = jnp.ones((cache_rows, HD), jnp.bfloat16)
    filled = cache_at + len(offsets) * cache_rows
    if filled < total_keys:
        spare = total_keys - filled
        for head in range(kv_heads):
            row = key_refs[0][window_rows : window_rows + 1, head * HD : (head + 1) * HD].astype(jnp.float32)
            keys[head, filled:, :] = jnp.broadcast_to(row, (spare, HD)).astype(jnp.bfloat16)
            values[head, filled:, :] = jnp.zeros((spare, 2 * HD), jnp.bfloat16)

    if own:
        key_iota = lax.broadcasted_iota(jnp.int32, (rows, window_rows), 1)
        query_iota = lax.broadcasted_iota(jnp.int32, (rows, window_rows), 0)
        seen = (key_iota <= query_iota) & (key_iota < valid_ref[me])
        bias = jnp.concatenate([jnp.where(seen, 0.0, HIDDEN)] * CHUNK_HEADS, axis=0)

    for head in range(kv_heads):
        for start in range(0, group, CHUNK_HEADS):
            base = head * group + start
            at = slice(base * rows, (base + CHUNK_HEADS) * rows)
            query = jnp.concatenate(
                [q_ref[:, (base + i) * HD : (base + i + 1) * HD] for i in range(CHUNK_HEADS)], axis=0
            )
            score = lax.dot_general(
                query, keys[head], (((1,), (1,)), ((), ())), preferred_element_type=jnp.float32
            )
            if own:
                score = jnp.concatenate([score[:, :window_rows] + bias, score[:, window_rows:]], axis=1)
            top = jnp.max(score, axis=1, keepdims=True)
            if not own:
                before = top_in[at, :]
                top = jnp.maximum(before[:, :1], top)
            weight = jnp.exp2((score - top) * EXP_SCALE).astype(jnp.bfloat16)
            acc = jnp.dot(weight, values[head], preferred_element_type=jnp.float32)
            if not own:
                fade = jnp.exp2((before - top) * EXP_SCALE)
                acc = acc + acc_in[at, :] * jnp.concatenate([fade, fade], axis=1)
            if last:
                result = (acc[:, :HD] / acc[:, HD:]).astype(jnp.bfloat16)
                for i in range(CHUNK_HEADS):
                    out_ref[:, (base + i) * HD : (base + i + 1) * HD] = result[i * rows : (i + 1) * rows]
            else:
                acc_out[at, :] = acc
                top_out[at, :] = jnp.broadcast_to(top, (top.shape[0], HD))


def attend(offsets, keys, values, state, last, queries, valid_counts, first_block, count, window_rows):
    own = state is None
    rows, width = queries.shape
    heads = width // HD
    kv_heads = keys[0].shape[1] // HD
    total_keys = -(-sum(k.shape[0] for k in keys) // HD) * HD
    vmem = pl.BlockSpec(memory_space=pltpu.VMEM)
    smem = pl.BlockSpec(memory_space=pltpu.SMEM)
    if last:
        out_shape = jax.ShapeDtypeStruct(queries.shape, jnp.bfloat16)
        out_specs = vmem
    else:
        out_shape = (
            jax.ShapeDtypeStruct((heads * rows, 2 * HD), jnp.float32),
            jax.ShapeDtypeStruct((heads * rows, HD), jnp.float32),
        )
        out_specs = (vmem, vmem)
    operands = [valid_counts, first_block, queries, *keys, *values, *(() if own else state)]
    return pl.pallas_call(
        functools.partial(attend_kernel, offsets, own, last, count, window_rows),
        out_shape=out_shape,
        in_specs=[smem, smem] + [vmem] * (len(operands) - 2),
        out_specs=out_specs,
        scratch_shapes=[
            pltpu.VMEM((kv_heads, total_keys, HD), jnp.bfloat16),
            pltpu.VMEM((kv_heads, total_keys, 2 * HD), jnp.bfloat16),
        ],
        compiler_params=pltpu.CompilerParams(vmem_limit_bytes=40 * 1024 * 1024),
        cost_estimate=pl.CostEstimate(
            flops=4 * heads * rows * total_keys * HD,
            bytes_accessed=2 * rows * width,
            transcendentals=heads * rows * total_keys,
        ),
        name="attend_%s" % ("first" if own else "last" if last else "next"),
    )(*operands)


def shards(count, queries, win_keys, win_values, cache_keys, cache_values, valid_counts, first_block):
    window_rows = win_keys.shape[0]
    ring = [place_at(p, count) for p in range(count)]
    onward = [(ring[p], ring[(p + 1) % count]) for p in range(count)]
    backward = [(b, a) for a, b in onward]
    keys = jnp.concatenate([win_keys, cache_keys], axis=0)
    values = jnp.concatenate([win_values, cache_values], axis=0)
    common = (queries, valid_counts, first_block, count, window_rows)

    arrived = []
    key_on = key_back = keys
    value_on = value_back = values
    half = count // 2
    for step in range(1, half + 1):
        key_on = lax.ppermute(key_on, "ctx", onward)
        value_back = lax.ppermute(value_back, "ctx", backward)
        if step < half:
            value_on = lax.ppermute(value_on, "ctx", onward)
            key_back = lax.ppermute(key_back, "ctx", backward)
            arrived.append([(-step, key_on, value_on), (step, key_back, value_back)])
        else:
            arrived.append([(step, key_on, value_back)])

    state = attend((0,), [keys], [values], None, False, *common)
    for begin in range(0, half, 2):
        pieces = [piece for step in arrived[begin : begin + 2] for piece in step]
        state = attend(
            tuple(p[0] for p in pieces),
            [p[1] for p in pieces],
            [p[2] for p in pieces],
            state,
            begin + 2 >= half,
            *common,
        )
    return state


def solution(mesh):
    in_specs = (
        P(("groups", "ctx"), "tp"),
        P(("groups", "ctx"), "tp"),
        P(("groups", "ctx"), "tp"),
        P(("groups", "ctx"), "tp"),
        P(("groups", "ctx"), "tp"),
        P("groups"),
        P("groups"),
    )
    out_specs = P(("groups", "ctx"), "tp")
    return jax.shard_map(
        functools.partial(shards, mesh.shape["ctx"]),
        mesh=mesh,
        in_specs=in_specs,
        out_specs=out_specs,
        check_vma=False,
    )
```

time: 145 us -> 34.7 us (0.24); the launches traced: 142 us -> 34.3 us
  blocking collectives: 66 us -> 0 us
  other arithmetic: 36.2 us -> 0 us
  starting transfers between devices: 0 us -> 15.2 us
  matrix products: 13.5 us -> 0 us
  loops' own time: 11.3 us -> 0 us
  Pallas kernels: 0 us -> 9.74 us
  local copies, waits for them, and re-layouts: 15 us -> 5.56 us
  waiting for transfers between devices: 0 us -> 3.74 us
    all_gather x2 -> x0, blocking collectives: 66 us -> none  [the longest x1 33.8 us: fold_ctx(): lax.all_gather(value_stack, 'ctx', axis=0, tiled=True)]
    ppermute x0 -> x14, starting transfers between devices: none -> 15.2 us  [the longest x4 8.89 us: shards(): value_back = lax.ppermute(value_back, 'ctx', backward)]
    dot_general x16 -> x0, matrix products: 13.5 us -> none  [the longest x8 11 us: absorb(): jnp.einsum('rhgk,khd->rhgd', exp_tile.astype(jnp.bfloat16), value_tile, p...]
    reduce_sum x17 -> x0, other arithmetic: 12.5 us -> none  [the longest x8 6.5 us: absorb(): run_total = run_total * factor + jnp.sum(exp_tile, axis=-1)]
    another operation x9 -> x0, loops' own time: 11.3 us -> none  [the longest x1 11 us: combine(): lax.scan(one_shard, carried, (key_tiles, value_tiles, jnp.arange(shard_to...]
    pallas_call x0 -> x3, Pallas kernels: none -> 9.74 us  [attend(): pl.pallas_call(functools.partial(attend_kernel, offsets, own, last, count...]
    dynamic_slice x32 -> x0, local copies, waits for them, and re-layouts: 6.08 us -> none  [combine(): lax.scan(one_shard, carried, (key_tiles, value_tiles, jnp.arange(shard_to...]
    reduce_or x8 -> x0, other arithmetic: 5.88 us -> none  [one_shard(): jnp.any(visible_win)]
  transfers between devices with their start and end apart: 0 -> 14, of which waited for: 0 -> 5; matrix products, arithmetic and copies ran while one was open for 0% -> 5% of each run, Pallas kernels for 0% -> 16%
where the time goes in v1:
time: 34.7 us; the launch traced here: 34.3 us
  starting transfers between devices  15.2 us (44%)
  Pallas kernels  9.74 us (28%)
  local copies, waits for them, and re-layouts  5.56 us (16%)
  waiting for transfers between devices  3.74 us (11%)
    pallas_call x3, Pallas kernels, attend(): pl.pallas_call(functools.partial(attend_kernel, offsets, own, last, count...  9.74 us
    ppermute x4, starting transfers between devices, shards(): value_back = lax.ppermute(value_back, 'ctx', backward)  8.89 us
    ppermute x3, starting transfers between devices, shards(): key_back = lax.ppermute(key_back, 'ctx', backward)  5.82 us
    unnamed x8, local copies, waits for them, and re-layouts  4.04 us
    ppermute x4, waiting for transfers between devices, shards(): key_on = lax.ppermute(key_on, 'ctx', onward)  3.56 us
    concatenate x1, local copies, waits for them, and re-layouts, shards(): values = jnp.concatenate([win_values, cache_values], axis=0)  0.76 us
    concatenate x1, local copies, waits for them, and re-layouts, shards(): keys = jnp.concatenate([win_keys, cache_keys], axis=0)  0.76 us
  transfers between devices with their start and end apart: 14, of which 5 were waited for; matrix products, arithmetic and copies ran while one was open for 5% of the time, Pallas kernels for 16%

profile of v1, /device:TPU:0, one launch (start us, length us, event | category | flops | bytes accessed | tf_op | source)
XLA Modules:
  0.0 34.3 jit_solution(9402730645349479610)
XLA Ops:
  0.0 0.8 %constant_dynamic-update-slice_fusion.3 = bf16[192,256]{1,0:T(8,128)(2,1)S(1)} fusion(bf16[128,256]{1,0:T(8,128)(2,1)} %param.9), kind=kLoop, calls=%fused_computation.3 | loop fusion | bytes 131072
  0.8 0.8 %constant_dynamic-update-slice_fusion.2.refs_4_ = bf16[192,256]{1,0:T(8,128)(2,1)S(1)} fusion(bf16[192,256]{1,0:T(8,128)(2,1)S(1)} %constant_dynamic-update-slice_fusion.3, bf16[64,256]{1,0:T(8,128)(2,1)} %param.11), kind=kLoop, calls=%fused_computation.2 | loop fusion | bytes 65536 | tf_op jit(solution)/shard_map/concatenate | solution.py:185
  1.6 3.0 %collective-permute-start.10 = (bf16[192,256]{1,0:T(8,128)(2,1)S(1)}, bf16[192,256]{1,0:T(8,128)(2,1)S(1)}, u32[]{:S(2)}, u32[]{:S(2)}) collective-permute-start(bf16[192,256]{1,0:T(8,128)(2,1)S(1)} %constant_dynamic-update-slice_fusion.2.refs_4_), channel_id=1, source_target_pairs={{6,2},{10,6},{14,10},{12,14},{8,12},{4,8},{0,4},{2,0},{7,3},{11,7}... | collective-permute-start | bytes 294920 | tf_op jit(solution)/shard_map/ppermute | solution.py:194
  4.6 0.8 %constant_dynamic-update-slice_fusion.1 = bf16[192,256]{1,0:T(8,128)(2,1)S(1)} fusion(bf16[128,256]{1,0:T(8,128)(2,1)} %param.8), kind=kLoop, calls=%fused_computation.1 | loop fusion | bytes 131072
  5.5 0.8 %constant_dynamic-update-slice_fusion.refs_3_ = bf16[192,256]{1,0:T(8,128)(2,1)S(1)} fusion(bf16[192,256]{1,0:T(8,128)(2,1)S(1)} %constant_dynamic-update-slice_fusion.1, bf16[64,256]{1,0:T(8,128)(2,1)} %param.10), kind=kLoop, calls=%fused_computation | loop fusion | bytes 65536 | tf_op jit(solution)/shard_map/concatenate | solution.py:184
  6.2 0.0 collective-permute-start
  6.2 2.0 %collective-permute-start.3 = (bf16[192,256]{1,0:T(8,128)(2,1)S(1)}, bf16[192,256]{1,0:T(8,128)(2,1)S(1)}, u32[]{:S(2)}, u32[]{:S(2)}) collective-permute-start(bf16[192,256]{1,0:T(8,128)(2,1)S(1)} %constant_dynamic-update-slice_fusion.refs_3_), channel_id=1, source_target_pairs={{6,2},{10,6},{14,10},{12,14},{8,12},{4,8},{0,4},{2,0},{7,3},{11,7}... | collective-permute-start | bytes 294920 | tf_op jit(solution)/shard_map/ppermute | solution.py:197
  8.3 0.0 collective-permute-start.7
  8.3 0.0 collective-permute-done.10.refs_8_
  8.3 2.0 %collective-permute-start.11 = (bf16[192,256]{1,0:T(8,128)(2,1)S(1)}, bf16[192,256]{1,0:T(8,128)(2,1)S(1)}, u32[]{:S(2)}, u32[]{:S(2)}) collective-permute-start(bf16[192,256]{1,0:T(8,128)(2,1)S(1)} %collective-permute-done.10.refs_8_), channel_id=1, source_target_pairs={{6,2},{10,6},{14,10},{12,14},{8,12},{4,8},{0,4},{2,0},{7,3},{11,7}... | collective-permute-start | bytes 294920 | tf_op jit(solution)/shard_map/ppermute | solution.py:194
  10.3 1.6 %collective-permute-done.refs_3_ = bf16[192,256]{1,0:T(8,128)(2,1)S(1)} collective-permute-done((bf16[192,256]{1,0:T(8,128)(2,1)S(1)}, bf16[192,256]{1,0:T(8,128)(2,1)S(1)}, u32[]{:S(2)}, u32[]{:S(2)}) %collective-permute-start) | collective-permute-done | bytes 98336 | tf_op jit(solution)/shard_map/ppermute | solution.py:193
  11.8 0.0 collective-permute-start.1
  11.9 0.0 collective-permute-done.3.refs_4_
  11.9 2.0 %collective-permute-start.4 = (bf16[192,256]{1,0:T(8,128)(2,1)S(1)}, bf16[192,256]{1,0:T(8,128)(2,1)S(1)}, u32[]{:S(2)}, u32[]{:S(2)}) collective-permute-start(bf16[192,256]{1,0:T(8,128)(2,1)S(1)} %collective-permute-done.3.refs_4_), channel_id=1, source_target_pairs={{6,2},{10,6},{14,10},{12,14},{8,12},{4,8},{0,4},{2,0},{7,3},{11,7}... | collective-permute-start | bytes 294920 | tf_op jit(solution)/shard_map/ppermute | solution.py:197
  13.9 0.1 collective-permute-done.7.refs_7_
  14.0 0.0 collective-permute-start.8
  14.0 0.0 collective-permute-done.11.refs_10_
  14.0 2.0 %collective-permute-start.12 = (bf16[192,256]{1,0:T(8,128)(2,1)S(1)}, bf16[192,256]{1,0:T(8,128)(2,1)S(1)}, u32[]{:S(2)}, u32[]{:S(2)}) collective-permute-start(bf16[192,256]{1,0:T(8,128)(2,1)S(1)} %collective-permute-done.11.refs_10_), channel_id=1, source_target_pairs={{6,2},{10,6},{14,10},{12,14},{8,12},{4,8},{0,4},{2,0},{7,3},{11,7}... | collective-permute-start | bytes 294920 | tf_op jit(solution)/shard_map/ppermute | solution.py:194
  16.0 0.9 %collective-permute-done.1.refs_5_ = bf16[192,256]{1,0:T(8,128)(2,1)S(1)} collective-permute-done((bf16[192,256]{1,0:T(8,128)(2,1)S(1)}, bf16[192,256]{1,0:T(8,128)(2,1)S(1)}, u32[]{:S(2)}, u32[]{:S(2)}) %collective-permute-start.1) | collective-permute-done | bytes 98336 | tf_op jit(solution)/shard_map/ppermute | solution.py:193
  16.8 0.2 collective-permute-start.2
  17.1 0.0 collective-permute-done.4.refs_6_
  17.1 1.8 %collective-permute-start.5 = (bf16[192,256]{1,0:T(8,128)(2,1)S(1)}, bf16[192,256]{1,0:T(8,128)(2,1)S(1)}, u32[]{:S(2)}, u32[]{:S(2)}) collective-permute-start(bf16[192,256]{1,0:T(8,128)(2,1)S(1)} %collective-permute-done.4.refs_6_), channel_id=1, source_target_pairs={{6,2},{10,6},{14,10},{12,14},{8,12},{4,8},{0,4},{2,0},{7,3},{11,7}... | collective-permute-start | bytes 294920 | tf_op jit(solution)/shard_map/ppermute | solution.py:197
  18.9 0.1 collective-permute-done.8.refs_9_
  19.0 0.2 collective-permute-start.9
  19.2 0.0 collective-permute-done.12.refs_7_
  19.2 1.8 %collective-permute-start.13 = (bf16[192,256]{1,0:T(8,128)(2,1)S(1)}, bf16[192,256]{1,0:T(8,128)(2,1)S(1)}, u32[]{:S(2)}, u32[]{:S(2)}) collective-permute-start(bf16[192,256]{1,0:T(8,128)(2,1)S(1)} %collective-permute-done.12.refs_7_), channel_id=1, source_target_pairs={{6,2},{10,6},{14,10},{12,14},{8,12},{4,8},{0,4},{2,0},{7,3},{11,7}... | collective-permute-start | bytes 294920 | tf_op jit(solution)/shard_map/ppermute | solution.py:194
  21.0 1.1 %collective-permute-done.2.refs_3_ = bf16[192,256]{1,0:T(8,128)(2,1)S(1)} collective-permute-done((bf16[192,256]{1,0:T(8,128)(2,1)S(1)}, bf16[192,256]{1,0:T(8,128)(2,1)S(1)}, u32[]{:S(2)}, u32[]{:S(2)}) %collective-permute-start.2) | collective-permute-done | bytes 98336 | tf_op jit(solution)/shard_map/ppermute | solution.py:193
  22.1 0.0 collective-permute-start.6
  22.1 0.0 copy-start
  22.1 1.0 %copy-done = bf16[128,2048]{1,0:T(8,128)(2,1)S(1)} copy-done((bf16[128,2048]{1,0:T(8,128)(2,1)S(1)}, bf16[128,2048]{1,0:T(8,128)(2,1)}, u32[]{:S(2)}) %copy-start) | copy-done | bytes 524312
  23.2 0.0 copy-start.1
  23.2 0.7 %copy-done.1 = s32[8]{0:T(128)S(1)} copy-done((s32[8]{0:T(128)S(1)}, s32[8]{0:T(128)}, u32[]{:S(2)}) %copy-start.1) | copy-done | bytes 56
  23.8 0.0 copy-start.2
  23.8 0.7 %copy-done.2 = s32[8]{0:T(128)S(1)} copy-done((s32[8]{0:T(128)S(1)}, s32[8]{0:T(128)}, u32[]{:S(2)}) %copy-start.2) | copy-done | bytes 56
  24.5 1.5 %attend_first.1 = (f32[2048,256]{1,0:T(8,128)S(1)}, f32[2048,128]{1,0:T(8,128)S(1)}) custom-call(s32[8]{0:T(128)S(1)} %copy-done.1, s32[8]{0:T(128)S(1)} %copy-done.2, bf16[128,2048]{1,0:T(8,128)(2,1)S(1)} %copy-done, bf16[192,256]{1,0:T(8,128)(2,1)S(1)} %constant_dynamic-update-slice_fusion.refs_3_, ...), custom_call_target="tpu_custom_call" | custom-call | flops 268435456 | bytes 524288 | tf_op jit(solution)/shard_map/attend_first/pallas_call | solution.py:160
  26.0 4.0 %attend_next.1 = (f32[2048,256]{1,0:T(8,128)S(1)}, f32[2048,128]{1,0:T(8,128)S(1)}) custom-call(s32[8]{0:T(128)S(1)} %copy-done.1, s32[8]{0:T(128)S(1)} %copy-done.2, bf16[128,2048]{1,0:T(8,128)(2,1)S(1)} %copy-done, bf16[192,256]{1,0:T(8,128)(2,1)S(1)} %collective-permute-done.refs_3_, bf16[192,256]{1,0:T(8,128)(2,1)S(1)} %collective-permute-done.3.refs_4_, ...), custom_call_target="tpu_custom_call" | custom-call | flops 805306368 | bytes 524288 | tf_op jit(solution)/shard_map/attend_next/pallas_call | solution.py:160
  30.0 0.0 collective-permute-done.5.refs_4_
  30.0 0.0 collective-permute-done.9.refs_6_
  30.0 0.0 collective-permute-done.13.refs_8_
  30.0 0.0 collective-permute-done.6.refs_5_
  30.0 4.3 %attend_last.1 = bf16[128,2048]{1,0:T(8,128)(2,1)} custom-call(s32[8]{0:T(128)S(1)} %copy-done.1, s32[8]{0:T(128)S(1)} %copy-done.2, bf16[128,2048]{1,0:T(8,128)(2,1)S(1)} %copy-done, bf16[192,256]{1,0:T(8,128)(2,1)S(1)} %collective-permute-done.2.refs_3_, bf16[192,256]{1,0:T(8,128)(2,1)S(1)} %collective-permute-done.5.refs_4_, ...), custom_call_target="tpu_custom_call" | custom-call | flops 671088640 | bytes 524288 | tf_op jit(solution)/shard_map/attend_last/pallas_call | solution.py:160
Async XLA Ops:
  1.6 6.7 %collective-permute-start.10 = (bf16[192,256]{1,0:T(8,128)(2,1)S(1)}, bf16[192,256]{1,0:T(8,128)(2,1)S(1)}, u32[]{:S(2)}, u32[]{:S(2)}) collective-permute-start(bf16[192,256]{1,0:T(8,128)(2,1)S(1)} %constant_dynamic-update-slice_fusion.2.refs_4_), channel_id=1, source_target_pairs={{6,2},{10,6},{14,10},{12,14},{8,12},{4,8},{0,4},{2,0},{7,3},{11,7}... | collective-permute-start | bytes 294920 | tf_op jit(solution)/shard_map/ppermute | solution.py:194
  6.2 5.6 %collective-permute-start = (bf16[192,256]{1,0:T(8,128)(2,1)S(1)}, bf16[192,256]{1,0:T(8,128)(2,1)S(1)}, u32[]{:S(2)}, u32[]{:S(2)}) collective-permute-start(bf16[192,256]{1,0:T(8,128)(2,1)S(1)} %constant_dynamic-update-slice_fusion.refs_3_), channel_id=1, source_target_pairs={{2,6},{6,10},{10,14},{14,12},{12,8},{8,4},{4,0},{0,2},{3,7},{7,11}... | collective-permute-start | bytes 294920 | tf_op jit(solution)/shard_map/ppermute | solution.py:193
  6.2 5.6 %collective-permute-start.3 = (bf16[192,256]{1,0:T(8,128)(2,1)S(1)}, bf16[192,256]{1,0:T(8,128)(2,1)S(1)}, u32[]{:S(2)}, u32[]{:S(2)}) collective-permute-start(bf16[192,256]{1,0:T(8,128)(2,1)S(1)} %constant_dynamic-update-slice_fusion.refs_3_), channel_id=1, source_target_pairs={{6,2},{10,6},{14,10},{12,14},{8,12},{4,8},{0,4},{2,0},{7,3},{11,7}... | collective-permute-start | bytes 294920 | tf_op jit(solution)/shard_map/ppermute | solution.py:197
  8.3 5.7 %collective-permute-start.7 = (bf16[192,256]{1,0:T(8,128)(2,1)S(1)}, bf16[192,256]{1,0:T(8,128)(2,1)S(1)}, u32[]{:S(2)}, u32[]{:S(2)}) collective-permute-start(bf16[192,256]{1,0:T(8,128)(2,1)S(1)} %constant_dynamic-update-slice_fusion.2.refs_4_), channel_id=1, source_target_pairs={{2,6},{6,10},{10,14},{14,12},{12,8},{8,4},{4,0},{0,2},{3,7},{7,11}... | collective-permute-start | bytes 294920 | tf_op jit(solution)/shard_map/ppermute | solution.py:196
  8.3 5.7 %collective-permute-start.11 = (bf16[192,256]{1,0:T(8,128)(2,1)S(1)}, bf16[192,256]{1,0:T(8,128)(2,1)S(1)}, u32[]{:S(2)}, u32[]{:S(2)}) collective-permute-start(bf16[192,256]{1,0:T(8,128)(2,1)S(1)} %collective-permute-done.10.refs_8_), channel_id=1, source_target_pairs={{6,2},{10,6},{14,10},{12,14},{8,12},{4,8},{0,4},{2,0},{7,3},{11,7}... | collective-permute-start | bytes 294920 | tf_op jit(solution)/shard_map/ppermute | solution.py:194
  11.8 5.0 %collective-permute-start.1 = (bf16[192,256]{1,0:T(8,128)(2,1)S(1)}, bf16[192,256]{1,0:T(8,128)(2,1)S(1)}, u32[]{:S(2)}, u32[]{:S(2)}) collective-permute-start(bf16[192,256]{1,0:T(8,128)(2,1)S(1)} %collective-permute-done.refs_3_), channel_id=1, source_target_pairs={{2,6},{6,10},{10,14},{14,12},{12,8},{8,4},{4,0},{0,2},{3,7},{7,11}... | collective-permute-start | bytes 294920 | tf_op jit(solution)/shard_map/ppermute | solution.py:193
  11.9 5.2 %collective-permute-start.4 = (bf16[192,256]{1,0:T(8,128)(2,1)S(1)}, bf16[192,256]{1,0:T(8,128)(2,1)S(1)}, u32[]{:S(2)}, u32[]{:S(2)}) collective-permute-start(bf16[192,256]{1,0:T(8,128)(2,1)S(1)} %collective-permute-done.3.refs_4_), channel_id=1, source_target_pairs={{6,2},{10,6},{14,10},{12,14},{8,12},{4,8},{0,4},{2,0},{7,3},{11,7}... | collective-permute-start | bytes 294920 | tf_op jit(solution)/shard_map/ppermute | solution.py:197
  14.0 5.0 %collective-permute-start.8 = (bf16[192,256]{1,0:T(8,128)(2,1)S(1)}, bf16[192,256]{1,0:T(8,128)(2,1)S(1)}, u32[]{:S(2)}, u32[]{:S(2)}) collective-permute-start(bf16[192,256]{1,0:T(8,128)(2,1)S(1)} %collective-permute-done.7.refs_7_), channel_id=1, source_target_pairs={{2,6},{6,10},{10,14},{14,12},{12,8},{8,4},{4,0},{0,2},{3,7},{7,11}... | collective-permute-start | bytes 294920 | tf_op jit(solution)/shard_map/ppermute | solution.py:196
  14.0 5.2 %collective-permute-start.12 = (bf16[192,256]{1,0:T(8,128)(2,1)S(1)}, bf16[192,256]{1,0:T(8,128)(2,1)S(1)}, u32[]{:S(2)}, u32[]{:S(2)}) collective-permute-start(bf16[192,256]{1,0:T(8,128)(2,1)S(1)} %collective-permute-done.11.refs_10_), channel_id=1, source_target_pairs={{6,2},{10,6},{14,10},{12,14},{8,12},{4,8},{0,4},{2,0},{7,3},{11,7}... | collective-permute-start | bytes 294920 | tf_op jit(solution)/shard_map/ppermute | solution.py:194
  16.8 5.3 %collective-permute-start.2 = (bf16[192,256]{1,0:T(8,128)(2,1)S(1)}, bf16[192,256]{1,0:T(8,128)(2,1)S(1)}, u32[]{:S(2)}, u32[]{:S(2)}) collective-permute-start(bf16[192,256]{1,0:T(8,128)(2,1)S(1)} %collective-permute-done.1.refs_5_), channel_id=1, source_target_pairs={{2,6},{6,10},{10,14},{14,12},{12,8},{8,4},{4,0},{0,2},{3,7},{7,11}... | collective-permute-start | bytes 294920 | tf_op jit(solution)/shard_map/ppermute | solution.py:193
  17.1 12.9 %collective-permute-start.5 = (bf16[192,256]{1,0:T(8,128)(2,1)S(1)}, bf16[192,256]{1,0:T(8,128)(2,1)S(1)}, u32[]{:S(2)}, u32[]{:S(2)}) collective-permute-start(bf16[192,256]{1,0:T(8,128)(2,1)S(1)} %collective-permute-done.4.refs_6_), channel_id=1, source_target_pairs={{6,2},{10,6},{14,10},{12,14},{8,12},{4,8},{0,4},{2,0},{7,3},{11,7}... | collective-permute-start | bytes 294920 | tf_op jit(solution)/shard_map/ppermute | solution.py:197
  19.0 11.0 %collective-permute-start.9 = (bf16[192,256]{1,0:T(8,128)(2,1)S(1)}, bf16[192,256]{1,0:T(8,128)(2,1)S(1)}, u32[]{:S(2)}, u32[]{:S(2)}) collective-permute-start(bf16[192,256]{1,0:T(8,128)(2,1)S(1)} %collective-permute-done.8.refs_9_), channel_id=1, source_target_pairs={{2,6},{6,10},{10,14},{14,12},{12,8},{8,4},{4,0},{0,2},{3,7},{7,11}... | collective-permute-start | bytes 294920 | tf_op jit(solution)/shard_map/ppermute | solution.py:196
  19.2 10.8 %collective-permute-start.13 = (bf16[192,256]{1,0:T(8,128)(2,1)S(1)}, bf16[192,256]{1,0:T(8,128)(2,1)S(1)}, u32[]{:S(2)}, u32[]{:S(2)}) collective-permute-start(bf16[192,256]{1,0:T(8,128)(2,1)S(1)} %collective-permute-done.12.refs_7_), channel_id=1, source_target_pairs={{6,2},{10,6},{14,10},{12,14},{8,12},{4,8},{0,4},{2,0},{7,3},{11,7}... | collective-permute-start | bytes 294920 | tf_op jit(solution)/shard_map/ppermute | solution.py:194
  22.1 7.9 %collective-permute-start.6 = (bf16[192,256]{1,0:T(8,128)(2,1)S(1)}, bf16[192,256]{1,0:T(8,128)(2,1)S(1)}, u32[]{:S(2)}, u32[]{:S(2)}) collective-permute-start(bf16[192,256]{1,0:T(8,128)(2,1)S(1)} %collective-permute-done.2.refs_3_), channel_id=1, source_target_pairs={{2,6},{6,10},{10,14},{14,12},{12,8},{8,4},{4,0},{0,2},{3,7},{7,11}... | collective-permute-start | bytes 294920 | tf_op jit(solution)/shard_map/ppermute | solution.py:193
  22.1 1.0 %copy-start = (bf16[128,2048]{1,0:T(8,128)(2,1)S(1)}, bf16[128,2048]{1,0:T(8,128)(2,1)}, u32[]{:S(2)}) copy-start(bf16[128,2048]{1,0:T(8,128)(2,1)} %refs_2_.5) | copy-start | bytes 1572868
  23.2 0.7 %copy-start.1 = (s32[8]{0:T(128)S(1)}, s32[8]{0:T(128)}, u32[]{:S(2)}) copy-start(s32[8]{0:T(128)} %refs_0_.5) | copy-start | bytes 100
  23.8 0.7 %copy-start.2 = (s32[8]{0:T(128)S(1)}, s32[8]{0:T(128)}, u32[]{:S(2)}) copy-start(s32[8]{0:T(128)} %refs_1_.5) | copy-start | bytes 100

commit v2 on v1

v2 whole, which is shorter than its diff:
```python
import functools
import math

import jax
import jax.numpy as jnp
from jax import lax
from jax.experimental import pallas as pl
from jax.experimental.pallas import tpu as pltpu
from jax.sharding import PartitionSpec as P

HD = 128
EXP_SCALE = HD**-0.5 * math.log2(math.e)
HIDDEN = -1.0e30
CHUNK_HEADS = 4


def ring_width(count):
    width = round(count ** (1 / 3))
    if width > 1 and count % width == 0 and (count // width) % 2 == 0:
        return width
    return 1


def place_at(position, count):
    width = ring_width(count)
    if width == 1:
        return position
    rows = count // width
    row, step = position // (width - 1), position % (width - 1)
    forth = row * width + 1 + step
    back = row * width + width - 1 - step
    home = (rows - 1 - (position - rows * (width - 1))) * width
    if isinstance(position, int):
        return home if position >= rows * (width - 1) else (back if row % 2 else forth)
    return jnp.where(position >= rows * (width - 1), home, jnp.where(row % 2 == 1, back, forth))


def position_of(place, count):
    width = ring_width(count)
    if width == 1:
        return place
    rows = count // width
    row, column = place // width, place % width
    snake = row * (width - 1) + jnp.where(row % 2 == 1, width - 1 - column, column - 1)
    return jnp.where(column == 0, rows * (width - 1) + rows - 1 - row, snake)


def pack_kernel(win_keys, win_values, cache_keys, cache_values, packed, sems):
    start = 0
    copies = []
    for index, piece in enumerate((win_keys, cache_keys, win_values, cache_values)):
        rows = piece.shape[0]
        copies.append(pltpu.make_async_copy(piece, packed.at[start : start + rows], sems.at[index]))
        start += rows
    for copy in copies:
        copy.start()
    for copy in copies:
        copy.wait()


def pack(win_keys, win_values, cache_keys, cache_values):
    rows = 2 * (win_keys.shape[0] + cache_keys.shape[0])
    return pl.pallas_call(
        pack_kernel,
        out_shape=jax.ShapeDtypeStruct((rows, win_keys.shape[1]), win_keys.dtype),
        in_specs=[pl.BlockSpec(memory_space=pltpu.HBM)] * 4,
        out_specs=pl.BlockSpec(memory_space=pltpu.VMEM),
        scratch_shapes=[pltpu.SemaphoreType.DMA((4,))],
        cost_estimate=pl.CostEstimate(flops=0, bytes_accessed=4 * rows * win_keys.shape[1], transcendentals=0),
        name="pack",
    )(win_keys, win_values, cache_keys, cache_values)


def ring_offsets(count):
    half = count // 2
    return [sign * step for step in range(1, half) for sign in (-1, 1)] + [half]


def place_pieces(pieces, own, window_rows, cache_rows, limits, key_refs, value_refs, keys, values):
    stride = window_rows + cache_rows
    kv_heads, total_keys = keys.shape[:2]
    cache_at = len(pieces) * window_rows
    row_iota = lax.broadcasted_iota(jnp.int32, (window_rows, HD), 0)
    for index, (limit_row, key_base, value_base) in enumerate(pieces):
        key, value = key_refs[index], value_refs[index]
        if not own:
            shown = row_iota < limits[limit_row : limit_row + 1, :]
        for head in range(kv_heads):
            lanes = slice(head * HD, (head + 1) * HD)
            at = slice(index * window_rows, (index + 1) * window_rows)
            win_key = key[key_base : key_base + window_rows, lanes]
            win_value = value[value_base : value_base + window_rows, lanes]
            if own:
                keys[head, at, :] = win_key
                values[head, at, :HD] = win_value
                values[head, at, HD:] = jnp.ones((window_rows, HD), jnp.bfloat16)
            else:
                fill = key[key_base + window_rows : key_base + window_rows + 1, lanes].astype(jnp.float32)
                keys[head, at, :] = jnp.where(shown, win_key.astype(jnp.float32), fill).astype(jnp.bfloat16)
                values[head, at, :HD] = jnp.where(shown, win_value.astype(jnp.float32), 0.0).astype(jnp.bfloat16)
                values[head, at, HD:] = jnp.where(shown, 1.0, 0.0).astype(jnp.bfloat16)
            at = slice(cache_at + index * cache_rows, cache_at + (index + 1) * cache_rows)
            keys[head, at, :] = key[key_base + window_rows : key_base + stride, lanes]
            values[head, at, :HD] = value[value_base + window_rows : value_base + stride, lanes]
            values[head, at, HD:] = jnp.ones((cache_rows, HD), jnp.bfloat16)
    filled = len(pieces) * stride
    if filled < total_keys:
        key_base = pieces[0][1] + window_rows
        for head in range(kv_heads):
            row = key_refs[0][key_base : key_base + 1, head * HD : (head + 1) * HD].astype(jnp.float32)
            keys[head, filled:, :] = jnp.broadcast_to(row, (total_keys - filled, HD)).astype(jnp.bfloat16)
            values[head, filled:, :] = jnp.zeros((total_keys - filled, 2 * HD), jnp.bfloat16)


def absorb(query, keys, values, bias, before, acc_before):
    score = lax.dot_general(query, keys, (((1,), (1,)), ((), ())), preferred_element_type=jnp.float32)
    if bias is not None:
        width = bias.shape[1]
        score = jnp.concatenate([score[:, :width] + bias, score[:, width:]], axis=1)
    top = jnp.max(score, axis=1, keepdims=True)
    if before is not None:
        top = jnp.maximum(before[:, :1], top)
    weight = jnp.exp2((score - top) * EXP_SCALE).astype(jnp.bfloat16)
    acc = jnp.dot(weight, values, preferred_element_type=jnp.float32)
    if before is not None:
        fade = jnp.exp2((before - top) * EXP_SCALE)
        acc = acc + acc_before * jnp.concatenate([fade, fade], axis=1)
    return top, acc


def chunks(q_ref, kv_heads):
    rows = q_ref.shape[0]
    group = q_ref.shape[1] // HD // kv_heads
    for head in range(kv_heads):
        for start in range(0, group, CHUNK_HEADS):
            base = head * group + start
            query = jnp.concatenate(
                [q_ref[:, (base + i) * HD : (base + i + 1) * HD] for i in range(CHUNK_HEADS)], axis=0
            )
            yield head, slice(base * rows, (base + CHUNK_HEADS) * rows), query, base


def first_kernel(
    count, window_rows, cache_rows, valid_hbm, first_hbm, q_hbm, packed, acc_out, top_out, q_ref, limits,
    keys, values, valid_ref, first_ref, sems,
):
    copies = [
        pltpu.make_async_copy(valid_hbm, valid_ref, sems.at[0]),
        pltpu.make_async_copy(first_hbm, first_ref, sems.at[1]),
        pltpu.make_async_copy(q_hbm, q_ref, sems.at[2]),
    ]
    for copy in copies:
        copy.start()
    stride = window_rows + cache_rows
    place_pieces(((0, 0, stride),), True, window_rows, cache_rows, None, (packed,), (packed,), keys, values)
    for copy in copies:
        copy.wait()

    me = lax.axis_index("ctx")
    position = position_of(me, count)
    first = first_ref[me]
    for row, offset in enumerate(ring_offsets(count)):
        place = place_at(lax.rem(position + offset + count, count), count)
        limit = jnp.where((place >= first) & (place <= me), valid_ref[place], 0)
        limits[row : row + 1, :] = jnp.full((1, HD), limit, jnp.int32)

    rows = q_ref.shape[0]
    key_iota = lax.broadcasted_iota(jnp.int32, (rows, window_rows), 1)
    query_iota = lax.broadcasted_iota(jnp.int32, (rows, window_rows), 0)
    seen = (key_iota <= query_iota) & (key_iota < valid_ref[me])
    bias = jnp.concatenate([jnp.where(seen, 0.0, HIDDEN)] * CHUNK_HEADS, axis=0)
    for head, at, query, _ in chunks(q_ref, keys.shape[0]):
        top, acc = absorb(query, keys[head], values[head], bias, None, None)
        acc_out[at, :] = acc
        top_out[at, :] = jnp.broadcast_to(top, (top.shape[0], HD))


def next_kernel(pieces, last, window_rows, cache_rows, q_ref, limits, *refs):
    number = len(pieces)
    key_refs, value_refs = refs[:number], refs[number : 2 * number]
    acc_in, top_in, *outs, keys, values = refs[2 * number :]
    place_pieces(pieces, False, window_rows, cache_rows, limits, key_refs, value_refs, keys, values)
    rows = q_ref.shape[0]
    for head, at, query, base in chunks(q_ref, keys.shape[0]):
        top, acc = absorb(query, keys[head], values[head], None, top_in[at, :], acc_in[at, :])
        if last:
            result = (acc[:, :HD] / acc[:, HD:]).astype(jnp.bfloat16)
            for i in range(CHUNK_HEADS):
                outs[0][:, (base + i) * HD : (base + i + 1) * HD] = result[i * rows : (i + 1) * rows]
        else:
            outs[0][at, :] = acc
            outs[1][at, :] = jnp.broadcast_to(top, (top.shape[0], HD))


def kernel_options(queries, total_keys, kv_heads):
    rows, width = queries.shape
    return {
        "compiler_params": pltpu.CompilerParams(vmem_limit_bytes=40 * 1024 * 1024),
        "cost_estimate": pl.CostEstimate(
            flops=6 * rows * width * total_keys,
            bytes_accessed=2 * rows * width,
            transcendentals=rows * (width // HD) * total_keys,
        ),
    }


def room(kv_heads, total_keys):
    return [
        pltpu.VMEM((kv_heads, total_keys, HD), jnp.bfloat16),
        pltpu.VMEM((kv_heads, total_keys, 2 * HD), jnp.bfloat16),
    ]


def state_shapes(queries):
    rows = queries.shape[0] * queries.shape[1] // HD
    return [jax.ShapeDtypeStruct((rows, 2 * HD), jnp.float32), jax.ShapeDtypeStruct((rows, HD), jnp.float32)]


def attend_first(count, window_rows, cache_rows, valid_counts, first_block, queries, packed):
    kv_heads = packed.shape[1] // HD
    total_keys = -(-(window_rows + cache_rows) // HD) * HD
    vmem, anywhere = pl.BlockSpec(memory_space=pltpu.VMEM), pl.BlockSpec(memory_space=pltpu.HBM)
    acc, top, q_near, limits = pl.pallas_call(
        functools.partial(first_kernel, count, window_rows, cache_rows),
        out_shape=[
            *state_shapes(queries),
            jax.ShapeDtypeStruct(queries.shape, queries.dtype),
            jax.ShapeDtypeStruct((-(-count // 8) * 8, HD), jnp.int32),
        ],
        in_specs=[anywhere, anywhere, anywhere, vmem],
        out_specs=[vmem] * 4,
        scratch_shapes=[
            *room(kv_heads, total_keys),
            pltpu.SMEM(valid_counts.shape, jnp.int32),
            pltpu.SMEM(first_block.shape, jnp.int32),
            pltpu.SemaphoreType.DMA((3,)),
        ],
        name="attend_first",
        **kernel_options(queries, total_keys, kv_heads),
    )(valid_counts, first_block, queries, packed)
    return (acc, top), q_near, limits


def attend_next(pieces, keys, values, state, last, window_rows, cache_rows, queries, limits):
    kv_heads = keys[0].shape[1] // HD
    total_keys = -(-len(pieces) * (window_rows + cache_rows) // HD) * HD
    vmem = pl.BlockSpec(memory_space=pltpu.VMEM)
    operands = [queries, limits, *keys, *values, *state]
    shapes = [jax.ShapeDtypeStruct(queries.shape, queries.dtype)] if last else state_shapes(queries)
    outs = pl.pallas_call(
        functools.partial(next_kernel, tuple(pieces), last, window_rows, cache_rows),
        out_shape=shapes,
        in_specs=[vmem] * len(operands),
        out_specs=[vmem] * len(shapes),
        scratch_shapes=room(kv_heads, total_keys),
        name="attend_last" if last else "attend_next",
        **kernel_options(queries, total_keys, kv_heads),
    )(*operands)
    return outs[0] if last else tuple(outs)


def shards(count, queries, win_keys, win_values, cache_keys, cache_values, valid_counts, first_block):
    window_rows, cache_rows = win_keys.shape[0], cache_keys.shape[0]
    stride = window_rows + cache_rows
    half = count // 2
    ring = [place_at(p, count) for p in range(count)]
    onward = [(ring[p], ring[(p + 1) % count]) for p in range(count)]
    backward = [(b, a) for a, b in onward]

    win_keys, win_values, cache_keys, cache_values, valid_counts, first_block, queries = [
        pltpu.with_memory_space_constraint(x, pltpu.HBM)
        for x in (win_keys, win_values, cache_keys, cache_values, valid_counts, first_block, queries)
    ]
    on = back = pack(win_keys, win_values, cache_keys, cache_values)
    state = near = limits = None
    for step in range(1, half + 1):
        if step < half:
            next_on = lax.ppermute(on, "ctx", onward)
            next_back = lax.ppermute(back, "ctx", backward)
        else:
            next_on = lax.ppermute(on[:stride], "ctx", onward)
            next_back = lax.ppermute(back[stride:], "ctx", backward)
        if step == 1:
            state, near, limits = attend_first(
                count, window_rows, cache_rows, valid_counts, first_block, queries, on
            )
        else:
            row = 2 * (step - 2)
            pieces = [(row, 0, stride), (row + 1, 0, stride)]
            state = attend_next(
                pieces, [on, back], [on, back], state, False, window_rows, cache_rows, near, limits
            )
        on, top = lax.optimization_barrier((next_on, state[1]))
        back, top = lax.optimization_barrier((next_back, top))
        state = (state[0], top)
    pieces = [(2 * (half - 1), 0, 0)]
    return attend_next(pieces, [on], [back], state, True, window_rows, cache_rows, near, limits)


def solution(mesh):
    in_specs = (
        P(("groups", "ctx"), "tp"),
        P(("groups", "ctx"), "tp"),
        P(("groups", "ctx"), "tp"),
        P(("groups", "ctx"), "tp"),
        P(("groups", "ctx"), "tp"),
        P("groups"),
        P("groups"),
    )
    out_specs = P(("groups", "ctx"), "tp")
    return jax.shard_map(
        functools.partial(shards, mesh.shape["ctx"]),
        mesh=mesh,
        in_specs=in_specs,
        out_specs=out_specs,
        check_vma=False,
    )
```

time: 34.7 us -> 31.3 us (0.902)
  starting transfers between devices: 15.2 us -> 9.47 us
  local copies, waits for them, and re-layouts: 5.56 us -> 0.97 us
  waiting for transfers between devices: 3.74 us -> 7.92 us
  Pallas kernels: 9.74 us -> 12.7 us
    ppermute x14 -> x8, starting transfers between devices: 15.2 us -> 9.47 us  [the longest x3 5.98 us: shards(): next_on = lax.ppermute(on, 'ctx', onward)]
    ppermute x14 -> x8, waiting for transfers between devices: 3.74 us -> 7.92 us  [the longest x3 5.83 us: shards(): next_on = lax.ppermute(on, 'ctx', onward)]
    unnamed x8 -> x2, local copies, waits for them, and re-layouts: 4.04 us -> 0.96 us
    pallas_call x3 -> x6, Pallas kernels: 9.74 us -> 12.7 us  [the longest x4 9.09 us: attend_next(): pl.pallas_call(functools.partial(next_kernel, tuple(pieces), last, window...]
    concatenate x2 -> x0, local copies, waits for them, and re-layouts: 1.52 us -> none  [the longest x1 0.76 us: shards(): values = jnp.concatenate([win_values, cache_values], axis=0)]
  transfers between devices with their start and end apart: 14 -> 8, of which waited for: 5 -> 5; matrix products, arithmetic and copies ran while one was open for 5% -> 0% of each run, Pallas kernels for 16% -> 26%
where the time goes in v2:
time: 31.3 us; the launch traced here: 31.1 us
  Pallas kernels  12.7 us (41%)
  starting transfers between devices  9.47 us (30%)
  waiting for transfers between devices  7.92 us (25%)
  local copies, waits for them, and re-layouts  0.97 us (3%)
    pallas_call x4, Pallas kernels, attend_next(): pl.pallas_call(functools.partial(next_kernel, tuple(pieces), last, window...  9.09 us
    ppermute x3, starting transfers between devices, shards(): next_on = lax.ppermute(on, 'ctx', onward)  5.98 us
    ppermute x3, waiting for transfers between devices, shards(): next_on = lax.ppermute(on, 'ctx', onward)  5.83 us
    pallas_call x1, Pallas kernels, attend_first(): pl.pallas_call(functools.partial(first_kernel, count, window_rows, cache_...  1.97 us
    ppermute x1, waiting for transfers between devices, shards(): next_back = lax.ppermute(back[stride:], 'ctx', backward)  1.72 us
    ppermute x1, starting transfers between devices, shards(): next_on = lax.ppermute(on[:stride], 'ctx', onward)  1.71 us
    pallas_call x1, Pallas kernels, pack(): pl.pallas_call(pack_kernel, out_shape=jax.ShapeDtypeStruct((rows, win_key...  1.6 us
    ppermute x3, starting transfers between devices, shards(): next_back = lax.ppermute(back, 'ctx', backward)  1.21 us
  transfers between devices with their start and end apart: 8, of which 5 were waited for; matrix products, arithmetic and copies ran while one was open for 0% of the time, Pallas kernels for 26%

profile of v2, /device:TPU:0, one launch (start us, length us, event | category | flops | bytes accessed | tf_op | source)
XLA Modules:
  0.0 31.1 jit_solution(2800454932112813011)
XLA Ops:
  0.0 1.6 %pack.1.packed = bf16[384,256]{1,0:T(8,128)(2,1)} custom-call(bf16[128,256]{1,0:T(8,128)(2,1)} %win_keys.1, bf16[128,256]{1,0:T(8,128)(2,1)} %win_values.1, bf16[64,256]{1,0:T(8,128)(2,1)} %cache_keys.1, bf16[64,256]{1,0:T(8,128)(2,1)} %cache_values.1), custom_call_target="tpu_custom_call" | custom-call | bytes 393216 | tf_op jit(solution)/shard_map/pack/pallas_call | solution.py:63
  1.6 3.0 %collective-permute-start = (bf16[384,256]{1,0:T(8,128)(2,1)}, bf16[384,256]{1,0:T(8,128)(2,1)S(1)}, u32[]{:S(2)}, u32[]{:S(2)}) collective-permute-start(bf16[384,256]{1,0:T(8,128)(2,1)} %pack.1.packed), channel_id=1, source_target_pairs={{2,6},{6,10},{10,14},{14,12},{12,8},{8,4},{4,0},{0,2},{3,7},{7,11}... | collective-permute-start | bytes 589832 | tf_op jit(solution)/shard_map/ppermute | solution.py:278
  4.6 0.1 collective-permute-start.2
  4.8 0.0 copy-start
  4.8 1.0 %copy-done = bf16[384,256]{1,0:T(8,128)(2,1)S(1)} copy-done((bf16[384,256]{1,0:T(8,128)(2,1)S(1)}, bf16[384,256]{1,0:T(8,128)(2,1)}, u32[]{:S(2)}) %copy-start) | copy-done | bytes 196632
  5.7 2.0 %attend_first.1 = (f32[2048,256]{1,0:T(8,128)S(1)}, f32[2048,128]{1,0:T(8,128)S(1)}, bf16[128,2048]{1,0:T(8,128)(2,1)S(1)}, s32[8,128]{1,0:T(8,128)S(1)}) custom-call(s32[8]{0:T(128)} %valid_hbm.1, s32[8]{0:T(128)} %first_hbm.1, bf16[128,2048]{1,0:T(8,128)(2,1)} %q_hbm.1, bf16[384,256]{1,0:T(8,128)(2,1)S(1)} %copy-done), custom_call_target="tpu_custom_call" | custom-call | flops 402653184 | bytes 524288 | tf_op jit(solution)/shard_map/attend_first/pallas_call | solution.py:223
  7.7 2.1 %collective-permute-done.refs_0_.refs_2_ = bf16[384,256]{1,0:T(8,128)(2,1)S(1)} collective-permute-done((bf16[384,256]{1,0:T(8,128)(2,1)}, bf16[384,256]{1,0:T(8,128)(2,1)S(1)}, u32[]{:S(2)}, u32[]{:S(2)}) %collective-permute-start) | collective-permute-done | bytes 196640 | tf_op jit(solution)/shard_map/ppermute | solution.py:278
  9.8 1.7 %collective-permute-start.1 = (bf16[384,256]{1,0:T(8,128)(2,1)S(1)}, bf16[384,256]{1,0:T(8,128)(2,1)S(1)}, u32[]{:S(2)}, u32[]{:S(2)}) collective-permute-start(bf16[384,256]{1,0:T(8,128)(2,1)S(1)} %collective-permute-done.refs_0_.refs_2_), channel_id=1, source_target_pairs={{2,6},{6,10},{10,14},{14,12},{12,8},{8,4},{4,0},{0,2},{3,7},{7,11}... | collective-permute-start | bytes 589832 | tf_op jit(solution)/shard_map/ppermute | solution.py:278
  11.5 0.0 collective-permute-done.2.refs_1_.refs_3_
  11.5 0.4 %collective-permute-start.4 = (bf16[384,256]{1,0:T(8,128)(2,1)S(1)}, bf16[384,256]{1,0:T(8,128)(2,1)S(1)}, u32[]{:S(2)}, u32[]{:S(2)}) collective-permute-start(bf16[384,256]{1,0:T(8,128)(2,1)S(1)} %collective-permute-done.2.refs_1_.refs_3_), channel_id=1, source_target_pairs={{6,2},{10,6},{14,10},{12,14},{8,12},{4,8},{0,4},{2,0},{7,3},{11,7}... | collective-permute-start | bytes 589832 | tf_op jit(solution)/shard_map/ppermute | solution.py:279
  11.8 2.0 %attend_next.3 = (f32[2048,256]{1,0:T(8,128)S(1)}, f32[2048,128]{1,0:T(8,128)S(1)}) custom-call(bf16[128,2048]{1,0:T(8,128)(2,1)S(1)} %get-tuple-element.31.q_ref, s32[8,128]{1,0:T(8,128)S(1)} %get-tuple-element.32.limits, bf16[384,256]{1,0:T(8,128)(2,1)S(1)} %collective-permute-done.refs_0_.refs_2_, ...), custom_call_target="tpu_custom_call" | custom-call | flops 603979776 | bytes 524288 | tf_op jit(solution)/shard_map/attend_next/pallas_call | solution.py:250
  13.8 2.0 %collective-permute-done.1.refs_0_.refs_2_ = bf16[384,256]{1,0:T(8,128)(2,1)S(1)} collective-permute-done((bf16[384,256]{1,0:T(8,128)(2,1)S(1)}, bf16[384,256]{1,0:T(8,128)(2,1)S(1)}, u32[]{:S(2)}, u32[]{:S(2)}) %collective-permute-start.1) | collective-permute-done | bytes 196640 | tf_op jit(solution)/shard_map/ppermute | solution.py:278
  15.9 1.3 %collective-permute-start.3 = (bf16[384,256]{1,0:T(8,128)(2,1)S(1)}, bf16[384,256]{1,0:T(8,128)(2,1)S(1)}, u32[]{:S(2)}, u32[]{:S(2)}) collective-permute-start(bf16[384,256]{1,0:T(8,128)(2,1)S(1)} %collective-permute-done.1.refs_0_.refs_2_), channel_id=1, source_target_pairs={{2,6},{6,10},{10,14},{14,12},{12,8},{8,4},{4,0},{0,2},{3,7},{7,11}... | collective-permute-start | bytes 589832 | tf_op jit(solution)/shard_map/ppermute | solution.py:278
  17.2 0.0 collective-permute-done.4.refs_1_.refs_3_
  17.2 0.7 %collective-permute-start.6 = (bf16[384,256]{1,0:T(8,128)(2,1)S(1)}, bf16[384,256]{1,0:T(8,128)(2,1)S(1)}, u32[]{:S(2)}, u32[]{:S(2)}) collective-permute-start(bf16[384,256]{1,0:T(8,128)(2,1)S(1)} %collective-permute-done.4.refs_1_.refs_3_), channel_id=1, source_target_pairs={{6,2},{10,6},{14,10},{12,14},{8,12},{4,8},{0,4},{2,0},{7,3},{11,7}... | collective-permute-start | bytes 589832 | tf_op jit(solution)/shard_map/ppermute | solution.py:279
  17.9 2.0 %attend_next.4 = (f32[2048,256]{1,0:T(8,128)S(1)}, f32[2048,128]{1,0:T(8,128)S(1)}) custom-call(bf16[128,2048]{1,0:T(8,128)(2,1)S(1)} %get-tuple-element.31.q_ref, s32[8,128]{1,0:T(8,128)S(1)} %get-tuple-element.32.limits, bf16[384,256]{1,0:T(8,128)(2,1)S(1)} %collective-permute-done.1.refs_0_.refs_2_, ...), custom_call_target="tpu_custom_call" | custom-call | flops 603979776 | bytes 524288 | tf_op jit(solution)/shard_map/attend_next/pallas_call | solution.py:250
  19.9 1.7 %collective-permute-done.3.refs_0_.refs_2_ = bf16[384,256]{1,0:T(8,128)(2,1)S(1)} collective-permute-done((bf16[384,256]{1,0:T(8,128)(2,1)S(1)}, bf16[384,256]{1,0:T(8,128)(2,1)S(1)}, u32[]{:S(2)}, u32[]{:S(2)}) %collective-permute-start.3) | collective-permute-done | bytes 196640 | tf_op jit(solution)/shard_map/ppermute | solution.py:278
  21.6 1.7 %collective-permute-start.5 = (bf16[192,256]{1,0:T(8,128)(2,1)S(1)}, bf16[192,256]{1,0:T(8,128)(2,1)S(1)}, u32[]{:S(2)}, u32[]{:S(2)}) collective-permute-start(bf16[192,256]{1,0:T(8,128)(2,1)S(1)} %slice.6), channel_id=1, source_target_pairs={{2,6},{6,10},{10,14},{14,12},{12,8},{8,4},{4,0},{0,2},{3,7},{7,11}... | collective-permute-start | bytes 294920 | tf_op jit(solution)/shard_map/ppermute | solution.py:281
  23.3 0.0 collective-permute-done.6.refs_1_.refs_3_
  23.4 0.6 %collective-permute-start.7 = (bf16[192,256]{1,0:T(8,128)(2,1)S(1)}, bf16[192,256]{1,0:T(8,128)(2,1)S(1)}, u32[]{:S(2)}, u32[]{:S(2)}) collective-permute-start(bf16[192,256]{1,0:T(8,128)(2,1)S(1)} %slice.7), channel_id=1, source_target_pairs={{6,2},{10,6},{14,10},{12,14},{8,12},{4,8},{0,4},{2,0},{7,3},{11,7}... | collective-permute-start | bytes 294920 | tf_op jit(solution)/shard_map/ppermute | solution.py:282
  23.9 2.0 %attend_next.5 = (f32[2048,256]{1,0:T(8,128)S(1)}, f32[2048,128]{1,0:T(8,128)S(1)}) custom-call(bf16[128,2048]{1,0:T(8,128)(2,1)S(1)} %get-tuple-element.31.q_ref, s32[8,128]{1,0:T(8,128)S(1)} %get-tuple-element.32.limits, bf16[384,256]{1,0:T(8,128)(2,1)S(1)} %collective-permute-done.3.refs_0_.refs_2_, ...), custom_call_target="tpu_custom_call" | custom-call | flops 603979776 | bytes 524288 | tf_op jit(solution)/shard_map/attend_next/pallas_call | solution.py:250
  25.9 0.4 %collective-permute-done.5.refs_0_ = bf16[192,256]{1,0:T(8,128)(2,1)S(1)} collective-permute-done((bf16[192,256]{1,0:T(8,128)(2,1)S(1)}, bf16[192,256]{1,0:T(8,128)(2,1)S(1)}, u32[]{:S(2)}, u32[]{:S(2)}) %collective-permute-start.5) | collective-permute-done | bytes 98336 | tf_op jit(solution)/shard_map/ppermute | solution.py:281
  26.3 1.7 %collective-permute-done.7.refs_1_ = bf16[192,256]{1,0:T(8,128)(2,1)S(1)} collective-permute-done((bf16[192,256]{1,0:T(8,128)(2,1)S(1)}, bf16[192,256]{1,0:T(8,128)(2,1)S(1)}, u32[]{:S(2)}, u32[]{:S(2)}) %collective-permute-start.7) | collective-permute-done | bytes 98336 | tf_op jit(solution)/shard_map/ppermute | solution.py:282
  28.0 3.1 %attend_last.1 = bf16[128,2048]{1,0:T(8,128)(2,1)} custom-call(bf16[128,2048]{1,0:T(8,128)(2,1)S(1)} %get-tuple-element.31.q_ref, s32[8,128]{1,0:T(8,128)S(1)} %get-tuple-element.32.limits, bf16[192,256]{1,0:T(8,128)(2,1)S(1)} %collective-permute-done.5.refs_0_, bf16[192,256]{1,0:T(8,128)(2,1)S(1)} %collective-permute-done.7.refs_1_, ...), custom_call_target="tpu_custom_call" | custom-call | flops 402653184 | bytes 524288 | tf_op jit(solution)/shard_map/attend_last/pallas_call | solution.py:250
  (2 shorter events, 0.0 us)
Async XLA Ops:
  1.6 8.2 %collective-permute-start = (bf16[384,256]{1,0:T(8,128)(2,1)}, bf16[384,256]{1,0:T(8,128)(2,1)S(1)}, u32[]{:S(2)}, u32[]{:S(2)}) collective-permute-start(bf16[384,256]{1,0:T(8,128)(2,1)} %pack.1.packed), channel_id=1, source_target_pairs={{2,6},{6,10},{10,14},{14,12},{12,8},{8,4},{4,0},{0,2},{3,7},{7,11}... | collective-permute-start | bytes 589832 | tf_op jit(solution)/shard_map/ppermute | solution.py:278
  4.6 6.9 %collective-permute-start.2 = (bf16[384,256]{1,0:T(8,128)(2,1)}, bf16[384,256]{1,0:T(8,128)(2,1)S(1)}, u32[]{:S(2)}, u32[]{:S(2)}) collective-permute-start(bf16[384,256]{1,0:T(8,128)(2,1)} %pack.1.packed), channel_id=1, source_target_pairs={{6,2},{10,6},{14,10},{12,14},{8,12},{4,8},{0,4},{2,0},{7,3},{11,7}... | collective-permute-start | bytes 589832 | tf_op jit(solution)/shard_map/ppermute | solution.py:279
  4.8 1.0 %copy-start = (bf16[384,256]{1,0:T(8,128)(2,1)S(1)}, bf16[384,256]{1,0:T(8,128)(2,1)}, u32[]{:S(2)}) copy-start(bf16[384,256]{1,0:T(8,128)(2,1)} %pack.1.packed) | copy-start | bytes 589828
  9.8 6.1 %collective-permute-start.1 = (bf16[384,256]{1,0:T(8,128)(2,1)S(1)}, bf16[384,256]{1,0:T(8,128)(2,1)S(1)}, u32[]{:S(2)}, u32[]{:S(2)}) collective-permute-start(bf16[384,256]{1,0:T(8,128)(2,1)S(1)} %collective-permute-done.refs_0_.refs_2_), channel_id=1, source_target_pairs={{2,6},{6,10},{10,14},{14,12},{12,8},{8,4},{4,0},{0,2},{3,7},{7,11}... | collective-permute-start | bytes 589832 | tf_op jit(solution)/shard_map/ppermute | solution.py:278
  11.5 5.8 %collective-permute-start.4 = (bf16[384,256]{1,0:T(8,128)(2,1)S(1)}, bf16[384,256]{1,0:T(8,128)(2,1)S(1)}, u32[]{:S(2)}, u32[]{:S(2)}) collective-permute-start(bf16[384,256]{1,0:T(8,128)(2,1)S(1)} %collective-permute-done.2.refs_1_.refs_3_), channel_id=1, source_target_pairs={{6,2},{10,6},{14,10},{12,14},{8,12},{4,8},{0,4},{2,0},{7,3},{11,7}... | collective-permute-start | bytes 589832 | tf_op jit(solution)/shard_map/ppermute | solution.py:279
  15.9 5.7 %collective-permute-start.3 = (bf16[384,256]{1,0:T(8,128)(2,1)S(1)}, bf16[384,256]{1,0:T(8,128)(2,1)S(1)}, u32[]{:S(2)}, u32[]{:S(2)}) collective-permute-start(bf16[384,256]{1,0:T(8,128)(2,1)S(1)} %collective-permute-done.1.refs_0_.refs_2_), channel_id=1, source_target_pairs={{2,6},{6,10},{10,14},{14,12},{12,8},{8,4},{4,0},{0,2},{3,7},{7,11}... | collective-permute-start | bytes 589832 | tf_op jit(solution)/shard_map/ppermute | solution.py:278
  17.2 6.1 %collective-permute-start.6 = (bf16[384,256]{1,0:T(8,128)(2,1)S(1)}, bf16[384,256]{1,0:T(8,128)(2,1)S(1)}, u32[]{:S(2)}, u32[]{:S(2)}) collective-permute-start(bf16[384,256]{1,0:T(8,128)(2,1)S(1)} %collective-permute-done.4.refs_1_.refs_3_), channel_id=1, source_target_pairs={{6,2},{10,6},{14,10},{12,14},{8,12},{4,8},{0,4},{2,0},{7,3},{11,7}... | collective-permute-start | bytes 589832 | tf_op jit(solution)/shard_map/ppermute | solution.py:279
  21.6 4.7 %collective-permute-start.5 = (bf16[192,256]{1,0:T(8,128)(2,1)S(1)}, bf16[192,256]{1,0:T(8,128)(2,1)S(1)}, u32[]{:S(2)}, u32[]{:S(2)}) collective-permute-start(bf16[192,256]{1,0:T(8,128)(2,1)S(1)} %slice.6), channel_id=1, source_target_pairs={{2,6},{6,10},{10,14},{14,12},{12,8},{8,4},{4,0},{0,2},{3,7},{7,11}... | collective-permute-start | bytes 294920 | tf_op jit(solution)/shard_map/ppermute | solution.py:281
  23.4 4.7 %collective-permute-start.7 = (bf16[192,256]{1,0:T(8,128)(2,1)S(1)}, bf16[192,256]{1,0:T(8,128)(2,1)S(1)}, u32[]{:S(2)}, u32[]{:S(2)}) collective-permute-start(bf16[192,256]{1,0:T(8,128)(2,1)S(1)} %slice.7), channel_id=1, source_target_pairs={{6,2},{10,6},{14,10},{12,14},{8,12},{4,8},{0,4},{2,0},{7,3},{11,7}... | collective-permute-start | bytes 294920 | tf_op jit(solution)/shard_map/ppermute | solution.py:282

commit v3 on v2

--- a/solution.py
+++ b/solution.py
@@ -12,6 +12,7 @@
 EXP_SCALE = HD**-0.5 * math.log2(math.e)
 HIDDEN = -1.0e30
 CHUNK_HEADS = 4
+LARGEST_TOTAL = 2.0**100
 
 
 def ring_width(count):
@@ -66,6 +67,7 @@
         in_specs=[pl.BlockSpec(memory_space=pltpu.HBM)] * 4,
         out_specs=pl.BlockSpec(memory_space=pltpu.VMEM),
         scratch_shapes=[pltpu.SemaphoreType.DMA((4,))],
+        compiler_params=pltpu.CompilerParams(vmem_limit_bytes=4 * 1024 * 1024),
         cost_estimate=pl.CostEstimate(flops=0, bytes_accessed=4 * rows * win_keys.shape[1], transcendentals=0),
         name="pack",
     )(win_keys, win_values, cache_keys, cache_values)
@@ -112,20 +114,24 @@
             values[head, filled:, :] = jnp.zeros((total_keys - filled, 2 * HD), jnp.bfloat16)
 
 
-def absorb(query, keys, values, bias, before, acc_before):
-    score = lax.dot_general(query, keys, (((1,), (1,)), ((), ())), preferred_element_type=jnp.float32)
-    if bias is not None:
-        width = bias.shape[1]
-        score = jnp.concatenate([score[:, :width] + bias, score[:, width:]], axis=1)
-    top = jnp.max(score, axis=1, keepdims=True)
-    if before is not None:
-        top = jnp.maximum(before[:, :1], top)
-    weight = jnp.exp2((score - top) * EXP_SCALE).astype(jnp.bfloat16)
-    acc = jnp.dot(weight, values, preferred_element_type=jnp.float32)
-    if before is not None:
-        fade = jnp.exp2((before - top) * EXP_SCALE)
-        acc = acc + acc_before * jnp.concatenate([fade, fade], axis=1)
-    return top, acc
+def scores(query, keys):
+    return lax.dot_general(query, keys, (((1,), (1,)), ((), ())), preferred_element_type=jnp.float32)
+
+
+def weigh(score, top, values):
+    lanes = score.shape[1] // HD
+    weight = jnp.exp2(score * EXP_SCALE - jnp.concatenate([top] * lanes, axis=1)).astype(jnp.bfloat16)
+    return jnp.dot(weight, values, preferred_element_type=jnp.float32)
+
+
+def wide_top(score):
+    return jnp.broadcast_to(jnp.max(score, axis=1, keepdims=True) * EXP_SCALE, (score.shape[0], HD))
+
+
+def normalised(acc):
+    total = acc[:, HD:]
+    inverse = pl.reciprocal(total, approx=True)
+    return (acc[:, :HD] * (inverse * (2.0 - total * inverse))).astype(jnp.bfloat16)
 
 
 def chunks(q_ref, kv_heads):
@@ -170,26 +176,63 @@
     seen = (key_iota <= query_iota) & (key_iota < valid_ref[me])
     bias = jnp.concatenate([jnp.where(seen, 0.0, HIDDEN)] * CHUNK_HEADS, axis=0)
     for head, at, query, _ in chunks(q_ref, keys.shape[0]):
-        top, acc = absorb(query, keys[head], values[head], bias, None, None)
-        acc_out[at, :] = acc
-        top_out[at, :] = jnp.broadcast_to(top, (top.shape[0], HD))
+        score = scores(query, keys[head])
+        score = jnp.concatenate([score[:, :window_rows] + bias, score[:, window_rows:]], axis=1)
+        top = wide_top(score)
+        acc_out[at, :] = weigh(score, top, values[head])
+        top_out[at, :] = top
 
 
 def next_kernel(pieces, last, window_rows, cache_rows, q_ref, limits, *refs):
     number = len(pieces)
     key_refs, value_refs = refs[:number], refs[number : 2 * number]
-    acc_in, top_in, *outs, keys, values = refs[2 * number :]
+    if last:
+        acc_in, top_in, out, keys, values, result, sems = refs[2 * number :]
+    else:
+        acc_in, top_in, acc_out, top_out, keys, values = refs[2 * number :]
     place_pieces(pieces, False, window_rows, cache_rows, limits, key_refs, value_refs, keys, values)
     rows = q_ref.shape[0]
-    for head, at, query, base in chunks(q_ref, keys.shape[0]):
-        top, acc = absorb(query, keys[head], values[head], None, top_in[at, :], acc_in[at, :])
+    kv_heads = keys.shape[0]
+
+    def sent(base):
+        lanes = slice(base * HD, (base + CHUNK_HEADS) * HD)
+        return pltpu.make_async_copy(result.at[:, lanes], out.at[:, lanes], sems.at[base // CHUNK_HEADS])
+
+    def settle(base, acc):
+        done = normalised(acc)
+        for i in range(CHUNK_HEADS):
+            result[:, (base + i) * HD : (base + i + 1) * HD] = done[i * rows : (i + 1) * rows]
+        sent(base).start()
+
+    fine = jnp.ones((8, HD), jnp.float32)
+    for head, at, query, base in chunks(q_ref, kv_heads):
+        top = top_in[at, :]
+        acc = acc_in[at, :] + weigh(scores(query, keys[head]), top, values[head])
+        safe = jnp.where(acc[:, HD:] < LARGEST_TOTAL, 1.0, 0.0).reshape(-1, 8, HD)
+        fine = jnp.minimum(fine, jnp.min(safe, axis=0))
         if last:
-            result = (acc[:, :HD] / acc[:, HD:]).astype(jnp.bfloat16)
-            for i in range(CHUNK_HEADS):
-                outs[0][:, (base + i) * HD : (base + i + 1) * HD] = result[i * rows : (i + 1) * rows]
+            settle(base, acc)
         else:
-            outs[0][at, :] = acc
-            outs[1][at, :] = jnp.broadcast_to(top, (top.shape[0], HD))
+            acc_out[at, :] = acc
+            top_out[at, :] = top
+    if last:
+        for base in range(0, kv_heads * (q_ref.shape[1] // HD // kv_heads), CHUNK_HEADS):
+            sent(base).wait()
+
+    @pl.when(jnp.min(fine) < 0.5)
+    def _():
+        for head, at, query, base in chunks(q_ref, kv_heads):
+            score = scores(query, keys[head])
+            before = top_in[at, :]
+            top = jnp.maximum(before, wide_top(score))
+            fade = jnp.exp2(before - top)
+            acc = acc_in[at, :] * jnp.concatenate([fade, fade], axis=1) + weigh(score, top, values[head])
+            if last:
+                settle(base, acc)
+                sent(base).wait()
+            else:
+                acc_out[at, :] = acc
+                top_out[at, :] = top
 
 
 def kernel_options(queries, total_keys, kv_heads):
@@ -247,12 +290,16 @@
     vmem = pl.BlockSpec(memory_space=pltpu.VMEM)
     operands = [queries, limits, *keys, *values, *state]
     shapes = [jax.ShapeDtypeStruct(queries.shape, queries.dtype)] if last else state_shapes(queries)
+    scratch = room(kv_heads, total_keys)
+    if last:
+        chunk_count = queries.shape[1] // HD // CHUNK_HEADS
+        scratch += [pltpu.VMEM(queries.shape, queries.dtype), pltpu.SemaphoreType.DMA((chunk_count,))]
     outs = pl.pallas_call(
         functools.partial(next_kernel, tuple(pieces), last, window_rows, cache_rows),
         out_shape=shapes,
         in_specs=[vmem] * len(operands),
-        out_specs=[vmem] * len(shapes),
-        scratch_shapes=room(kv_heads, total_keys),
+        out_specs=[pl.BlockSpec(memory_space=pltpu.HBM)] if last else [vmem] * len(shapes),
+        scratch_shapes=scratch,
         name="attend_last" if last else "attend_next",
         **kernel_options(queries, total_keys, kv_heads),
     )(*operands)

time: 31.3 us -> 29 us (0.927)
  Pallas kernels: 12.7 us -> 8.8 us
  waiting for transfers between devices: 7.92 us -> 10.5 us
  local copies, waits for them, and re-layouts: 0.97 us -> 0.01 us
    pallas_call x4, Pallas kernels: 9.09 us -> 5.9 us  [attend_next(): pl.pallas_call(functools.partial(next_kernel, tuple(pieces), last, window...]
    ppermute x3, waiting for transfers between devices: 5.83 us -> 7.78 us  [shards(): next_on = lax.ppermute(on, 'ctx', onward)]
    unnamed x2 -> x0, local copies, waits for them, and re-layouts: 0.96 us -> none
    pallas_call x1, Pallas kernels: 1.6 us -> 0.93 us  [pack(): pl.pallas_call(pack_kernel, out_shape=jax.ShapeDtypeStruct((rows, win_key...]
    ppermute x1, waiting for transfers between devices: 0.35 us -> 0.96 us  [shards(): next_on = lax.ppermute(on[:stride], 'ctx', onward)]
  transfers between devices with their start and end apart: 8 -> 8, of which waited for: 5 -> 5; matrix products, arithmetic and copies ran while one was open for 0% -> 0% of each run, Pallas kernels for 26% -> 22%
where the time goes in v3:
time: 29 us; the launch traced here: 28.8 us
  waiting for transfers between devices  10.5 us (36%)
  starting transfers between devices  9.48 us (33%)
  Pallas kernels  8.8 us (30%)
    ppermute x3, waiting for transfers between devices, shards(): next_on = lax.ppermute(on, 'ctx', onward)  7.78 us
    ppermute x3, starting transfers between devices, shards(): next_on = lax.ppermute(on, 'ctx', onward)  5.98 us
    pallas_call x4, Pallas kernels, attend_next(): pl.pallas_call(functools.partial(next_kernel, tuple(pieces), last, window...  5.9 us
    pallas_call x1, Pallas kernels, attend_first(): pl.pallas_call(functools.partial(first_kernel, count, window_rows, cache_...  1.97 us
    ppermute x1, waiting for transfers between devices, shards(): next_back = lax.ppermute(back[stride:], 'ctx', backward)  1.72 us
    ppermute x1, starting transfers between devices, shards(): next_on = lax.ppermute(on[:stride], 'ctx', onward)  1.71 us
    ppermute x3, starting transfers between devices, shards(): next_back = lax.ppermute(back, 'ctx', backward)  1.21 us
    ppermute x1, waiting for transfers between devices, shards(): next_on = lax.ppermute(on[:stride], 'ctx', onward)  0.96 us
  transfers between devices with their start and end apart: 8, of which 5 were waited for; matrix products, arithmetic and copies ran while one was open for 0% of the time, Pallas kernels for 22%

profile of v3, /device:TPU:0, one launch (start us, length us, event | category | flops | bytes accessed | tf_op | source)
XLA Modules:
  0.0 28.8 jit_solution(15466197195867492455)
XLA Ops:
  0.0 0.9 %pack.1.packed = bf16[384,256]{1,0:T(8,128)(2,1)S(1)} custom-call(bf16[128,256]{1,0:T(8,128)(2,1)} %win_keys.1, bf16[128,256]{1,0:T(8,128)(2,1)} %win_values.1, bf16[64,256]{1,0:T(8,128)(2,1)} %cache_keys.1, bf16[64,256]{1,0:T(8,128)(2,1)} %cache_values.1), custom_call_target="tpu_custom_call" | custom-call | bytes 393216 | tf_op jit(solution)/shard_map/pack/pallas_call | solution.py:64
  0.9 3.0 %collective-permute-start = (bf16[384,256]{1,0:T(8,128)(2,1)S(1)}, bf16[384,256]{1,0:T(8,128)(2,1)S(1)}, u32[]{:S(2)}, u32[]{:S(2)}) collective-permute-start(bf16[384,256]{1,0:T(8,128)(2,1)S(1)} %pack.1.packed), channel_id=1, source_target_pairs={{2,6},{6,10},{10,14},{14,12},{12,8},{8,4},{4,0},{0,2},{3,7},{7,11}... | collective-permute-start | bytes 589832 | tf_op jit(solution)/shard_map/ppermute | solution.py:325
  3.9 0.2 collective-permute-start.2
  4.1 2.0 %attend_first.1 = (f32[2048,256]{1,0:T(8,128)S(1)}, f32[2048,128]{1,0:T(8,128)S(1)}, bf16[128,2048]{1,0:T(8,128)(2,1)S(1)}, s32[8,128]{1,0:T(8,128)S(1)}) custom-call(s32[8]{0:T(128)} %valid_hbm.1, s32[8]{0:T(128)} %first_hbm.1, bf16[128,2048]{1,0:T(8,128)(2,1)} %q_hbm.1, bf16[384,256]{1,0:T(8,128)(2,1)S(1)} %pack.1.packed), custom_call_target="tpu_custom_call" | custom-call | flops 402653184 | bytes 524288 | tf_op jit(solution)/shard_map/attend_first/pallas_call | solution.py:266
  6.1 2.9 %collective-permute-done.refs_0_.refs_2_ = bf16[384,256]{1,0:T(8,128)(2,1)S(1)} collective-permute-done((bf16[384,256]{1,0:T(8,128)(2,1)S(1)}, bf16[384,256]{1,0:T(8,128)(2,1)S(1)}, u32[]{:S(2)}, u32[]{:S(2)}) %collective-permute-start) | collective-permute-done | bytes 196640 | tf_op jit(solution)/shard_map/ppermute | solution.py:325
  8.9 1.7 %collective-permute-start.1 = (bf16[384,256]{1,0:T(8,128)(2,1)S(1)}, bf16[384,256]{1,0:T(8,128)(2,1)S(1)}, u32[]{:S(2)}, u32[]{:S(2)}) collective-permute-start(bf16[384,256]{1,0:T(8,128)(2,1)S(1)} %collective-permute-done.refs_0_.refs_2_), channel_id=1, source_target_pairs={{2,6},{6,10},{10,14},{14,12},{12,8},{8,4},{4,0},{0,2},{3,7},{7,11}... | collective-permute-start | bytes 589832 | tf_op jit(solution)/shard_map/ppermute | solution.py:325
  10.6 0.0 collective-permute-done.2.refs_1_.refs_3_
  10.6 0.4 %collective-permute-start.4 = (bf16[384,256]{1,0:T(8,128)(2,1)S(1)}, bf16[384,256]{1,0:T(8,128)(2,1)S(1)}, u32[]{:S(2)}, u32[]{:S(2)}) collective-permute-start(bf16[384,256]{1,0:T(8,128)(2,1)S(1)} %collective-permute-done.2.refs_1_.refs_3_), channel_id=1, source_target_pairs={{6,2},{10,6},{14,10},{12,14},{8,12},{4,8},{0,4},{2,0},{7,3},{11,7}... | collective-permute-start | bytes 589832 | tf_op jit(solution)/shard_map/ppermute | solution.py:326
  10.9 1.4 %attend_next.3 = (f32[2048,256]{1,0:T(8,128)S(1)}, f32[2048,128]{1,0:T(8,128)S(1)}) custom-call(bf16[128,2048]{1,0:T(8,128)(2,1)S(1)} %get-tuple-element.31.q_ref, s32[8,128]{1,0:T(8,128)S(1)} %get-tuple-element.32.limits, bf16[384,256]{1,0:T(8,128)(2,1)S(1)} %collective-permute-done.refs_0_.refs_2_, ...), custom_call_target="tpu_custom_call" | custom-call | flops 603979776 | bytes 524288 | tf_op jit(solution)/shard_map/attend_next/pallas_call | solution.py:297
  12.4 2.6 %collective-permute-done.1.refs_0_.refs_2_ = bf16[384,256]{1,0:T(8,128)(2,1)S(1)} collective-permute-done((bf16[384,256]{1,0:T(8,128)(2,1)S(1)}, bf16[384,256]{1,0:T(8,128)(2,1)S(1)}, u32[]{:S(2)}, u32[]{:S(2)}) %collective-permute-start.1) | collective-permute-done | bytes 196640 | tf_op jit(solution)/shard_map/ppermute | solution.py:325
  15.0 1.3 %collective-permute-start.3 = (bf16[384,256]{1,0:T(8,128)(2,1)S(1)}, bf16[384,256]{1,0:T(8,128)(2,1)S(1)}, u32[]{:S(2)}, u32[]{:S(2)}) collective-permute-start(bf16[384,256]{1,0:T(8,128)(2,1)S(1)} %collective-permute-done.1.refs_0_.refs_2_), channel_id=1, source_target_pairs={{2,6},{6,10},{10,14},{14,12},{12,8},{8,4},{4,0},{0,2},{3,7},{7,11}... | collective-permute-start | bytes 589832 | tf_op jit(solution)/shard_map/ppermute | solution.py:325
  16.3 0.0 collective-permute-done.4.refs_1_.refs_3_
  16.3 0.7 %collective-permute-start.6 = (bf16[384,256]{1,0:T(8,128)(2,1)S(1)}, bf16[384,256]{1,0:T(8,128)(2,1)S(1)}, u32[]{:S(2)}, u32[]{:S(2)}) collective-permute-start(bf16[384,256]{1,0:T(8,128)(2,1)S(1)} %collective-permute-done.4.refs_1_.refs_3_), channel_id=1, source_target_pairs={{6,2},{10,6},{14,10},{12,14},{8,12},{4,8},{0,4},{2,0},{7,3},{11,7}... | collective-permute-start | bytes 589832 | tf_op jit(solution)/shard_map/ppermute | solution.py:326
  17.0 1.4 %attend_next.4 = (f32[2048,256]{1,0:T(8,128)S(1)}, f32[2048,128]{1,0:T(8,128)S(1)}) custom-call(bf16[128,2048]{1,0:T(8,128)(2,1)S(1)} %get-tuple-element.31.q_ref, s32[8,128]{1,0:T(8,128)S(1)} %get-tuple-element.32.limits, bf16[384,256]{1,0:T(8,128)(2,1)S(1)} %collective-permute-done.1.refs_0_.refs_2_, ...), custom_call_target="tpu_custom_call" | custom-call | flops 603979776 | bytes 524288 | tf_op jit(solution)/shard_map/attend_next/pallas_call | solution.py:297
  18.4 2.3 %collective-permute-done.3.refs_0_.refs_2_ = bf16[384,256]{1,0:T(8,128)(2,1)S(1)} collective-permute-done((bf16[384,256]{1,0:T(8,128)(2,1)S(1)}, bf16[384,256]{1,0:T(8,128)(2,1)S(1)}, u32[]{:S(2)}, u32[]{:S(2)}) %collective-permute-start.3) | collective-permute-done | bytes 196640 | tf_op jit(solution)/shard_map/ppermute | solution.py:325
  20.7 1.7 %collective-permute-start.5 = (bf16[192,256]{1,0:T(8,128)(2,1)S(1)}, bf16[192,256]{1,0:T(8,128)(2,1)S(1)}, u32[]{:S(2)}, u32[]{:S(2)}) collective-permute-start(bf16[192,256]{1,0:T(8,128)(2,1)S(1)} %slice.6), channel_id=1, source_target_pairs={{2,6},{6,10},{10,14},{14,12},{12,8},{8,4},{4,0},{0,2},{3,7},{7,11}... | collective-permute-start | bytes 294920 | tf_op jit(solution)/shard_map/ppermute | solution.py:328
  22.5 0.0 collective-permute-done.6.refs_1_.refs_3_
  22.5 0.6 %collective-permute-start.7 = (bf16[192,256]{1,0:T(8,128)(2,1)S(1)}, bf16[192,256]{1,0:T(8,128)(2,1)S(1)}, u32[]{:S(2)}, u32[]{:S(2)}) collective-permute-start(bf16[192,256]{1,0:T(8,128)(2,1)S(1)} %slice.7), channel_id=1, source_target_pairs={{6,2},{10,6},{14,10},{12,14},{8,12},{4,8},{0,4},{2,0},{7,3},{11,7}... | collective-permute-start | bytes 294920 | tf_op jit(solution)/shard_map/ppermute | solution.py:329
  23.0 1.4 %attend_next.5 = (f32[2048,256]{1,0:T(8,128)S(1)}, f32[2048,128]{1,0:T(8,128)S(1)}) custom-call(bf16[128,2048]{1,0:T(8,128)(2,1)S(1)} %get-tuple-element.31.q_ref, s32[8,128]{1,0:T(8,128)S(1)} %get-tuple-element.32.limits, bf16[384,256]{1,0:T(8,128)(2,1)S(1)} %collective-permute-done.3.refs_0_.refs_2_, ...), custom_call_target="tpu_custom_call" | custom-call | flops 603979776 | bytes 524288 | tf_op jit(solution)/shard_map/attend_next/pallas_call | solution.py:297
  24.5 1.0 %collective-permute-done.5.refs_0_ = bf16[192,256]{1,0:T(8,128)(2,1)S(1)} collective-permute-done((bf16[192,256]{1,0:T(8,128)(2,1)S(1)}, bf16[192,256]{1,0:T(8,128)(2,1)S(1)}, u32[]{:S(2)}, u32[]{:S(2)}) %collective-permute-start.5) | collective-permute-done | bytes 98336 | tf_op jit(solution)/shard_map/ppermute | solution.py:328
  25.4 1.7 %collective-permute-done.7.refs_1_ = bf16[192,256]{1,0:T(8,128)(2,1)S(1)} collective-permute-done((bf16[192,256]{1,0:T(8,128)(2,1)S(1)}, bf16[192,256]{1,0:T(8,128)(2,1)S(1)}, u32[]{:S(2)}, u32[]{:S(2)}) %collective-permute-start.7) | collective-permute-done | bytes 98336 | tf_op jit(solution)/shard_map/ppermute | solution.py:329
  27.1 1.7 %attend_last.1 = bf16[128,2048]{1,0:T(8,128)(2,1)} custom-call(bf16[128,2048]{1,0:T(8,128)(2,1)S(1)} %get-tuple-element.31.q_ref, s32[8,128]{1,0:T(8,128)S(1)} %get-tuple-element.32.limits, bf16[192,256]{1,0:T(8,128)(2,1)S(1)} %collective-permute-done.5.refs_0_, bf16[192,256]{1,0:T(8,128)(2,1)S(1)} %collective-permute-done.7.refs_1_, ...), custom_call_target="tpu_custom_call" | custom-call | flops 402653184 | bytes 524288 | tf_op jit(solution)/shard_map/attend_last/pallas_call | solution.py:297
  (2 shorter events, 0.0 us)
Async XLA Ops:
  0.9 8.0 %collective-permute-start = (bf16[384,256]{1,0:T(8,128)(2,1)S(1)}, bf16[384,256]{1,0:T(8,128)(2,1)S(1)}, u32[]{:S(2)}, u32[]{:S(2)}) collective-permute-start(bf16[384,256]{1,0:T(8,128)(2,1)S(1)} %pack.1.packed), channel_id=1, source_target_pairs={{2,6},{6,10},{10,14},{14,12},{12,8},{8,4},{4,0},{0,2},{3,7},{7,11}... | collective-permute-start | bytes 589832 | tf_op jit(solution)/shard_map/ppermute | solution.py:325
  3.9 6.6 %collective-permute-start.2 = (bf16[384,256]{1,0:T(8,128)(2,1)S(1)}, bf16[384,256]{1,0:T(8,128)(2,1)S(1)}, u32[]{:S(2)}, u32[]{:S(2)}) collective-permute-start(bf16[384,256]{1,0:T(8,128)(2,1)S(1)} %pack.1.packed), channel_id=1, source_target_pairs={{6,2},{10,6},{14,10},{12,14},{8,12},{4,8},{0,4},{2,0},{7,3},{11,7}... | collective-permute-start | bytes 589832 | tf_op jit(solution)/shard_map/ppermute | solution.py:326
  8.9 6.1 %collective-permute-start.1 = (bf16[384,256]{1,0:T(8,128)(2,1)S(1)}, bf16[384,256]{1,0:T(8,128)(2,1)S(1)}, u32[]{:S(2)}, u32[]{:S(2)}) collective-permute-start(bf16[384,256]{1,0:T(8,128)(2,1)S(1)} %collective-permute-done.refs_0_.refs_2_), channel_id=1, source_target_pairs={{2,6},{6,10},{10,14},{14,12},{12,8},{8,4},{4,0},{0,2},{3,7},{7,11}... | collective-permute-start | bytes 589832 | tf_op jit(solution)/shard_map/ppermute | solution.py:325
  10.6 5.8 %collective-permute-start.4 = (bf16[384,256]{1,0:T(8,128)(2,1)S(1)}, bf16[384,256]{1,0:T(8,128)(2,1)S(1)}, u32[]{:S(2)}, u32[]{:S(2)}) collective-permute-start(bf16[384,256]{1,0:T(8,128)(2,1)S(1)} %collective-permute-done.2.refs_1_.refs_3_), channel_id=1, source_target_pairs={{6,2},{10,6},{14,10},{12,14},{8,12},{4,8},{0,4},{2,0},{7,3},{11,7}... | collective-permute-start | bytes 589832 | tf_op jit(solution)/shard_map/ppermute | solution.py:326
  15.0 5.7 %collective-permute-start.3 = (bf16[384,256]{1,0:T(8,128)(2,1)S(1)}, bf16[384,256]{1,0:T(8,128)(2,1)S(1)}, u32[]{:S(2)}, u32[]{:S(2)}) collective-permute-start(bf16[384,256]{1,0:T(8,128)(2,1)S(1)} %collective-permute-done.1.refs_0_.refs_2_), channel_id=1, source_target_pairs={{2,6},{6,10},{10,14},{14,12},{12,8},{8,4},{4,0},{0,2},{3,7},{7,11}... | collective-permute-start | bytes 589832 | tf_op jit(solution)/shard_map/ppermute | solution.py:325
  16.3 6.1 %collective-permute-start.6 = (bf16[384,256]{1,0:T(8,128)(2,1)S(1)}, bf16[384,256]{1,0:T(8,128)(2,1)S(1)}, u32[]{:S(2)}, u32[]{:S(2)}) collective-permute-start(bf16[384,256]{1,0:T(8,128)(2,1)S(1)} %collective-permute-done.4.refs_1_.refs_3_), channel_id=1, source_target_pairs={{6,2},{10,6},{14,10},{12,14},{8,12},{4,8},{0,4},{2,0},{7,3},{11,7}... | collective-permute-start | bytes 589832 | tf_op jit(solution)/shard_map/ppermute | solution.py:326
  20.7 4.7 %collective-permute-start.5 = (bf16[192,256]{1,0:T(8,128)(2,1)S(1)}, bf16[192,256]{1,0:T(8,128)(2,1)S(1)}, u32[]{:S(2)}, u32[]{:S(2)}) collective-permute-start(bf16[192,256]{1,0:T(8,128)(2,1)S(1)} %slice.6), channel_id=1, source_target_pairs={{2,6},{6,10},{10,14},{14,12},{12,8},{8,4},{4,0},{0,2},{3,7},{7,11}... | collective-permute-start | bytes 294920 | tf_op jit(solution)/shard_map/ppermute | solution.py:328
  22.5 4.7 %collective-permute-start.7 = (bf16[192,256]{1,0:T(8,128)(2,1)S(1)}, bf16[192,256]{1,0:T(8,128)(2,1)S(1)}, u32[]{:S(2)}, u32[]{:S(2)}) collective-permute-start(bf16[192,256]{1,0:T(8,128)(2,1)S(1)} %slice.7), channel_id=1, source_target_pairs={{6,2},{10,6},{14,10},{12,14},{8,12},{4,8},{0,4},{2,0},{7,3},{11,7}... | collective-permute-start | bytes 294920 | tf_op jit(solution)/shard_map/ppermute | solution.py:329

commit v4 on v3

--- a/solution.py
+++ b/solution.py
@@ -165,8 +165,9 @@
     me = lax.axis_index("ctx")
     position = position_of(me, count)
     first = first_ref[me]
+    sign = 1 - 2 * lax.rem(lax.axis_index("tp"), 2)
     for row, offset in enumerate(ring_offsets(count)):
-        place = place_at(lax.rem(position + offset + count, count), count)
+        place = place_at(lax.rem(position + sign * offset + count, count), count)
         limit = jnp.where((place >= first) & (place <= me), valid_ref[place], 0)
         limits[row : row + 1, :] = jnp.full((1, HD), limit, jnp.int32)
 
@@ -306,42 +307,43 @@
     return outs[0] if last else tuple(outs)
 
 
-def shards(count, queries, win_keys, win_values, cache_keys, cache_values, valid_counts, first_block):
+def ring_pairs(count, cores, flip):
+    ring = [place_at(p, count) for p in range(count)]
+    pairs = []
+    for core in range(cores):
+        step = -1 if (core + flip) % 2 else 1
+        for p in range(count):
+            pairs.append((ring[p] * cores + core, ring[(p + step) % count] * cores + core))
+    return pairs
+
+
+def shards(count, cores, queries, win_keys, win_values, cache_keys, cache_values, valid_counts, first_block):
     window_rows, cache_rows = win_keys.shape[0], cache_keys.shape[0]
     stride = window_rows + cache_rows
     half = count // 2
-    ring = [place_at(p, count) for p in range(count)]
-    onward = [(ring[p], ring[(p + 1) % count]) for p in range(count)]
-    backward = [(b, a) for a, b in onward]
+    sizes = (window_rows, cache_rows)
+    send_a = functools.partial(lax.ppermute, axis_name=("ctx", "tp"), perm=ring_pairs(count, cores, 0))
+    send_b = functools.partial(lax.ppermute, axis_name=("ctx", "tp"), perm=ring_pairs(count, cores, 1))
 
     win_keys, win_values, cache_keys, cache_values, valid_counts, first_block, queries = [
         pltpu.with_memory_space_constraint(x, pltpu.HBM)
         for x in (win_keys, win_values, cache_keys, cache_values, valid_counts, first_block, queries)
     ]
-    on = back = pack(win_keys, win_values, cache_keys, cache_values)
-    state = near = limits = None
-    for step in range(1, half + 1):
-        if step < half:
-            next_on = lax.ppermute(on, "ctx", onward)
-            next_back = lax.ppermute(back, "ctx", backward)
-        else:
-            next_on = lax.ppermute(on[:stride], "ctx", onward)
-            next_back = lax.ppermute(back[stride:], "ctx", backward)
-        if step == 1:
-            state, near, limits = attend_first(
-                count, window_rows, cache_rows, valid_counts, first_block, queries, on
-            )
-        else:
-            row = 2 * (step - 2)
-            pieces = [(row, 0, stride), (row + 1, 0, stride)]
-            state = attend_next(
-                pieces, [on, back], [on, back], state, False, window_rows, cache_rows, near, limits
-            )
-        on, top = lax.optimization_barrier((next_on, state[1]))
-        back, top = lax.optimization_barrier((next_back, top))
-        state = (state[0], top)
-    pieces = [(2 * (half - 1), 0, 0)]
-    return attend_next(pieces, [on], [back], state, True, window_rows, cache_rows, near, limits)
+    packed = pack(win_keys, win_values, cache_keys, cache_values)
+    a = send_a(packed)
+    state, near, limits = attend_first(count, *sizes, valid_counts, first_block, queries, packed)
+    packed, top = lax.optimization_barrier((packed, state[1]))
+    state = (state[0], top)
+    b = send_b(packed) if half > 1 else None
+    for step in range(1, half):
+        a, top = lax.optimization_barrier((a, state[1]))
+        next_a = send_a(a)
+        next_b = send_b(b) if step + 1 < half else None
+        row = 2 * (step - 1)
+        pieces = [(row, 0, stride), (row + 1, 0, stride)]
+        state = attend_next(pieces, [a, b], [a, b], (state[0], top), False, *sizes, near, limits)
+        a, b = next_a, next_b
+    return attend_next([(2 * (half - 1), 0, stride)], [a], [a], state, True, *sizes, near, limits)
 
 
 def solution(mesh):
@@ -356,7 +358,7 @@
     )
     out_specs = P(("groups", "ctx"), "tp")
     return jax.shard_map(
-        functools.partial(shards, mesh.shape["ctx"]),
+        functools.partial(shards, mesh.shape["ctx"], mesh.shape["tp"]),
         mesh=mesh,
         in_specs=in_specs,
         out_specs=out_specs,

time: 29 us -> 30.5 us (1.052)
  starting transfers between devices: 9.48 us -> 10.7 us
    ppermute x8 -> x7, starting transfers between devices: 9.48 us -> 10.7 us  [the longest x3 7.24 us: shards(): next_a = send_a(a)]
    ppermute x8 -> x7, waiting for transfers between devices: 10.5 us -> 10.8 us  [the longest x2 3.52 us: shards(): next_b = send_b(b) if step + 1 < half else None]
  transfers between devices with their start and end apart: 8 -> 7, of which waited for: 5 -> 7; matrix products, arithmetic and copies ran while one was open for 0% -> 0% of each run, Pallas kernels for 22% -> 20%
where the time goes in v4:
time: 30.5 us; the launch traced here: 30.3 us
  waiting for transfers between devices  10.8 us (35%)
  starting transfers between devices  10.7 us (35%)
  Pallas kernels  8.78 us (29%)
    ppermute x3, starting transfers between devices, shards(): next_a = send_a(a)  7.24 us
    pallas_call x4, Pallas kernels, attend_next(): pl.pallas_call(functools.partial(next_kernel, tuple(pieces), last, window...  5.89 us
    ppermute x2, waiting for transfers between devices, shards(): next_b = send_b(b) if step + 1 < half else None  3.52 us
    ppermute x1, starting transfers between devices, shards(): a = send_a(packed)  2.99 us
    ppermute x1, waiting for transfers between devices, shards(): b = send_b(packed) if half > 1 else None  2.93 us
    ppermute x3, waiting for transfers between devices, shards(): next_a = send_a(a)  2.22 us
    ppermute x1, waiting for transfers between devices, shards(): a = send_a(packed)  2.17 us
    pallas_call x1, Pallas kernels, attend_first(): pl.pallas_call(functools.partial(first_kernel, count, window_rows, cache_...  1.97 us
  transfers between devices with their start and end apart: 7, of which 7 were waited for; matrix products, arithmetic and copies ran while one was open for 0% of the time, Pallas kernels for 20%

profile of v4, /device:TPU:0, one launch (start us, length us, event | category | flops | bytes accessed | tf_op | source)
XLA Modules:
  0.0 30.3 jit_solution(8656309412983423078)
XLA Ops:
  0.0 0.9 %pack.1.packed = bf16[384,256]{1,0:T(8,128)(2,1)S(1)} custom-call(bf16[128,256]{1,0:T(8,128)(2,1)} %win_keys.1, bf16[128,256]{1,0:T(8,128)(2,1)} %win_values.1, bf16[64,256]{1,0:T(8,128)(2,1)} %cache_keys.1, bf16[64,256]{1,0:T(8,128)(2,1)} %cache_values.1), custom_call_target="tpu_custom_call" | custom-call | bytes 393216 | tf_op jit(solution)/shard_map/pack/pallas_call | solution.py:64
  0.9 3.0 %collective-permute-start = (bf16[384,256]{1,0:T(8,128)(2,1)S(1)}, bf16[384,256]{1,0:T(8,128)(2,1)S(1)}, u32[]{:S(2)}, u32[]{:S(2)}) collective-permute-start(bf16[384,256]{1,0:T(8,128)(2,1)S(1)} %pack.1.packed), channel_id=1, source_target_pairs={{2,6},{6,10},{10,14},{14,12},{12,8},{8,4},{4,0},{0,2},{3,1},{7,3},... | collective-permute-start | bytes 589832 | tf_op jit(solution)/shard_map/ppermute | solution.py:333
  3.9 2.0 %attend_first.1 = (f32[2048,256]{1,0:T(8,128)S(1)}, f32[2048,128]{1,0:T(8,128)S(1)}, bf16[128,2048]{1,0:T(8,128)(2,1)S(1)}, s32[8,128]{1,0:T(8,128)S(1)}) custom-call(s32[8]{0:T(128)} %valid_hbm.1, s32[8]{0:T(128)} %first_hbm.1, bf16[128,2048]{1,0:T(8,128)(2,1)} %q_hbm.1, bf16[384,256]{1,0:T(8,128)(2,1)S(1)} %pack.1.packed), custom_call_target="tpu_custom_call" | custom-call | flops 402653184 | bytes 524288 | tf_op jit(solution)/shard_map/attend_first/pallas_call | solution.py:267
  5.9 0.2 collective-permute-start.2
  6.1 2.2 %collective-permute-done.refs_0_.refs_2_ = bf16[384,256]{1,0:T(8,128)(2,1)S(1)} collective-permute-done((bf16[384,256]{1,0:T(8,128)(2,1)S(1)}, bf16[384,256]{1,0:T(8,128)(2,1)S(1)}, u32[]{:S(2)}, u32[]{:S(2)}) %collective-permute-start) | collective-permute-done | bytes 196640 | tf_op jit(solution)/shard_map/ppermute | solution.py:333
  8.2 2.5 %collective-permute-start.1 = (bf16[384,256]{1,0:T(8,128)(2,1)S(1)}, bf16[384,256]{1,0:T(8,128)(2,1)S(1)}, u32[]{:S(2)}, u32[]{:S(2)}) collective-permute-start(bf16[384,256]{1,0:T(8,128)(2,1)S(1)} %collective-permute-done.refs_0_.refs_2_), channel_id=1, source_target_pairs={{2,6},{6,10},{10,14},{14,12},{12,8},{8,4},{4,0},{0,2},{3,1},{7,3},... | collective-permute-start | bytes 589832 | tf_op jit(solution)/shard_map/ppermute | solution.py:340
  10.7 2.9 %collective-permute-done.2.refs_1_.refs_3_ = bf16[384,256]{1,0:T(8,128)(2,1)S(1)} collective-permute-done((bf16[384,256]{1,0:T(8,128)(2,1)S(1)}, bf16[384,256]{1,0:T(8,128)(2,1)S(1)}, u32[]{:S(2)}, u32[]{:S(2)}) %collective-permute-start.2) | collective-permute-done | bytes 196640 | tf_op jit(solution)/shard_map/ppermute | solution.py:337
  13.6 0.0 collective-permute-start.4
  13.6 1.4 %attend_next.3 = (f32[2048,256]{1,0:T(8,128)S(1)}, f32[2048,128]{1,0:T(8,128)S(1)}) custom-call(bf16[128,2048]{1,0:T(8,128)(2,1)S(1)} %get-tuple-element.23.q_ref, s32[8,128]{1,0:T(8,128)S(1)} %get-tuple-element.24.limits, bf16[384,256]{1,0:T(8,128)(2,1)S(1)} %collective-permute-done.refs_0_.refs_2_, ...), custom_call_target="tpu_custom_call" | custom-call | flops 603979776 | bytes 524288 | tf_op jit(solution)/shard_map/attend_next/pallas_call | solution.py:298
  15.1 0.8 %collective-permute-done.1.refs_0_.refs_2_ = bf16[384,256]{1,0:T(8,128)(2,1)S(1)} collective-permute-done((bf16[384,256]{1,0:T(8,128)(2,1)S(1)}, bf16[384,256]{1,0:T(8,128)(2,1)S(1)}, u32[]{:S(2)}, u32[]{:S(2)}) %collective-permute-start.1) | collective-permute-done | bytes 196640 | tf_op jit(solution)/shard_map/ppermute | solution.py:340
  15.9 2.5 %collective-permute-start.3 = (bf16[384,256]{1,0:T(8,128)(2,1)S(1)}, bf16[384,256]{1,0:T(8,128)(2,1)S(1)}, u32[]{:S(2)}, u32[]{:S(2)}) collective-permute-start(bf16[384,256]{1,0:T(8,128)(2,1)S(1)} %collective-permute-done.1.refs_0_.refs_2_), channel_id=1, source_target_pairs={{2,6},{6,10},{10,14},{14,12},{12,8},{8,4},{4,0},{0,2},{3,1},{7,3},... | collective-permute-start | bytes 589832 | tf_op jit(solution)/shard_map/ppermute | solution.py:340
  18.4 2.1 %collective-permute-done.4.refs_1_.refs_3_ = bf16[384,256]{1,0:T(8,128)(2,1)S(1)} collective-permute-done((bf16[384,256]{1,0:T(8,128)(2,1)S(1)}, bf16[384,256]{1,0:T(8,128)(2,1)S(1)}, u32[]{:S(2)}, u32[]{:S(2)}) %collective-permute-start.4) | collective-permute-done | bytes 196640 | tf_op jit(solution)/shard_map/ppermute | solution.py:341
  20.5 0.3 collective-permute-start.6
  20.8 1.4 %attend_next.4 = (f32[2048,256]{1,0:T(8,128)S(1)}, f32[2048,128]{1,0:T(8,128)S(1)}) custom-call(bf16[128,2048]{1,0:T(8,128)(2,1)S(1)} %get-tuple-element.23.q_ref, s32[8,128]{1,0:T(8,128)S(1)} %get-tuple-element.24.limits, bf16[384,256]{1,0:T(8,128)(2,1)S(1)} %collective-permute-done.1.refs_0_.refs_2_, ...), custom_call_target="tpu_custom_call" | custom-call | flops 603979776 | bytes 524288 | tf_op jit(solution)/shard_map/attend_next/pallas_call | solution.py:298
  22.2 0.8 %collective-permute-done.3.refs_0_.refs_2_ = bf16[384,256]{1,0:T(8,128)(2,1)S(1)} collective-permute-done((bf16[384,256]{1,0:T(8,128)(2,1)S(1)}, bf16[384,256]{1,0:T(8,128)(2,1)S(1)}, u32[]{:S(2)}, u32[]{:S(2)}) %collective-permute-start.3) | collective-permute-done | bytes 196640 | tf_op jit(solution)/shard_map/ppermute | solution.py:340
  23.0 2.3 %collective-permute-start.5 = (bf16[384,256]{1,0:T(8,128)(2,1)S(1)}, bf16[384,256]{1,0:T(8,128)(2,1)S(1)}, u32[]{:S(2)}, u32[]{:S(2)}) collective-permute-start(bf16[384,256]{1,0:T(8,128)(2,1)S(1)} %collective-permute-done.3.refs_0_.refs_2_), channel_id=1, source_target_pairs={{2,6},{6,10},{10,14},{14,12},{12,8},{8,4},{4,0},{0,2},{3,1},{7,3},... | collective-permute-start | bytes 589832 | tf_op jit(solution)/shard_map/ppermute | solution.py:340
  25.3 1.4 %collective-permute-done.6.refs_1_.refs_3_ = bf16[384,256]{1,0:T(8,128)(2,1)S(1)} collective-permute-done((bf16[384,256]{1,0:T(8,128)(2,1)S(1)}, bf16[384,256]{1,0:T(8,128)(2,1)S(1)}, u32[]{:S(2)}, u32[]{:S(2)}) %collective-permute-start.6) | collective-permute-done | bytes 196640 | tf_op jit(solution)/shard_map/ppermute | solution.py:341
  26.7 1.4 %attend_next.5 = (f32[2048,256]{1,0:T(8,128)S(1)}, f32[2048,128]{1,0:T(8,128)S(1)}) custom-call(bf16[128,2048]{1,0:T(8,128)(2,1)S(1)} %get-tuple-element.23.q_ref, s32[8,128]{1,0:T(8,128)S(1)} %get-tuple-element.24.limits, bf16[384,256]{1,0:T(8,128)(2,1)S(1)} %collective-permute-done.3.refs_0_.refs_2_, ...), custom_call_target="tpu_custom_call" | custom-call | flops 603979776 | bytes 524288 | tf_op jit(solution)/shard_map/attend_next/pallas_call | solution.py:298
  28.1 0.6 %collective-permute-done.5.refs_0_.refs_1_ = bf16[384,256]{1,0:T(8,128)(2,1)S(1)} collective-permute-done((bf16[384,256]{1,0:T(8,128)(2,1)S(1)}, bf16[384,256]{1,0:T(8,128)(2,1)S(1)}, u32[]{:S(2)}, u32[]{:S(2)}) %collective-permute-start.5) | collective-permute-done | bytes 196640 | tf_op jit(solution)/shard_map/ppermute | solution.py:340
  28.7 1.7 %attend_last.1 = bf16[128,2048]{1,0:T(8,128)(2,1)} custom-call(bf16[128,2048]{1,0:T(8,128)(2,1)S(1)} %get-tuple-element.23.q_ref, s32[8,128]{1,0:T(8,128)S(1)} %get-tuple-element.24.limits, bf16[384,256]{1,0:T(8,128)(2,1)S(1)} %collective-permute-done.5.refs_0_.refs_1_, bf16[384,256]{1,0:T(8,128)(2,1)S(1)} %collective-permute-done.5.refs_0_.refs_1_, ...), custom_call_target="tpu_custom_call" | custom-call | flops 402653184 | bytes 524288 | tf_op jit(solution)/shard_map/attend_last/pallas_call | solution.py:298
Async XLA Ops:
  0.9 7.3 %collective-permute-start = (bf16[384,256]{1,0:T(8,128)(2,1)S(1)}, bf16[384,256]{1,0:T(8,128)(2,1)S(1)}, u32[]{:S(2)}, u32[]{:S(2)}) collective-permute-start(bf16[384,256]{1,0:T(8,128)(2,1)S(1)} %pack.1.packed), channel_id=1, source_target_pairs={{2,6},{6,10},{10,14},{14,12},{12,8},{8,4},{4,0},{0,2},{3,1},{7,3},... | collective-permute-start | bytes 589832 | tf_op jit(solution)/shard_map/ppermute | solution.py:333
  5.9 7.7 %collective-permute-start.2 = (bf16[384,256]{1,0:T(8,128)(2,1)S(1)}, bf16[384,256]{1,0:T(8,128)(2,1)S(1)}, u32[]{:S(2)}, u32[]{:S(2)}) collective-permute-start(bf16[384,256]{1,0:T(8,128)(2,1)S(1)} %pack.1.packed), channel_id=1, source_target_pairs={{2,0},{6,2},{10,6},{14,10},{12,14},{8,12},{4,8},{0,4},{3,7},{7,11}... | collective-permute-start | bytes 589832 | tf_op jit(solution)/shard_map/ppermute | solution.py:337
  8.2 7.6 %collective-permute-start.1 = (bf16[384,256]{1,0:T(8,128)(2,1)S(1)}, bf16[384,256]{1,0:T(8,128)(2,1)S(1)}, u32[]{:S(2)}, u32[]{:S(2)}) collective-permute-start(bf16[384,256]{1,0:T(8,128)(2,1)S(1)} %collective-permute-done.refs_0_.refs_2_), channel_id=1, source_target_pairs={{2,6},{6,10},{10,14},{14,12},{12,8},{8,4},{4,0},{0,2},{3,1},{7,3},... | collective-permute-start | bytes 589832 | tf_op jit(solution)/shard_map/ppermute | solution.py:340
  13.6 6.8 %collective-permute-start.4 = (bf16[384,256]{1,0:T(8,128)(2,1)S(1)}, bf16[384,256]{1,0:T(8,128)(2,1)S(1)}, u32[]{:S(2)}, u32[]{:S(2)}) collective-permute-start(bf16[384,256]{1,0:T(8,128)(2,1)S(1)} %collective-permute-done.2.refs_1_.refs_3_), channel_id=1, source_target_pairs={{2,0},{6,2},{10,6},{14,10},{12,14},{8,12},{4,8},{0,4},{3,7},{7,11}... | collective-permute-start | bytes 589832 | tf_op jit(solution)/shard_map/ppermute | solution.py:341
  15.9 7.1 %collective-permute-start.3 = (bf16[384,256]{1,0:T(8,128)(2,1)S(1)}, bf16[384,256]{1,0:T(8,128)(2,1)S(1)}, u32[]{:S(2)}, u32[]{:S(2)}) collective-permute-start(bf16[384,256]{1,0:T(8,128)(2,1)S(1)} %collective-permute-done.1.refs_0_.refs_2_), channel_id=1, source_target_pairs={{2,6},{6,10},{10,14},{14,12},{12,8},{8,4},{4,0},{0,2},{3,1},{7,3},... | collective-permute-start | bytes 589832 | tf_op jit(solution)/shard_map/ppermute | solution.py:340
  20.5 6.2 %collective-permute-start.6 = (bf16[384,256]{1,0:T(8,128)(2,1)S(1)}, bf16[384,256]{1,0:T(8,128)(2,1)S(1)}, u32[]{:S(2)}, u32[]{:S(2)}) collective-permute-start(bf16[384,256]{1,0:T(8,128)(2,1)S(1)} %collective-permute-done.4.refs_1_.refs_3_), channel_id=1, source_target_pairs={{2,0},{6,2},{10,6},{14,10},{12,14},{8,12},{4,8},{0,4},{3,7},{7,11}... | collective-permute-start | bytes 589832 | tf_op jit(solution)/shard_map/ppermute | solution.py:341
  23.0 5.7 %collective-permute-start.5 = (bf16[384,256]{1,0:T(8,128)(2,1)S(1)}, bf16[384,256]{1,0:T(8,128)(2,1)S(1)}, u32[]{:S(2)}, u32[]{:S(2)}) collective-permute-start(bf16[384,256]{1,0:T(8,128)(2,1)S(1)} %collective-permute-done.3.refs_0_.refs_2_), channel_id=1, source_target_pairs={{2,6},{6,10},{10,14},{14,12},{12,8},{8,4},{4,0},{0,2},{3,1},{7,3},... | collective-permute-start | bytes 589832 | tf_op jit(solution)/shard_map/ppermute | solution.py:340

commit v5 on v4

--- a/solution.py
+++ b/solution.py
@@ -75,7 +75,11 @@
 
 def ring_offsets(count):
     half = count // 2
-    return [sign * step for step in range(1, half) for sign in (-1, 1)] + [half]
+    offsets = []
+    for step in range(1, half):
+        side = 1 if step % 2 else -1
+        offsets += [side * step, -side * step]
+    return offsets + [half]
 
 
 def place_pieces(pieces, own, window_rows, cache_rows, limits, key_refs, value_refs, keys, values):
@@ -165,7 +169,7 @@
     me = lax.axis_index("ctx")
     position = position_of(me, count)
     first = first_ref[me]
-    sign = 1 - 2 * lax.rem(lax.axis_index("tp"), 2)
+    sign = 2 * lax.rem(position, 2) - 1
     for row, offset in enumerate(ring_offsets(count)):
         place = place_at(lax.rem(position + sign * offset + count, count), count)
         limit = jnp.where((place >= first) & (place <= me), valid_ref[place], 0)
@@ -307,43 +311,51 @@
     return outs[0] if last else tuple(outs)
 
 
-def ring_pairs(count, cores, flip):
+def swap_pairs(count, distance, parity):
     ring = [place_at(p, count) for p in range(count)]
     pairs = []
-    for core in range(cores):
-        step = -1 if (core + flip) % 2 else 1
-        for p in range(count):
-            pairs.append((ring[p] * cores + core, ring[(p + step) % count] * cores + core))
+    for p in range(parity, count, 2):
+        first, second = ring[p], ring[(p + distance) % count]
+        pairs += [(first, second), (second, first)]
     return pairs
 
 
-def shards(count, cores, queries, win_keys, win_values, cache_keys, cache_values, valid_counts, first_block):
+def shards(count, queries, win_keys, win_values, cache_keys, cache_values, valid_counts, first_block):
     window_rows, cache_rows = win_keys.shape[0], cache_keys.shape[0]
     stride = window_rows + cache_rows
     half = count // 2
     sizes = (window_rows, cache_rows)
-    send_a = functools.partial(lax.ppermute, axis_name=("ctx", "tp"), perm=ring_pairs(count, cores, 0))
-    send_b = functools.partial(lax.ppermute, axis_name=("ctx", "tp"), perm=ring_pairs(count, cores, 1))
+    odd = functools.partial(lax.ppermute, axis_name="ctx", perm=swap_pairs(count, 1, 1))
+    even = functools.partial(lax.ppermute, axis_name="ctx", perm=swap_pairs(count, 1, 0))
+    across = functools.partial(lax.ppermute, axis_name="ctx", perm=swap_pairs(count, half - 1, 0))
 
     win_keys, win_values, cache_keys, cache_values, valid_counts, first_block, queries = [
         pltpu.with_memory_space_constraint(x, pltpu.HBM)
         for x in (win_keys, win_values, cache_keys, cache_values, valid_counts, first_block, queries)
     ]
-    packed = pack(win_keys, win_values, cache_keys, cache_values)
-    a = send_a(packed)
-    state, near, limits = attend_first(count, *sizes, valid_counts, first_block, queries, packed)
-    packed, top = lax.optimization_barrier((packed, state[1]))
-    state = (state[0], top)
-    b = send_b(packed) if half > 1 else None
+    p = q = pack(win_keys, win_values, cache_keys, cache_values)
+    opposite = None
+    state, near, limits = attend_first(count, *sizes, valid_counts, first_block, queries, p)
     for step in range(1, half):
-        a, top = lax.optimization_barrier((a, state[1]))
-        next_a = send_a(a)
-        next_b = send_b(b) if step + 1 < half else None
-        row = 2 * (step - 1)
-        pieces = [(row, 0, stride), (row + 1, 0, stride)]
-        state = attend_next(pieces, [a, b], [a, b], (state[0], top), False, *sizes, near, limits)
-        a, b = next_a, next_b
-    return attend_next([(2 * (half - 1), 0, stride)], [a], [a], state, True, *sizes, near, limits)
+        next_p = (odd if step % 2 else even)(p)
+        next_q = (even if step % 2 else odd)(q)
+        if step == 2:
+            opposite = across(p)
+        if step > 1:
+            row = 2 * (step - 2)
+            pieces, arrived = [(row, 0, stride), (row + 1, 0, stride)], [p, q]
+            if step == half - 1:
+                pieces.append((2 * (half - 1), 0, stride))
+                arrived.append(opposite)
+            state = attend_next(pieces, arrived, arrived, state, False, *sizes, near, limits)
+        if step < half - 1:
+            p, top = lax.optimization_barrier((next_p, state[1]))
+            q, top = lax.optimization_barrier((next_q, top))
+            state = (state[0], top)
+        else:
+            p, q = next_p, next_q
+    row = 2 * (half - 2)
+    return attend_next([(row, 0, stride), (row + 1, 0, stride)], [p, q], [p, q], state, True, *sizes, near, limits)
 
 
 def solution(mesh):
@@ -358,7 +370,7 @@
     )
     out_specs = P(("groups", "ctx"), "tp")
     return jax.shard_map(
-        functools.partial(shards, mesh.shape["ctx"], mesh.shape["tp"]),
+        functools.partial(shards, mesh.shape["ctx"]),
         mesh=mesh,
         in_specs=in_specs,
         out_specs=out_specs,

time: 30.5 us -> 30.3 us (level)
  starting transfers between devices: 10.7 us -> 17.9 us
  waiting for transfers between devices: 10.8 us -> 3.68 us
    ppermute x7, starting transfers between devices: 10.7 us -> 17.9 us  [the longest x3 9.07 us: shards(): next_q = (even if step % 2 else odd)(q)]
    ppermute x7, waiting for transfers between devices: 10.8 us -> 3.68 us  [the longest x3 3.28 us: shards(): next_p = (odd if step % 2 else even)(p)]
    pallas_call x4 -> x3, Pallas kernels: 5.89 us -> 5.65 us  [attend_next(): pl.pallas_call(functools.partial(next_kernel, tuple(pieces), last, window...]
  transfers between devices with their start and end apart: 7 -> 7, of which waited for: 7 -> 4; matrix products, arithmetic and copies ran while one was open for 0% -> 0% of each run, Pallas kernels for 20% -> 18%
where the time goes in v5:
time: 30.3 us; the launch traced here: 30.2 us
  starting transfers between devices  17.9 us (59%)
  Pallas kernels  8.55 us (28%)
  waiting for transfers between devices  3.68 us (12%)
    ppermute x3, starting transfers between devices, shards(): next_q = (even if step % 2 else odd)(q)  9.07 us
    ppermute x3, starting transfers between devices, shards(): next_p = (odd if step % 2 else even)(p)  6.36 us
    pallas_call x3, Pallas kernels, attend_next(): pl.pallas_call(functools.partial(next_kernel, tuple(pieces), last, window...  5.65 us
    ppermute x3, waiting for transfers between devices, shards(): next_p = (odd if step % 2 else even)(p)  3.28 us
    ppermute x1, starting transfers between devices, shards(): opposite = across(p)  2.47 us
    pallas_call x1, Pallas kernels, attend_first(): pl.pallas_call(functools.partial(first_kernel, count, window_rows, cache_...  1.97 us
    pallas_call x1, Pallas kernels, pack(): pl.pallas_call(pack_kernel, out_shape=jax.ShapeDtypeStruct((rows, win_key...  0.93 us
  transfers between devices with their start and end apart: 7, of which 4 were waited for; matrix products, arithmetic and copies ran while one was open for 0% of the time, Pallas kernels for 18%

profile of v5, /device:TPU:0, one launch (start us, length us, event | category | flops | bytes accessed | tf_op | source)
XLA Modules:
  0.0 30.2 jit_solution(1147634331125140558)
XLA Ops:
  0.0 0.9 %pack.1.packed = bf16[384,256]{1,0:T(8,128)(2,1)S(1)} custom-call(bf16[128,256]{1,0:T(8,128)(2,1)} %win_keys.1, bf16[128,256]{1,0:T(8,128)(2,1)} %win_values.1, bf16[64,256]{1,0:T(8,128)(2,1)} %cache_keys.1, bf16[64,256]{1,0:T(8,128)(2,1)} %cache_values.1), custom_call_target="tpu_custom_call" | custom-call | bytes 393216 | tf_op jit(solution)/shard_map/pack/pallas_call | solution.py:64
  0.9 3.0 %collective-permute-start = (bf16[384,256]{1,0:T(8,128)(2,1)S(1)}, bf16[384,256]{1,0:T(8,128)(2,1)S(1)}, u32[]{:S(2)}, u32[]{:S(2)}) collective-permute-start(bf16[384,256]{1,0:T(8,128)(2,1)S(1)} %pack.1.packed), channel_id=1, source_target_pairs={{6,10},{10,6},{14,12},{12,14},{8,4},{4,8},{0,2},{2,0},{7,11},{11,7... | collective-permute-start | bytes 589832 | tf_op jit(solution)/shard_map/ppermute | solution.py:340
  3.9 1.7 %collective-permute-start.2 = (bf16[384,256]{1,0:T(8,128)(2,1)S(1)}, bf16[384,256]{1,0:T(8,128)(2,1)S(1)}, u32[]{:S(2)}, u32[]{:S(2)}) collective-permute-start(bf16[384,256]{1,0:T(8,128)(2,1)S(1)} %pack.1.packed), channel_id=1, source_target_pairs={{2,6},{6,2},{10,14},{14,10},{12,8},{8,12},{4,0},{0,4},{3,7},{7,3},... | collective-permute-start | bytes 589832 | tf_op jit(solution)/shard_map/ppermute | solution.py:341
  5.6 2.0 %attend_first.1 = (f32[2048,256]{1,0:T(8,128)S(1)}, f32[2048,128]{1,0:T(8,128)S(1)}, bf16[128,2048]{1,0:T(8,128)(2,1)S(1)}, s32[8,128]{1,0:T(8,128)S(1)}) custom-call(s32[8]{0:T(128)} %valid_hbm.1, s32[8]{0:T(128)} %first_hbm.1, bf16[128,2048]{1,0:T(8,128)(2,1)} %q_hbm.1, bf16[384,256]{1,0:T(8,128)(2,1)S(1)} %pack.1.packed), custom_call_target="tpu_custom_call" | custom-call | flops 402653184 | bytes 524288 | tf_op jit(solution)/shard_map/attend_first/pallas_call | solution.py:271
  7.6 1.3 %collective-permute-done.refs_0_.refs_2_ = bf16[384,256]{1,0:T(8,128)(2,1)S(1)} collective-permute-done((bf16[384,256]{1,0:T(8,128)(2,1)S(1)}, bf16[384,256]{1,0:T(8,128)(2,1)S(1)}, u32[]{:S(2)}, u32[]{:S(2)}) %collective-permute-start) | collective-permute-done | bytes 196640 | tf_op jit(solution)/shard_map/ppermute | solution.py:340
  8.8 1.8 %collective-permute-start.1 = (bf16[384,256]{1,0:T(8,128)(2,1)S(1)}, bf16[384,256]{1,0:T(8,128)(2,1)S(1)}, u32[]{:S(2)}, u32[]{:S(2)}) collective-permute-start(bf16[384,256]{1,0:T(8,128)(2,1)S(1)} %collective-permute-done.refs_0_.refs_2_), channel_id=1, source_target_pairs={{2,6},{6,2},{10,14},{14,10},{12,8},{8,12},{4,0},{0,4},{3,7},{7,3},... | collective-permute-start | bytes 589832 | tf_op jit(solution)/shard_map/ppermute | solution.py:340
  10.7 0.0 collective-permute-done.2.refs_1_.refs_3_
  10.7 1.5 %collective-permute-start.4 = (bf16[384,256]{1,0:T(8,128)(2,1)S(1)}, bf16[384,256]{1,0:T(8,128)(2,1)S(1)}, u32[]{:S(2)}, u32[]{:S(2)}) collective-permute-start(bf16[384,256]{1,0:T(8,128)(2,1)S(1)} %collective-permute-done.2.refs_1_.refs_3_), channel_id=1, source_target_pairs={{6,10},{10,6},{14,12},{12,14},{8,4},{4,8},{0,2},{2,0},{7,11},{11,7... | collective-permute-start | bytes 589832 | tf_op jit(solution)/shard_map/ppermute | solution.py:341
  12.2 2.5 %collective-permute-start.6 = (bf16[384,256]{1,0:T(8,128)(2,1)S(1)}, bf16[384,256]{1,0:T(8,128)(2,1)S(1)}, u32[]{:S(2)}, u32[]{:S(2)}) collective-permute-start(bf16[384,256]{1,0:T(8,128)(2,1)S(1)} %collective-permute-done.refs_0_.refs_2_), channel_id=1, source_target_pairs={{2,14},{14,2},{10,8},{8,10},{12,0},{0,12},{4,6},{6,4},{3,15},{15,3... | collective-permute-start | bytes 589832 | tf_op jit(solution)/shard_map/ppermute | solution.py:343
  14.6 1.4 %attend_next.2 = (f32[2048,256]{1,0:T(8,128)S(1)}, f32[2048,128]{1,0:T(8,128)S(1)}) custom-call(bf16[128,2048]{1,0:T(8,128)(2,1)S(1)} %get-tuple-element.21.q_ref, s32[8,128]{1,0:T(8,128)S(1)} %get-tuple-element.22.limits, bf16[384,256]{1,0:T(8,128)(2,1)S(1)} %collective-permute-done.refs_0_.refs_2_, ...), custom_call_target="tpu_custom_call" | custom-call | flops 603979776 | bytes 524288 | tf_op jit(solution)/shard_map/attend_next/pallas_call | solution.py:302
  16.0 0.0 collective-permute-done.1.refs_0_.refs_3_
  16.1 0.3 collective-permute-done.4.refs_1_.refs_4_
  16.3 5.9 %collective-permute-start.5 = (bf16[384,256]{1,0:T(8,128)(2,1)S(1)}, bf16[384,256]{1,0:T(8,128)(2,1)S(1)}, u32[]{:S(2)}, u32[]{:S(2)}) collective-permute-start(bf16[384,256]{1,0:T(8,128)(2,1)S(1)} %collective-permute-done.4.refs_1_.refs_4_), channel_id=1, source_target_pairs={{2,6},{6,2},{10,14},{14,10},{12,8},{8,12},{4,0},{0,4},{3,7},{7,3},... | collective-permute-start | bytes 589832 | tf_op jit(solution)/shard_map/ppermute | solution.py:341
  22.3 1.5 %collective-permute-start.3 = (bf16[384,256]{1,0:T(8,128)(2,1)S(1)}, bf16[384,256]{1,0:T(8,128)(2,1)S(1)}, u32[]{:S(2)}, u32[]{:S(2)}) collective-permute-start(bf16[384,256]{1,0:T(8,128)(2,1)S(1)} %collective-permute-done.1.refs_0_.refs_3_), channel_id=1, source_target_pairs={{6,10},{10,6},{14,12},{12,14},{8,4},{4,8},{0,2},{2,0},{7,11},{11,7... | collective-permute-start | bytes 589832 | tf_op jit(solution)/shard_map/ppermute | solution.py:340
  23.8 0.0 collective-permute-done.6.refs_2_.refs_5_
  23.8 2.0 %attend_next.3 = (f32[2048,256]{1,0:T(8,128)S(1)}, f32[2048,128]{1,0:T(8,128)S(1)}) custom-call(bf16[128,2048]{1,0:T(8,128)(2,1)S(1)} %get-tuple-element.21.q_ref, s32[8,128]{1,0:T(8,128)S(1)} %get-tuple-element.22.limits, bf16[384,256]{1,0:T(8,128)(2,1)S(1)} %collective-permute-done.1.refs_0_.refs_3_, ...), custom_call_target="tpu_custom_call" | custom-call | flops 1006632960 | bytes 524288 | tf_op jit(solution)/shard_map/attend_next/pallas_call | solution.py:302
  25.8 0.1 collective-permute-done.5.refs_1_.refs_3_
  25.9 2.0 %collective-permute-done.3.refs_0_.refs_2_ = bf16[384,256]{1,0:T(8,128)(2,1)S(1)} collective-permute-done((bf16[384,256]{1,0:T(8,128)(2,1)S(1)}, bf16[384,256]{1,0:T(8,128)(2,1)S(1)}, u32[]{:S(2)}, u32[]{:S(2)}) %collective-permute-start.3) | collective-permute-done | bytes 196640 | tf_op jit(solution)/shard_map/ppermute | solution.py:340
  27.9 2.2 %attend_last.1 = bf16[128,2048]{1,0:T(8,128)(2,1)} custom-call(bf16[128,2048]{1,0:T(8,128)(2,1)S(1)} %get-tuple-element.21.q_ref, s32[8,128]{1,0:T(8,128)S(1)} %get-tuple-element.22.limits, bf16[384,256]{1,0:T(8,128)(2,1)S(1)} %collective-permute-done.3.refs_0_.refs_2_, bf16[384,256]{1,0:T(8,128)(2,1)S(1)} %collective-permute-done.5.refs_1_.refs_3_, ...), custom_call_target="tpu_custom_call" | custom-call | flops 603979776 | bytes 524288 | tf_op jit(solution)/shard_map/attend_last/pallas_call | solution.py:302
Async XLA Ops:
  0.9 7.9 %collective-permute-start = (bf16[384,256]{1,0:T(8,128)(2,1)S(1)}, bf16[384,256]{1,0:T(8,128)(2,1)S(1)}, u32[]{:S(2)}, u32[]{:S(2)}) collective-permute-start(bf16[384,256]{1,0:T(8,128)(2,1)S(1)} %pack.1.packed), channel_id=1, source_target_pairs={{6,10},{10,6},{14,12},{12,14},{8,4},{4,8},{0,2},{2,0},{7,11},{11,7... | collective-permute-start | bytes 589832 | tf_op jit(solution)/shard_map/ppermute | solution.py:340
  3.9 6.7 %collective-permute-start.2 = (bf16[384,256]{1,0:T(8,128)(2,1)S(1)}, bf16[384,256]{1,0:T(8,128)(2,1)S(1)}, u32[]{:S(2)}, u32[]{:S(2)}) collective-permute-start(bf16[384,256]{1,0:T(8,128)(2,1)S(1)} %pack.1.packed), channel_id=1, source_target_pairs={{2,6},{6,2},{10,14},{14,10},{12,8},{8,12},{4,0},{0,4},{3,7},{7,3},... | collective-permute-start | bytes 589832 | tf_op jit(solution)/shard_map/ppermute | solution.py:341
  8.8 7.2 %collective-permute-start.1 = (bf16[384,256]{1,0:T(8,128)(2,1)S(1)}, bf16[384,256]{1,0:T(8,128)(2,1)S(1)}, u32[]{:S(2)}, u32[]{:S(2)}) collective-permute-start(bf16[384,256]{1,0:T(8,128)(2,1)S(1)} %collective-permute-done.refs_0_.refs_2_), channel_id=1, source_target_pairs={{2,6},{6,2},{10,14},{14,10},{12,8},{8,12},{4,0},{0,4},{3,7},{7,3},... | collective-permute-start | bytes 589832 | tf_op jit(solution)/shard_map/ppermute | solution.py:340
  10.7 5.7 %collective-permute-start.4 = (bf16[384,256]{1,0:T(8,128)(2,1)S(1)}, bf16[384,256]{1,0:T(8,128)(2,1)S(1)}, u32[]{:S(2)}, u32[]{:S(2)}) collective-permute-start(bf16[384,256]{1,0:T(8,128)(2,1)S(1)} %collective-permute-done.2.refs_1_.refs_3_), channel_id=1, source_target_pairs={{6,10},{10,6},{14,12},{12,14},{8,4},{4,8},{0,2},{2,0},{7,11},{11,7... | collective-permute-start | bytes 589832 | tf_op jit(solution)/shard_map/ppermute | solution.py:341
  12.2 11.6 %collective-permute-start.6 = (bf16[384,256]{1,0:T(8,128)(2,1)S(1)}, bf16[384,256]{1,0:T(8,128)(2,1)S(1)}, u32[]{:S(2)}, u32[]{:S(2)}) collective-permute-start(bf16[384,256]{1,0:T(8,128)(2,1)S(1)} %collective-permute-done.refs_0_.refs_2_), channel_id=1, source_target_pairs={{2,14},{14,2},{10,8},{8,10},{12,0},{0,12},{4,6},{6,4},{3,15},{15,3... | collective-permute-start | bytes 589832 | tf_op jit(solution)/shard_map/ppermute | solution.py:343
  16.3 9.6 %collective-permute-start.5 = (bf16[384,256]{1,0:T(8,128)(2,1)S(1)}, bf16[384,256]{1,0:T(8,128)(2,1)S(1)}, u32[]{:S(2)}, u32[]{:S(2)}) collective-permute-start(bf16[384,256]{1,0:T(8,128)(2,1)S(1)} %collective-permute-done.4.refs_1_.refs_4_), channel_id=1, source_target_pairs={{2,6},{6,2},{10,14},{14,10},{12,8},{8,12},{4,0},{0,4},{3,7},{7,3},... | collective-permute-start | bytes 589832 | tf_op jit(solution)/shard_map/ppermute | solution.py:341
  22.3 5.7 %collective-permute-start.3 = (bf16[384,256]{1,0:T(8,128)(2,1)S(1)}, bf16[384,256]{1,0:T(8,128)(2,1)S(1)}, u32[]{:S(2)}, u32[]{:S(2)}) collective-permute-start(bf16[384,256]{1,0:T(8,128)(2,1)S(1)} %collective-permute-done.1.refs_0_.refs_3_), channel_id=1, source_target_pairs={{6,10},{10,6},{14,12},{12,14},{8,4},{4,8},{0,2},{2,0},{7,11},{11,7... | collective-permute-start | bytes 589832 | tf_op jit(solution)/shard_map/ppermute | solution.py:340

commit v6 on v3

--- a/solution.py
+++ b/solution.py
@@ -11,7 +11,7 @@
 HD = 128
 EXP_SCALE = HD**-0.5 * math.log2(math.e)
 HIDDEN = -1.0e30
-CHUNK_HEADS = 4
+CHUNK_HEADS = 2
 LARGEST_TOTAL = 2.0**100
 
 
@@ -84,7 +84,7 @@
     cache_at = len(pieces) * window_rows
     row_iota = lax.broadcasted_iota(jnp.int32, (window_rows, HD), 0)
     for index, (limit_row, key_base, value_base) in enumerate(pieces):
-        key, value = key_refs[index], value_refs[index]
+        key, value = key_refs[0], value_refs[0]
         if not own:
             shown = row_iota < limits[limit_row : limit_row + 1, :]
         for head in range(kv_heads):
@@ -103,8 +103,14 @@
                 values[head, at, HD:] = jnp.where(shown, 1.0, 0.0).astype(jnp.bfloat16)
             at = slice(cache_at + index * cache_rows, cache_at + (index + 1) * cache_rows)
             keys[head, at, :] = key[key_base + window_rows : key_base + stride, lanes]
-            values[head, at, :HD] = value[value_base + window_rows : value_base + stride, lanes]
-            values[head, at, HD:] = jnp.ones((cache_rows, HD), jnp.bfloat16)
+            cache_value = value[value_base + window_rows : value_base + stride, lanes]
+            if own:
+                values[head, at, :HD] = cache_value
+                values[head, at, HD:] = jnp.ones((cache_rows, HD), jnp.bfloat16)
+            else:
+                shown_cache = row_iota[:cache_rows] < limits[limits.shape[0] // 2 + limit_row : limits.shape[0] // 2 + limit_row + 1, :]
+                values[head, at, :HD] = jnp.where(shown_cache, cache_value.astype(jnp.float32), 0.0).astype(jnp.bfloat16)
+                values[head, at, HD:] = jnp.where(shown_cache, 1.0, 0.0).astype(jnp.bfloat16)
     filled = len(pieces) * stride
     if filled < total_keys:
         key_base = pieces[0][1] + window_rows
@@ -163,12 +169,12 @@
         copy.wait()
 
     me = lax.axis_index("ctx")
-    position = position_of(me, count)
     first = first_ref[me]
-    for row, offset in enumerate(ring_offsets(count)):
-        place = place_at(lax.rem(position + offset + count, count), count)
-        limit = jnp.where((place >= first) & (place <= me), valid_ref[place], 0)
-        limits[row : row + 1, :] = jnp.full((1, HD), limit, jnp.int32)
+    for place in range(count):
+        limit = jnp.where((place >= first) & (place < me), valid_ref[place], 0)
+        limits[place : place + 1, :] = jnp.full((1, HD), limit, jnp.int32)
+        others = jnp.where(place == me, 0, cache_rows)
+        limits[count + place : count + place + 1, :] = jnp.full((1, HD), others, jnp.int32)
 
     rows = q_ref.shape[0]
     key_iota = lax.broadcasted_iota(jnp.int32, (rows, window_rows), 1)
@@ -184,12 +190,11 @@
 
 
 def next_kernel(pieces, last, window_rows, cache_rows, q_ref, limits, *refs):
-    number = len(pieces)
-    key_refs, value_refs = refs[:number], refs[number : 2 * number]
+    key_refs = value_refs = refs[:1]
     if last:
-        acc_in, top_in, out, keys, values, result, sems = refs[2 * number :]
+        acc_in, top_in, out, keys, values, result, sems = refs[1:]
     else:
-        acc_in, top_in, acc_out, top_out, keys, values = refs[2 * number :]
+        acc_in, top_in, acc_out, top_out, keys, values = refs[1:]
     place_pieces(pieces, False, window_rows, cache_rows, limits, key_refs, value_refs, keys, values)
     rows = q_ref.shape[0]
     kv_heads = keys.shape[0]
@@ -268,7 +273,7 @@
         out_shape=[
             *state_shapes(queries),
             jax.ShapeDtypeStruct(queries.shape, queries.dtype),
-            jax.ShapeDtypeStruct((-(-count // 8) * 8, HD), jnp.int32),
+            jax.ShapeDtypeStruct((-(-2 * count // 8) * 8, HD), jnp.int32),
         ],
         in_specs=[anywhere, anywhere, anywhere, vmem],
         out_specs=[vmem] * 4,
@@ -288,7 +293,7 @@
     kv_heads = keys[0].shape[1] // HD
     total_keys = -(-len(pieces) * (window_rows + cache_rows) // HD) * HD
     vmem = pl.BlockSpec(memory_space=pltpu.VMEM)
-    operands = [queries, limits, *keys, *values, *state]
+    operands = [queries, limits, *keys, *state]
     shapes = [jax.ShapeDtypeStruct(queries.shape, queries.dtype)] if last else state_shapes(queries)
     scratch = room(kv_heads, total_keys)
     if last:
@@ -309,39 +314,20 @@
 def shards(count, queries, win_keys, win_values, cache_keys, cache_values, valid_counts, first_block):
     window_rows, cache_rows = win_keys.shape[0], cache_keys.shape[0]
     stride = window_rows + cache_rows
-    half = count // 2
-    ring = [place_at(p, count) for p in range(count)]
-    onward = [(ring[p], ring[(p + 1) % count]) for p in range(count)]
-    backward = [(b, a) for a, b in onward]
-
     win_keys, win_values, cache_keys, cache_values, valid_counts, first_block, queries = [
         pltpu.with_memory_space_constraint(x, pltpu.HBM)
         for x in (win_keys, win_values, cache_keys, cache_values, valid_counts, first_block, queries)
     ]
-    on = back = pack(win_keys, win_values, cache_keys, cache_values)
-    state = near = limits = None
-    for step in range(1, half + 1):
-        if step < half:
-            next_on = lax.ppermute(on, "ctx", onward)
-            next_back = lax.ppermute(back, "ctx", backward)
-        else:
-            next_on = lax.ppermute(on[:stride], "ctx", onward)
-            next_back = lax.ppermute(back[stride:], "ctx", backward)
-        if step == 1:
-            state, near, limits = attend_first(
-                count, window_rows, cache_rows, valid_counts, first_block, queries, on
-            )
-        else:
-            row = 2 * (step - 2)
-            pieces = [(row, 0, stride), (row + 1, 0, stride)]
-            state = attend_next(
-                pieces, [on, back], [on, back], state, False, window_rows, cache_rows, near, limits
-            )
-        on, top = lax.optimization_barrier((next_on, state[1]))
-        back, top = lax.optimization_barrier((next_back, top))
-        state = (state[0], top)
-    pieces = [(2 * (half - 1), 0, 0)]
-    return attend_next(pieces, [on], [back], state, True, window_rows, cache_rows, near, limits)
+    packed = pack(win_keys, win_values, cache_keys, cache_values)
+    gathered = lax.all_gather(packed, "ctx", axis=0, tiled=True)
+    state, near, limits = attend_first(count, window_rows, cache_rows, valid_counts, first_block, queries, packed)
+    for start in range(0, count, 8):
+        stop = min(start + 8, count)
+        pieces = [(i, 2 * stride * i, 2 * stride * i + stride) for i in range(start, stop)]
+        state = attend_next(
+            pieces, [gathered], [gathered], state, stop == count, window_rows, cache_rows, near, limits
+        )
+    return state
 
 
 def solution(mesh):

time: 29 us -> 70.5 us (2.43)
  waiting for transfers between devices: 10.5 us -> 44.6 us
  between operations: 0.06 us -> 13.4 us
  starting transfers between devices: 9.48 us -> 0.01 us
  local copies, waits for them, and re-layouts: 0.01 us -> 3.24 us
    all_gather x0 -> x1, waiting for transfers between devices: none -> 44.6 us  [shards(): gathered = lax.all_gather(packed, 'ctx', axis=0, tiled=True)]
    ppermute x8 -> x0, waiting for transfers between devices: 10.5 us -> none  [the longest x3 7.78 us: shards(): next_on = lax.ppermute(on, 'ctx', onward)]
    ppermute x8 -> x0, starting transfers between devices: 9.48 us -> none  [the longest x3 5.98 us: shards(): next_on = lax.ppermute(on, 'ctx', onward)]
    unnamed x0 -> x6, local copies, waits for them, and re-layouts: none -> 3.24 us
    pallas_call x4 -> x1, Pallas kernels: 5.9 us -> 4.44 us  [attend_next(): pl.pallas_call(functools.partial(next_kernel, tuple(pieces), last, window...]
    pallas_call x1, Pallas kernels: 1.97 us -> 2.9 us  [attend_first(): pl.pallas_call(functools.partial(first_kernel, count, window_rows, cache_...]
  transfers between devices with their start and end apart: 8 -> 1, of which waited for: 5 -> 1; matrix products, arithmetic and copies ran while one was open for 0% -> 0% of each run, Pallas kernels for 22% -> 4%
where the time goes in v6:
time: 70.5 us; the launch traced here: 70.2 us
  waiting for transfers between devices  44.6 us (63%)
  between operations  13.4 us (19%)
  Pallas kernels  8.95 us (13%)
  local copies, waits for them, and re-layouts  3.24 us (5%)
    all_gather x1, waiting for transfers between devices, shards(): gathered = lax.all_gather(packed, 'ctx', axis=0, tiled=True)  44.6 us
    pallas_call x1, Pallas kernels, attend_next(): pl.pallas_call(functools.partial(next_kernel, tuple(pieces), last, window...  4.44 us
    unnamed x6, local copies, waits for them, and re-layouts  3.24 us
    pallas_call x1, Pallas kernels, attend_first(): pl.pallas_call(functools.partial(first_kernel, count, window_rows, cache_...  2.9 us
    pallas_call x1, Pallas kernels, pack(): pl.pallas_call(pack_kernel, out_shape=jax.ShapeDtypeStruct((rows, win_key...  1.6 us
  transfers between devices with their start and end apart: 1, of which 1 were waited for; matrix products, arithmetic and copies ran while one was open for 0% of the time, Pallas kernels for 4%

profile of v6, /device:TPU:0, one launch (start us, length us, event | category | flops | bytes accessed | tf_op | source)
XLA Modules:
  0.0 70.2 jit_solution(8784983592705953892)
XLA Ops:
  6.5 0.0 all-gather.2.cloned.1.call-start
  6.5 1.6 %pack.1.packed = bf16[384,256]{1,0:T(8,128)(2,1)} custom-call(bf16[128,256]{1,0:T(8,128)(2,1)} %win_keys.1, bf16[128,256]{1,0:T(8,128)(2,1)} %win_values.1, bf16[64,256]{1,0:T(8,128)(2,1)} %cache_keys.1, bf16[64,256]{1,0:T(8,128)(2,1)} %cache_values.1), custom_call_target="tpu_custom_call" | custom-call | bytes 393216 | tf_op jit(solution)/shard_map/pack/pallas_call | solution.py:64
  8.2 0.0 all-gather.2.cloned.1.call-update
  8.2 2.9 %attend_first.1 = (f32[2048,256]{1,0:T(8,128)S(1)}, f32[2048,128]{1,0:T(8,128)S(1)}, bf16[128,2048]{1,0:T(8,128)(2,1)S(1)}, s32[16,128]{1,0:T(8,128)S(1)}) custom-call(s32[8]{0:T(128)} %valid_hbm.1, s32[8]{0:T(128)} %first_hbm.1, bf16[128,2048]{1,0:T(8,128)(2,1)} %q_hbm.1, bf16[384,256]{1,0:T(8,128)(2,1)} %pack.1.packed), custom_call_target="tpu_custom_call" | custom-call | flops 402653184 | bytes 524288 | tf_op jit(solution)/shard_map/attend_first/pallas_call | solution.py:271
  11.1 0.0 copy-start.1
  11.1 0.8 %copy-done.1 = bf16[128,2048]{1,0:T(8,128)(2,1)} copy-done((bf16[128,2048]{1,0:T(8,128)(2,1)}, bf16[128,2048]{1,0:T(8,128)(2,1)S(1)}, u32[]{:S(2)}) %copy-start.1) | copy-done | bytes 524312
  11.9 44.6 %all-gather.2.cloned.1.call-done.refs_0_ = bf16[3072,256]{1,0:T(8,128)(2,1)} async-done(((bf16[384,256]{1,0:T(8,128)(2,1)}), bf16[3072,256]{1,0:T(8,128)(2,1)}) %all-gather.2.cloned.1.call-update) | async-done | bytes 1572880 | tf_op jit(solution)/shard_map/all_gather | solution.py:322
  56.5 0.0 copy-start
  56.5 1.4 %copy-done = bf16[3072,256]{1,0:T(8,128)(2,1)S(1)} copy-done((bf16[3072,256]{1,0:T(8,128)(2,1)S(1)}, bf16[3072,256]{1,0:T(8,128)(2,1)}, u32[]{:S(2)}) %copy-start) | copy-done | bytes 1572888
  57.9 0.0 copy-start.2
  57.9 1.0 %copy-done.2 = bf16[128,2048]{1,0:T(8,128)(2,1)S(1)} copy-done((bf16[128,2048]{1,0:T(8,128)(2,1)S(1)}, bf16[128,2048]{1,0:T(8,128)(2,1)}, u32[]{:S(2)}) %copy-start.2) | copy-done | bytes 524312
  58.9 4.4 %attend_last.1 = bf16[128,2048]{1,0:T(8,128)(2,1)} custom-call(bf16[128,2048]{1,0:T(8,128)(2,1)S(1)} %copy-done.2, s32[16,128]{1,0:T(8,128)S(1)} %get-tuple-element.10.limits, bf16[3072,256]{1,0:T(8,128)(2,1)S(1)} %copy-done, f32[2048,256]{1,0:T(8,128)S(1)} %get-tuple-element.11.refs_1_, f32[2048,128]{1,0:T(8,128)S(1)} %get-tuple-element.12.refs_2_), custom_call_target="tpu_custom_call" | custom-call | flops 2415919104 | bytes 524288 | tf_op jit(solution)/shard_map/attend_last/pallas_call | solution.py:302
Async XLA Ops:
  6.5 49.9 %all-gather.2.cloned.1.call-start = ((), (), s32[]{:S(2)}) async-start(), calls=%async_computation | async-start | bytes 1769472 | tf_op jit(solution)/shard_map/all_gather | solution.py:322
  11.1 0.8 %copy-start.1 = (bf16[128,2048]{1,0:T(8,128)(2,1)}, bf16[128,2048]{1,0:T(8,128)(2,1)S(1)}, u32[]{:S(2)}) copy-start(bf16[128,2048]{1,0:T(8,128)(2,1)S(1)} %get-tuple-element.9.q_ref) | copy-start | bytes 1572868
  56.5 1.4 %copy-start = (bf16[3072,256]{1,0:T(8,128)(2,1)S(1)}, bf16[3072,256]{1,0:T(8,128)(2,1)}, u32[]{:S(2)}) copy-start(bf16[3072,256]{1,0:T(8,128)(2,1)} %all-gather.2.cloned.1.call-done.refs_0_) | copy-start | bytes 4718596
  57.9 1.0 %copy-start.2 = (bf16[128,2048]{1,0:T(8,128)(2,1)S(1)}, bf16[128,2048]{1,0:T(8,128)(2,1)}, u32[]{:S(2)}) copy-start(bf16[128,2048]{1,0:T(8,128)(2,1)} %copy-done.1) | copy-start | bytes 1572868
Sparse Core Ops, SparseCore 0:
  9.5 46.8 all-gather.1

commit v7 on v5

--- a/solution.py
+++ b/solution.py
@@ -82,40 +82,40 @@
     return offsets + [half]
 
 
-def place_pieces(pieces, own, window_rows, cache_rows, limits, key_refs, value_refs, keys, values):
+def place_piece(index, number, limit_row, own, sizes, limits, key, key_base, value, value_base, keys, values):
+    window_rows, cache_rows = sizes
     stride = window_rows + cache_rows
-    kv_heads, total_keys = keys.shape[:2]
-    cache_at = len(pieces) * window_rows
-    row_iota = lax.broadcasted_iota(jnp.int32, (window_rows, HD), 0)
-    for index, (limit_row, key_base, value_base) in enumerate(pieces):
-        key, value = key_refs[index], value_refs[index]
-        if not own:
-            shown = row_iota < limits[limit_row : limit_row + 1, :]
-        for head in range(kv_heads):
-            lanes = slice(head * HD, (head + 1) * HD)
-            at = slice(index * window_rows, (index + 1) * window_rows)
-            win_key = key[key_base : key_base + window_rows, lanes]
-            win_value = value[value_base : value_base + window_rows, lanes]
-            if own:
-                keys[head, at, :] = win_key
-                values[head, at, :HD] = win_value
-                values[head, at, HD:] = jnp.ones((window_rows, HD), jnp.bfloat16)
-            else:
-                fill = key[key_base + window_rows : key_base + window_rows + 1, lanes].astype(jnp.float32)
-                keys[head, at, :] = jnp.where(shown, win_key.astype(jnp.float32), fill).astype(jnp.bfloat16)
-                values[head, at, :HD] = jnp.where(shown, win_value.astype(jnp.float32), 0.0).astype(jnp.bfloat16)
-                values[head, at, HD:] = jnp.where(shown, 1.0, 0.0).astype(jnp.bfloat16)
-            at = slice(cache_at + index * cache_rows, cache_at + (index + 1) * cache_rows)
-            keys[head, at, :] = key[key_base + window_rows : key_base + stride, lanes]
-            values[head, at, :HD] = value[value_base + window_rows : value_base + stride, lanes]
-            values[head, at, HD:] = jnp.ones((cache_rows, HD), jnp.bfloat16)
-    filled = len(pieces) * stride
-    if filled < total_keys:
-        key_base = pieces[0][1] + window_rows
-        for head in range(kv_heads):
-            row = key_refs[0][key_base : key_base + 1, head * HD : (head + 1) * HD].astype(jnp.float32)
-            keys[head, filled:, :] = jnp.broadcast_to(row, (total_keys - filled, HD)).astype(jnp.bfloat16)
-            values[head, filled:, :] = jnp.zeros((total_keys - filled, 2 * HD), jnp.bfloat16)
+    cache_at = number * window_rows + index * cache_rows
+    if not own:
+        row_iota = lax.broadcasted_iota(jnp.int32, (window_rows, HD), 0)
+        shown = row_iota < limits[limit_row : limit_row + 1, :]
+    for head in range(keys.shape[0]):
+        lanes = slice(head * HD, (head + 1) * HD)
+        at = slice(index * window_rows, (index + 1) * window_rows)
+        win_key = key[key_base : key_base + window_rows, lanes]
+        win_value = value[value_base : value_base + window_rows, lanes]
+        if own:
+            keys[head, at, :] = win_key
+            values[head, at, :HD] = win_value
+            values[head, at, HD:] = jnp.ones((window_rows, HD), jnp.bfloat16)
+        else:
+            fill = key[key_base + window_rows : key_base + window_rows + 1, lanes].astype(jnp.float32)
+            keys[head, at, :] = jnp.where(shown, win_key.astype(jnp.float32), fill).astype(jnp.bfloat16)
+            values[head, at, :HD] = jnp.where(shown, win_value.astype(jnp.float32), 0.0).astype(jnp.bfloat16)
+            values[head, at, HD:] = jnp.where(shown, 1.0, 0.0).astype(jnp.bfloat16)
+        at = slice(cache_at, cache_at + cache_rows)
+        keys[head, at, :] = key[key_base + window_rows : key_base + stride, lanes]
+        values[head, at, :HD] = value[value_base + window_rows : value_base + stride, lanes]
+        values[head, at, HD:] = jnp.ones((cache_rows, HD), jnp.bfloat16)
+
+
+def fill_up(filled, keys, values):
+    spare = keys.shape[1] - filled
+    if spare:
+        for head in range(keys.shape[0]):
+            row = keys[head, filled - 1 : filled, :].astype(jnp.float32)
+            keys[head, filled:, :] = jnp.broadcast_to(row, (spare, HD)).astype(jnp.bfloat16)
+            values[head, filled:, :] = jnp.zeros((spare, 2 * HD), jnp.bfloat16)
 
 
 def scores(query, keys):
@@ -162,7 +162,8 @@
     for copy in copies:
         copy.start()
     stride = window_rows + cache_rows
-    place_pieces(((0, 0, stride),), True, window_rows, cache_rows, None, (packed,), (packed,), keys, values)
+    place_piece(0, 1, 0, True, (window_rows, cache_rows), None, packed, 0, packed, stride, keys, values)
+    fill_up(stride, keys, values)
     for copy in copies:
         copy.wait()
 
@@ -188,14 +189,35 @@
         top_out[at, :] = top
 
 
-def next_kernel(pieces, last, window_rows, cache_rows, q_ref, limits, *refs):
-    number = len(pieces)
-    key_refs, value_refs = refs[:number], refs[number : 2 * number]
+def next_kernel(rows_of, split, last, count, sizes, q_ref, limits, *refs):
+    number = len(rows_of)
+    whole = number - split
+    blocks, halves = refs[:whole], refs[whole : whole + 2 * split]
+    refs = refs[whole + 2 * split :]
     if last:
-        acc_in, top_in, out, keys, values, result, sems = refs[2 * number :]
+        acc_in, top_in, out, keys, values, result, sems = refs
     else:
-        acc_in, top_in, acc_out, top_out, keys, values = refs[2 * number :]
-    place_pieces(pieces, False, window_rows, cache_rows, limits, key_refs, value_refs, keys, values)
+        acc_in, top_in, acc_out, top_out, keys, values = refs
+    stride = sum(sizes)
+    for index, block in enumerate(blocks):
+        place_piece(index, number, rows_of[index], False, sizes, limits, block, 0, block, stride, keys, values)
+    if split:
+        place = functools.partial(place_piece, whole, number, rows_of[whole], False, sizes, limits)
+        if halves[0].shape[0] == stride:
+            place(halves[0], 0, halves[1], 0, keys, values)
+        else:
+            me = lax.axis_index("ctx")
+            corner = (me < 2) | (me >= count - 2)
+
+            @pl.when(corner)
+            def _():
+                place(halves[0], 0, halves[0], stride, keys, values)
+
+            @pl.when(jnp.logical_not(corner))
+            def _():
+                place(halves[1], 0, halves[1], stride, keys, values)
+
+    fill_up(number * stride, keys, values)
     rows = q_ref.shape[0]
     kv_heads = keys.shape[0]
 
@@ -289,18 +311,18 @@
     return (acc, top), q_near, limits
 
 
-def attend_next(pieces, keys, values, state, last, window_rows, cache_rows, queries, limits):
-    kv_heads = keys[0].shape[1] // HD
-    total_keys = -(-len(pieces) * (window_rows + cache_rows) // HD) * HD
+def attend_next(rows_of, blocks, halves, state, last, count, window_rows, cache_rows, queries, limits):
+    kv_heads = blocks[0].shape[1] // HD
+    total_keys = -(-len(rows_of) * (window_rows + cache_rows) // HD) * HD
     vmem = pl.BlockSpec(memory_space=pltpu.VMEM)
-    operands = [queries, limits, *keys, *values, *state]
+    operands = [queries, limits, *blocks, *halves, *state]
     shapes = [jax.ShapeDtypeStruct(queries.shape, queries.dtype)] if last else state_shapes(queries)
     scratch = room(kv_heads, total_keys)
     if last:
         chunk_count = queries.shape[1] // HD // CHUNK_HEADS
         scratch += [pltpu.VMEM(queries.shape, queries.dtype), pltpu.SemaphoreType.DMA((chunk_count,))]
     outs = pl.pallas_call(
-        functools.partial(next_kernel, tuple(pieces), last, window_rows, cache_rows),
+        functools.partial(next_kernel, tuple(rows_of), bool(halves), last, count, (window_rows, cache_rows)),
         out_shape=shapes,
         in_specs=[vmem] * len(operands),
         out_specs=[pl.BlockSpec(memory_space=pltpu.HBM)] if last else [vmem] * len(shapes),
@@ -311,11 +333,10 @@
     return outs[0] if last else tuple(outs)
 
 
-def swap_pairs(count, distance, parity):
-    ring = [place_at(p, count) for p in range(count)]
+def swap_pairs(count, parity):
     pairs = []
     for p in range(parity, count, 2):
-        first, second = ring[p], ring[(p + distance) % count]
+        first, second = place_at(p, count), place_at((p + 1) % count, count)
         pairs += [(first, second), (second, first)]
     return pairs
 
@@ -325,37 +346,51 @@
     stride = window_rows + cache_rows
     half = count // 2
     sizes = (window_rows, cache_rows)
-    odd = functools.partial(lax.ppermute, axis_name="ctx", perm=swap_pairs(count, 1, 1))
-    even = functools.partial(lax.ppermute, axis_name="ctx", perm=swap_pairs(count, 1, 0))
-    across = functools.partial(lax.ppermute, axis_name="ctx", perm=swap_pairs(count, half - 1, 0))
+    send = functools.partial(lax.ppermute, axis_name="ctx")
+    odd, even = swap_pairs(count, 1), swap_pairs(count, 0)
+    short = ring_width(count) == 2 and count == 8
+    corners = [(0, 7), (7, 0), (1, 6), (6, 1)]
+    rungs = [(2, 3), (3, 2), (4, 5), (5, 4)]
 
     win_keys, win_values, cache_keys, cache_values, valid_counts, first_block, queries = [
         pltpu.with_memory_space_constraint(x, pltpu.HBM)
         for x in (win_keys, win_values, cache_keys, cache_values, valid_counts, first_block, queries)
     ]
-    p = q = pack(win_keys, win_values, cache_keys, cache_values)
-    opposite = None
-    state, near, limits = attend_first(count, *sizes, valid_counts, first_block, queries, p)
+    p = q = own = pack(win_keys, win_values, cache_keys, cache_values)
+    state, near, limits = attend_first(count, *sizes, valid_counts, first_block, queries, own)
+    common = (count, *sizes, near, limits)
+    opposite = []
     for step in range(1, half):
-        next_p = (odd if step % 2 else even)(p)
-        next_q = (even if step % 2 else odd)(q)
-        if step == 2:
-            opposite = across(p)
-        if step > 1:
-            row = 2 * (step - 2)
-            pieces, arrived = [(row, 0, stride), (row + 1, 0, stride)], [p, q]
-            if step == half - 1:
-                pieces.append((2 * (half - 1), 0, stride))
-                arrived.append(opposite)
-            state = attend_next(pieces, arrived, arrived, state, False, *sizes, near, limits)
+        next_p = send(p, perm=odd if step % 2 else even)
+        next_q = send(q, perm=even if step % 2 else odd)
+        row = 2 * (step - 2)
+        rows_of = [row, row + 1]
+        if short and step == 3:
+            state = attend_next([*rows_of, 2 * (half - 1)], [p, q], opposite, state, False, *common)
+        elif step > 1:
+            state = attend_next(rows_of, [p, q], [], state, False, *common)
+        acc, top = state
+        if short and step == 1:
+            own, top = lax.optimization_barrier((own, top))
+            opposite = [send(own, perm=corners)]
+        elif short and step == 2:
+            p, top = lax.optimization_barrier((p, top))
+            opposite.append(send(p, perm=rungs))
         if step < half - 1:
-            p, top = lax.optimization_barrier((next_p, state[1]))
+            if short and step == 2:
+                opposite[0], next_p = lax.optimization_barrier((opposite[0], next_p))
+            p, top = lax.optimization_barrier((next_p, top))
             q, top = lax.optimization_barrier((next_q, top))
-            state = (state[0], top)
         else:
             p, q = next_p, next_q
+        state = (acc, top)
     row = 2 * (half - 2)
-    return attend_next([(row, 0, stride), (row + 1, 0, stride)], [p, q], [p, q], state, True, *sizes, near, limits)
+    if short:
+        state = attend_next([row], [p], [], state, False, *common)
+        return attend_next([row + 1], [q], [], state, True, *common)
+    key_half = send(p[:stride], perm=even if half % 2 == 0 else odd)
+    value_half = send(q[stride:], perm=odd if half % 2 == 0 else even)
+    return attend_next([row, row + 1, row + 2], [p, q], [key_half, value_half], state, True, *common)
 
 
 def solution(mesh):

time: 30.3 us -> 31.5 us (1.040)
  waiting for transfers between devices: 3.68 us -> 9.61 us
  starting transfers between devices: 17.9 us -> 12.6 us
  Pallas kernels: 8.55 us -> 8.96 us
    ppermute x7 -> x8, waiting for transfers between devices: 3.68 us -> 9.61 us  [the longest x1 4.86 us: shards(): opposite = [send(own, perm=corners)]]
    ppermute x7 -> x8, starting transfers between devices: 17.9 us -> 12.6 us  [the longest x3 4.24 us: shards(): next_p = send(p, perm=odd if step % 2 else even)]
    pallas_call x3 -> x4, Pallas kernels: 5.65 us -> 6.07 us  [attend_next(): pl.pallas_call(functools.partial(next_kernel, tuple(rows_of), bool(halves...]
  transfers between devices with their start and end apart: 7 -> 8, of which waited for: 4 -> 4; matrix products, arithmetic and copies ran while one was open for 0% -> 0% of each run, Pallas kernels for 18% -> 20%
where the time goes in v7:
time: 31.5 us; the launch traced here: 31.3 us
  starting transfers between devices  12.6 us (40%)
  waiting for transfers between devices  9.61 us (31%)
  Pallas kernels  8.96 us (28%)
    pallas_call x4, Pallas kernels, attend_next(): pl.pallas_call(functools.partial(next_kernel, tuple(rows_of), bool(halves...  6.07 us
    ppermute x1, waiting for transfers between devices, shards(): opposite = [send(own, perm=corners)]  4.86 us
    ppermute x3, waiting for transfers between devices, shards(): next_p = send(p, perm=odd if step % 2 else even)  4.28 us
    ppermute x3, starting transfers between devices, shards(): next_p = send(p, perm=odd if step % 2 else even)  4.24 us
    ppermute x1, starting transfers between devices, shards(): opposite = [send(own, perm=corners)]  4.18 us
    ppermute x3, starting transfers between devices, shards(): next_q = send(q, perm=even if step % 2 else odd)  3.5 us
    pallas_call x1, Pallas kernels, attend_first(): pl.pallas_call(functools.partial(first_kernel, count, window_rows, cache_...  1.97 us
    pallas_call x1, Pallas kernels, pack(): pl.pallas_call(pack_kernel, out_shape=jax.ShapeDtypeStruct((rows, win_key...  0.93 us
  transfers between devices with their start and end apart: 8, of which 4 were waited for; matrix products, arithmetic and copies ran while one was open for 0% of the time, Pallas kernels for 20%

profile of v7, /device:TPU:0, one launch (start us, length us, event | category | flops | bytes accessed | tf_op | source)
XLA Modules:
  0.0 31.3 jit_solution(10435530605426721580)
XLA Ops:
  0.0 0.9 %pack.1.packed = bf16[384,256]{1,0:T(8,128)(2,1)S(1)} custom-call(bf16[128,256]{1,0:T(8,128)(2,1)} %win_keys.1, bf16[128,256]{1,0:T(8,128)(2,1)} %win_values.1, bf16[64,256]{1,0:T(8,128)(2,1)} %cache_keys.1, bf16[64,256]{1,0:T(8,128)(2,1)} %cache_values.1), custom_call_target="tpu_custom_call" | custom-call | bytes 393216 | tf_op jit(solution)/shard_map/pack/pallas_call | solution.py:64
  0.9 3.0 %collective-permute-start.1 = (bf16[384,256]{1,0:T(8,128)(2,1)S(1)}, bf16[384,256]{1,0:T(8,128)(2,1)S(1)}, u32[]{:S(2)}, u32[]{:S(2)}) collective-permute-start(bf16[384,256]{1,0:T(8,128)(2,1)S(1)} %pack.1.packed), channel_id=1, source_target_pairs={{6,10},{10,6},{14,12},{12,14},{8,4},{4,8},{0,2},{2,0},{7,11},{11,7... | collective-permute-start | bytes 589832 | tf_op jit(solution)/shard_map/ppermute | solution.py:364
  3.9 1.7 %collective-permute-start = (bf16[384,256]{1,0:T(8,128)(2,1)S(1)}, bf16[384,256]{1,0:T(8,128)(2,1)S(1)}, u32[]{:S(2)}, u32[]{:S(2)}) collective-permute-start(bf16[384,256]{1,0:T(8,128)(2,1)S(1)} %pack.1.packed), channel_id=1, source_target_pairs={{2,6},{6,2},{10,14},{14,10},{12,8},{8,12},{4,0},{0,4},{3,7},{7,3},... | collective-permute-start | bytes 589832 | tf_op jit(solution)/shard_map/ppermute | solution.py:365
  5.6 2.0 %attend_first.1 = (f32[2048,256]{1,0:T(8,128)S(1)}, f32[2048,128]{1,0:T(8,128)S(1)}, bf16[128,2048]{1,0:T(8,128)(2,1)S(1)}, s32[8,128]{1,0:T(8,128)S(1)}) custom-call(s32[8]{0:T(128)} %valid_hbm.1, s32[8]{0:T(128)} %first_hbm.1, bf16[128,2048]{1,0:T(8,128)(2,1)} %q_hbm.1, bf16[384,256]{1,0:T(8,128)(2,1)S(1)} %pack.1.packed), custom_call_target="tpu_custom_call" | custom-call | flops 402653184 | bytes 524288 | tf_op jit(solution)/shard_map/attend_first/pallas_call | solution.py:293
  7.6 4.2 %collective-permute-start.3 = (bf16[384,256]{1,0:T(8,128)(2,1)S(1)}, bf16[384,256]{1,0:T(8,128)(2,1)S(1)}, u32[]{:S(2)}, u32[]{:S(2)}) collective-permute-start(bf16[384,256]{1,0:T(8,128)(2,1)S(1)} %pack.1.packed), channel_id=1, source_target_pairs={{0,14},{14,0},{2,12},{12,2},{1,15},{15,1},{3,13},{13,3},{16,30},{3... | collective-permute-start | bytes 589832 | tf_op jit(solution)/shard_map/ppermute | solution.py:375
  11.8 0.0 collective-permute-done.1.refs_0_
  11.8 0.1 collective-permute-start.4
  11.9 0.0 collective-permute-done.refs_1_
  11.9 1.2 %collective-permute-start.2 = (bf16[384,256]{1,0:T(8,128)(2,1)S(1)}, bf16[384,256]{1,0:T(8,128)(2,1)S(1)}, u32[]{:S(2)}, u32[]{:S(2)}) collective-permute-start(bf16[384,256]{1,0:T(8,128)(2,1)S(1)} %collective-permute-done.refs_1_), channel_id=1, source_target_pairs={{6,10},{10,6},{14,12},{12,14},{8,4},{4,8},{0,2},{2,0},{7,11},{11,7... | collective-permute-start | bytes 589832 | tf_op jit(solution)/shard_map/ppermute | solution.py:365
  13.1 1.4 %attend_next.3 = (f32[2048,256]{1,0:T(8,128)S(1)}, f32[2048,128]{1,0:T(8,128)S(1)}) custom-call(bf16[128,2048]{1,0:T(8,128)(2,1)S(1)} %get-tuple-element.29.q_ref, s32[8,128]{1,0:T(8,128)S(1)} %get-tuple-element.30.limits, bf16[384,256]{1,0:T(8,128)(2,1)S(1)} %collective-permute-done.1.refs_0_, bf16[384,256]{1,0:T(8,128)(2,1)S(1)} %collective-permute-done.refs_1_, ...), custom_call_target="tpu_custom_call" | custom-call | flops 603979776 | bytes 524288 | tf_op jit(solution)/shard_map/attend_next/pallas_call | solution.py:324
  14.5 0.7 %collective-permute-start.7 = (bf16[384,256]{1,0:T(8,128)(2,1)S(1)}, bf16[384,256]{1,0:T(8,128)(2,1)S(1)}, u32[]{:S(2)}, u32[]{:S(2)}) collective-permute-start(bf16[384,256]{1,0:T(8,128)(2,1)S(1)} %collective-permute-done.1.refs_0_), channel_id=1, source_target_pairs={{4,6},{6,4},{8,10},{10,8},{5,7},{7,5},{9,11},{11,9},{20,22},{22,20... | collective-permute-start | bytes 589832 | tf_op jit(solution)/shard_map/ppermute | solution.py:378
  15.2 4.9 %collective-permute-done.3.refs_2_ = bf16[384,256]{1,0:T(8,128)(2,1)S(1)} collective-permute-done((bf16[384,256]{1,0:T(8,128)(2,1)S(1)}, bf16[384,256]{1,0:T(8,128)(2,1)S(1)}, u32[]{:S(2)}, u32[]{:S(2)}) %collective-permute-start.3) | collective-permute-done | bytes 196640 | tf_op jit(solution)/shard_map/ppermute | solution.py:375
  20.0 1.8 %collective-permute-done.4.refs_0_ = bf16[384,256]{1,0:T(8,128)(2,1)S(1)} collective-permute-done((bf16[384,256]{1,0:T(8,128)(2,1)S(1)}, bf16[384,256]{1,0:T(8,128)(2,1)S(1)}, u32[]{:S(2)}, u32[]{:S(2)}) %collective-permute-start.4) | collective-permute-done | bytes 196640 | tf_op jit(solution)/shard_map/ppermute | solution.py:364
  21.9 1.2 %collective-permute-start.6 = (bf16[384,256]{1,0:T(8,128)(2,1)S(1)}, bf16[384,256]{1,0:T(8,128)(2,1)S(1)}, u32[]{:S(2)}, u32[]{:S(2)}) collective-permute-start(bf16[384,256]{1,0:T(8,128)(2,1)S(1)} %collective-permute-done.4.refs_0_), channel_id=1, source_target_pairs={{6,10},{10,6},{14,12},{12,14},{8,4},{4,8},{0,2},{2,0},{7,11},{11,7... | collective-permute-start | bytes 589832 | tf_op jit(solution)/shard_map/ppermute | solution.py:364
  23.0 0.0 collective-permute-done.2.refs_1_
  23.0 0.6 %collective-permute-start.5 = (bf16[384,256]{1,0:T(8,128)(2,1)S(1)}, bf16[384,256]{1,0:T(8,128)(2,1)S(1)}, u32[]{:S(2)}, u32[]{:S(2)}) collective-permute-start(bf16[384,256]{1,0:T(8,128)(2,1)S(1)} %collective-permute-done.2.refs_1_), channel_id=1, source_target_pairs={{2,6},{6,2},{10,14},{14,10},{12,8},{8,12},{4,0},{0,4},{3,7},{7,3},... | collective-permute-start | bytes 589832 | tf_op jit(solution)/shard_map/ppermute | solution.py:365
  23.7 0.0 collective-permute-done.7.refs_3_
  23.7 2.0 %attend_next.4 = (f32[2048,256]{1,0:T(8,128)S(1)}, f32[2048,128]{1,0:T(8,128)S(1)}) custom-call(bf16[128,2048]{1,0:T(8,128)(2,1)S(1)} %get-tuple-element.29.q_ref, s32[8,128]{1,0:T(8,128)S(1)} %get-tuple-element.30.limits, bf16[384,256]{1,0:T(8,128)(2,1)S(1)} %collective-permute-done.4.refs_0_, bf16[384,256]{1,0:T(8,128)(2,1)S(1)} %collective-permute-done.2.refs_1_, ...), custom_call_target="tpu_custom_call" | custom-call | flops 1006632960 | bytes 524288 | tf_op jit(solution)/shard_map/attend_next/pallas_call | solution.py:324
  25.7 2.4 %collective-permute-done.6.refs_0_ = bf16[384,256]{1,0:T(8,128)(2,1)S(1)} collective-permute-done((bf16[384,256]{1,0:T(8,128)(2,1)S(1)}, bf16[384,256]{1,0:T(8,128)(2,1)S(1)}, u32[]{:S(2)}, u32[]{:S(2)}) %collective-permute-start.6) | collective-permute-done | bytes 196640 | tf_op jit(solution)/shard_map/ppermute | solution.py:364
  28.1 1.0 %attend_next.5 = (f32[2048,256]{1,0:T(8,128)S(1)}, f32[2048,128]{1,0:T(8,128)S(1)}) custom-call(bf16[128,2048]{1,0:T(8,128)(2,1)S(1)} %get-tuple-element.29.q_ref, s32[8,128]{1,0:T(8,128)S(1)} %get-tuple-element.30.limits, bf16[384,256]{1,0:T(8,128)(2,1)S(1)} %collective-permute-done.6.refs_0_, f32[2048,256]{1,0:T(8,128)S(1)} %get-tuple-element.49.refs_1_, ...), custom_call_target="tpu_custom_call" | custom-call | flops 402653184 | bytes 524288 | tf_op jit(solution)/shard_map/attend_next/pallas_call | solution.py:324
  29.1 0.5 %collective-permute-done.5.refs_0_ = bf16[384,256]{1,0:T(8,128)(2,1)S(1)} collective-permute-done((bf16[384,256]{1,0:T(8,128)(2,1)S(1)}, bf16[384,256]{1,0:T(8,128)(2,1)S(1)}, u32[]{:S(2)}, u32[]{:S(2)}) %collective-permute-start.5) | collective-permute-done | bytes 196640 | tf_op jit(solution)/shard_map/ppermute | solution.py:365
  29.6 1.7 %attend_last.1 = bf16[128,2048]{1,0:T(8,128)(2,1)} custom-call(bf16[128,2048]{1,0:T(8,128)(2,1)S(1)} %get-tuple-element.29.q_ref, s32[8,128]{1,0:T(8,128)S(1)} %get-tuple-element.30.limits, bf16[384,256]{1,0:T(8,128)(2,1)S(1)} %collective-permute-done.5.refs_0_, f32[2048,256]{1,0:T(8,128)S(1)} %get-tuple-element.51.refs_1_, ...), custom_call_target="tpu_custom_call" | custom-call | flops 402653184 | bytes 524288 | tf_op jit(solution)/shard_map/attend_last/pallas_call | solution.py:324
Async XLA Ops:
  0.9 10.8 %collective-permute-start.1 = (bf16[384,256]{1,0:T(8,128)(2,1)S(1)}, bf16[384,256]{1,0:T(8,128)(2,1)S(1)}, u32[]{:S(2)}, u32[]{:S(2)}) collective-permute-start(bf16[384,256]{1,0:T(8,128)(2,1)S(1)} %pack.1.packed), channel_id=1, source_target_pairs={{6,10},{10,6},{14,12},{12,14},{8,4},{4,8},{0,2},{2,0},{7,11},{11,7... | collective-permute-start | bytes 589832 | tf_op jit(solution)/shard_map/ppermute | solution.py:364
  3.9 7.9 %collective-permute-start = (bf16[384,256]{1,0:T(8,128)(2,1)S(1)}, bf16[384,256]{1,0:T(8,128)(2,1)S(1)}, u32[]{:S(2)}, u32[]{:S(2)}) collective-permute-start(bf16[384,256]{1,0:T(8,128)(2,1)S(1)} %pack.1.packed), channel_id=1, source_target_pairs={{2,6},{6,2},{10,14},{14,10},{12,8},{8,12},{4,0},{0,4},{3,7},{7,3},... | collective-permute-start | bytes 589832 | tf_op jit(solution)/shard_map/ppermute | solution.py:365
  7.6 12.4 %collective-permute-start.3 = (bf16[384,256]{1,0:T(8,128)(2,1)S(1)}, bf16[384,256]{1,0:T(8,128)(2,1)S(1)}, u32[]{:S(2)}, u32[]{:S(2)}) collective-permute-start(bf16[384,256]{1,0:T(8,128)(2,1)S(1)} %pack.1.packed), channel_id=1, source_target_pairs={{0,14},{14,0},{2,12},{12,2},{1,15},{15,1},{3,13},{13,3},{16,30},{3... | collective-permute-start | bytes 589832 | tf_op jit(solution)/shard_map/ppermute | solution.py:375
  11.8 10.1 %collective-permute-start.4 = (bf16[384,256]{1,0:T(8,128)(2,1)S(1)}, bf16[384,256]{1,0:T(8,128)(2,1)S(1)}, u32[]{:S(2)}, u32[]{:S(2)}) collective-permute-start(bf16[384,256]{1,0:T(8,128)(2,1)S(1)} %collective-permute-done.1.refs_0_), channel_id=1, source_target_pairs={{2,6},{6,2},{10,14},{14,10},{12,8},{8,12},{4,0},{0,4},{3,7},{7,3},... | collective-permute-start | bytes 589832 | tf_op jit(solution)/shard_map/ppermute | solution.py:364
  11.9 11.2 %collective-permute-start.2 = (bf16[384,256]{1,0:T(8,128)(2,1)S(1)}, bf16[384,256]{1,0:T(8,128)(2,1)S(1)}, u32[]{:S(2)}, u32[]{:S(2)}) collective-permute-start(bf16[384,256]{1,0:T(8,128)(2,1)S(1)} %collective-permute-done.refs_1_), channel_id=1, source_target_pairs={{6,10},{10,6},{14,12},{12,14},{8,4},{4,8},{0,2},{2,0},{7,11},{11,7... | collective-permute-start | bytes 589832 | tf_op jit(solution)/shard_map/ppermute | solution.py:365
  14.5 9.2 %collective-permute-start.7 = (bf16[384,256]{1,0:T(8,128)(2,1)S(1)}, bf16[384,256]{1,0:T(8,128)(2,1)S(1)}, u32[]{:S(2)}, u32[]{:S(2)}) collective-permute-start(bf16[384,256]{1,0:T(8,128)(2,1)S(1)} %collective-permute-done.1.refs_0_), channel_id=1, source_target_pairs={{4,6},{6,4},{8,10},{10,8},{5,7},{7,5},{9,11},{11,9},{20,22},{22,20... | collective-permute-start | bytes 589832 | tf_op jit(solution)/shard_map/ppermute | solution.py:378
  21.9 6.2 %collective-permute-start.6 = (bf16[384,256]{1,0:T(8,128)(2,1)S(1)}, bf16[384,256]{1,0:T(8,128)(2,1)S(1)}, u32[]{:S(2)}, u32[]{:S(2)}) collective-permute-start(bf16[384,256]{1,0:T(8,128)(2,1)S(1)} %collective-permute-done.4.refs_0_), channel_id=1, source_target_pairs={{6,10},{10,6},{14,12},{12,14},{8,4},{4,8},{0,2},{2,0},{7,11},{11,7... | collective-permute-start | bytes 589832 | tf_op jit(solution)/shard_map/ppermute | solution.py:364
  23.0 6.5 %collective-permute-start.5 = (bf16[384,256]{1,0:T(8,128)(2,1)S(1)}, bf16[384,256]{1,0:T(8,128)(2,1)S(1)}, u32[]{:S(2)}, u32[]{:S(2)}) collective-permute-start(bf16[384,256]{1,0:T(8,128)(2,1)S(1)} %collective-permute-done.2.refs_1_), channel_id=1, source_target_pairs={{2,6},{6,2},{10,14},{14,10},{12,8},{8,12},{4,0},{0,4},{3,7},{7,3},... | collective-permute-start | bytes 589832 | tf_op jit(solution)/shard_map/ppermute | solution.py:365

commit v8 on v3

--- a/solution.py
+++ b/solution.py
@@ -46,13 +46,14 @@
     return jnp.where(column == 0, rows * (width - 1) + rows - 1 - row, snake)
 
 
-def pack_kernel(win_keys, win_values, cache_keys, cache_values, packed, sems):
-    start = 0
-    copies = []
-    for index, piece in enumerate((win_keys, cache_keys, win_values, cache_values)):
-        rows = piece.shape[0]
-        copies.append(pltpu.make_async_copy(piece, packed.at[start : start + rows], sems.at[index]))
-        start += rows
+def pack_kernel(win_keys, win_values, cache_keys, cache_values, keys, values, sems):
+    window_rows = win_keys.shape[0]
+    copies = [
+        pltpu.make_async_copy(win_keys, keys.at[:window_rows], sems.at[0]),
+        pltpu.make_async_copy(cache_keys, keys.at[window_rows:], sems.at[1]),
+        pltpu.make_async_copy(win_values, values.at[:window_rows], sems.at[2]),
+        pltpu.make_async_copy(cache_values, values.at[window_rows:], sems.at[3]),
+    ]
     for copy in copies:
         copy.start()
     for copy in copies:
@@ -60,15 +61,15 @@
 
 
 def pack(win_keys, win_values, cache_keys, cache_values):
-    rows = 2 * (win_keys.shape[0] + cache_keys.shape[0])
+    rows, width = win_keys.shape[0] + cache_keys.shape[0], win_keys.shape[1]
     return pl.pallas_call(
         pack_kernel,
-        out_shape=jax.ShapeDtypeStruct((rows, win_keys.shape[1]), win_keys.dtype),
+        out_shape=[jax.ShapeDtypeStruct((rows, width), win_keys.dtype)] * 2,
         in_specs=[pl.BlockSpec(memory_space=pltpu.HBM)] * 4,
-        out_specs=pl.BlockSpec(memory_space=pltpu.VMEM),
+        out_specs=[pl.BlockSpec(memory_space=pltpu.VMEM)] * 2,
         scratch_shapes=[pltpu.SemaphoreType.DMA((4,))],
         compiler_params=pltpu.CompilerParams(vmem_limit_bytes=4 * 1024 * 1024),
-        cost_estimate=pl.CostEstimate(flops=0, bytes_accessed=4 * rows * win_keys.shape[1], transcendentals=0),
+        cost_estimate=pl.CostEstimate(flops=0, bytes_accessed=8 * rows * width, transcendentals=0),
         name="pack",
     )(win_keys, win_values, cache_keys, cache_values)
 
@@ -78,40 +79,38 @@
     return [sign * step for step in range(1, half) for sign in (-1, 1)] + [half]
 
 
-def place_pieces(pieces, own, window_rows, cache_rows, limits, key_refs, value_refs, keys, values):
-    stride = window_rows + cache_rows
-    kv_heads, total_keys = keys.shape[:2]
-    cache_at = len(pieces) * window_rows
-    row_iota = lax.broadcasted_iota(jnp.int32, (window_rows, HD), 0)
-    for index, (limit_row, key_base, value_base) in enumerate(pieces):
-        key, value = key_refs[index], value_refs[index]
-        if not own:
-            shown = row_iota < limits[limit_row : limit_row + 1, :]
-        for head in range(kv_heads):
-            lanes = slice(head * HD, (head + 1) * HD)
-            at = slice(index * window_rows, (index + 1) * window_rows)
-            win_key = key[key_base : key_base + window_rows, lanes]
-            win_value = value[value_base : value_base + window_rows, lanes]
-            if own:
-                keys[head, at, :] = win_key
-                values[head, at, :HD] = win_value
-                values[head, at, HD:] = jnp.ones((window_rows, HD), jnp.bfloat16)
-            else:
-                fill = key[key_base + window_rows : key_base + window_rows + 1, lanes].astype(jnp.float32)
-                keys[head, at, :] = jnp.where(shown, win_key.astype(jnp.float32), fill).astype(jnp.bfloat16)
-                values[head, at, :HD] = jnp.where(shown, win_value.astype(jnp.float32), 0.0).astype(jnp.bfloat16)
-                values[head, at, HD:] = jnp.where(shown, 1.0, 0.0).astype(jnp.bfloat16)
-            at = slice(cache_at + index * cache_rows, cache_at + (index + 1) * cache_rows)
-            keys[head, at, :] = key[key_base + window_rows : key_base + stride, lanes]
-            values[head, at, :HD] = value[value_base + window_rows : value_base + stride, lanes]
-            values[head, at, HD:] = jnp.ones((cache_rows, HD), jnp.bfloat16)
-    filled = len(pieces) * stride
-    if filled < total_keys:
-        key_base = pieces[0][1] + window_rows
-        for head in range(kv_heads):
-            row = key_refs[0][key_base : key_base + 1, head * HD : (head + 1) * HD].astype(jnp.float32)
-            keys[head, filled:, :] = jnp.broadcast_to(row, (total_keys - filled, HD)).astype(jnp.bfloat16)
-            values[head, filled:, :] = jnp.zeros((total_keys - filled, 2 * HD), jnp.bfloat16)
+def place_piece(index, number, limit_row, own, sizes, limits, key, value, keys, values):
+    window_rows, cache_rows = sizes
+    cache_at = number * window_rows + index * cache_rows
+    if not own:
+        row_iota = lax.broadcasted_iota(jnp.int32, (window_rows, HD), 0)
+        shown = row_iota < limits[limit_row : limit_row + 1, :]
+    for head in range(keys.shape[0]):
+        lanes = slice(head * HD, (head + 1) * HD)
+        at = slice(index * window_rows, (index + 1) * window_rows)
+        win_key, win_value = key[:window_rows, lanes], value[:window_rows, lanes]
+        if own:
+            keys[head, at, :] = win_key
+            values[head, at, :HD] = win_value
+            values[head, at, HD:] = jnp.ones((window_rows, HD), jnp.bfloat16)
+        else:
+            fill = key[window_rows : window_rows + 1, lanes].astype(jnp.float32)
+            keys[head, at, :] = jnp.where(shown, win_key.astype(jnp.float32), fill).astype(jnp.bfloat16)
+            values[head, at, :HD] = jnp.where(shown, win_value.astype(jnp.float32), 0.0).astype(jnp.bfloat16)
+            values[head, at, HD:] = jnp.where(shown, 1.0, 0.0).astype(jnp.bfloat16)
+        at = slice(cache_at, cache_at + cache_rows)
+        keys[head, at, :] = key[window_rows:, lanes]
+        values[head, at, :HD] = value[window_rows:, lanes]
+        values[head, at, HD:] = jnp.ones((cache_rows, HD), jnp.bfloat16)
+
+
+def fill_up(filled, keys, values):
+    spare = keys.shape[1] - filled
+    if spare:
+        for head in range(keys.shape[0]):
+            row = keys[head, filled - 1 : filled, :].astype(jnp.float32)
+            keys[head, filled:, :] = jnp.broadcast_to(row, (spare, HD)).astype(jnp.bfloat16)
+            values[head, filled:, :] = jnp.zeros((spare, 2 * HD), jnp.bfloat16)
 
 
 def scores(query, keys):
@@ -147,7 +146,7 @@
 
 
 def first_kernel(
-    count, window_rows, cache_rows, valid_hbm, first_hbm, q_hbm, packed, acc_out, top_out, q_ref, limits,
+    count, window_rows, cache_rows, valid_hbm, first_hbm, q_hbm, own_keys, own_values, acc_out, top_out, q_ref, limits,
     keys, values, valid_ref, first_ref, sems,
 ):
     copies = [
@@ -157,8 +156,8 @@
     ]
     for copy in copies:
         copy.start()
-    stride = window_rows + cache_rows
-    place_pieces(((0, 0, stride),), True, window_rows, cache_rows, None, (packed,), (packed,), keys, values)
+    place_piece(0, 1, 0, True, (window_rows, cache_rows), None, own_keys, own_values, keys, values)
+    fill_up(window_rows + cache_rows, keys, values)
     for copy in copies:
         copy.wait()
 
@@ -183,14 +182,16 @@
         top_out[at, :] = top
 
 
-def next_kernel(pieces, last, window_rows, cache_rows, q_ref, limits, *refs):
-    number = len(pieces)
+def next_kernel(rows_of, last, sizes, q_ref, limits, *refs):
+    number = len(rows_of)
     key_refs, value_refs = refs[:number], refs[number : 2 * number]
     if last:
         acc_in, top_in, out, keys, values, result, sems = refs[2 * number :]
     else:
         acc_in, top_in, acc_out, top_out, keys, values = refs[2 * number :]
-    place_pieces(pieces, False, window_rows, cache_rows, limits, key_refs, value_refs, keys, values)
+    for index, row in enumerate(rows_of):
+        place_piece(index, number, row, False, sizes, limits, key_refs[index], value_refs[index], keys, values)
+    fill_up(number * sum(sizes), keys, values)
     rows = q_ref.shape[0]
     kv_heads = keys.shape[0]
 
@@ -259,8 +260,8 @@
     return [jax.ShapeDtypeStruct((rows, 2 * HD), jnp.float32), jax.ShapeDtypeStruct((rows, HD), jnp.float32)]
 
 
-def attend_first(count, window_rows, cache_rows, valid_counts, first_block, queries, packed):
-    kv_heads = packed.shape[1] // HD
+def attend_first(count, window_rows, cache_rows, valid_counts, first_block, queries, own_keys, own_values):
+    kv_heads = own_keys.shape[1] // HD
     total_keys = -(-(window_rows + cache_rows) // HD) * HD
     vmem, anywhere = pl.BlockSpec(memory_space=pltpu.VMEM), pl.BlockSpec(memory_space=pltpu.HBM)
     acc, top, q_near, limits = pl.pallas_call(
@@ -270,7 +271,7 @@
             jax.ShapeDtypeStruct(queries.shape, queries.dtype),
             jax.ShapeDtypeStruct((-(-count // 8) * 8, HD), jnp.int32),
         ],
-        in_specs=[anywhere, anywhere, anywhere, vmem],
+        in_specs=[anywhere, anywhere, anywhere, vmem, vmem],
         out_specs=[vmem] * 4,
         scratch_shapes=[
             *room(kv_heads, total_keys),
@@ -280,22 +281,23 @@
         ],
         name="attend_first",
         **kernel_options(queries, total_keys, kv_heads),
-    )(valid_counts, first_block, queries, packed)
+    )(valid_counts, first_block, queries, own_keys, own_values)
     return (acc, top), q_near, limits
 
 
-def attend_next(pieces, keys, values, state, last, window_rows, cache_rows, queries, limits):
-    kv_heads = keys[0].shape[1] // HD
-    total_keys = -(-len(pieces) * (window_rows + cache_rows) // HD) * HD
+def attend_next(pieces, state, last, sizes, queries, limits):
+    rows_of, key_blocks, value_blocks = zip(*pieces)
+    kv_heads = key_blocks[0].shape[1] // HD
+    total_keys = -(-len(pieces) * sum(sizes) // HD) * HD
     vmem = pl.BlockSpec(memory_space=pltpu.VMEM)
-    operands = [queries, limits, *keys, *values, *state]
+    operands = [queries, limits, *key_blocks, *value_blocks, *state]
     shapes = [jax.ShapeDtypeStruct(queries.shape, queries.dtype)] if last else state_shapes(queries)
     scratch = room(kv_heads, total_keys)
     if last:
         chunk_count = queries.shape[1] // HD // CHUNK_HEADS
         scratch += [pltpu.VMEM(queries.shape, queries.dtype), pltpu.SemaphoreType.DMA((chunk_count,))]
     outs = pl.pallas_call(
-        functools.partial(next_kernel, tuple(pieces), last, window_rows, cache_rows),
+        functools.partial(next_kernel, rows_of, last, sizes),
         out_shape=shapes,
         in_specs=[vmem] * len(operands),
         out_specs=[pl.BlockSpec(memory_space=pltpu.HBM)] if last else [vmem] * len(shapes),
@@ -307,8 +309,7 @@
 
 
 def shards(count, queries, win_keys, win_values, cache_keys, cache_values, valid_counts, first_block):
-    window_rows, cache_rows = win_keys.shape[0], cache_keys.shape[0]
-    stride = window_rows + cache_rows
+    sizes = (win_keys.shape[0], cache_keys.shape[0])
     half = count // 2
     ring = [place_at(p, count) for p in range(count)]
     onward = [(ring[p], ring[(p + 1) % count]) for p in range(count)]
@@ -318,30 +319,29 @@
         pltpu.with_memory_space_constraint(x, pltpu.HBM)
         for x in (win_keys, win_values, cache_keys, cache_values, valid_counts, first_block, queries)
     ]
-    on = back = pack(win_keys, win_values, cache_keys, cache_values)
-    state = near = limits = None
+    own_keys, own_values = pack(win_keys, win_values, cache_keys, cache_values)
+    key_on = key_back = own_keys
+    value_on = value_back = own_values
+    state, near, limits = attend_first(count, *sizes, valid_counts, first_block, queries, own_keys, own_values)
+    arrived = []
     for step in range(1, half + 1):
+        key_on = lax.ppermute(key_on, "ctx", onward)
+        value_back = lax.ppermute(value_back, "ctx", backward)
         if step < half:
-            next_on = lax.ppermute(on, "ctx", onward)
-            next_back = lax.ppermute(back, "ctx", backward)
+            value_on = lax.ppermute(value_on, "ctx", onward)
+            key_back = lax.ppermute(key_back, "ctx", backward)
+            row = 2 * (step - 1)
+            arrived.append([(row, key_on, value_on), (row + 1, key_back, value_back)])
         else:
-            next_on = lax.ppermute(on[:stride], "ctx", onward)
-            next_back = lax.ppermute(back[stride:], "ctx", backward)
+            arrived.append([(2 * (half - 1), key_on, value_back)])
         if step == 1:
-            state, near, limits = attend_first(
-                count, window_rows, cache_rows, valid_counts, first_block, queries, on
-            )
-        else:
-            row = 2 * (step - 2)
-            pieces = [(row, 0, stride), (row + 1, 0, stride)]
-            state = attend_next(
-                pieces, [on, back], [on, back], state, False, window_rows, cache_rows, near, limits
-            )
-        on, top = lax.optimization_barrier((next_on, state[1]))
-        back, top = lax.optimization_barrier((next_back, top))
-        state = (state[0], top)
-    pieces = [(2 * (half - 1), 0, 0)]
-    return attend_next(pieces, [on], [back], state, True, window_rows, cache_rows, near, limits)
+            key_on, top = lax.optimization_barrier((key_on, state[1]))
+            state = (state[0], top)
+    for begin in range(0, half - 2, 2):
+        pieces = [piece for step in arrived[begin : min(begin + 2, half - 2)] for piece in step]
+        state = attend_next(pieces, state, False, sizes, near, limits)
+    state = attend_next(arrived[half - 2], state, False, sizes, near, limits)
+    return attend_next(arrived[half - 1], state, True, sizes, near, limits)
 
 
 def solution(mesh):

time: 29 us -> 27.3 us (0.941)
  waiting for transfers between devices: 10.5 us -> 3.14 us
  starting transfers between devices: 9.48 us -> 15.7 us
  Pallas kernels: 8.8 us -> 8.18 us
    ppermute x8 -> x14, waiting for transfers between devices: 10.5 us -> 3.14 us  [the longest x3 1.33 us: shards(): key_back = lax.ppermute(key_back, 'ctx', backward)]
    ppermute x8 -> x14, starting transfers between devices: 9.48 us -> 15.7 us  [the longest x4 9.09 us: shards(): key_on = lax.ppermute(key_on, 'ctx', onward)]
    pallas_call x5 -> x4, Pallas kernels: 6.83 us -> 6.21 us  [the longest x3 5.28 us: attend_next(): pl.pallas_call(functools.partial(next_kernel, rows_of, last, sizes), out_...]
  transfers between devices with their start and end apart: 8 -> 14, of which waited for: 5 -> 5; matrix products, arithmetic and copies ran while one was open for 0% -> 0% of each run, Pallas kernels for 22% -> 21%
where the time goes in v8:
time: 27.3 us; the launch traced here: 27.1 us
  starting transfers between devices  15.7 us (58%)
  Pallas kernels  8.18 us (30%)
  waiting for transfers between devices  3.14 us (12%)
    ppermute x4, starting transfers between devices, shards(): key_on = lax.ppermute(key_on, 'ctx', onward)  9.09 us
    pallas_call x3, Pallas kernels, attend_next(): pl.pallas_call(functools.partial(next_kernel, rows_of, last, sizes), out_...  5.28 us
    ppermute x3, starting transfers between devices, shards(): key_back = lax.ppermute(key_back, 'ctx', backward)  3.25 us
    ppermute x3, starting transfers between devices, shards(): value_on = lax.ppermute(value_on, 'ctx', onward)  2.83 us
    pallas_call x1, Pallas kernels, attend_first(): pl.pallas_call(functools.partial(first_kernel, count, window_rows, cache_...  1.97 us
    ppermute x3, waiting for transfers between devices, shards(): key_back = lax.ppermute(key_back, 'ctx', backward)  1.33 us
    ppermute x4, waiting for transfers between devices, shards(): key_on = lax.ppermute(key_on, 'ctx', onward)  0.99 us
    pallas_call x1, Pallas kernels, pack(): pl.pallas_call(pack_kernel, out_shape=[jax.ShapeDtypeStruct((rows, width)...  0.93 us
  transfers between devices with their start and end apart: 14, of which 5 were waited for; matrix products, arithmetic and copies ran while one was open for 0% of the time, Pallas kernels for 21%

profile of v8, /device:TPU:0, one launch (start us, length us, event | category | flops | bytes accessed | tf_op | source)
XLA Modules:
  0.0 27.1 jit_solution(7129127728939853662)
XLA Ops:
  0.0 0.9 %pack.1 = (bf16[192,256]{1,0:T(8,128)(2,1)S(1)}, bf16[192,256]{1,0:T(8,128)(2,1)S(1)}) custom-call(bf16[128,256]{1,0:T(8,128)(2,1)} %win_keys.1, bf16[128,256]{1,0:T(8,128)(2,1)} %win_values.1, bf16[64,256]{1,0:T(8,128)(2,1)} %cache_keys.1, bf16[64,256]{1,0:T(8,128)(2,1)} %cache_values.1), custom_call_target="tpu_custom_call" | custom-call | bytes 393216 | tf_op jit(solution)/shard_map/pack/pallas_call | solution.py:65
  0.9 3.0 %collective-permute-start = (bf16[192,256]{1,0:T(8,128)(2,1)S(1)}, bf16[192,256]{1,0:T(8,128)(2,1)S(1)}, u32[]{:S(2)}, u32[]{:S(2)}) collective-permute-start(bf16[192,256]{1,0:T(8,128)(2,1)S(1)} %get-tuple-element.17.own_keys), channel_id=1, source_target_pairs={{2,6},{6,10},{10,14},{14,12},{12,8},{8,4},{4,0},{0,2},{3,7},{7,11}... | collective-permute-start | bytes 294920 | tf_op jit(solution)/shard_map/ppermute | solution.py:328
  3.9 0.2 collective-permute-start.4
  4.1 1.9 %collective-permute-start.11 = (bf16[192,256]{1,0:T(8,128)(2,1)S(1)}, bf16[192,256]{1,0:T(8,128)(2,1)S(1)}, u32[]{:S(2)}, u32[]{:S(2)}) collective-permute-start(bf16[192,256]{1,0:T(8,128)(2,1)S(1)} %get-tuple-element.18.own_values), channel_id=1, source_target_pairs={{2,6},{6,10},{10,14},{14,12},{12,8},{8,4},{4,0},{0,2},{3,7},{7,11}... | collective-permute-start | bytes 294920 | tf_op jit(solution)/shard_map/ppermute | solution.py:331
  6.0 0.2 collective-permute-start.8
  6.1 2.0 %attend_first.1 = (f32[2048,256]{1,0:T(8,128)S(1)}, f32[2048,128]{1,0:T(8,128)S(1)}, bf16[128,2048]{1,0:T(8,128)(2,1)S(1)}, s32[8,128]{1,0:T(8,128)S(1)}) custom-call(s32[8]{0:T(128)} %valid_hbm.1, s32[8]{0:T(128)} %first_hbm.1, bf16[128,2048]{1,0:T(8,128)(2,1)} %q_hbm.1, bf16[192,256]{1,0:T(8,128)(2,1)S(1)} %get-tuple-element.17.own_keys, ...), custom_call_target="tpu_custom_call" | custom-call | flops 402653184 | bytes 524288 | tf_op jit(solution)/shard_map/attend_first/pallas_call | solution.py:267
  8.1 0.0 collective-permute-done.refs_0_
  8.1 1.9 %collective-permute-start.1 = (bf16[192,256]{1,0:T(8,128)(2,1)S(1)}, bf16[192,256]{1,0:T(8,128)(2,1)S(1)}, u32[]{:S(2)}, u32[]{:S(2)}) collective-permute-start(bf16[192,256]{1,0:T(8,128)(2,1)S(1)} %collective-permute-done.refs_0_), channel_id=1, source_target_pairs={{2,6},{6,10},{10,14},{14,12},{12,8},{8,4},{4,0},{0,2},{3,7},{7,11}... | collective-permute-start | bytes 294920 | tf_op jit(solution)/shard_map/ppermute | solution.py:328
  10.0 0.0 collective-permute-done.4.refs_5_
  10.0 0.2 collective-permute-start.5
  10.2 0.5 %collective-permute-done.8.refs_1_ = bf16[192,256]{1,0:T(8,128)(2,1)S(1)} collective-permute-done((bf16[192,256]{1,0:T(8,128)(2,1)S(1)}, bf16[192,256]{1,0:T(8,128)(2,1)S(1)}, u32[]{:S(2)}, u32[]{:S(2)}) %collective-permute-start.8) | collective-permute-done | bytes 98336 | tf_op jit(solution)/shard_map/ppermute | solution.py:332
  10.6 1.5 %collective-permute-start.9 = (bf16[192,256]{1,0:T(8,128)(2,1)S(1)}, bf16[192,256]{1,0:T(8,128)(2,1)S(1)}, u32[]{:S(2)}, u32[]{:S(2)}) collective-permute-start(bf16[192,256]{1,0:T(8,128)(2,1)S(1)} %collective-permute-done.8.refs_1_), channel_id=1, source_target_pairs={{6,2},{10,6},{14,10},{12,14},{8,12},{4,8},{0,4},{2,0},{7,3},{11,7}... | collective-permute-start | bytes 294920 | tf_op jit(solution)/shard_map/ppermute | solution.py:332
  12.1 0.0 collective-permute-done.11.refs_4_
  12.1 0.5 %collective-permute-start.12 = (bf16[192,256]{1,0:T(8,128)(2,1)S(1)}, bf16[192,256]{1,0:T(8,128)(2,1)S(1)}, u32[]{:S(2)}, u32[]{:S(2)}) collective-permute-start(bf16[192,256]{1,0:T(8,128)(2,1)S(1)} %collective-permute-done.11.refs_4_), channel_id=1, source_target_pairs={{2,6},{6,10},{10,14},{14,12},{12,8},{8,4},{4,0},{0,2},{3,7},{7,11}... | collective-permute-start | bytes 294920 | tf_op jit(solution)/shard_map/ppermute | solution.py:331
  12.7 0.2 collective-permute-done.1.refs_2_
  12.9 2.3 %collective-permute-start.2 = (bf16[192,256]{1,0:T(8,128)(2,1)S(1)}, bf16[192,256]{1,0:T(8,128)(2,1)S(1)}, u32[]{:S(2)}, u32[]{:S(2)}) collective-permute-start(bf16[192,256]{1,0:T(8,128)(2,1)S(1)} %collective-permute-done.1.refs_2_), channel_id=1, source_target_pairs={{2,6},{6,10},{10,14},{14,12},{12,8},{8,4},{4,0},{0,2},{3,7},{7,11}... | collective-permute-start | bytes 294920 | tf_op jit(solution)/shard_map/ppermute | solution.py:328
  15.2 0.0 collective-permute-done.5.refs_7_
  15.2 0.1 collective-permute-start.6
  15.3 0.9 %collective-permute-done.9.refs_3_ = bf16[192,256]{1,0:T(8,128)(2,1)S(1)} collective-permute-done((bf16[192,256]{1,0:T(8,128)(2,1)S(1)}, bf16[192,256]{1,0:T(8,128)(2,1)S(1)}, u32[]{:S(2)}, u32[]{:S(2)}) %collective-permute-start.9) | collective-permute-done | bytes 98336 | tf_op jit(solution)/shard_map/ppermute | solution.py:332
  16.2 1.6 %collective-permute-start.10 = (bf16[192,256]{1,0:T(8,128)(2,1)S(1)}, bf16[192,256]{1,0:T(8,128)(2,1)S(1)}, u32[]{:S(2)}, u32[]{:S(2)}) collective-permute-start(bf16[192,256]{1,0:T(8,128)(2,1)S(1)} %collective-permute-done.9.refs_3_), channel_id=1, source_target_pairs={{6,2},{10,6},{14,10},{12,14},{8,12},{4,8},{0,4},{2,0},{7,3},{11,7}... | collective-permute-start | bytes 294920 | tf_op jit(solution)/shard_map/ppermute | solution.py:332
  17.8 0.0 collective-permute-done.12.refs_6_
  17.8 0.4 %collective-permute-start.13 = (bf16[192,256]{1,0:T(8,128)(2,1)S(1)}, bf16[192,256]{1,0:T(8,128)(2,1)S(1)}, u32[]{:S(2)}, u32[]{:S(2)}) collective-permute-start(bf16[192,256]{1,0:T(8,128)(2,1)S(1)} %collective-permute-done.12.refs_6_), channel_id=1, source_target_pairs={{2,6},{6,10},{10,14},{14,12},{12,8},{8,4},{4,0},{0,2},{3,7},{7,11}... | collective-permute-start | bytes 294920 | tf_op jit(solution)/shard_map/ppermute | solution.py:331
  18.2 0.7 %collective-permute-done.2.refs_0_ = bf16[192,256]{1,0:T(8,128)(2,1)S(1)} collective-permute-done((bf16[192,256]{1,0:T(8,128)(2,1)S(1)}, bf16[192,256]{1,0:T(8,128)(2,1)S(1)}, u32[]{:S(2)}, u32[]{:S(2)}) %collective-permute-start.2) | collective-permute-done | bytes 98336 | tf_op jit(solution)/shard_map/ppermute | solution.py:328
  19.0 1.9 %collective-permute-start.3 = (bf16[192,256]{1,0:T(8,128)(2,1)S(1)}, bf16[192,256]{1,0:T(8,128)(2,1)S(1)}, u32[]{:S(2)}, u32[]{:S(2)}) collective-permute-start(bf16[192,256]{1,0:T(8,128)(2,1)S(1)} %collective-permute-done.2.refs_0_), channel_id=1, source_target_pairs={{2,6},{6,10},{10,14},{14,12},{12,8},{8,4},{4,0},{0,2},{3,7},{7,11}... | collective-permute-start | bytes 294920 | tf_op jit(solution)/shard_map/ppermute | solution.py:328
  20.8 0.0 collective-permute-done.6.refs_3_
  20.8 0.2 collective-permute-start.7
  21.0 2.2 %attend_next.2 = (f32[2048,256]{1,0:T(8,128)S(1)}, f32[2048,128]{1,0:T(8,128)S(1)}) custom-call(bf16[128,2048]{1,0:T(8,128)(2,1)S(1)} %get-tuple-element.19.q_ref, s32[8,128]{1,0:T(8,128)S(1)} %get-tuple-element.20.limits, bf16[192,256]{1,0:T(8,128)(2,1)S(1)} %collective-permute-done.refs_0_, bf16[192,256]{1,0:T(8,128)(2,1)S(1)} %collective-permute-done.8.refs_1_, ...), custom_call_target="tpu_custom_call" | custom-call | flops 1207959552 | bytes 524288 | tf_op jit(solution)/shard_map/attend_next/pallas_call | solution.py:299
  23.2 0.0 collective-permute-done.10.refs_1_
  23.2 0.0 collective-permute-done.13.refs_2_
  23.2 1.4 %attend_next.3 = (f32[2048,256]{1,0:T(8,128)S(1)}, f32[2048,128]{1,0:T(8,128)S(1)}) custom-call(bf16[128,2048]{1,0:T(8,128)(2,1)S(1)} %get-tuple-element.19.q_ref, s32[8,128]{1,0:T(8,128)S(1)} %get-tuple-element.20.limits, bf16[192,256]{1,0:T(8,128)(2,1)S(1)} %collective-permute-done.2.refs_0_, bf16[192,256]{1,0:T(8,128)(2,1)S(1)} %collective-permute-done.10.refs_1_, ...), custom_call_target="tpu_custom_call" | custom-call | flops 603979776 | bytes 524288 | tf_op jit(solution)/shard_map/attend_next/pallas_call | solution.py:299
  24.6 0.0 collective-permute-done.3.refs_0_
  24.6 0.8 %collective-permute-done.7.refs_1_ = bf16[192,256]{1,0:T(8,128)(2,1)S(1)} collective-permute-done((bf16[192,256]{1,0:T(8,128)(2,1)S(1)}, bf16[192,256]{1,0:T(8,128)(2,1)S(1)}, u32[]{:S(2)}, u32[]{:S(2)}) %collective-permute-start.7) | collective-permute-done | bytes 98336 | tf_op jit(solution)/shard_map/ppermute | solution.py:329
  25.4 1.7 %attend_last.1 = bf16[128,2048]{1,0:T(8,128)(2,1)} custom-call(bf16[128,2048]{1,0:T(8,128)(2,1)S(1)} %get-tuple-element.19.q_ref, s32[8,128]{1,0:T(8,128)S(1)} %get-tuple-element.20.limits, bf16[192,256]{1,0:T(8,128)(2,1)S(1)} %collective-permute-done.3.refs_0_, bf16[192,256]{1,0:T(8,128)(2,1)S(1)} %collective-permute-done.7.refs_1_, ...), custom_call_target="tpu_custom_call" | custom-call | flops 402653184 | bytes 524288 | tf_op jit(solution)/shard_map/attend_last/pallas_call | solution.py:299
Async XLA Ops:
  0.9 7.2 %collective-permute-start = (bf16[192,256]{1,0:T(8,128)(2,1)S(1)}, bf16[192,256]{1,0:T(8,128)(2,1)S(1)}, u32[]{:S(2)}, u32[]{:S(2)}) collective-permute-start(bf16[192,256]{1,0:T(8,128)(2,1)S(1)} %get-tuple-element.17.own_keys), channel_id=1, source_target_pairs={{2,6},{6,10},{10,14},{14,12},{12,8},{8,4},{4,0},{0,2},{3,7},{7,11}... | collective-permute-start | bytes 294920 | tf_op jit(solution)/shard_map/ppermute | solution.py:328
  3.9 6.1 %collective-permute-start.4 = (bf16[192,256]{1,0:T(8,128)(2,1)S(1)}, bf16[192,256]{1,0:T(8,128)(2,1)S(1)}, u32[]{:S(2)}, u32[]{:S(2)}) collective-permute-start(bf16[192,256]{1,0:T(8,128)(2,1)S(1)} %get-tuple-element.18.own_values), channel_id=1, source_target_pairs={{6,2},{10,6},{14,10},{12,14},{8,12},{4,8},{0,4},{2,0},{7,3},{11,7}... | collective-permute-start | bytes 294920 | tf_op jit(solution)/shard_map/ppermute | solution.py:329
  4.1 8.1 %collective-permute-start.11 = (bf16[192,256]{1,0:T(8,128)(2,1)S(1)}, bf16[192,256]{1,0:T(8,128)(2,1)S(1)}, u32[]{:S(2)}, u32[]{:S(2)}) collective-permute-start(bf16[192,256]{1,0:T(8,128)(2,1)S(1)} %get-tuple-element.18.own_values), channel_id=1, source_target_pairs={{2,6},{6,10},{10,14},{14,12},{12,8},{8,4},{4,0},{0,2},{3,7},{7,11}... | collective-permute-start | bytes 294920 | tf_op jit(solution)/shard_map/ppermute | solution.py:331
  6.0 4.7 %collective-permute-start.8 = (bf16[192,256]{1,0:T(8,128)(2,1)S(1)}, bf16[192,256]{1,0:T(8,128)(2,1)S(1)}, u32[]{:S(2)}, u32[]{:S(2)}) collective-permute-start(bf16[192,256]{1,0:T(8,128)(2,1)S(1)} %get-tuple-element.17.own_keys), channel_id=1, source_target_pairs={{6,2},{10,6},{14,10},{12,14},{8,12},{4,8},{0,4},{2,0},{7,3},{11,7}... | collective-permute-start | bytes 294920 | tf_op jit(solution)/shard_map/ppermute | solution.py:332
  8.1 4.8 %collective-permute-start.1 = (bf16[192,256]{1,0:T(8,128)(2,1)S(1)}, bf16[192,256]{1,0:T(8,128)(2,1)S(1)}, u32[]{:S(2)}, u32[]{:S(2)}) collective-permute-start(bf16[192,256]{1,0:T(8,128)(2,1)S(1)} %collective-permute-done.refs_0_), channel_id=1, source_target_pairs={{2,6},{6,10},{10,14},{14,12},{12,8},{8,4},{4,0},{0,2},{3,7},{7,11}... | collective-permute-start | bytes 294920 | tf_op jit(solution)/shard_map/ppermute | solution.py:328
  10.0 5.2 %collective-permute-start.5 = (bf16[192,256]{1,0:T(8,128)(2,1)S(1)}, bf16[192,256]{1,0:T(8,128)(2,1)S(1)}, u32[]{:S(2)}, u32[]{:S(2)}) collective-permute-start(bf16[192,256]{1,0:T(8,128)(2,1)S(1)} %collective-permute-done.4.refs_5_), channel_id=1, source_target_pairs={{6,2},{10,6},{14,10},{12,14},{8,12},{4,8},{0,4},{2,0},{7,3},{11,7}... | collective-permute-start | bytes 294920 | tf_op jit(solution)/shard_map/ppermute | solution.py:329
  10.6 5.5 %collective-permute-start.9 = (bf16[192,256]{1,0:T(8,128)(2,1)S(1)}, bf16[192,256]{1,0:T(8,128)(2,1)S(1)}, u32[]{:S(2)}, u32[]{:S(2)}) collective-permute-start(bf16[192,256]{1,0:T(8,128)(2,1)S(1)} %collective-permute-done.8.refs_1_), channel_id=1, source_target_pairs={{6,2},{10,6},{14,10},{12,14},{8,12},{4,8},{0,4},{2,0},{7,3},{11,7}... | collective-permute-start | bytes 294920 | tf_op jit(solution)/shard_map/ppermute | solution.py:332
  12.1 5.7 %collective-permute-start.12 = (bf16[192,256]{1,0:T(8,128)(2,1)S(1)}, bf16[192,256]{1,0:T(8,128)(2,1)S(1)}, u32[]{:S(2)}, u32[]{:S(2)}) collective-permute-start(bf16[192,256]{1,0:T(8,128)(2,1)S(1)} %collective-permute-done.11.refs_4_), channel_id=1, source_target_pairs={{2,6},{6,10},{10,14},{14,12},{12,8},{8,4},{4,0},{0,2},{3,7},{7,11}... | collective-permute-start | bytes 294920 | tf_op jit(solution)/shard_map/ppermute | solution.py:331
  12.9 6.0 %collective-permute-start.2 = (bf16[192,256]{1,0:T(8,128)(2,1)S(1)}, bf16[192,256]{1,0:T(8,128)(2,1)S(1)}, u32[]{:S(2)}, u32[]{:S(2)}) collective-permute-start(bf16[192,256]{1,0:T(8,128)(2,1)S(1)} %collective-permute-done.1.refs_2_), channel_id=1, source_target_pairs={{2,6},{6,10},{10,14},{14,12},{12,8},{8,4},{4,0},{0,2},{3,7},{7,11}... | collective-permute-start | bytes 294920 | tf_op jit(solution)/shard_map/ppermute | solution.py:328
  15.2 5.6 %collective-permute-start.6 = (bf16[192,256]{1,0:T(8,128)(2,1)S(1)}, bf16[192,256]{1,0:T(8,128)(2,1)S(1)}, u32[]{:S(2)}, u32[]{:S(2)}) collective-permute-start(bf16[192,256]{1,0:T(8,128)(2,1)S(1)} %collective-permute-done.5.refs_7_), channel_id=1, source_target_pairs={{6,2},{10,6},{14,10},{12,14},{8,12},{4,8},{0,4},{2,0},{7,3},{11,7}... | collective-permute-start | bytes 294920 | tf_op jit(solution)/shard_map/ppermute | solution.py:329
  16.2 7.0 %collective-permute-start.10 = (bf16[192,256]{1,0:T(8,128)(2,1)S(1)}, bf16[192,256]{1,0:T(8,128)(2,1)S(1)}, u32[]{:S(2)}, u32[]{:S(2)}) collective-permute-start(bf16[192,256]{1,0:T(8,128)(2,1)S(1)} %collective-permute-done.9.refs_3_), channel_id=1, source_target_pairs={{6,2},{10,6},{14,10},{12,14},{8,12},{4,8},{0,4},{2,0},{7,3},{11,7}... | collective-permute-start | bytes 294920 | tf_op jit(solution)/shard_map/ppermute | solution.py:332
  17.8 5.4 %collective-permute-start.13 = (bf16[192,256]{1,0:T(8,128)(2,1)S(1)}, bf16[192,256]{1,0:T(8,128)(2,1)S(1)}, u32[]{:S(2)}, u32[]{:S(2)}) collective-permute-start(bf16[192,256]{1,0:T(8,128)(2,1)S(1)} %collective-permute-done.12.refs_6_), channel_id=1, source_target_pairs={{2,6},{6,10},{10,14},{14,12},{12,8},{8,4},{4,0},{0,2},{3,7},{7,11}... | collective-permute-start | bytes 294920 | tf_op jit(solution)/shard_map/ppermute | solution.py:331
  19.0 5.7 %collective-permute-start.3 = (bf16[192,256]{1,0:T(8,128)(2,1)S(1)}, bf16[192,256]{1,0:T(8,128)(2,1)S(1)}, u32[]{:S(2)}, u32[]{:S(2)}) collective-permute-start(bf16[192,256]{1,0:T(8,128)(2,1)S(1)} %collective-permute-done.2.refs_0_), channel_id=1, source_target_pairs={{2,6},{6,10},{10,14},{14,12},{12,8},{8,4},{4,0},{0,2},{3,7},{7,11}... | collective-permute-start | bytes 294920 | tf_op jit(solution)/shard_map/ppermute | solution.py:328
  20.8 4.6 %collective-permute-start.7 = (bf16[192,256]{1,0:T(8,128)(2,1)S(1)}, bf16[192,256]{1,0:T(8,128)(2,1)S(1)}, u32[]{:S(2)}, u32[]{:S(2)}) collective-permute-start(bf16[192,256]{1,0:T(8,128)(2,1)S(1)} %collective-permute-done.6.refs_3_), channel_id=1, source_target_pairs={{6,2},{10,6},{14,10},{12,14},{8,12},{4,8},{0,4},{2,0},{7,3},{11,7}... | collective-permute-start | bytes 294920 | tf_op jit(solution)/shard_map/ppermute | solution.py:329

commit v9 on v8

--- a/solution.py
+++ b/solution.py
@@ -46,32 +46,56 @@
     return jnp.where(column == 0, rows * (width - 1) + rows - 1 - row, snake)
 
 
-def pack_kernel(win_keys, win_values, cache_keys, cache_values, keys, values, sems):
+def load_kernel(count, win_keys, win_values, cache_keys, cache_values, q_hbm, valid_hbm, first_hbm, *refs):
+    keys, values, q_ref, limits, valid_ref, first_ref, sems = refs
     window_rows = win_keys.shape[0]
-    copies = [
-        pltpu.make_async_copy(win_keys, keys.at[:window_rows], sems.at[0]),
-        pltpu.make_async_copy(cache_keys, keys.at[window_rows:], sems.at[1]),
-        pltpu.make_async_copy(win_values, values.at[:window_rows], sems.at[2]),
-        pltpu.make_async_copy(cache_values, values.at[window_rows:], sems.at[3]),
+    pairs = [
+        (valid_hbm, valid_ref),
+        (first_hbm, first_ref),
+        (win_keys, keys.at[:window_rows]),
+        (cache_keys, keys.at[window_rows:]),
+        (win_values, values.at[:window_rows]),
+        (cache_values, values.at[window_rows:]),
+        (q_hbm, q_ref),
     ]
+    copies = [pltpu.make_async_copy(*pair, sems.at[index]) for index, pair in enumerate(pairs)]
     for copy in copies:
         copy.start()
-    for copy in copies:
+    for copy in copies[:2]:
         copy.wait()
-
-
-def pack(win_keys, win_values, cache_keys, cache_values):
+    me = lax.axis_index("ctx")
+    position = position_of(me, count)
+    first = first_ref[me]
+    for row, offset in enumerate(ring_offsets(count)):
+        place = place_at(lax.rem(position + offset + count, count), count)
+        limit = jnp.where((place >= first) & (place <= me), valid_ref[place], 0)
+        limits[row : row + 1, :] = jnp.full((1, HD), limit, jnp.int32)
+    limits[count - 1 : count, :] = jnp.full((1, HD), valid_ref[me], jnp.int32)
+    for copy in copies[2:]:
+        copy.wait()
+
+
+def load(count, win_keys, win_values, cache_keys, cache_values, queries, valid_counts, first_block):
     rows, width = win_keys.shape[0] + cache_keys.shape[0], win_keys.shape[1]
     return pl.pallas_call(
-        pack_kernel,
-        out_shape=[jax.ShapeDtypeStruct((rows, width), win_keys.dtype)] * 2,
-        in_specs=[pl.BlockSpec(memory_space=pltpu.HBM)] * 4,
-        out_specs=[pl.BlockSpec(memory_space=pltpu.VMEM)] * 2,
-        scratch_shapes=[pltpu.SemaphoreType.DMA((4,))],
+        functools.partial(load_kernel, count),
+        out_shape=[
+            jax.ShapeDtypeStruct((rows, width), win_keys.dtype),
+            jax.ShapeDtypeStruct((rows, width), win_keys.dtype),
+            jax.ShapeDtypeStruct(queries.shape, queries.dtype),
+            jax.ShapeDtypeStruct((-(-count // 8) * 8, HD), jnp.int32),
+        ],
+        in_specs=[pl.BlockSpec(memory_space=pltpu.HBM)] * 7,
+        out_specs=[pl.BlockSpec(memory_space=pltpu.VMEM)] * 4,
+        scratch_shapes=[
+            pltpu.SMEM(valid_counts.shape, jnp.int32),
+            pltpu.SMEM(first_block.shape, jnp.int32),
+            pltpu.SemaphoreType.DMA((7,)),
+        ],
         compiler_params=pltpu.CompilerParams(vmem_limit_bytes=4 * 1024 * 1024),
         cost_estimate=pl.CostEstimate(flops=0, bytes_accessed=8 * rows * width, transcendentals=0),
-        name="pack",
-    )(win_keys, win_values, cache_keys, cache_values)
+        name="load",
+    )(win_keys, win_values, cache_keys, cache_values, queries, valid_counts, first_block)
 
 
 def ring_offsets(count):
@@ -145,34 +169,14 @@
             yield head, slice(base * rows, (base + CHUNK_HEADS) * rows), query, base
 
 
-def first_kernel(
-    count, window_rows, cache_rows, valid_hbm, first_hbm, q_hbm, own_keys, own_values, acc_out, top_out, q_ref, limits,
-    keys, values, valid_ref, first_ref, sems,
-):
-    copies = [
-        pltpu.make_async_copy(valid_hbm, valid_ref, sems.at[0]),
-        pltpu.make_async_copy(first_hbm, first_ref, sems.at[1]),
-        pltpu.make_async_copy(q_hbm, q_ref, sems.at[2]),
-    ]
-    for copy in copies:
-        copy.start()
-    place_piece(0, 1, 0, True, (window_rows, cache_rows), None, own_keys, own_values, keys, values)
-    fill_up(window_rows + cache_rows, keys, values)
-    for copy in copies:
-        copy.wait()
-
-    me = lax.axis_index("ctx")
-    position = position_of(me, count)
-    first = first_ref[me]
-    for row, offset in enumerate(ring_offsets(count)):
-        place = place_at(lax.rem(position + offset + count, count), count)
-        limit = jnp.where((place >= first) & (place <= me), valid_ref[place], 0)
-        limits[row : row + 1, :] = jnp.full((1, HD), limit, jnp.int32)
-
+def first_kernel(count, sizes, q_ref, limits, own_keys, own_values, acc_out, top_out, keys, values):
+    window_rows = sizes[0]
+    place_piece(0, 1, 0, True, sizes, None, own_keys, own_values, keys, values)
+    fill_up(sum(sizes), keys, values)
     rows = q_ref.shape[0]
     key_iota = lax.broadcasted_iota(jnp.int32, (rows, window_rows), 1)
     query_iota = lax.broadcasted_iota(jnp.int32, (rows, window_rows), 0)
-    seen = (key_iota <= query_iota) & (key_iota < valid_ref[me])
+    seen = (key_iota <= query_iota) & (key_iota < limits[count - 1 : count, :])
     bias = jnp.concatenate([jnp.where(seen, 0.0, HIDDEN)] * CHUNK_HEADS, axis=0)
     for head, at, query, _ in chunks(q_ref, keys.shape[0]):
         score = scores(query, keys[head])
@@ -184,7 +188,7 @@
 
 def next_kernel(rows_of, last, sizes, q_ref, limits, *refs):
     number = len(rows_of)
-    key_refs, value_refs = refs[:number], refs[number : 2 * number]
+    key_refs, value_refs = refs[: 2 * number : 2], refs[1 : 2 * number : 2]
     if last:
         acc_in, top_in, out, keys, values, result, sems = refs[2 * number :]
     else:
@@ -260,37 +264,30 @@
     return [jax.ShapeDtypeStruct((rows, 2 * HD), jnp.float32), jax.ShapeDtypeStruct((rows, HD), jnp.float32)]
 
 
-def attend_first(count, window_rows, cache_rows, valid_counts, first_block, queries, own_keys, own_values):
+def attend_first(count, sizes, queries, limits, own_keys, own_values):
     kv_heads = own_keys.shape[1] // HD
-    total_keys = -(-(window_rows + cache_rows) // HD) * HD
-    vmem, anywhere = pl.BlockSpec(memory_space=pltpu.VMEM), pl.BlockSpec(memory_space=pltpu.HBM)
-    acc, top, q_near, limits = pl.pallas_call(
-        functools.partial(first_kernel, count, window_rows, cache_rows),
-        out_shape=[
-            *state_shapes(queries),
-            jax.ShapeDtypeStruct(queries.shape, queries.dtype),
-            jax.ShapeDtypeStruct((-(-count // 8) * 8, HD), jnp.int32),
-        ],
-        in_specs=[anywhere, anywhere, anywhere, vmem, vmem],
-        out_specs=[vmem] * 4,
-        scratch_shapes=[
-            *room(kv_heads, total_keys),
-            pltpu.SMEM(valid_counts.shape, jnp.int32),
-            pltpu.SMEM(first_block.shape, jnp.int32),
-            pltpu.SemaphoreType.DMA((3,)),
-        ],
-        name="attend_first",
-        **kernel_options(queries, total_keys, kv_heads),
-    )(valid_counts, first_block, queries, own_keys, own_values)
-    return (acc, top), q_near, limits
+    total_keys = -(-sum(sizes) // HD) * HD
+    vmem = pl.BlockSpec(memory_space=pltpu.VMEM)
+    return tuple(
+        pl.pallas_call(
+            functools.partial(first_kernel, count, sizes),
+            out_shape=state_shapes(queries),
+            in_specs=[vmem] * 4,
+            out_specs=[vmem] * 2,
+            scratch_shapes=room(kv_heads, total_keys),
+            name="attend_first",
+            **kernel_options(queries, total_keys, kv_heads),
+        )(queries, limits, own_keys, own_values)
+    )
 
 
 def attend_next(pieces, state, last, sizes, queries, limits):
-    rows_of, key_blocks, value_blocks = zip(*pieces)
-    kv_heads = key_blocks[0].shape[1] // HD
+    rows_of = tuple(piece[0] for piece in pieces)
+    blocks = [block for piece in pieces for block in piece[1:]]
+    kv_heads = blocks[0].shape[1] // HD
     total_keys = -(-len(pieces) * sum(sizes) // HD) * HD
     vmem = pl.BlockSpec(memory_space=pltpu.VMEM)
-    operands = [queries, limits, *key_blocks, *value_blocks, *state]
+    operands = [queries, limits, *blocks, *state]
     shapes = [jax.ShapeDtypeStruct(queries.shape, queries.dtype)] if last else state_shapes(queries)
     scratch = room(kv_heads, total_keys)
     if last:
@@ -319,10 +316,12 @@
         pltpu.with_memory_space_constraint(x, pltpu.HBM)
         for x in (win_keys, win_values, cache_keys, cache_values, valid_counts, first_block, queries)
     ]
-    own_keys, own_values = pack(win_keys, win_values, cache_keys, cache_values)
+    own_keys, own_values, near, limits = load(
+        count, win_keys, win_values, cache_keys, cache_values, queries, valid_counts, first_block
+    )
     key_on = key_back = own_keys
     value_on = value_back = own_values
-    state, near, limits = attend_first(count, *sizes, valid_counts, first_block, queries, own_keys, own_values)
+    state = attend_first(count, sizes, near, limits, own_keys, own_values)
     arrived = []
     for step in range(1, half + 1):
         key_on = lax.ppermute(key_on, "ctx", onward)

time: 27.3 us -> 26.3 us (0.963)
  Pallas kernels: 8.18 us -> 7.41 us
  waiting for transfers between devices: 3.14 us -> 2.69 us
  starting transfers between devices: 15.7 us -> 16 us
    ppermute x3, waiting for transfers between devices: 0.01 us -> 1.68 us  [shards(): value_on = lax.ppermute(value_on, 'ctx', onward)]
    ppermute x4, starting transfers between devices: 0.56 us -> 2.19 us  [shards(): value_back = lax.ppermute(value_back, 'ctx', backward)]
    ppermute x4, starting transfers between devices: 9.09 us -> 7.72 us  [shards(): key_on = lax.ppermute(key_on, 'ctx', onward)]
    ppermute x3, waiting for transfers between devices: 1.33 us -> 0.01 us  [shards(): key_back = lax.ppermute(key_back, 'ctx', backward)]
    ppermute x3, starting transfers between devices: 3.25 us -> 4.36 us  [shards(): key_back = lax.ppermute(key_back, 'ctx', backward)]
    ppermute x3, starting transfers between devices: 2.83 us -> 1.72 us  [shards(): value_on = lax.ppermute(value_on, 'ctx', onward)]
    pallas_call x2, Pallas kernels: 2.9 us -> 2.15 us  [the longest x1 1.22 us: load(): pl.pallas_call(functools.partial(load_kernel, count), out_shape=[jax.Shap...]
    ppermute x4, waiting for transfers between devices: 0.8 us -> 0.33 us  [shards(): value_back = lax.ppermute(value_back, 'ctx', backward)]
  transfers between devices with their start and end apart: 14 -> 14, of which waited for: 5 -> 4; matrix products, arithmetic and copies ran while one was open for 0% -> 0% of each run, Pallas kernels for 21% -> 17%
where the time goes in v9:
time: 26.3 us; the launch traced here: 26.2 us
  starting transfers between devices  16 us (61%)
  Pallas kernels  7.41 us (28%)
  waiting for transfers between devices  2.69 us (10%)
    ppermute x4, starting transfers between devices, shards(): key_on = lax.ppermute(key_on, 'ctx', onward)  7.72 us
    pallas_call x3, Pallas kernels, attend_next(): pl.pallas_call(functools.partial(next_kernel, rows_of, last, sizes), out_...  5.27 us
    ppermute x3, starting transfers between devices, shards(): key_back = lax.ppermute(key_back, 'ctx', backward)  4.36 us
    ppermute x4, starting transfers between devices, shards(): value_back = lax.ppermute(value_back, 'ctx', backward)  2.19 us
    ppermute x3, starting transfers between devices, shards(): value_on = lax.ppermute(value_on, 'ctx', onward)  1.72 us
    ppermute x3, waiting for transfers between devices, shards(): value_on = lax.ppermute(value_on, 'ctx', onward)  1.68 us
    pallas_call x1, Pallas kernels, load(): pl.pallas_call(functools.partial(load_kernel, count), out_shape=[jax.Shap...  1.22 us
    pallas_call x1, Pallas kernels, attend_first(): pl.pallas_call(functools.partial(first_kernel, count, sizes), out_shape=s...  0.93 us
  transfers between devices with their start and end apart: 14, of which 4 were waited for; matrix products, arithmetic and copies ran while one was open for 0% of the time, Pallas kernels for 17%

profile of v9, /device:TPU:0, one launch (start us, length us, event | category | flops | bytes accessed | tf_op | source)
XLA Modules:
  0.0 26.2 jit_solution(13688646586430727927)
XLA Ops:
  0.0 1.2 %load.1 = (bf16[192,256]{1,0:T(8,128)(2,1)S(1)}, bf16[192,256]{1,0:T(8,128)(2,1)S(1)}, bf16[128,2048]{1,0:T(8,128)(2,1)S(1)}, s32[8,128]{1,0:T(8,128)S(1)}) custom-call(bf16[128,256]{1,0:T(8,128)(2,1)} %win_keys.1, bf16[128,256]{1,0:T(8,128)(2,1)} %win_values.1, bf16[64,256]{1,0:T(8,128)(2,1)} %cache_keys.1, bf16[64,256]{1,0:T(8,128)(2,1)} %cache_values.1, ...), custom_call_target="tpu_custom_call" | custom-call | bytes 393216 | tf_op jit(solution)/shard_map/load/pallas_call | solution.py:80
  1.2 3.0 %collective-permute-start = (bf16[192,256]{1,0:T(8,128)(2,1)S(1)}, bf16[192,256]{1,0:T(8,128)(2,1)S(1)}, u32[]{:S(2)}, u32[]{:S(2)}) collective-permute-start(bf16[192,256]{1,0:T(8,128)(2,1)S(1)} %get-tuple-element.19.own_keys), channel_id=1, source_target_pairs={{2,6},{6,10},{10,14},{14,12},{12,8},{8,4},{4,0},{0,2},{3,7},{7,11}... | collective-permute-start | bytes 294920 | tf_op jit(solution)/shard_map/ppermute | solution.py:327
  4.2 0.2 collective-permute-start.4
  4.4 2.0 %collective-permute-start.11 = (bf16[192,256]{1,0:T(8,128)(2,1)S(1)}, bf16[192,256]{1,0:T(8,128)(2,1)S(1)}, u32[]{:S(2)}, u32[]{:S(2)}) collective-permute-start(bf16[192,256]{1,0:T(8,128)(2,1)S(1)} %get-tuple-element.19.own_keys), channel_id=1, source_target_pairs={{6,2},{10,6},{14,10},{12,14},{8,12},{4,8},{0,4},{2,0},{7,3},{11,7}... | collective-permute-start | bytes 294920 | tf_op jit(solution)/shard_map/ppermute | solution.py:331
  6.3 0.1 collective-permute-start.8
  6.4 0.9 %attend_first.1 = (f32[2048,256]{1,0:T(8,128)S(1)}, f32[2048,128]{1,0:T(8,128)S(1)}) custom-call(bf16[128,2048]{1,0:T(8,128)(2,1)S(1)} %get-tuple-element.17.q_ref, s32[8,128]{1,0:T(8,128)S(1)} %get-tuple-element.18.limits, bf16[192,256]{1,0:T(8,128)(2,1)S(1)} %get-tuple-element.19.own_keys, bf16[192,256]{1,0:T(8,128)(2,1)S(1)} %get-tuple-element.20.own_values), custom_call_target="tpu_custom_call" | custom-call | flops 402653184 | bytes 524288 | tf_op jit(solution)/shard_map/attend_first/pallas_call | solution.py:272
  7.3 0.0 collective-permute-done.refs_0_
  7.3 2.1 %collective-permute-start.1 = (bf16[192,256]{1,0:T(8,128)(2,1)S(1)}, bf16[192,256]{1,0:T(8,128)(2,1)S(1)}, u32[]{:S(2)}, u32[]{:S(2)}) collective-permute-start(bf16[192,256]{1,0:T(8,128)(2,1)S(1)} %collective-permute-done.refs_0_), channel_id=1, source_target_pairs={{2,6},{6,10},{10,14},{14,12},{12,8},{8,4},{4,0},{0,2},{3,7},{7,11}... | collective-permute-start | bytes 294920 | tf_op jit(solution)/shard_map/ppermute | solution.py:327
  9.5 0.0 collective-permute-done.4.refs_3_
  9.5 0.2 collective-permute-start.5
  9.8 1.3 %collective-permute-done.8.refs_1_ = bf16[192,256]{1,0:T(8,128)(2,1)S(1)} collective-permute-done((bf16[192,256]{1,0:T(8,128)(2,1)S(1)}, bf16[192,256]{1,0:T(8,128)(2,1)S(1)}, u32[]{:S(2)}, u32[]{:S(2)}) %collective-permute-start.8) | collective-permute-done | bytes 98336 | tf_op jit(solution)/shard_map/ppermute | solution.py:330
  11.1 0.5 %collective-permute-start.9 = (bf16[192,256]{1,0:T(8,128)(2,1)S(1)}, bf16[192,256]{1,0:T(8,128)(2,1)S(1)}, u32[]{:S(2)}, u32[]{:S(2)}) collective-permute-start(bf16[192,256]{1,0:T(8,128)(2,1)S(1)} %collective-permute-done.8.refs_1_), channel_id=1, source_target_pairs={{2,6},{6,10},{10,14},{14,12},{12,8},{8,4},{4,0},{0,2},{3,7},{7,11}... | collective-permute-start | bytes 294920 | tf_op jit(solution)/shard_map/ppermute | solution.py:330
  11.6 0.0 collective-permute-done.11.refs_2_
  11.6 1.6 %collective-permute-start.12 = (bf16[192,256]{1,0:T(8,128)(2,1)S(1)}, bf16[192,256]{1,0:T(8,128)(2,1)S(1)}, u32[]{:S(2)}, u32[]{:S(2)}) collective-permute-start(bf16[192,256]{1,0:T(8,128)(2,1)S(1)} %collective-permute-done.11.refs_2_), channel_id=1, source_target_pairs={{6,2},{10,6},{14,10},{12,14},{8,12},{4,8},{0,4},{2,0},{7,3},{11,7}... | collective-permute-start | bytes 294920 | tf_op jit(solution)/shard_map/ppermute | solution.py:331
  13.1 0.0 collective-permute-done.1.refs_4_
  13.1 1.6 %collective-permute-start.2 = (bf16[192,256]{1,0:T(8,128)(2,1)S(1)}, bf16[192,256]{1,0:T(8,128)(2,1)S(1)}, u32[]{:S(2)}, u32[]{:S(2)}) collective-permute-start(bf16[192,256]{1,0:T(8,128)(2,1)S(1)} %collective-permute-done.1.refs_4_), channel_id=1, source_target_pairs={{2,6},{6,10},{10,14},{14,12},{12,8},{8,4},{4,0},{0,2},{3,7},{7,11}... | collective-permute-start | bytes 294920 | tf_op jit(solution)/shard_map/ppermute | solution.py:327
  14.7 0.0 collective-permute-done.5.refs_7_
  14.7 0.6 %collective-permute-start.6 = (bf16[192,256]{1,0:T(8,128)(2,1)S(1)}, bf16[192,256]{1,0:T(8,128)(2,1)S(1)}, u32[]{:S(2)}, u32[]{:S(2)}) collective-permute-start(bf16[192,256]{1,0:T(8,128)(2,1)S(1)} %collective-permute-done.5.refs_7_), channel_id=1, source_target_pairs={{6,2},{10,6},{14,10},{12,14},{8,12},{4,8},{0,4},{2,0},{7,3},{11,7}... | collective-permute-start | bytes 294920 | tf_op jit(solution)/shard_map/ppermute | solution.py:328
  15.3 0.4 %collective-permute-done.9.refs_5_ = bf16[192,256]{1,0:T(8,128)(2,1)S(1)} collective-permute-done((bf16[192,256]{1,0:T(8,128)(2,1)S(1)}, bf16[192,256]{1,0:T(8,128)(2,1)S(1)}, u32[]{:S(2)}, u32[]{:S(2)}) %collective-permute-start.9) | collective-permute-done | bytes 98336 | tf_op jit(solution)/shard_map/ppermute | solution.py:330
  15.7 1.2 %collective-permute-start.10 = (bf16[192,256]{1,0:T(8,128)(2,1)S(1)}, bf16[192,256]{1,0:T(8,128)(2,1)S(1)}, u32[]{:S(2)}, u32[]{:S(2)}) collective-permute-start(bf16[192,256]{1,0:T(8,128)(2,1)S(1)} %collective-permute-done.9.refs_5_), channel_id=1, source_target_pairs={{2,6},{6,10},{10,14},{14,12},{12,8},{8,4},{4,0},{0,2},{3,7},{7,11}... | collective-permute-start | bytes 294920 | tf_op jit(solution)/shard_map/ppermute | solution.py:330
  16.9 0.0 collective-permute-done.12.refs_6_
  16.9 0.8 %collective-permute-start.13 = (bf16[192,256]{1,0:T(8,128)(2,1)S(1)}, bf16[192,256]{1,0:T(8,128)(2,1)S(1)}, u32[]{:S(2)}, u32[]{:S(2)}) collective-permute-start(bf16[192,256]{1,0:T(8,128)(2,1)S(1)} %collective-permute-done.12.refs_6_), channel_id=1, source_target_pairs={{6,2},{10,6},{14,10},{12,14},{8,12},{4,8},{0,4},{2,0},{7,3},{11,7}... | collective-permute-start | bytes 294920 | tf_op jit(solution)/shard_map/ppermute | solution.py:331
  17.7 0.7 %collective-permute-done.2.refs_0_ = bf16[192,256]{1,0:T(8,128)(2,1)S(1)} collective-permute-done((bf16[192,256]{1,0:T(8,128)(2,1)S(1)}, bf16[192,256]{1,0:T(8,128)(2,1)S(1)}, u32[]{:S(2)}, u32[]{:S(2)}) %collective-permute-start.2) | collective-permute-done | bytes 98336 | tf_op jit(solution)/shard_map/ppermute | solution.py:327
  18.4 1.0 %collective-permute-start.3 = (bf16[192,256]{1,0:T(8,128)(2,1)S(1)}, bf16[192,256]{1,0:T(8,128)(2,1)S(1)}, u32[]{:S(2)}, u32[]{:S(2)}) collective-permute-start(bf16[192,256]{1,0:T(8,128)(2,1)S(1)} %collective-permute-done.2.refs_0_), channel_id=1, source_target_pairs={{2,6},{6,10},{10,14},{14,12},{12,8},{8,4},{4,0},{0,2},{3,7},{7,11}... | collective-permute-start | bytes 294920 | tf_op jit(solution)/shard_map/ppermute | solution.py:327
  19.4 0.3 %collective-permute-done.6.refs_3_ = bf16[192,256]{1,0:T(8,128)(2,1)S(1)} collective-permute-done((bf16[192,256]{1,0:T(8,128)(2,1)S(1)}, bf16[192,256]{1,0:T(8,128)(2,1)S(1)}, u32[]{:S(2)}, u32[]{:S(2)}) %collective-permute-start.6) | collective-permute-done | bytes 98336 | tf_op jit(solution)/shard_map/ppermute | solution.py:328
  19.7 1.2 %collective-permute-start.7 = (bf16[192,256]{1,0:T(8,128)(2,1)S(1)}, bf16[192,256]{1,0:T(8,128)(2,1)S(1)}, u32[]{:S(2)}, u32[]{:S(2)}) collective-permute-start(bf16[192,256]{1,0:T(8,128)(2,1)S(1)} %collective-permute-done.6.refs_3_), channel_id=1, source_target_pairs={{6,2},{10,6},{14,10},{12,14},{8,12},{4,8},{0,4},{2,0},{7,3},{11,7}... | collective-permute-start | bytes 294920 | tf_op jit(solution)/shard_map/ppermute | solution.py:328
  20.8 2.2 %attend_next.2 = (f32[2048,256]{1,0:T(8,128)S(1)}, f32[2048,128]{1,0:T(8,128)S(1)}) custom-call(bf16[128,2048]{1,0:T(8,128)(2,1)S(1)} %get-tuple-element.17.q_ref, s32[8,128]{1,0:T(8,128)S(1)} %get-tuple-element.18.limits, bf16[192,256]{1,0:T(8,128)(2,1)S(1)} %collective-permute-done.refs_0_, bf16[192,256]{1,0:T(8,128)(2,1)S(1)} %collective-permute-done.8.refs_1_, ...), custom_call_target="tpu_custom_call" | custom-call | flops 1207959552 | bytes 524288 | tf_op jit(solution)/shard_map/attend_next/pallas_call | solution.py:296
  23.0 0.0 collective-permute-done.10.refs_1_
  23.0 0.0 collective-permute-done.13.refs_2_
  23.1 1.4 %attend_next.3 = (f32[2048,256]{1,0:T(8,128)S(1)}, f32[2048,128]{1,0:T(8,128)S(1)}) custom-call(bf16[128,2048]{1,0:T(8,128)(2,1)S(1)} %get-tuple-element.17.q_ref, s32[8,128]{1,0:T(8,128)S(1)} %get-tuple-element.18.limits, bf16[192,256]{1,0:T(8,128)(2,1)S(1)} %collective-permute-done.2.refs_0_, bf16[192,256]{1,0:T(8,128)(2,1)S(1)} %collective-permute-done.10.refs_1_, ...), custom_call_target="tpu_custom_call" | custom-call | flops 603979776 | bytes 524288 | tf_op jit(solution)/shard_map/attend_next/pallas_call | solution.py:296
  24.5 0.0 collective-permute-done.3.refs_0_
  24.5 0.0 collective-permute-done.7.refs_1_
  24.5 1.7 %attend_last.1 = bf16[128,2048]{1,0:T(8,128)(2,1)} custom-call(bf16[128,2048]{1,0:T(8,128)(2,1)S(1)} %get-tuple-element.17.q_ref, s32[8,128]{1,0:T(8,128)S(1)} %get-tuple-element.18.limits, bf16[192,256]{1,0:T(8,128)(2,1)S(1)} %collective-permute-done.3.refs_0_, bf16[192,256]{1,0:T(8,128)(2,1)S(1)} %collective-permute-done.7.refs_1_, ...), custom_call_target="tpu_custom_call" | custom-call | flops 402653184 | bytes 524288 | tf_op jit(solution)/shard_map/attend_last/pallas_call | solution.py:296
Async XLA Ops:
  1.2 6.1 %collective-permute-start = (bf16[192,256]{1,0:T(8,128)(2,1)S(1)}, bf16[192,256]{1,0:T(8,128)(2,1)S(1)}, u32[]{:S(2)}, u32[]{:S(2)}) collective-permute-start(bf16[192,256]{1,0:T(8,128)(2,1)S(1)} %get-tuple-element.19.own_keys), channel_id=1, source_target_pairs={{2,6},{6,10},{10,14},{14,12},{12,8},{8,4},{4,0},{0,2},{3,7},{7,11}... | collective-permute-start | bytes 294920 | tf_op jit(solution)/shard_map/ppermute | solution.py:327
  4.2 5.3 %collective-permute-start.4 = (bf16[192,256]{1,0:T(8,128)(2,1)S(1)}, bf16[192,256]{1,0:T(8,128)(2,1)S(1)}, u32[]{:S(2)}, u32[]{:S(2)}) collective-permute-start(bf16[192,256]{1,0:T(8,128)(2,1)S(1)} %get-tuple-element.20.own_values), channel_id=1, source_target_pairs={{6,2},{10,6},{14,10},{12,14},{8,12},{4,8},{0,4},{2,0},{7,3},{11,7}... | collective-permute-start | bytes 294920 | tf_op jit(solution)/shard_map/ppermute | solution.py:328
  4.4 7.2 %collective-permute-start.11 = (bf16[192,256]{1,0:T(8,128)(2,1)S(1)}, bf16[192,256]{1,0:T(8,128)(2,1)S(1)}, u32[]{:S(2)}, u32[]{:S(2)}) collective-permute-start(bf16[192,256]{1,0:T(8,128)(2,1)S(1)} %get-tuple-element.19.own_keys), channel_id=1, source_target_pairs={{6,2},{10,6},{14,10},{12,14},{8,12},{4,8},{0,4},{2,0},{7,3},{11,7}... | collective-permute-start | bytes 294920 | tf_op jit(solution)/shard_map/ppermute | solution.py:331
  6.3 4.8 %collective-permute-start.8 = (bf16[192,256]{1,0:T(8,128)(2,1)S(1)}, bf16[192,256]{1,0:T(8,128)(2,1)S(1)}, u32[]{:S(2)}, u32[]{:S(2)}) collective-permute-start(bf16[192,256]{1,0:T(8,128)(2,1)S(1)} %get-tuple-element.20.own_values), channel_id=1, source_target_pairs={{2,6},{6,10},{10,14},{14,12},{12,8},{8,4},{4,0},{0,2},{3,7},{7,11}... | collective-permute-start | bytes 294920 | tf_op jit(solution)/shard_map/ppermute | solution.py:330
  7.3 5.8 %collective-permute-start.1 = (bf16[192,256]{1,0:T(8,128)(2,1)S(1)}, bf16[192,256]{1,0:T(8,128)(2,1)S(1)}, u32[]{:S(2)}, u32[]{:S(2)}) collective-permute-start(bf16[192,256]{1,0:T(8,128)(2,1)S(1)} %collective-permute-done.refs_0_), channel_id=1, source_target_pairs={{2,6},{6,10},{10,14},{14,12},{12,8},{8,4},{4,0},{0,2},{3,7},{7,11}... | collective-permute-start | bytes 294920 | tf_op jit(solution)/shard_map/ppermute | solution.py:327
  9.5 5.2 %collective-permute-start.5 = (bf16[192,256]{1,0:T(8,128)(2,1)S(1)}, bf16[192,256]{1,0:T(8,128)(2,1)S(1)}, u32[]{:S(2)}, u32[]{:S(2)}) collective-permute-start(bf16[192,256]{1,0:T(8,128)(2,1)S(1)} %collective-permute-done.4.refs_3_), channel_id=1, source_target_pairs={{6,2},{10,6},{14,10},{12,14},{8,12},{4,8},{0,4},{2,0},{7,3},{11,7}... | collective-permute-start | bytes 294920 | tf_op jit(solution)/shard_map/ppermute | solution.py:328
  11.1 4.6 %collective-permute-start.9 = (bf16[192,256]{1,0:T(8,128)(2,1)S(1)}, bf16[192,256]{1,0:T(8,128)(2,1)S(1)}, u32[]{:S(2)}, u32[]{:S(2)}) collective-permute-start(bf16[192,256]{1,0:T(8,128)(2,1)S(1)} %collective-permute-done.8.refs_1_), channel_id=1, source_target_pairs={{2,6},{6,10},{10,14},{14,12},{12,8},{8,4},{4,0},{0,2},{3,7},{7,11}... | collective-permute-start | bytes 294920 | tf_op jit(solution)/shard_map/ppermute | solution.py:330
  11.6 5.3 %collective-permute-start.12 = (bf16[192,256]{1,0:T(8,128)(2,1)S(1)}, bf16[192,256]{1,0:T(8,128)(2,1)S(1)}, u32[]{:S(2)}, u32[]{:S(2)}) collective-permute-start(bf16[192,256]{1,0:T(8,128)(2,1)S(1)} %collective-permute-done.11.refs_2_), channel_id=1, source_target_pairs={{6,2},{10,6},{14,10},{12,14},{8,12},{4,8},{0,4},{2,0},{7,3},{11,7}... | collective-permute-start | bytes 294920 | tf_op jit(solution)/shard_map/ppermute | solution.py:331
  13.1 5.3 %collective-permute-start.2 = (bf16[192,256]{1,0:T(8,128)(2,1)S(1)}, bf16[192,256]{1,0:T(8,128)(2,1)S(1)}, u32[]{:S(2)}, u32[]{:S(2)}) collective-permute-start(bf16[192,256]{1,0:T(8,128)(2,1)S(1)} %collective-permute-done.1.refs_4_), channel_id=1, source_target_pairs={{2,6},{6,10},{10,14},{14,12},{12,8},{8,4},{4,0},{0,2},{3,7},{7,11}... | collective-permute-start | bytes 294920 | tf_op jit(solution)/shard_map/ppermute | solution.py:327
  14.7 5.0 %collective-permute-start.6 = (bf16[192,256]{1,0:T(8,128)(2,1)S(1)}, bf16[192,256]{1,0:T(8,128)(2,1)S(1)}, u32[]{:S(2)}, u32[]{:S(2)}) collective-permute-start(bf16[192,256]{1,0:T(8,128)(2,1)S(1)} %collective-permute-done.5.refs_7_), channel_id=1, source_target_pairs={{6,2},{10,6},{14,10},{12,14},{8,12},{4,8},{0,4},{2,0},{7,3},{11,7}... | collective-permute-start | bytes 294920 | tf_op jit(solution)/shard_map/ppermute | solution.py:328
  15.7 7.3 %collective-permute-start.10 = (bf16[192,256]{1,0:T(8,128)(2,1)S(1)}, bf16[192,256]{1,0:T(8,128)(2,1)S(1)}, u32[]{:S(2)}, u32[]{:S(2)}) collective-permute-start(bf16[192,256]{1,0:T(8,128)(2,1)S(1)} %collective-permute-done.9.refs_5_), channel_id=1, source_target_pairs={{2,6},{6,10},{10,14},{14,12},{12,8},{8,4},{4,0},{0,2},{3,7},{7,11}... | collective-permute-start | bytes 294920 | tf_op jit(solution)/shard_map/ppermute | solution.py:330
  16.9 6.2 %collective-permute-start.13 = (bf16[192,256]{1,0:T(8,128)(2,1)S(1)}, bf16[192,256]{1,0:T(8,128)(2,1)S(1)}, u32[]{:S(2)}, u32[]{:S(2)}) collective-permute-start(bf16[192,256]{1,0:T(8,128)(2,1)S(1)} %collective-permute-done.12.refs_6_), channel_id=1, source_target_pairs={{6,2},{10,6},{14,10},{12,14},{8,12},{4,8},{0,4},{2,0},{7,3},{11,7}... | collective-permute-start | bytes 294920 | tf_op jit(solution)/shard_map/ppermute | solution.py:331
  18.4 6.1 %collective-permute-start.3 = (bf16[192,256]{1,0:T(8,128)(2,1)S(1)}, bf16[192,256]{1,0:T(8,128)(2,1)S(1)}, u32[]{:S(2)}, u32[]{:S(2)}) collective-permute-start(bf16[192,256]{1,0:T(8,128)(2,1)S(1)} %collective-permute-done.2.refs_0_), channel_id=1, source_target_pairs={{2,6},{6,10},{10,14},{14,12},{12,8},{8,4},{4,0},{0,2},{3,7},{7,11}... | collective-permute-start | bytes 294920 | tf_op jit(solution)/shard_map/ppermute | solution.py:327
  19.7 4.8 %collective-permute-start.7 = (bf16[192,256]{1,0:T(8,128)(2,1)S(1)}, bf16[192,256]{1,0:T(8,128)(2,1)S(1)}, u32[]{:S(2)}, u32[]{:S(2)}) collective-permute-start(bf16[192,256]{1,0:T(8,128)(2,1)S(1)} %collective-permute-done.6.refs_3_), channel_id=1, source_target_pairs={{6,2},{10,6},{14,10},{12,14},{8,12},{4,8},{0,4},{2,0},{7,3},{11,7}... | collective-permute-start | bytes 294920 | tf_op jit(solution)/shard_map/ppermute | solution.py:328

commit v10 on v9

--- a/solution.py
+++ b/solution.py
@@ -12,6 +12,7 @@
 EXP_SCALE = HD**-0.5 * math.log2(math.e)
 HIDDEN = -1.0e30
 CHUNK_HEADS = 4
+QUERY_COPIES = 4
 LARGEST_TOTAL = 2.0**100
 
 
@@ -49,6 +50,7 @@
 def load_kernel(count, win_keys, win_values, cache_keys, cache_values, q_hbm, valid_hbm, first_hbm, *refs):
     keys, values, q_ref, limits, valid_ref, first_ref, sems = refs
     window_rows = win_keys.shape[0]
+    rows = q_ref.shape[0] // QUERY_COPIES
     pairs = [
         (valid_hbm, valid_ref),
         (first_hbm, first_ref),
@@ -56,8 +58,7 @@
         (cache_keys, keys.at[window_rows:]),
         (win_values, values.at[:window_rows]),
         (cache_values, values.at[window_rows:]),
-        (q_hbm, q_ref),
-    ]
+    ] + [(q_hbm.at[i * rows : (i + 1) * rows], q_ref.at[i * rows : (i + 1) * rows]) for i in range(QUERY_COPIES)]
     copies = [pltpu.make_async_copy(*pair, sems.at[index]) for index, pair in enumerate(pairs)]
     for copy in copies:
         copy.start()
@@ -90,7 +91,7 @@
         scratch_shapes=[
             pltpu.SMEM(valid_counts.shape, jnp.int32),
             pltpu.SMEM(first_block.shape, jnp.int32),
-            pltpu.SemaphoreType.DMA((7,)),
+            pltpu.SemaphoreType.DMA((6 + QUERY_COPIES,)),
         ],
         compiler_params=pltpu.CompilerParams(vmem_limit_bytes=4 * 1024 * 1024),
         cost_estimate=pl.CostEstimate(flops=0, bytes_accessed=8 * rows * width, transcendentals=0),
@@ -151,10 +152,23 @@
     return jnp.broadcast_to(jnp.max(score, axis=1, keepdims=True) * EXP_SCALE, (score.shape[0], HD))
 
 
-def normalised(acc):
-    total = acc[:, HD:]
-    inverse = pl.reciprocal(total, approx=True)
-    return (acc[:, :HD] * (inverse * (2.0 - total * inverse))).astype(jnp.bfloat16)
+def head_lanes(head, heads, rows):
+    width = HD // heads
+    lane = lax.broadcasted_iota(jnp.int32, (rows, HD), 1)
+    return (lane >= head * width) & (lane < (head + 1) * width)
+
+
+def pack_totals(packed, sums, base, heads):
+    rows = packed.shape[0]
+    for i in range(CHUNK_HEADS):
+        packed = jnp.where(head_lanes(base + i, heads, rows), sums[i * rows : (i + 1) * rows], packed)
+    return packed
+
+
+def by_row(packed, base, heads):
+    rows, width = packed.shape[0], HD // heads
+    columns = [packed[:, (base + i) * width : (base + i) * width + 1] for i in range(CHUNK_HEADS)]
+    return jnp.concatenate([jnp.broadcast_to(column, (rows, HD)) for column in columns], axis=0)
 
 
 def chunks(q_ref, kv_heads):
@@ -169,75 +183,109 @@
             yield head, slice(base * rows, (base + CHUNK_HEADS) * rows), query, base
 
 
-def first_kernel(count, sizes, q_ref, limits, own_keys, own_values, acc_out, top_out, keys, values):
+def first_kernel(count, sizes, q_ref, limits, own_keys, own_values, acc_out, total_out, flag_out, top_out, keys, values):
     window_rows = sizes[0]
     place_piece(0, 1, 0, True, sizes, None, own_keys, own_values, keys, values)
     fill_up(sum(sizes), keys, values)
-    rows = q_ref.shape[0]
+    rows, heads = q_ref.shape[0], q_ref.shape[1] // HD
     key_iota = lax.broadcasted_iota(jnp.int32, (rows, window_rows), 1)
     query_iota = lax.broadcasted_iota(jnp.int32, (rows, window_rows), 0)
     seen = (key_iota <= query_iota) & (key_iota < limits[count - 1 : count, :])
     bias = jnp.concatenate([jnp.where(seen, 0.0, HIDDEN)] * CHUNK_HEADS, axis=0)
-    for head, at, query, _ in chunks(q_ref, keys.shape[0]):
+    packed = jnp.zeros((rows, HD), jnp.float32)
+    for head, at, query, base in chunks(q_ref, keys.shape[0]):
         score = scores(query, keys[head])
         score = jnp.concatenate([score[:, :window_rows] + bias, score[:, window_rows:]], axis=1)
         top = wide_top(score)
-        acc_out[at, :] = weigh(score, top, values[head])
+        added = weigh(score, top, values[head])
+        acc_out[at, :] = added[:, :HD]
         top_out[at, :] = top
-
-
-def next_kernel(rows_of, last, sizes, q_ref, limits, *refs):
+        packed = pack_totals(packed, added[:, HD:], base, heads)
+    total_out[...] = packed
+    flag_out[...] = jnp.zeros(flag_out.shape, jnp.float32)
+
+
+def next_kernel(rows_of, last, sizes, q_ref, limits, top_ref, *refs):
     number = len(rows_of)
     key_refs, value_refs = refs[: 2 * number : 2], refs[1 : 2 * number : 2]
+    acc_in, total_in, flag_in, other_in, *refs = refs[2 * number :]
     if last:
-        acc_in, top_in, out, keys, values, result, sems = refs[2 * number :]
+        out, keys, values, before_ref, result, sems = refs
     else:
-        acc_in, top_in, acc_out, top_out, keys, values = refs[2 * number :]
+        acc_out, total_out, flag_out, other_out, keys, values, before_ref = refs
     for index, row in enumerate(rows_of):
         place_piece(index, number, row, False, sizes, limits, key_refs[index], value_refs[index], keys, values)
     fill_up(number * sum(sizes), keys, values)
-    rows = q_ref.shape[0]
+    rows, heads = q_ref.shape[0], q_ref.shape[1] // HD
     kv_heads = keys.shape[0]
 
-    def sent(base):
-        lanes = slice(base * HD, (base + CHUNK_HEADS) * HD)
-        return pltpu.make_async_copy(result.at[:, lanes], out.at[:, lanes], sems.at[base // CHUNK_HEADS])
-
-    def settle(base, acc):
-        done = normalised(acc)
+    def sent(head):
+        lanes = slice(head * HD, (head + 2) * HD)
+        return pltpu.make_async_copy(result.at[:, lanes], out.at[:, lanes], sems.at[head // 2])
+
+    def settle(base, acc, total):
+        inverse = pl.reciprocal(total, approx=True)
+        inverse = inverse * (2.0 - total * inverse)
+        done = (acc * by_row(inverse, base, heads)).astype(jnp.bfloat16)
         for i in range(CHUNK_HEADS):
             result[:, (base + i) * HD : (base + i + 1) * HD] = done[i * rows : (i + 1) * rows]
-        sent(base).start()
-
-    fine = jnp.ones((8, HD), jnp.float32)
+            if i % 2:
+                sent(base + i - 1).start()
+
+    def wait_all():
+        for head in range(0, heads, 2):
+            sent(head).wait()
+
+    packed = jnp.zeros((rows, HD), jnp.float32)
     for head, at, query, base in chunks(q_ref, kv_heads):
-        top = top_in[at, :]
-        acc = acc_in[at, :] + weigh(scores(query, keys[head]), top, values[head])
-        safe = jnp.where(acc[:, HD:] < LARGEST_TOTAL, 1.0, 0.0).reshape(-1, 8, HD)
-        fine = jnp.minimum(fine, jnp.min(safe, axis=0))
+        added = weigh(scores(query, keys[head]), top_ref[at, :], values[head])
+        acc = acc_in[at, :] + added[:, :HD]
+        packed = pack_totals(packed, added[:, HD:], base, heads)
         if last:
-            settle(base, acc)
+            settle(base, acc, total_in[...] + packed)
         else:
             acc_out[at, :] = acc
-            top_out[at, :] = top
+    total = total_in[...] + packed
+    large = jnp.where(total < LARGEST_TOTAL, 0.0, 1.0).reshape(-1, 8, HD)
+    large = jnp.maximum(jnp.max(large, axis=0), flag_in[...])
+    again = jnp.max(large) > 0.5
     if last:
-        for base in range(0, kv_heads * (q_ref.shape[1] // HD // kv_heads), CHUNK_HEADS):
-            sent(base).wait()
-
-    @pl.when(jnp.min(fine) < 0.5)
+        wait_all()
+    else:
+        total_out[...] = total
+        flag_out[...] = jnp.broadcast_to(jnp.where(again, 1.0, 0.0), flag_out.shape)
+
+    @pl.when(again)
     def _():
+        moved = jnp.max(flag_in[...]) > 0.5
+
+        @pl.when(moved)
+        def _():
+            before_ref[...] = other_in[...]
+
+        @pl.when(jnp.logical_not(moved))
+        def _():
+            before_ref[...] = top_ref[...]
+
+        packed = jnp.zeros((rows, HD), jnp.float32)
         for head, at, query, base in chunks(q_ref, kv_heads):
             score = scores(query, keys[head])
-            before = top_in[at, :]
+            before = before_ref[at, :]
             top = jnp.maximum(before, wide_top(score))
             fade = jnp.exp2(before - top)
-            acc = acc_in[at, :] * jnp.concatenate([fade, fade], axis=1) + weigh(score, top, values[head])
+            added = weigh(score, top, values[head])
+            acc = acc_in[at, :] * fade + added[:, :HD]
+            total = by_row(total_in[...], base, heads) * fade + added[:, HD:]
+            packed = pack_totals(packed, total, base, heads)
             if last:
-                settle(base, acc)
-                sent(base).wait()
+                settle(base, acc, packed)
             else:
                 acc_out[at, :] = acc
-                top_out[at, :] = top
+                other_out[at, :] = top
+        if last:
+            wait_all()
+        else:
+            total_out[...] = packed
 
 
 def kernel_options(queries, total_keys, kv_heads):
@@ -261,7 +309,8 @@
 
 def state_shapes(queries):
     rows = queries.shape[0] * queries.shape[1] // HD
-    return [jax.ShapeDtypeStruct((rows, 2 * HD), jnp.float32), jax.ShapeDtypeStruct((rows, HD), jnp.float32)]
+    shapes = [(rows, HD), (queries.shape[0], HD), (8, HD), (rows, HD)]
+    return [jax.ShapeDtypeStruct(shape, jnp.float32) for shape in shapes]
 
 
 def attend_first(count, sizes, queries, limits, own_keys, own_values):
@@ -273,7 +322,7 @@
             functools.partial(first_kernel, count, sizes),
             out_shape=state_shapes(queries),
             in_specs=[vmem] * 4,
-            out_specs=[vmem] * 2,
+            out_specs=[vmem] * 4,
             scratch_shapes=room(kv_heads, total_keys),
             name="attend_first",
             **kernel_options(queries, total_keys, kv_heads),
@@ -281,18 +330,18 @@
     )
 
 
-def attend_next(pieces, state, last, sizes, queries, limits):
+def attend_next(pieces, state, last, sizes, queries, limits, top):
     rows_of = tuple(piece[0] for piece in pieces)
     blocks = [block for piece in pieces for block in piece[1:]]
     kv_heads = blocks[0].shape[1] // HD
     total_keys = -(-len(pieces) * sum(sizes) // HD) * HD
     vmem = pl.BlockSpec(memory_space=pltpu.VMEM)
-    operands = [queries, limits, *blocks, *state]
+    operands = [queries, limits, top, *blocks, *state]
     shapes = [jax.ShapeDtypeStruct(queries.shape, queries.dtype)] if last else state_shapes(queries)
-    scratch = room(kv_heads, total_keys)
+    scratch = [*room(kv_heads, total_keys), pltpu.VMEM(top.shape, top.dtype)]
     if last:
-        chunk_count = queries.shape[1] // HD // CHUNK_HEADS
-        scratch += [pltpu.VMEM(queries.shape, queries.dtype), pltpu.SemaphoreType.DMA((chunk_count,))]
+        pairs_of_heads = queries.shape[1] // HD // 2
+        scratch += [pltpu.VMEM(queries.shape, queries.dtype), pltpu.SemaphoreType.DMA((pairs_of_heads,))]
     outs = pl.pallas_call(
         functools.partial(next_kernel, rows_of, last, sizes),
         out_shape=shapes,
@@ -334,13 +383,13 @@
         else:
             arrived.append([(2 * (half - 1), key_on, value_back)])
         if step == 1:
-            key_on, top = lax.optimization_barrier((key_on, state[1]))
-            state = (state[0], top)
+            key_on, *state = lax.optimization_barrier((key_on, *state))
+    top = state[3]
     for begin in range(0, half - 2, 2):
         pieces = [piece for step in arrived[begin : min(begin + 2, half - 2)] for piece in step]
-        state = attend_next(pieces, state, False, sizes, near, limits)
-    state = attend_next(arrived[half - 2], state, False, sizes, near, limits)
-    return attend_next(arrived[half - 1], state, True, sizes, near, limits)
+        state = attend_next(pieces, state, False, sizes, near, limits, top)
+    state = attend_next(arrived[half - 2], state, False, sizes, near, limits, top)
+    return attend_next(arrived[half - 1], state, True, sizes, near, limits, top)
 
 
 def solution(mesh):

time: 26.3 us -> 26.5 us (level)
  no operation moved by 1% of the time
where the time goes in v10:
time: 26.5 us; the launch traced here: 26.3 us
  starting transfers between devices  15.9 us (60%)
  Pallas kernels  7.59 us (29%)
  waiting for transfers between devices  2.73 us (10%)
    ppermute x4, starting transfers between devices, shards(): key_on = lax.ppermute(key_on, 'ctx', onward)  7.69 us
    pallas_call x3, Pallas kernels, attend_next(): pl.pallas_call(functools.partial(next_kernel, rows_of, last, sizes), out_...  5.36 us
    ppermute x3, starting transfers between devices, shards(): key_back = lax.ppermute(key_back, 'ctx', backward)  4.37 us
    ppermute x4, starting transfers between devices, shards(): value_back = lax.ppermute(value_back, 'ctx', backward)  2.16 us
    ppermute x3, starting transfers between devices, shards(): value_on = lax.ppermute(value_on, 'ctx', onward)  1.7 us
    ppermute x3, waiting for transfers between devices, shards(): value_on = lax.ppermute(value_on, 'ctx', onward)  1.69 us
    pallas_call x1, Pallas kernels, load(): pl.pallas_call(functools.partial(load_kernel, count), out_shape=[jax.Shap...  1.29 us
    pallas_call x1, Pallas kernels, attend_first(): pl.pallas_call(functools.partial(first_kernel, count, sizes), out_shape=s...  0.93 us
  transfers between devices with their start and end apart: 14, of which 4 were waited for; matrix products, arithmetic and copies ran while one was open for 0% of the time, Pallas kernels for 17%

profile of v10, /device:TPU:0, one launch (start us, length us, event | category | flops | bytes accessed | tf_op | source)
XLA Modules:
  0.0 26.3 jit_solution(6628685949603371766)
XLA Ops:
  0.0 1.3 %load.1 = (bf16[192,256]{1,0:T(8,128)(2,1)S(1)}, bf16[192,256]{1,0:T(8,128)(2,1)S(1)}, bf16[128,2048]{1,0:T(8,128)(2,1)S(1)}, s32[8,128]{1,0:T(8,128)S(1)}) custom-call(bf16[128,256]{1,0:T(8,128)(2,1)} %win_keys.1, bf16[128,256]{1,0:T(8,128)(2,1)} %win_values.1, bf16[64,256]{1,0:T(8,128)(2,1)} %cache_keys.1, bf16[64,256]{1,0:T(8,128)(2,1)} %cache_values.1, ...), custom_call_target="tpu_custom_call" | custom-call | bytes 393216 | tf_op jit(solution)/shard_map/load/pallas_call | solution.py:81
  1.3 3.0 %collective-permute-start = (bf16[192,256]{1,0:T(8,128)(2,1)S(1)}, bf16[192,256]{1,0:T(8,128)(2,1)S(1)}, u32[]{:S(2)}, u32[]{:S(2)}) collective-permute-start(bf16[192,256]{1,0:T(8,128)(2,1)S(1)} %get-tuple-element.28.own_keys), channel_id=1, source_target_pairs={{2,6},{6,10},{10,14},{14,12},{12,8},{8,4},{4,0},{0,2},{3,7},{7,11}... | collective-permute-start | bytes 294920 | tf_op jit(solution)/shard_map/ppermute | solution.py:376
  4.3 0.2 collective-permute-start.4
  4.4 2.0 %collective-permute-start.11 = (bf16[192,256]{1,0:T(8,128)(2,1)S(1)}, bf16[192,256]{1,0:T(8,128)(2,1)S(1)}, u32[]{:S(2)}, u32[]{:S(2)}) collective-permute-start(bf16[192,256]{1,0:T(8,128)(2,1)S(1)} %get-tuple-element.28.own_keys), channel_id=1, source_target_pairs={{6,2},{10,6},{14,10},{12,14},{8,12},{4,8},{0,4},{2,0},{7,3},{11,7}... | collective-permute-start | bytes 294920 | tf_op jit(solution)/shard_map/ppermute | solution.py:380
  6.4 0.1 collective-permute-start.8
  6.5 0.9 %attend_first.1 = (f32[2048,128]{1,0:T(8,128)S(1)}, f32[128,128]{1,0:T(8,128)S(1)}, f32[8,128]{1,0:T(8,128)S(1)}, f32[2048,128]{1,0:T(8,128)S(1)}) custom-call(bf16[128,2048]{1,0:T(8,128)(2,1)S(1)} %get-tuple-element.26.q_ref, s32[8,128]{1,0:T(8,128)S(1)} %get-tuple-element.27.limits, bf16[192,256]{1,0:T(8,128)(2,1)S(1)} %get-tuple-element.28.own_keys, ...), custom_call_target="tpu_custom_call" | custom-call | flops 402653184 | bytes 524288 | tf_op jit(solution)/shard_map/attend_first/pallas_call | solution.py:321
  7.4 0.0 collective-permute-done.refs_0_
  7.4 2.1 %collective-permute-start.1 = (bf16[192,256]{1,0:T(8,128)(2,1)S(1)}, bf16[192,256]{1,0:T(8,128)(2,1)S(1)}, u32[]{:S(2)}, u32[]{:S(2)}) collective-permute-start(bf16[192,256]{1,0:T(8,128)(2,1)S(1)} %collective-permute-done.refs_0_), channel_id=1, source_target_pairs={{2,6},{6,10},{10,14},{14,12},{12,8},{8,4},{4,0},{0,2},{3,7},{7,11}... | collective-permute-start | bytes 294920 | tf_op jit(solution)/shard_map/ppermute | solution.py:376
  9.6 0.0 collective-permute-done.4.refs_3_
  9.6 0.2 collective-permute-start.5
  9.8 1.3 %collective-permute-done.8.refs_1_ = bf16[192,256]{1,0:T(8,128)(2,1)S(1)} collective-permute-done((bf16[192,256]{1,0:T(8,128)(2,1)S(1)}, bf16[192,256]{1,0:T(8,128)(2,1)S(1)}, u32[]{:S(2)}, u32[]{:S(2)}) %collective-permute-start.8) | collective-permute-done | bytes 98336 | tf_op jit(solution)/shard_map/ppermute | solution.py:379
  11.2 0.5 %collective-permute-start.9 = (bf16[192,256]{1,0:T(8,128)(2,1)S(1)}, bf16[192,256]{1,0:T(8,128)(2,1)S(1)}, u32[]{:S(2)}, u32[]{:S(2)}) collective-permute-start(bf16[192,256]{1,0:T(8,128)(2,1)S(1)} %collective-permute-done.8.refs_1_), channel_id=1, source_target_pairs={{2,6},{6,10},{10,14},{14,12},{12,8},{8,4},{4,0},{0,2},{3,7},{7,11}... | collective-permute-start | bytes 294920 | tf_op jit(solution)/shard_map/ppermute | solution.py:379
  11.6 0.0 collective-permute-done.11.refs_2_
  11.6 1.6 %collective-permute-start.12 = (bf16[192,256]{1,0:T(8,128)(2,1)S(1)}, bf16[192,256]{1,0:T(8,128)(2,1)S(1)}, u32[]{:S(2)}, u32[]{:S(2)}) collective-permute-start(bf16[192,256]{1,0:T(8,128)(2,1)S(1)} %collective-permute-done.11.refs_2_), channel_id=1, source_target_pairs={{6,2},{10,6},{14,10},{12,14},{8,12},{4,8},{0,4},{2,0},{7,3},{11,7}... | collective-permute-start | bytes 294920 | tf_op jit(solution)/shard_map/ppermute | solution.py:380
  13.2 0.0 collective-permute-done.1.refs_4_
  13.2 1.6 %collective-permute-start.2 = (bf16[192,256]{1,0:T(8,128)(2,1)S(1)}, bf16[192,256]{1,0:T(8,128)(2,1)S(1)}, u32[]{:S(2)}, u32[]{:S(2)}) collective-permute-start(bf16[192,256]{1,0:T(8,128)(2,1)S(1)} %collective-permute-done.1.refs_4_), channel_id=1, source_target_pairs={{2,6},{6,10},{10,14},{14,12},{12,8},{8,4},{4,0},{0,2},{3,7},{7,11}... | collective-permute-start | bytes 294920 | tf_op jit(solution)/shard_map/ppermute | solution.py:376
  14.8 0.0 collective-permute-done.5.refs_7_
  14.8 0.6 %collective-permute-start.6 = (bf16[192,256]{1,0:T(8,128)(2,1)S(1)}, bf16[192,256]{1,0:T(8,128)(2,1)S(1)}, u32[]{:S(2)}, u32[]{:S(2)}) collective-permute-start(bf16[192,256]{1,0:T(8,128)(2,1)S(1)} %collective-permute-done.5.refs_7_), channel_id=1, source_target_pairs={{6,2},{10,6},{14,10},{12,14},{8,12},{4,8},{0,4},{2,0},{7,3},{11,7}... | collective-permute-start | bytes 294920 | tf_op jit(solution)/shard_map/ppermute | solution.py:377
  15.4 0.4 %collective-permute-done.9.refs_5_ = bf16[192,256]{1,0:T(8,128)(2,1)S(1)} collective-permute-done((bf16[192,256]{1,0:T(8,128)(2,1)S(1)}, bf16[192,256]{1,0:T(8,128)(2,1)S(1)}, u32[]{:S(2)}, u32[]{:S(2)}) %collective-permute-start.9) | collective-permute-done | bytes 98336 | tf_op jit(solution)/shard_map/ppermute | solution.py:379
  15.8 1.2 %collective-permute-start.10 = (bf16[192,256]{1,0:T(8,128)(2,1)S(1)}, bf16[192,256]{1,0:T(8,128)(2,1)S(1)}, u32[]{:S(2)}, u32[]{:S(2)}) collective-permute-start(bf16[192,256]{1,0:T(8,128)(2,1)S(1)} %collective-permute-done.9.refs_5_), channel_id=1, source_target_pairs={{2,6},{6,10},{10,14},{14,12},{12,8},{8,4},{4,0},{0,2},{3,7},{7,11}... | collective-permute-start | bytes 294920 | tf_op jit(solution)/shard_map/ppermute | solution.py:379
  17.0 0.0 collective-permute-done.12.refs_6_
  17.0 0.9 %collective-permute-start.13 = (bf16[192,256]{1,0:T(8,128)(2,1)S(1)}, bf16[192,256]{1,0:T(8,128)(2,1)S(1)}, u32[]{:S(2)}, u32[]{:S(2)}) collective-permute-start(bf16[192,256]{1,0:T(8,128)(2,1)S(1)} %collective-permute-done.12.refs_6_), channel_id=1, source_target_pairs={{6,2},{10,6},{14,10},{12,14},{8,12},{4,8},{0,4},{2,0},{7,3},{11,7}... | collective-permute-start | bytes 294920 | tf_op jit(solution)/shard_map/ppermute | solution.py:380
  17.8 0.7 %collective-permute-done.2.refs_0_ = bf16[192,256]{1,0:T(8,128)(2,1)S(1)} collective-permute-done((bf16[192,256]{1,0:T(8,128)(2,1)S(1)}, bf16[192,256]{1,0:T(8,128)(2,1)S(1)}, u32[]{:S(2)}, u32[]{:S(2)}) %collective-permute-start.2) | collective-permute-done | bytes 98336 | tf_op jit(solution)/shard_map/ppermute | solution.py:376
  18.5 1.0 %collective-permute-start.3 = (bf16[192,256]{1,0:T(8,128)(2,1)S(1)}, bf16[192,256]{1,0:T(8,128)(2,1)S(1)}, u32[]{:S(2)}, u32[]{:S(2)}) collective-permute-start(bf16[192,256]{1,0:T(8,128)(2,1)S(1)} %collective-permute-done.2.refs_0_), channel_id=1, source_target_pairs={{2,6},{6,10},{10,14},{14,12},{12,8},{8,4},{4,0},{0,2},{3,7},{7,11}... | collective-permute-start | bytes 294920 | tf_op jit(solution)/shard_map/ppermute | solution.py:376
  19.5 0.3 %collective-permute-done.6.refs_3_ = bf16[192,256]{1,0:T(8,128)(2,1)S(1)} collective-permute-done((bf16[192,256]{1,0:T(8,128)(2,1)S(1)}, bf16[192,256]{1,0:T(8,128)(2,1)S(1)}, u32[]{:S(2)}, u32[]{:S(2)}) %collective-permute-start.6) | collective-permute-done | bytes 98336 | tf_op jit(solution)/shard_map/ppermute | solution.py:377
  19.8 1.1 %collective-permute-start.7 = (bf16[192,256]{1,0:T(8,128)(2,1)S(1)}, bf16[192,256]{1,0:T(8,128)(2,1)S(1)}, u32[]{:S(2)}, u32[]{:S(2)}) collective-permute-start(bf16[192,256]{1,0:T(8,128)(2,1)S(1)} %collective-permute-done.6.refs_3_), channel_id=1, source_target_pairs={{6,2},{10,6},{14,10},{12,14},{8,12},{4,8},{0,4},{2,0},{7,3},{11,7}... | collective-permute-start | bytes 294920 | tf_op jit(solution)/shard_map/ppermute | solution.py:377
  20.9 2.2 %attend_next.2 = (f32[2048,128]{1,0:T(8,128)S(1)}, f32[128,128]{1,0:T(8,128)S(1)}, f32[8,128]{1,0:T(8,128)S(1)}, f32[2048,128]{1,0:T(8,128)S(1)}) custom-call(bf16[128,2048]{1,0:T(8,128)(2,1)S(1)} %get-tuple-element.26.q_ref, s32[8,128]{1,0:T(8,128)S(1)} %get-tuple-element.27.limits, f32[2048,128]{1,0:T(8,128)S(1)} %get-tuple-element.34.top_ref.refs_11_, ...), custom_call_target="tpu_custom_call" | custom-call | flops 1207959552 | bytes 524288 | tf_op jit(solution)/shard_map/attend_next/pallas_call | solution.py:345
  23.1 0.0 collective-permute-done.10.refs_1_
  23.1 0.0 collective-permute-done.13.refs_2_
  23.1 1.4 %attend_next.3 = (f32[2048,128]{1,0:T(8,128)S(1)}, f32[128,128]{1,0:T(8,128)S(1)}, f32[8,128]{1,0:T(8,128)S(1)}, f32[2048,128]{1,0:T(8,128)S(1)}) custom-call(bf16[128,2048]{1,0:T(8,128)(2,1)S(1)} %get-tuple-element.26.q_ref, s32[8,128]{1,0:T(8,128)S(1)} %get-tuple-element.27.limits, f32[2048,128]{1,0:T(8,128)S(1)} %get-tuple-element.34.top_ref.refs_11_, ...), custom_call_target="tpu_custom_call" | custom-call | flops 603979776 | bytes 524288 | tf_op jit(solution)/shard_map/attend_next/pallas_call | solution.py:345
  24.5 0.0 collective-permute-done.3.refs_0_
  24.5 0.0 collective-permute-done.7.refs_1_
  24.5 1.8 %attend_last.1 = bf16[128,2048]{1,0:T(8,128)(2,1)} custom-call(bf16[128,2048]{1,0:T(8,128)(2,1)S(1)} %get-tuple-element.26.q_ref, s32[8,128]{1,0:T(8,128)S(1)} %get-tuple-element.27.limits, f32[2048,128]{1,0:T(8,128)S(1)} %get-tuple-element.34.top_ref.refs_11_, bf16[192,256]{1,0:T(8,128)(2,1)S(1)} %collective-permute-done.3.refs_0_, ...), custom_call_target="tpu_custom_call" | custom-call | flops 402653184 | bytes 524288 | tf_op jit(solution)/shard_map/attend_last/pallas_call | solution.py:345
Async XLA Ops:
  1.3 6.1 %collective-permute-start = (bf16[192,256]{1,0:T(8,128)(2,1)S(1)}, bf16[192,256]{1,0:T(8,128)(2,1)S(1)}, u32[]{:S(2)}, u32[]{:S(2)}) collective-permute-start(bf16[192,256]{1,0:T(8,128)(2,1)S(1)} %get-tuple-element.28.own_keys), channel_id=1, source_target_pairs={{2,6},{6,10},{10,14},{14,12},{12,8},{8,4},{4,0},{0,2},{3,7},{7,11}... | collective-permute-start | bytes 294920 | tf_op jit(solution)/shard_map/ppermute | solution.py:376
  4.3 5.3 %collective-permute-start.4 = (bf16[192,256]{1,0:T(8,128)(2,1)S(1)}, bf16[192,256]{1,0:T(8,128)(2,1)S(1)}, u32[]{:S(2)}, u32[]{:S(2)}) collective-permute-start(bf16[192,256]{1,0:T(8,128)(2,1)S(1)} %get-tuple-element.29.own_values), channel_id=1, source_target_pairs={{6,2},{10,6},{14,10},{12,14},{8,12},{4,8},{0,4},{2,0},{7,3},{11,7}... | collective-permute-start | bytes 294920 | tf_op jit(solution)/shard_map/ppermute | solution.py:377
  4.4 7.2 %collective-permute-start.11 = (bf16[192,256]{1,0:T(8,128)(2,1)S(1)}, bf16[192,256]{1,0:T(8,128)(2,1)S(1)}, u32[]{:S(2)}, u32[]{:S(2)}) collective-permute-start(bf16[192,256]{1,0:T(8,128)(2,1)S(1)} %get-tuple-element.28.own_keys), channel_id=1, source_target_pairs={{6,2},{10,6},{14,10},{12,14},{8,12},{4,8},{0,4},{2,0},{7,3},{11,7}... | collective-permute-start | bytes 294920 | tf_op jit(solution)/shard_map/ppermute | solution.py:380
  6.4 4.8 %collective-permute-start.8 = (bf16[192,256]{1,0:T(8,128)(2,1)S(1)}, bf16[192,256]{1,0:T(8,128)(2,1)S(1)}, u32[]{:S(2)}, u32[]{:S(2)}) collective-permute-start(bf16[192,256]{1,0:T(8,128)(2,1)S(1)} %get-tuple-element.29.own_values), channel_id=1, source_target_pairs={{2,6},{6,10},{10,14},{14,12},{12,8},{8,4},{4,0},{0,2},{3,7},{7,11}... | collective-permute-start | bytes 294920 | tf_op jit(solution)/shard_map/ppermute | solution.py:379
  7.4 5.8 %collective-permute-start.1 = (bf16[192,256]{1,0:T(8,128)(2,1)S(1)}, bf16[192,256]{1,0:T(8,128)(2,1)S(1)}, u32[]{:S(2)}, u32[]{:S(2)}) collective-permute-start(bf16[192,256]{1,0:T(8,128)(2,1)S(1)} %collective-permute-done.refs_0_), channel_id=1, source_target_pairs={{2,6},{6,10},{10,14},{14,12},{12,8},{8,4},{4,0},{0,2},{3,7},{7,11}... | collective-permute-start | bytes 294920 | tf_op jit(solution)/shard_map/ppermute | solution.py:376
  9.6 5.2 %collective-permute-start.5 = (bf16[192,256]{1,0:T(8,128)(2,1)S(1)}, bf16[192,256]{1,0:T(8,128)(2,1)S(1)}, u32[]{:S(2)}, u32[]{:S(2)}) collective-permute-start(bf16[192,256]{1,0:T(8,128)(2,1)S(1)} %collective-permute-done.4.refs_3_), channel_id=1, source_target_pairs={{6,2},{10,6},{14,10},{12,14},{8,12},{4,8},{0,4},{2,0},{7,3},{11,7}... | collective-permute-start | bytes 294920 | tf_op jit(solution)/shard_map/ppermute | solution.py:377
  11.2 4.6 %collective-permute-start.9 = (bf16[192,256]{1,0:T(8,128)(2,1)S(1)}, bf16[192,256]{1,0:T(8,128)(2,1)S(1)}, u32[]{:S(2)}, u32[]{:S(2)}) collective-permute-start(bf16[192,256]{1,0:T(8,128)(2,1)S(1)} %collective-permute-done.8.refs_1_), channel_id=1, source_target_pairs={{2,6},{6,10},{10,14},{14,12},{12,8},{8,4},{4,0},{0,2},{3,7},{7,11}... | collective-permute-start | bytes 294920 | tf_op jit(solution)/shard_map/ppermute | solution.py:379
  11.6 5.3 %collective-permute-start.12 = (bf16[192,256]{1,0:T(8,128)(2,1)S(1)}, bf16[192,256]{1,0:T(8,128)(2,1)S(1)}, u32[]{:S(2)}, u32[]{:S(2)}) collective-permute-start(bf16[192,256]{1,0:T(8,128)(2,1)S(1)} %collective-permute-done.11.refs_2_), channel_id=1, source_target_pairs={{6,2},{10,6},{14,10},{12,14},{8,12},{4,8},{0,4},{2,0},{7,3},{11,7}... | collective-permute-start | bytes 294920 | tf_op jit(solution)/shard_map/ppermute | solution.py:380
  13.2 5.3 %collective-permute-start.2 = (bf16[192,256]{1,0:T(8,128)(2,1)S(1)}, bf16[192,256]{1,0:T(8,128)(2,1)S(1)}, u32[]{:S(2)}, u32[]{:S(2)}) collective-permute-start(bf16[192,256]{1,0:T(8,128)(2,1)S(1)} %collective-permute-done.1.refs_4_), channel_id=1, source_target_pairs={{2,6},{6,10},{10,14},{14,12},{12,8},{8,4},{4,0},{0,2},{3,7},{7,11}... | collective-permute-start | bytes 294920 | tf_op jit(solution)/shard_map/ppermute | solution.py:376
  14.8 5.0 %collective-permute-start.6 = (bf16[192,256]{1,0:T(8,128)(2,1)S(1)}, bf16[192,256]{1,0:T(8,128)(2,1)S(1)}, u32[]{:S(2)}, u32[]{:S(2)}) collective-permute-start(bf16[192,256]{1,0:T(8,128)(2,1)S(1)} %collective-permute-done.5.refs_7_), channel_id=1, source_target_pairs={{6,2},{10,6},{14,10},{12,14},{8,12},{4,8},{0,4},{2,0},{7,3},{11,7}... | collective-permute-start | bytes 294920 | tf_op jit(solution)/shard_map/ppermute | solution.py:377
  15.8 7.3 %collective-permute-start.10 = (bf16[192,256]{1,0:T(8,128)(2,1)S(1)}, bf16[192,256]{1,0:T(8,128)(2,1)S(1)}, u32[]{:S(2)}, u32[]{:S(2)}) collective-permute-start(bf16[192,256]{1,0:T(8,128)(2,1)S(1)} %collective-permute-done.9.refs_5_), channel_id=1, source_target_pairs={{2,6},{6,10},{10,14},{14,12},{12,8},{8,4},{4,0},{0,2},{3,7},{7,11}... | collective-permute-start | bytes 294920 | tf_op jit(solution)/shard_map/ppermute | solution.py:379
  17.0 6.2 %collective-permute-start.13 = (bf16[192,256]{1,0:T(8,128)(2,1)S(1)}, bf16[192,256]{1,0:T(8,128)(2,1)S(1)}, u32[]{:S(2)}, u32[]{:S(2)}) collective-permute-start(bf16[192,256]{1,0:T(8,128)(2,1)S(1)} %collective-permute-done.12.refs_6_), channel_id=1, source_target_pairs={{6,2},{10,6},{14,10},{12,14},{8,12},{4,8},{0,4},{2,0},{7,3},{11,7}... | collective-permute-start | bytes 294920 | tf_op jit(solution)/shard_map/ppermute | solution.py:380
  18.5 6.0 %collective-permute-start.3 = (bf16[192,256]{1,0:T(8,128)(2,1)S(1)}, bf16[192,256]{1,0:T(8,128)(2,1)S(1)}, u32[]{:S(2)}, u32[]{:S(2)}) collective-permute-start(bf16[192,256]{1,0:T(8,128)(2,1)S(1)} %collective-permute-done.2.refs_0_), channel_id=1, source_target_pairs={{2,6},{6,10},{10,14},{14,12},{12,8},{8,4},{4,0},{0,2},{3,7},{7,11}... | collective-permute-start | bytes 294920 | tf_op jit(solution)/shard_map/ppermute | solution.py:376
  19.8 4.7 %collective-permute-start.7 = (bf16[192,256]{1,0:T(8,128)(2,1)S(1)}, bf16[192,256]{1,0:T(8,128)(2,1)S(1)}, u32[]{:S(2)}, u32[]{:S(2)}) collective-permute-start(bf16[192,256]{1,0:T(8,128)(2,1)S(1)} %collective-permute-done.6.refs_3_), channel_id=1, source_target_pairs={{6,2},{10,6},{14,10},{12,14},{8,12},{4,8},{0,4},{2,0},{7,3},{11,7}... | collective-permute-start | bytes 294920 | tf_op jit(solution)/shard_map/ppermute | solution.py:377

commit v11 on v9

--- a/solution.py
+++ b/solution.py
@@ -103,15 +103,14 @@
     return [sign * step for step in range(1, half) for sign in (-1, 1)] + [half]
 
 
-def place_piece(index, number, limit_row, own, sizes, limits, key, value, keys, values):
-    window_rows, cache_rows = sizes
-    cache_at = number * window_rows + index * cache_rows
+def place_window(index, limit_row, own, sizes, limits, key, value, keys, values):
+    window_rows = sizes[0]
     if not own:
         row_iota = lax.broadcasted_iota(jnp.int32, (window_rows, HD), 0)
         shown = row_iota < limits[limit_row : limit_row + 1, :]
+    at = slice(index * window_rows, (index + 1) * window_rows)
     for head in range(keys.shape[0]):
         lanes = slice(head * HD, (head + 1) * HD)
-        at = slice(index * window_rows, (index + 1) * window_rows)
         win_key, win_value = key[:window_rows, lanes], value[:window_rows, lanes]
         if own:
             keys[head, at, :] = win_key
@@ -122,7 +121,14 @@
             keys[head, at, :] = jnp.where(shown, win_key.astype(jnp.float32), fill).astype(jnp.bfloat16)
             values[head, at, :HD] = jnp.where(shown, win_value.astype(jnp.float32), 0.0).astype(jnp.bfloat16)
             values[head, at, HD:] = jnp.where(shown, 1.0, 0.0).astype(jnp.bfloat16)
-        at = slice(cache_at, cache_at + cache_rows)
+
+
+def place_cache(index, number, sizes, key, value, keys, values):
+    window_rows, cache_rows = sizes
+    start = number * window_rows + index * cache_rows
+    at = slice(start, start + cache_rows)
+    for head in range(keys.shape[0]):
+        lanes = slice(head * HD, (head + 1) * HD)
         keys[head, at, :] = key[window_rows:, lanes]
         values[head, at, :HD] = value[window_rows:, lanes]
         values[head, at, HD:] = jnp.ones((cache_rows, HD), jnp.bfloat16)
@@ -171,7 +177,8 @@
 
 def first_kernel(count, sizes, q_ref, limits, own_keys, own_values, acc_out, top_out, keys, values):
     window_rows = sizes[0]
-    place_piece(0, 1, 0, True, sizes, None, own_keys, own_values, keys, values)
+    place_window(0, 0, True, sizes, None, own_keys, own_values, keys, values)
+    place_cache(0, 1, sizes, own_keys, own_values, keys, values)
     fill_up(sum(sizes), keys, values)
     rows = q_ref.shape[0]
     key_iota = lax.broadcasted_iota(jnp.int32, (rows, window_rows), 1)
@@ -186,17 +193,14 @@
         top_out[at, :] = top
 
 
-def next_kernel(rows_of, last, sizes, q_ref, limits, *refs):
+def next_kernel(rows_of, last, count, sizes, q_ref, limits, *refs):
     number = len(rows_of)
     key_refs, value_refs = refs[: 2 * number : 2], refs[1 : 2 * number : 2]
     if last:
         acc_in, top_in, out, keys, values, result, sems = refs[2 * number :]
     else:
         acc_in, top_in, acc_out, top_out, keys, values = refs[2 * number :]
-    for index, row in enumerate(rows_of):
-        place_piece(index, number, row, False, sizes, limits, key_refs[index], value_refs[index], keys, values)
-    fill_up(number * sum(sizes), keys, values)
-    rows = q_ref.shape[0]
+    rows, heads = q_ref.shape[0], q_ref.shape[1] // HD
     kv_heads = keys.shape[0]
 
     def sent(base):
@@ -209,35 +213,56 @@
             result[:, (base + i) * HD : (base + i + 1) * HD] = done[i * rows : (i + 1) * rows]
         sent(base).start()
 
-    fine = jnp.ones((8, HD), jnp.float32)
-    for head, at, query, base in chunks(q_ref, kv_heads):
-        top = top_in[at, :]
-        acc = acc_in[at, :] + weigh(scores(query, keys[head]), top, values[head])
-        safe = jnp.where(acc[:, HD:] < LARGEST_TOTAL, 1.0, 0.0).reshape(-1, 8, HD)
-        fine = jnp.minimum(fine, jnp.min(safe, axis=0))
-        if last:
-            settle(base, acc)
-        else:
-            acc_out[at, :] = acc
-            top_out[at, :] = top
-    if last:
-        for base in range(0, kv_heads * (q_ref.shape[1] // HD // kv_heads), CHUNK_HEADS):
-            sent(base).wait()
-
-    @pl.when(jnp.min(fine) < 0.5)
-    def _():
+    def take_in(begin):
+        fine = jnp.ones((8, HD), jnp.float32)
         for head, at, query, base in chunks(q_ref, kv_heads):
-            score = scores(query, keys[head])
-            before = top_in[at, :]
-            top = jnp.maximum(before, wide_top(score))
-            fade = jnp.exp2(before - top)
-            acc = acc_in[at, :] * jnp.concatenate([fade, fade], axis=1) + weigh(score, top, values[head])
+            top = top_in[at, :]
+            acc = acc_in[at, :] + weigh(scores(query, keys[head, begin:]), top, values[head, begin:])
+            safe = jnp.where(acc[:, HD:] < LARGEST_TOTAL, 1.0, 0.0).reshape(-1, 8, HD)
+            fine = jnp.minimum(fine, jnp.min(safe, axis=0))
             if last:
                 settle(base, acc)
-                sent(base).wait()
             else:
                 acc_out[at, :] = acc
                 top_out[at, :] = top
+        if last:
+            for base in range(0, heads, CHUNK_HEADS):
+                sent(base).wait()
+
+        @pl.when(jnp.min(fine) < 0.5)
+        def _():
+            for head, at, query, base in chunks(q_ref, kv_heads):
+                score = scores(query, keys[head, begin:])
+                before = top_in[at, :]
+                top = jnp.maximum(before, wide_top(score))
+                fade = jnp.exp2(before - top)
+                acc = acc_in[at, :] * jnp.concatenate([fade, fade], axis=1)
+                acc = acc + weigh(score, top, values[head, begin:])
+                if last:
+                    settle(base, acc)
+                    sent(base).wait()
+                else:
+                    acc_out[at, :] = acc
+                    top_out[at, :] = top
+
+    for index in range(number):
+        place_cache(index, number, sizes, key_refs[index], value_refs[index], keys, values)
+    fill_up(number * sum(sizes), keys, values)
+    me = lax.axis_index("ctx")
+    position = position_of(me, count)
+    offsets = ring_offsets(count)
+    places = [place_at(lax.rem(position + offsets[row] + count, count), count) for row in rows_of]
+    earlier = functools.reduce(jnp.logical_or, [place < me for place in places])
+
+    @pl.when(earlier)
+    def _():
+        for index, row in enumerate(rows_of):
+            place_window(index, row, False, sizes, limits, key_refs[index], value_refs[index], keys, values)
+        take_in(0)
+
+    @pl.when(jnp.logical_not(earlier))
+    def _():
+        take_in(number * sizes[0])
 
 
 def kernel_options(queries, total_keys, kv_heads):
@@ -281,7 +306,7 @@
     )
 
 
-def attend_next(pieces, state, last, sizes, queries, limits):
+def attend_next(pieces, state, last, count, sizes, queries, limits):
     rows_of = tuple(piece[0] for piece in pieces)
     blocks = [block for piece in pieces for block in piece[1:]]
     kv_heads = blocks[0].shape[1] // HD
@@ -294,7 +319,7 @@
         chunk_count = queries.shape[1] // HD // CHUNK_HEADS
         scratch += [pltpu.VMEM(queries.shape, queries.dtype), pltpu.SemaphoreType.DMA((chunk_count,))]
     outs = pl.pallas_call(
-        functools.partial(next_kernel, rows_of, last, sizes),
+        functools.partial(next_kernel, rows_of, last, count, sizes),
         out_shape=shapes,
         in_specs=[vmem] * len(operands),
         out_specs=[pl.BlockSpec(memory_space=pltpu.HBM)] if last else [vmem] * len(shapes),
@@ -338,9 +363,9 @@
             state = (state[0], top)
     for begin in range(0, half - 2, 2):
         pieces = [piece for step in arrived[begin : min(begin + 2, half - 2)] for piece in step]
-        state = attend_next(pieces, state, False, sizes, near, limits)
-    state = attend_next(arrived[half - 2], state, False, sizes, near, limits)
-    return attend_next(arrived[half - 1], state, True, sizes, near, limits)
+        state = attend_next(pieces, state, False, count, sizes, near, limits)
+    state = attend_next(arrived[half - 2], state, False, count, sizes, near, limits)
+    return attend_next(arrived[half - 1], state, True, count, sizes, near, limits)
 
 
 def solution(mesh):

time: 26.3 us -> 26.3 us (level)
  Pallas kernels: 7.41 us -> 6.13 us
  waiting for transfers between devices: 2.69 us -> 3.82 us
    pallas_call x3, Pallas kernels: 5.27 us -> 3.98 us  [attend_next(): pl.pallas_call(functools.partial(next_kernel, rows_of, last, count, sizes...]
    ppermute x4, waiting for transfers between devices: 0.33 us -> 1.46 us  [shards(): value_back = lax.ppermute(value_back, 'ctx', backward)]
  transfers between devices with their start and end apart: 14 -> 14, of which waited for: 4 -> 5; matrix products, arithmetic and copies ran while one was open for 0% -> 0% of each run, Pallas kernels for 17% -> 12%
where the time goes in v11:
time: 26.3 us; the launch traced here: 26.2 us
  starting transfers between devices  16 us (61%)
  Pallas kernels  6.13 us (23%)
  waiting for transfers between devices  3.82 us (15%)
    ppermute x4, starting transfers between devices, shards(): key_on = lax.ppermute(key_on, 'ctx', onward)  7.72 us
    ppermute x3, starting transfers between devices, shards(): key_back = lax.ppermute(key_back, 'ctx', backward)  4.36 us
    pallas_call x3, Pallas kernels, attend_next(): pl.pallas_call(functools.partial(next_kernel, rows_of, last, count, sizes...  3.98 us
    ppermute x4, starting transfers between devices, shards(): value_back = lax.ppermute(value_back, 'ctx', backward)  2.19 us
    ppermute x3, starting transfers between devices, shards(): value_on = lax.ppermute(value_on, 'ctx', onward)  1.72 us
    ppermute x3, waiting for transfers between devices, shards(): value_on = lax.ppermute(value_on, 'ctx', onward)  1.68 us
    ppermute x4, waiting for transfers between devices, shards(): value_back = lax.ppermute(value_back, 'ctx', backward)  1.46 us
    pallas_call x1, Pallas kernels, load(): pl.pallas_call(functools.partial(load_kernel, count), out_shape=[jax.Shap...  1.22 us
  transfers between devices with their start and end apart: 14, of which 5 were waited for; matrix products, arithmetic and copies ran while one was open for 0% of the time, Pallas kernels for 12%

profile of v11, /device:TPU:0, one launch (start us, length us, event | category | flops | bytes accessed | tf_op | source)
XLA Modules:
  0.0 26.2 jit_solution(3839281749444235532)
XLA Ops:
  0.0 1.2 %load.1 = (bf16[192,256]{1,0:T(8,128)(2,1)S(1)}, bf16[192,256]{1,0:T(8,128)(2,1)S(1)}, bf16[128,2048]{1,0:T(8,128)(2,1)S(1)}, s32[8,128]{1,0:T(8,128)S(1)}) custom-call(bf16[128,256]{1,0:T(8,128)(2,1)} %win_keys.1, bf16[128,256]{1,0:T(8,128)(2,1)} %win_values.1, bf16[64,256]{1,0:T(8,128)(2,1)} %cache_keys.1, bf16[64,256]{1,0:T(8,128)(2,1)} %cache_values.1, ...), custom_call_target="tpu_custom_call" | custom-call | bytes 393216 | tf_op jit(solution)/shard_map/load/pallas_call | solution.py:80
  1.2 3.0 %collective-permute-start = (bf16[192,256]{1,0:T(8,128)(2,1)S(1)}, bf16[192,256]{1,0:T(8,128)(2,1)S(1)}, u32[]{:S(2)}, u32[]{:S(2)}) collective-permute-start(bf16[192,256]{1,0:T(8,128)(2,1)S(1)} %get-tuple-element.19.own_keys), channel_id=1, source_target_pairs={{2,6},{6,10},{10,14},{14,12},{12,8},{8,4},{4,0},{0,2},{3,7},{7,11}... | collective-permute-start | bytes 294920 | tf_op jit(solution)/shard_map/ppermute | solution.py:352
  4.2 0.2 collective-permute-start.4
  4.4 2.0 %collective-permute-start.11 = (bf16[192,256]{1,0:T(8,128)(2,1)S(1)}, bf16[192,256]{1,0:T(8,128)(2,1)S(1)}, u32[]{:S(2)}, u32[]{:S(2)}) collective-permute-start(bf16[192,256]{1,0:T(8,128)(2,1)S(1)} %get-tuple-element.19.own_keys), channel_id=1, source_target_pairs={{6,2},{10,6},{14,10},{12,14},{8,12},{4,8},{0,4},{2,0},{7,3},{11,7}... | collective-permute-start | bytes 294920 | tf_op jit(solution)/shard_map/ppermute | solution.py:356
  6.3 0.1 collective-permute-start.8
  6.4 0.9 %attend_first.1 = (f32[2048,256]{1,0:T(8,128)S(1)}, f32[2048,128]{1,0:T(8,128)S(1)}) custom-call(bf16[128,2048]{1,0:T(8,128)(2,1)S(1)} %get-tuple-element.17.q_ref, s32[8,128]{1,0:T(8,128)S(1)} %get-tuple-element.18.limits, bf16[192,256]{1,0:T(8,128)(2,1)S(1)} %get-tuple-element.19.own_keys, bf16[192,256]{1,0:T(8,128)(2,1)S(1)} %get-tuple-element.20.own_values), custom_call_target="tpu_custom_call" | custom-call | flops 402653184 | bytes 524288 | tf_op jit(solution)/shard_map/attend_first/pallas_call | solution.py:297
  7.3 0.0 collective-permute-done.refs_0_
  7.3 2.1 %collective-permute-start.1 = (bf16[192,256]{1,0:T(8,128)(2,1)S(1)}, bf16[192,256]{1,0:T(8,128)(2,1)S(1)}, u32[]{:S(2)}, u32[]{:S(2)}) collective-permute-start(bf16[192,256]{1,0:T(8,128)(2,1)S(1)} %collective-permute-done.refs_0_), channel_id=1, source_target_pairs={{2,6},{6,10},{10,14},{14,12},{12,8},{8,4},{4,0},{0,2},{3,7},{7,11}... | collective-permute-start | bytes 294920 | tf_op jit(solution)/shard_map/ppermute | solution.py:352
  9.5 0.0 collective-permute-done.4.refs_3_
  9.5 0.2 collective-permute-start.5
  9.8 1.3 %collective-permute-done.8.refs_1_ = bf16[192,256]{1,0:T(8,128)(2,1)S(1)} collective-permute-done((bf16[192,256]{1,0:T(8,128)(2,1)S(1)}, bf16[192,256]{1,0:T(8,128)(2,1)S(1)}, u32[]{:S(2)}, u32[]{:S(2)}) %collective-permute-start.8) | collective-permute-done | bytes 98336 | tf_op jit(solution)/shard_map/ppermute | solution.py:355
  11.1 0.5 %collective-permute-start.9 = (bf16[192,256]{1,0:T(8,128)(2,1)S(1)}, bf16[192,256]{1,0:T(8,128)(2,1)S(1)}, u32[]{:S(2)}, u32[]{:S(2)}) collective-permute-start(bf16[192,256]{1,0:T(8,128)(2,1)S(1)} %collective-permute-done.8.refs_1_), channel_id=1, source_target_pairs={{2,6},{6,10},{10,14},{14,12},{12,8},{8,4},{4,0},{0,2},{3,7},{7,11}... | collective-permute-start | bytes 294920 | tf_op jit(solution)/shard_map/ppermute | solution.py:355
  11.6 0.0 collective-permute-done.11.refs_2_
  11.6 1.6 %collective-permute-start.12 = (bf16[192,256]{1,0:T(8,128)(2,1)S(1)}, bf16[192,256]{1,0:T(8,128)(2,1)S(1)}, u32[]{:S(2)}, u32[]{:S(2)}) collective-permute-start(bf16[192,256]{1,0:T(8,128)(2,1)S(1)} %collective-permute-done.11.refs_2_), channel_id=1, source_target_pairs={{6,2},{10,6},{14,10},{12,14},{8,12},{4,8},{0,4},{2,0},{7,3},{11,7}... | collective-permute-start | bytes 294920 | tf_op jit(solution)/shard_map/ppermute | solution.py:356
  13.1 0.0 collective-permute-done.1.refs_4_
  13.1 1.6 %collective-permute-start.2 = (bf16[192,256]{1,0:T(8,128)(2,1)S(1)}, bf16[192,256]{1,0:T(8,128)(2,1)S(1)}, u32[]{:S(2)}, u32[]{:S(2)}) collective-permute-start(bf16[192,256]{1,0:T(8,128)(2,1)S(1)} %collective-permute-done.1.refs_4_), channel_id=1, source_target_pairs={{2,6},{6,10},{10,14},{14,12},{12,8},{8,4},{4,0},{0,2},{3,7},{7,11}... | collective-permute-start | bytes 294920 | tf_op jit(solution)/shard_map/ppermute | solution.py:352
  14.7 0.0 collective-permute-done.5.refs_7_
  14.7 0.6 %collective-permute-start.6 = (bf16[192,256]{1,0:T(8,128)(2,1)S(1)}, bf16[192,256]{1,0:T(8,128)(2,1)S(1)}, u32[]{:S(2)}, u32[]{:S(2)}) collective-permute-start(bf16[192,256]{1,0:T(8,128)(2,1)S(1)} %collective-permute-done.5.refs_7_), channel_id=1, source_target_pairs={{6,2},{10,6},{14,10},{12,14},{8,12},{4,8},{0,4},{2,0},{7,3},{11,7}... | collective-permute-start | bytes 294920 | tf_op jit(solution)/shard_map/ppermute | solution.py:353
  15.3 0.4 %collective-permute-done.9.refs_5_ = bf16[192,256]{1,0:T(8,128)(2,1)S(1)} collective-permute-done((bf16[192,256]{1,0:T(8,128)(2,1)S(1)}, bf16[192,256]{1,0:T(8,128)(2,1)S(1)}, u32[]{:S(2)}, u32[]{:S(2)}) %collective-permute-start.9) | collective-permute-done | bytes 98336 | tf_op jit(solution)/shard_map/ppermute | solution.py:355
  15.7 1.2 %collective-permute-start.10 = (bf16[192,256]{1,0:T(8,128)(2,1)S(1)}, bf16[192,256]{1,0:T(8,128)(2,1)S(1)}, u32[]{:S(2)}, u32[]{:S(2)}) collective-permute-start(bf16[192,256]{1,0:T(8,128)(2,1)S(1)} %collective-permute-done.9.refs_5_), channel_id=1, source_target_pairs={{2,6},{6,10},{10,14},{14,12},{12,8},{8,4},{4,0},{0,2},{3,7},{7,11}... | collective-permute-start | bytes 294920 | tf_op jit(solution)/shard_map/ppermute | solution.py:355
  16.9 0.0 collective-permute-done.12.refs_6_
  16.9 0.8 %collective-permute-start.13 = (bf16[192,256]{1,0:T(8,128)(2,1)S(1)}, bf16[192,256]{1,0:T(8,128)(2,1)S(1)}, u32[]{:S(2)}, u32[]{:S(2)}) collective-permute-start(bf16[192,256]{1,0:T(8,128)(2,1)S(1)} %collective-permute-done.12.refs_6_), channel_id=1, source_target_pairs={{6,2},{10,6},{14,10},{12,14},{8,12},{4,8},{0,4},{2,0},{7,3},{11,7}... | collective-permute-start | bytes 294920 | tf_op jit(solution)/shard_map/ppermute | solution.py:356
  17.7 0.7 %collective-permute-done.2.refs_0_ = bf16[192,256]{1,0:T(8,128)(2,1)S(1)} collective-permute-done((bf16[192,256]{1,0:T(8,128)(2,1)S(1)}, bf16[192,256]{1,0:T(8,128)(2,1)S(1)}, u32[]{:S(2)}, u32[]{:S(2)}) %collective-permute-start.2) | collective-permute-done | bytes 98336 | tf_op jit(solution)/shard_map/ppermute | solution.py:352
  18.4 1.0 %collective-permute-start.3 = (bf16[192,256]{1,0:T(8,128)(2,1)S(1)}, bf16[192,256]{1,0:T(8,128)(2,1)S(1)}, u32[]{:S(2)}, u32[]{:S(2)}) collective-permute-start(bf16[192,256]{1,0:T(8,128)(2,1)S(1)} %collective-permute-done.2.refs_0_), channel_id=1, source_target_pairs={{2,6},{6,10},{10,14},{14,12},{12,8},{8,4},{4,0},{0,2},{3,7},{7,11}... | collective-permute-start | bytes 294920 | tf_op jit(solution)/shard_map/ppermute | solution.py:352
  19.4 0.3 %collective-permute-done.6.refs_3_ = bf16[192,256]{1,0:T(8,128)(2,1)S(1)} collective-permute-done((bf16[192,256]{1,0:T(8,128)(2,1)S(1)}, bf16[192,256]{1,0:T(8,128)(2,1)S(1)}, u32[]{:S(2)}, u32[]{:S(2)}) %collective-permute-start.6) | collective-permute-done | bytes 98336 | tf_op jit(solution)/shard_map/ppermute | solution.py:353
  19.7 1.2 %collective-permute-start.7 = (bf16[192,256]{1,0:T(8,128)(2,1)S(1)}, bf16[192,256]{1,0:T(8,128)(2,1)S(1)}, u32[]{:S(2)}, u32[]{:S(2)}) collective-permute-start(bf16[192,256]{1,0:T(8,128)(2,1)S(1)} %collective-permute-done.6.refs_3_), channel_id=1, source_target_pairs={{6,2},{10,6},{14,10},{12,14},{8,12},{4,8},{0,4},{2,0},{7,3},{11,7}... | collective-permute-start | bytes 294920 | tf_op jit(solution)/shard_map/ppermute | solution.py:353
  20.8 1.0 %attend_next.2 = (f32[2048,256]{1,0:T(8,128)S(1)}, f32[2048,128]{1,0:T(8,128)S(1)}) custom-call(bf16[128,2048]{1,0:T(8,128)(2,1)S(1)} %get-tuple-element.17.q_ref, s32[8,128]{1,0:T(8,128)S(1)} %get-tuple-element.18.limits, bf16[192,256]{1,0:T(8,128)(2,1)S(1)} %collective-permute-done.refs_0_, bf16[192,256]{1,0:T(8,128)(2,1)S(1)} %collective-permute-done.8.refs_1_, ...), custom_call_target="tpu_custom_call" | custom-call | flops 1207959552 | bytes 524288 | tf_op jit(solution)/shard_map/attend_next/pallas_call | solution.py:321
  21.9 0.0 collective-permute-done.10.refs_1_
  21.9 0.0 collective-permute-done.13.refs_2_
  21.9 1.2 %attend_next.3 = (f32[2048,256]{1,0:T(8,128)S(1)}, f32[2048,128]{1,0:T(8,128)S(1)}) custom-call(bf16[128,2048]{1,0:T(8,128)(2,1)S(1)} %get-tuple-element.17.q_ref, s32[8,128]{1,0:T(8,128)S(1)} %get-tuple-element.18.limits, bf16[192,256]{1,0:T(8,128)(2,1)S(1)} %collective-permute-done.2.refs_0_, bf16[192,256]{1,0:T(8,128)(2,1)S(1)} %collective-permute-done.10.refs_1_, ...), custom_call_target="tpu_custom_call" | custom-call | flops 603979776 | bytes 524288 | tf_op jit(solution)/shard_map/attend_next/pallas_call | solution.py:321
  23.2 0.0 collective-permute-done.3.refs_0_
  23.2 1.1 %collective-permute-done.7.refs_1_ = bf16[192,256]{1,0:T(8,128)(2,1)S(1)} collective-permute-done((bf16[192,256]{1,0:T(8,128)(2,1)S(1)}, bf16[192,256]{1,0:T(8,128)(2,1)S(1)}, u32[]{:S(2)}, u32[]{:S(2)}) %collective-permute-start.7) | collective-permute-done | bytes 98336 | tf_op jit(solution)/shard_map/ppermute | solution.py:353
  24.3 1.7 %attend_last.1 = bf16[128,2048]{1,0:T(8,128)(2,1)} custom-call(bf16[128,2048]{1,0:T(8,128)(2,1)S(1)} %get-tuple-element.17.q_ref, s32[8,128]{1,0:T(8,128)S(1)} %get-tuple-element.18.limits, bf16[192,256]{1,0:T(8,128)(2,1)S(1)} %collective-permute-done.3.refs_0_, bf16[192,256]{1,0:T(8,128)(2,1)S(1)} %collective-permute-done.7.refs_1_, ...), custom_call_target="tpu_custom_call" | custom-call | flops 402653184 | bytes 524288 | tf_op jit(solution)/shard_map/attend_last/pallas_call | solution.py:321
Async XLA Ops:
  1.2 6.1 %collective-permute-start = (bf16[192,256]{1,0:T(8,128)(2,1)S(1)}, bf16[192,256]{1,0:T(8,128)(2,1)S(1)}, u32[]{:S(2)}, u32[]{:S(2)}) collective-permute-start(bf16[192,256]{1,0:T(8,128)(2,1)S(1)} %get-tuple-element.19.own_keys), channel_id=1, source_target_pairs={{2,6},{6,10},{10,14},{14,12},{12,8},{8,4},{4,0},{0,2},{3,7},{7,11}... | collective-permute-start | bytes 294920 | tf_op jit(solution)/shard_map/ppermute | solution.py:352
  4.2 5.3 %collective-permute-start.4 = (bf16[192,256]{1,0:T(8,128)(2,1)S(1)}, bf16[192,256]{1,0:T(8,128)(2,1)S(1)}, u32[]{:S(2)}, u32[]{:S(2)}) collective-permute-start(bf16[192,256]{1,0:T(8,128)(2,1)S(1)} %get-tuple-element.20.own_values), channel_id=1, source_target_pairs={{6,2},{10,6},{14,10},{12,14},{8,12},{4,8},{0,4},{2,0},{7,3},{11,7}... | collective-permute-start | bytes 294920 | tf_op jit(solution)/shard_map/ppermute | solution.py:353
  4.4 7.2 %collective-permute-start.11 = (bf16[192,256]{1,0:T(8,128)(2,1)S(1)}, bf16[192,256]{1,0:T(8,128)(2,1)S(1)}, u32[]{:S(2)}, u32[]{:S(2)}) collective-permute-start(bf16[192,256]{1,0:T(8,128)(2,1)S(1)} %get-tuple-element.19.own_keys), channel_id=1, source_target_pairs={{6,2},{10,6},{14,10},{12,14},{8,12},{4,8},{0,4},{2,0},{7,3},{11,7}... | collective-permute-start | bytes 294920 | tf_op jit(solution)/shard_map/ppermute | solution.py:356
  6.3 4.8 %collective-permute-start.8 = (bf16[192,256]{1,0:T(8,128)(2,1)S(1)}, bf16[192,256]{1,0:T(8,128)(2,1)S(1)}, u32[]{:S(2)}, u32[]{:S(2)}) collective-permute-start(bf16[192,256]{1,0:T(8,128)(2,1)S(1)} %get-tuple-element.20.own_values), channel_id=1, source_target_pairs={{2,6},{6,10},{10,14},{14,12},{12,8},{8,4},{4,0},{0,2},{3,7},{7,11}... | collective-permute-start | bytes 294920 | tf_op jit(solution)/shard_map/ppermute | solution.py:355
  7.3 5.8 %collective-permute-start.1 = (bf16[192,256]{1,0:T(8,128)(2,1)S(1)}, bf16[192,256]{1,0:T(8,128)(2,1)S(1)}, u32[]{:S(2)}, u32[]{:S(2)}) collective-permute-start(bf16[192,256]{1,0:T(8,128)(2,1)S(1)} %collective-permute-done.refs_0_), channel_id=1, source_target_pairs={{2,6},{6,10},{10,14},{14,12},{12,8},{8,4},{4,0},{0,2},{3,7},{7,11}... | collective-permute-start | bytes 294920 | tf_op jit(solution)/shard_map/ppermute | solution.py:352
  9.5 5.2 %collective-permute-start.5 = (bf16[192,256]{1,0:T(8,128)(2,1)S(1)}, bf16[192,256]{1,0:T(8,128)(2,1)S(1)}, u32[]{:S(2)}, u32[]{:S(2)}) collective-permute-start(bf16[192,256]{1,0:T(8,128)(2,1)S(1)} %collective-permute-done.4.refs_3_), channel_id=1, source_target_pairs={{6,2},{10,6},{14,10},{12,14},{8,12},{4,8},{0,4},{2,0},{7,3},{11,7}... | collective-permute-start | bytes 294920 | tf_op jit(solution)/shard_map/ppermute | solution.py:353
  11.1 4.6 %collective-permute-start.9 = (bf16[192,256]{1,0:T(8,128)(2,1)S(1)}, bf16[192,256]{1,0:T(8,128)(2,1)S(1)}, u32[]{:S(2)}, u32[]{:S(2)}) collective-permute-start(bf16[192,256]{1,0:T(8,128)(2,1)S(1)} %collective-permute-done.8.refs_1_), channel_id=1, source_target_pairs={{2,6},{6,10},{10,14},{14,12},{12,8},{8,4},{4,0},{0,2},{3,7},{7,11}... | collective-permute-start | bytes 294920 | tf_op jit(solution)/shard_map/ppermute | solution.py:355
  11.6 5.3 %collective-permute-start.12 = (bf16[192,256]{1,0:T(8,128)(2,1)S(1)}, bf16[192,256]{1,0:T(8,128)(2,1)S(1)}, u32[]{:S(2)}, u32[]{:S(2)}) collective-permute-start(bf16[192,256]{1,0:T(8,128)(2,1)S(1)} %collective-permute-done.11.refs_2_), channel_id=1, source_target_pairs={{6,2},{10,6},{14,10},{12,14},{8,12},{4,8},{0,4},{2,0},{7,3},{11,7}... | collective-permute-start | bytes 294920 | tf_op jit(solution)/shard_map/ppermute | solution.py:356
  13.1 5.3 %collective-permute-start.2 = (bf16[192,256]{1,0:T(8,128)(2,1)S(1)}, bf16[192,256]{1,0:T(8,128)(2,1)S(1)}, u32[]{:S(2)}, u32[]{:S(2)}) collective-permute-start(bf16[192,256]{1,0:T(8,128)(2,1)S(1)} %collective-permute-done.1.refs_4_), channel_id=1, source_target_pairs={{2,6},{6,10},{10,14},{14,12},{12,8},{8,4},{4,0},{0,2},{3,7},{7,11}... | collective-permute-start | bytes 294920 | tf_op jit(solution)/shard_map/ppermute | solution.py:352
  14.7 5.0 %collective-permute-start.6 = (bf16[192,256]{1,0:T(8,128)(2,1)S(1)}, bf16[192,256]{1,0:T(8,128)(2,1)S(1)}, u32[]{:S(2)}, u32[]{:S(2)}) collective-permute-start(bf16[192,256]{1,0:T(8,128)(2,1)S(1)} %collective-permute-done.5.refs_7_), channel_id=1, source_target_pairs={{6,2},{10,6},{14,10},{12,14},{8,12},{4,8},{0,4},{2,0},{7,3},{11,7}... | collective-permute-start | bytes 294920 | tf_op jit(solution)/shard_map/ppermute | solution.py:353
  15.7 6.2 %collective-permute-start.10 = (bf16[192,256]{1,0:T(8,128)(2,1)S(1)}, bf16[192,256]{1,0:T(8,128)(2,1)S(1)}, u32[]{:S(2)}, u32[]{:S(2)}) collective-permute-start(bf16[192,256]{1,0:T(8,128)(2,1)S(1)} %collective-permute-done.9.refs_5_), channel_id=1, source_target_pairs={{2,6},{6,10},{10,14},{14,12},{12,8},{8,4},{4,0},{0,2},{3,7},{7,11}... | collective-permute-start | bytes 294920 | tf_op jit(solution)/shard_map/ppermute | solution.py:355
  16.9 5.0 %collective-permute-start.13 = (bf16[192,256]{1,0:T(8,128)(2,1)S(1)}, bf16[192,256]{1,0:T(8,128)(2,1)S(1)}, u32[]{:S(2)}, u32[]{:S(2)}) collective-permute-start(bf16[192,256]{1,0:T(8,128)(2,1)S(1)} %collective-permute-done.12.refs_6_), channel_id=1, source_target_pairs={{6,2},{10,6},{14,10},{12,14},{8,12},{4,8},{0,4},{2,0},{7,3},{11,7}... | collective-permute-start | bytes 294920 | tf_op jit(solution)/shard_map/ppermute | solution.py:356
  18.4 4.8 %collective-permute-start.3 = (bf16[192,256]{1,0:T(8,128)(2,1)S(1)}, bf16[192,256]{1,0:T(8,128)(2,1)S(1)}, u32[]{:S(2)}, u32[]{:S(2)}) collective-permute-start(bf16[192,256]{1,0:T(8,128)(2,1)S(1)} %collective-permute-done.2.refs_0_), channel_id=1, source_target_pairs={{2,6},{6,10},{10,14},{14,12},{12,8},{8,4},{4,0},{0,2},{3,7},{7,11}... | collective-permute-start | bytes 294920 | tf_op jit(solution)/shard_map/ppermute | solution.py:352
  19.7 4.6 %collective-permute-start.7 = (bf16[192,256]{1,0:T(8,128)(2,1)S(1)}, bf16[192,256]{1,0:T(8,128)(2,1)S(1)}, u32[]{:S(2)}, u32[]{:S(2)}) collective-permute-start(bf16[192,256]{1,0:T(8,128)(2,1)S(1)} %collective-permute-done.6.refs_3_), channel_id=1, source_target_pairs={{6,2},{10,6},{14,10},{12,14},{8,12},{4,8},{0,4},{2,0},{7,3},{11,7}... | collective-permute-start | bytes 294920 | tf_op jit(solution)/shard_map/ppermute | solution.py:353

commit v12 on v11

--- a/solution.py
+++ b/solution.py
@@ -11,7 +11,8 @@
 HD = 128
 EXP_SCALE = HD**-0.5 * math.log2(math.e)
 HIDDEN = -1.0e30
-CHUNK_HEADS = 4
+CHUNK_HEADS = 8
+LAST_CHUNK_HEADS = 4
 LARGEST_TOTAL = 2.0**100
 
 
@@ -52,11 +53,11 @@
     pairs = [
         (valid_hbm, valid_ref),
         (first_hbm, first_ref),
+        (q_hbm, q_ref),
         (win_keys, keys.at[:window_rows]),
         (cache_keys, keys.at[window_rows:]),
         (win_values, values.at[:window_rows]),
         (cache_values, values.at[window_rows:]),
-        (q_hbm, q_ref),
     ]
     copies = [pltpu.make_async_copy(*pair, sems.at[index]) for index, pair in enumerate(pairs)]
     for copy in copies:
@@ -163,16 +164,16 @@
     return (acc[:, :HD] * (inverse * (2.0 - total * inverse))).astype(jnp.bfloat16)
 
 
-def chunks(q_ref, kv_heads):
+def chunks(q_ref, kv_heads, size):
     rows = q_ref.shape[0]
     group = q_ref.shape[1] // HD // kv_heads
     for head in range(kv_heads):
-        for start in range(0, group, CHUNK_HEADS):
+        for start in range(0, group, size):
             base = head * group + start
             query = jnp.concatenate(
-                [q_ref[:, (base + i) * HD : (base + i + 1) * HD] for i in range(CHUNK_HEADS)], axis=0
+                [q_ref[:, (base + i) * HD : (base + i + 1) * HD] for i in range(size)], axis=0
             )
-            yield head, slice(base * rows, (base + CHUNK_HEADS) * rows), query, base
+            yield head, slice(base * rows, (base + size) * rows), query, base
 
 
 def first_kernel(count, sizes, q_ref, limits, own_keys, own_values, acc_out, top_out, keys, values):
@@ -185,7 +186,7 @@
     query_iota = lax.broadcasted_iota(jnp.int32, (rows, window_rows), 0)
     seen = (key_iota <= query_iota) & (key_iota < limits[count - 1 : count, :])
     bias = jnp.concatenate([jnp.where(seen, 0.0, HIDDEN)] * CHUNK_HEADS, axis=0)
-    for head, at, query, _ in chunks(q_ref, keys.shape[0]):
+    for head, at, query, _ in chunks(q_ref, keys.shape[0], CHUNK_HEADS):
         score = scores(query, keys[head])
         score = jnp.concatenate([score[:, :window_rows] + bias, score[:, window_rows:]], axis=1)
         top = wide_top(score)
@@ -202,20 +203,21 @@
         acc_in, top_in, acc_out, top_out, keys, values = refs[2 * number :]
     rows, heads = q_ref.shape[0], q_ref.shape[1] // HD
     kv_heads = keys.shape[0]
+    size = LAST_CHUNK_HEADS if last else CHUNK_HEADS
 
     def sent(base):
-        lanes = slice(base * HD, (base + CHUNK_HEADS) * HD)
-        return pltpu.make_async_copy(result.at[:, lanes], out.at[:, lanes], sems.at[base // CHUNK_HEADS])
+        lanes = slice(base * HD, (base + size) * HD)
+        return pltpu.make_async_copy(result.at[:, lanes], out.at[:, lanes], sems.at[base // size])
 
     def settle(base, acc):
         done = normalised(acc)
-        for i in range(CHUNK_HEADS):
+        for i in range(size):
             result[:, (base + i) * HD : (base + i + 1) * HD] = done[i * rows : (i + 1) * rows]
         sent(base).start()
 
     def take_in(begin):
         fine = jnp.ones((8, HD), jnp.float32)
-        for head, at, query, base in chunks(q_ref, kv_heads):
+        for head, at, query, base in chunks(q_ref, kv_heads, size):
             top = top_in[at, :]
             acc = acc_in[at, :] + weigh(scores(query, keys[head, begin:]), top, values[head, begin:])
             safe = jnp.where(acc[:, HD:] < LARGEST_TOTAL, 1.0, 0.0).reshape(-1, 8, HD)
@@ -226,12 +228,12 @@
                 acc_out[at, :] = acc
                 top_out[at, :] = top
         if last:
-            for base in range(0, heads, CHUNK_HEADS):
+            for base in range(0, heads, size):
                 sent(base).wait()
 
         @pl.when(jnp.min(fine) < 0.5)
         def _():
-            for head, at, query, base in chunks(q_ref, kv_heads):
+            for head, at, query, base in chunks(q_ref, kv_heads, size):
                 score = scores(query, keys[head, begin:])
                 before = top_in[at, :]
                 top = jnp.maximum(before, wide_top(score))
@@ -316,7 +318,7 @@
     shapes = [jax.ShapeDtypeStruct(queries.shape, queries.dtype)] if last else state_shapes(queries)
     scratch = room(kv_heads, total_keys)
     if last:
-        chunk_count = queries.shape[1] // HD // CHUNK_HEADS
+        chunk_count = queries.shape[1] // HD // LAST_CHUNK_HEADS
         scratch += [pltpu.VMEM(queries.shape, queries.dtype), pltpu.SemaphoreType.DMA((chunk_count,))]
     outs = pl.pallas_call(
         functools.partial(next_kernel, rows_of, last, count, sizes),

time: 26.3 us -> 26.2 us (level)
  no operation moved by 1% of the time
where the time goes in v12:
time: 26.2 us; the launch traced here: 26.1 us
  starting transfers between devices  16 us (61%)
  Pallas kernels  5.95 us (23%)
  waiting for transfers between devices  3.89 us (15%)
    ppermute x4, starting transfers between devices, shards(): key_on = lax.ppermute(key_on, 'ctx', onward)  7.71 us
    ppermute x3, starting transfers between devices, shards(): key_back = lax.ppermute(key_back, 'ctx', backward)  4.37 us
    pallas_call x3, Pallas kernels, attend_next(): pl.pallas_call(functools.partial(next_kernel, rows_of, last, count, sizes...  3.91 us
    ppermute x4, starting transfers between devices, shards(): value_back = lax.ppermute(value_back, 'ctx', backward)  2.19 us
    ppermute x3, starting transfers between devices, shards(): value_on = lax.ppermute(value_on, 'ctx', onward)  1.71 us
    ppermute x3, waiting for transfers between devices, shards(): value_on = lax.ppermute(value_on, 'ctx', onward)  1.68 us
    ppermute x4, waiting for transfers between devices, shards(): value_back = lax.ppermute(value_back, 'ctx', backward)  1.53 us
    pallas_call x1, Pallas kernels, load(): pl.pallas_call(functools.partial(load_kernel, count), out_shape=[jax.Shap...  1.11 us
  transfers between devices with their start and end apart: 14, of which 5 were waited for; matrix products, arithmetic and copies ran while one was open for 0% of the time, Pallas kernels for 12%

profile of v12, /device:TPU:0, one launch (start us, length us, event | category | flops | bytes accessed | tf_op | source)
XLA Modules:
  0.0 26.1 jit_solution(4119130000981484608)
XLA Ops:
  0.0 1.1 %load.1 = (bf16[192,256]{1,0:T(8,128)(2,1)S(1)}, bf16[192,256]{1,0:T(8,128)(2,1)S(1)}, bf16[128,2048]{1,0:T(8,128)(2,1)S(1)}, s32[8,128]{1,0:T(8,128)S(1)}) custom-call(bf16[128,256]{1,0:T(8,128)(2,1)} %win_keys.1, bf16[128,256]{1,0:T(8,128)(2,1)} %win_values.1, bf16[64,256]{1,0:T(8,128)(2,1)} %cache_keys.1, bf16[64,256]{1,0:T(8,128)(2,1)} %cache_values.1, ...), custom_call_target="tpu_custom_call" | custom-call | bytes 393216 | tf_op jit(solution)/shard_map/load/pallas_call | solution.py:81
  1.1 3.0 %collective-permute-start = (bf16[192,256]{1,0:T(8,128)(2,1)S(1)}, bf16[192,256]{1,0:T(8,128)(2,1)S(1)}, u32[]{:S(2)}, u32[]{:S(2)}) collective-permute-start(bf16[192,256]{1,0:T(8,128)(2,1)S(1)} %get-tuple-element.19.own_keys), channel_id=1, source_target_pairs={{2,6},{6,10},{10,14},{14,12},{12,8},{8,4},{4,0},{0,2},{3,7},{7,11}... | collective-permute-start | bytes 294920 | tf_op jit(solution)/shard_map/ppermute | solution.py:354
  4.1 0.2 collective-permute-start.4
  4.3 2.0 %collective-permute-start.11 = (bf16[192,256]{1,0:T(8,128)(2,1)S(1)}, bf16[192,256]{1,0:T(8,128)(2,1)S(1)}, u32[]{:S(2)}, u32[]{:S(2)}) collective-permute-start(bf16[192,256]{1,0:T(8,128)(2,1)S(1)} %get-tuple-element.19.own_keys), channel_id=1, source_target_pairs={{6,2},{10,6},{14,10},{12,14},{8,12},{4,8},{0,4},{2,0},{7,3},{11,7}... | collective-permute-start | bytes 294920 | tf_op jit(solution)/shard_map/ppermute | solution.py:358
  6.2 0.1 collective-permute-start.8
  6.3 0.9 %attend_first.1 = (f32[2048,256]{1,0:T(8,128)S(1)}, f32[2048,128]{1,0:T(8,128)S(1)}) custom-call(bf16[128,2048]{1,0:T(8,128)(2,1)S(1)} %get-tuple-element.17.q_ref, s32[8,128]{1,0:T(8,128)S(1)} %get-tuple-element.18.limits, bf16[192,256]{1,0:T(8,128)(2,1)S(1)} %get-tuple-element.19.own_keys, bf16[192,256]{1,0:T(8,128)(2,1)S(1)} %get-tuple-element.20.own_values), custom_call_target="tpu_custom_call" | custom-call | flops 402653184 | bytes 524288 | tf_op jit(solution)/shard_map/attend_first/pallas_call | solution.py:299
  7.2 0.0 collective-permute-done.refs_0_
  7.2 2.1 %collective-permute-start.1 = (bf16[192,256]{1,0:T(8,128)(2,1)S(1)}, bf16[192,256]{1,0:T(8,128)(2,1)S(1)}, u32[]{:S(2)}, u32[]{:S(2)}) collective-permute-start(bf16[192,256]{1,0:T(8,128)(2,1)S(1)} %collective-permute-done.refs_0_), channel_id=1, source_target_pairs={{2,6},{6,10},{10,14},{14,12},{12,8},{8,4},{4,0},{0,2},{3,7},{7,11}... | collective-permute-start | bytes 294920 | tf_op jit(solution)/shard_map/ppermute | solution.py:354
  9.4 0.0 collective-permute-done.4.refs_3_
  9.4 0.2 collective-permute-start.5
  9.7 1.3 %collective-permute-done.8.refs_1_ = bf16[192,256]{1,0:T(8,128)(2,1)S(1)} collective-permute-done((bf16[192,256]{1,0:T(8,128)(2,1)S(1)}, bf16[192,256]{1,0:T(8,128)(2,1)S(1)}, u32[]{:S(2)}, u32[]{:S(2)}) %collective-permute-start.8) | collective-permute-done | bytes 98336 | tf_op jit(solution)/shard_map/ppermute | solution.py:357
  11.0 0.5 %collective-permute-start.9 = (bf16[192,256]{1,0:T(8,128)(2,1)S(1)}, bf16[192,256]{1,0:T(8,128)(2,1)S(1)}, u32[]{:S(2)}, u32[]{:S(2)}) collective-permute-start(bf16[192,256]{1,0:T(8,128)(2,1)S(1)} %collective-permute-done.8.refs_1_), channel_id=1, source_target_pairs={{2,6},{6,10},{10,14},{14,12},{12,8},{8,4},{4,0},{0,2},{3,7},{7,11}... | collective-permute-start | bytes 294920 | tf_op jit(solution)/shard_map/ppermute | solution.py:357
  11.4 0.0 collective-permute-done.11.refs_2_
  11.5 1.6 %collective-permute-start.12 = (bf16[192,256]{1,0:T(8,128)(2,1)S(1)}, bf16[192,256]{1,0:T(8,128)(2,1)S(1)}, u32[]{:S(2)}, u32[]{:S(2)}) collective-permute-start(bf16[192,256]{1,0:T(8,128)(2,1)S(1)} %collective-permute-done.11.refs_2_), channel_id=1, source_target_pairs={{6,2},{10,6},{14,10},{12,14},{8,12},{4,8},{0,4},{2,0},{7,3},{11,7}... | collective-permute-start | bytes 294920 | tf_op jit(solution)/shard_map/ppermute | solution.py:358
  13.0 0.0 collective-permute-done.1.refs_4_
  13.0 1.6 %collective-permute-start.2 = (bf16[192,256]{1,0:T(8,128)(2,1)S(1)}, bf16[192,256]{1,0:T(8,128)(2,1)S(1)}, u32[]{:S(2)}, u32[]{:S(2)}) collective-permute-start(bf16[192,256]{1,0:T(8,128)(2,1)S(1)} %collective-permute-done.1.refs_4_), channel_id=1, source_target_pairs={{2,6},{6,10},{10,14},{14,12},{12,8},{8,4},{4,0},{0,2},{3,7},{7,11}... | collective-permute-start | bytes 294920 | tf_op jit(solution)/shard_map/ppermute | solution.py:354
  14.6 0.0 collective-permute-done.5.refs_7_
  14.6 0.6 %collective-permute-start.6 = (bf16[192,256]{1,0:T(8,128)(2,1)S(1)}, bf16[192,256]{1,0:T(8,128)(2,1)S(1)}, u32[]{:S(2)}, u32[]{:S(2)}) collective-permute-start(bf16[192,256]{1,0:T(8,128)(2,1)S(1)} %collective-permute-done.5.refs_7_), channel_id=1, source_target_pairs={{6,2},{10,6},{14,10},{12,14},{8,12},{4,8},{0,4},{2,0},{7,3},{11,7}... | collective-permute-start | bytes 294920 | tf_op jit(solution)/shard_map/ppermute | solution.py:355
  15.2 0.4 %collective-permute-done.9.refs_5_ = bf16[192,256]{1,0:T(8,128)(2,1)S(1)} collective-permute-done((bf16[192,256]{1,0:T(8,128)(2,1)S(1)}, bf16[192,256]{1,0:T(8,128)(2,1)S(1)}, u32[]{:S(2)}, u32[]{:S(2)}) %collective-permute-start.9) | collective-permute-done | bytes 98336 | tf_op jit(solution)/shard_map/ppermute | solution.py:357
  15.6 1.2 %collective-permute-start.10 = (bf16[192,256]{1,0:T(8,128)(2,1)S(1)}, bf16[192,256]{1,0:T(8,128)(2,1)S(1)}, u32[]{:S(2)}, u32[]{:S(2)}) collective-permute-start(bf16[192,256]{1,0:T(8,128)(2,1)S(1)} %collective-permute-done.9.refs_5_), channel_id=1, source_target_pairs={{2,6},{6,10},{10,14},{14,12},{12,8},{8,4},{4,0},{0,2},{3,7},{7,11}... | collective-permute-start | bytes 294920 | tf_op jit(solution)/shard_map/ppermute | solution.py:357
  16.8 0.0 collective-permute-done.12.refs_6_
  16.8 0.8 %collective-permute-start.13 = (bf16[192,256]{1,0:T(8,128)(2,1)S(1)}, bf16[192,256]{1,0:T(8,128)(2,1)S(1)}, u32[]{:S(2)}, u32[]{:S(2)}) collective-permute-start(bf16[192,256]{1,0:T(8,128)(2,1)S(1)} %collective-permute-done.12.refs_6_), channel_id=1, source_target_pairs={{6,2},{10,6},{14,10},{12,14},{8,12},{4,8},{0,4},{2,0},{7,3},{11,7}... | collective-permute-start | bytes 294920 | tf_op jit(solution)/shard_map/ppermute | solution.py:358
  17.6 0.7 %collective-permute-done.2.refs_0_ = bf16[192,256]{1,0:T(8,128)(2,1)S(1)} collective-permute-done((bf16[192,256]{1,0:T(8,128)(2,1)S(1)}, bf16[192,256]{1,0:T(8,128)(2,1)S(1)}, u32[]{:S(2)}, u32[]{:S(2)}) %collective-permute-start.2) | collective-permute-done | bytes 98336 | tf_op jit(solution)/shard_map/ppermute | solution.py:354
  18.3 1.0 %collective-permute-start.3 = (bf16[192,256]{1,0:T(8,128)(2,1)S(1)}, bf16[192,256]{1,0:T(8,128)(2,1)S(1)}, u32[]{:S(2)}, u32[]{:S(2)}) collective-permute-start(bf16[192,256]{1,0:T(8,128)(2,1)S(1)} %collective-permute-done.2.refs_0_), channel_id=1, source_target_pairs={{2,6},{6,10},{10,14},{14,12},{12,8},{8,4},{4,0},{0,2},{3,7},{7,11}... | collective-permute-start | bytes 294920 | tf_op jit(solution)/shard_map/ppermute | solution.py:354
  19.3 0.3 %collective-permute-done.6.refs_3_ = bf16[192,256]{1,0:T(8,128)(2,1)S(1)} collective-permute-done((bf16[192,256]{1,0:T(8,128)(2,1)S(1)}, bf16[192,256]{1,0:T(8,128)(2,1)S(1)}, u32[]{:S(2)}, u32[]{:S(2)}) %collective-permute-start.6) | collective-permute-done | bytes 98336 | tf_op jit(solution)/shard_map/ppermute | solution.py:355
  19.6 1.2 %collective-permute-start.7 = (bf16[192,256]{1,0:T(8,128)(2,1)S(1)}, bf16[192,256]{1,0:T(8,128)(2,1)S(1)}, u32[]{:S(2)}, u32[]{:S(2)}) collective-permute-start(bf16[192,256]{1,0:T(8,128)(2,1)S(1)} %collective-permute-done.6.refs_3_), channel_id=1, source_target_pairs={{6,2},{10,6},{14,10},{12,14},{8,12},{4,8},{0,4},{2,0},{7,3},{11,7}... | collective-permute-start | bytes 294920 | tf_op jit(solution)/shard_map/ppermute | solution.py:355
  20.7 1.0 %attend_next.2 = (f32[2048,256]{1,0:T(8,128)S(1)}, f32[2048,128]{1,0:T(8,128)S(1)}) custom-call(bf16[128,2048]{1,0:T(8,128)(2,1)S(1)} %get-tuple-element.17.q_ref, s32[8,128]{1,0:T(8,128)S(1)} %get-tuple-element.18.limits, bf16[192,256]{1,0:T(8,128)(2,1)S(1)} %collective-permute-done.refs_0_, bf16[192,256]{1,0:T(8,128)(2,1)S(1)} %collective-permute-done.8.refs_1_, ...), custom_call_target="tpu_custom_call" | custom-call | flops 1207959552 | bytes 524288 | tf_op jit(solution)/shard_map/attend_next/pallas_call | solution.py:323
  21.8 0.0 collective-permute-done.10.refs_1_
  21.8 0.0 collective-permute-done.13.refs_2_
  21.8 1.2 %attend_next.3 = (f32[2048,256]{1,0:T(8,128)S(1)}, f32[2048,128]{1,0:T(8,128)S(1)}) custom-call(bf16[128,2048]{1,0:T(8,128)(2,1)S(1)} %get-tuple-element.17.q_ref, s32[8,128]{1,0:T(8,128)S(1)} %get-tuple-element.18.limits, bf16[192,256]{1,0:T(8,128)(2,1)S(1)} %collective-permute-done.2.refs_0_, bf16[192,256]{1,0:T(8,128)(2,1)S(1)} %collective-permute-done.10.refs_1_, ...), custom_call_target="tpu_custom_call" | custom-call | flops 603979776 | bytes 524288 | tf_op jit(solution)/shard_map/attend_next/pallas_call | solution.py:323
  23.0 0.0 collective-permute-done.3.refs_0_
  23.0 1.2 %collective-permute-done.7.refs_1_ = bf16[192,256]{1,0:T(8,128)(2,1)S(1)} collective-permute-done((bf16[192,256]{1,0:T(8,128)(2,1)S(1)}, bf16[192,256]{1,0:T(8,128)(2,1)S(1)}, u32[]{:S(2)}, u32[]{:S(2)}) %collective-permute-start.7) | collective-permute-done | bytes 98336 | tf_op jit(solution)/shard_map/ppermute | solution.py:355
  24.2 1.7 %attend_last.1 = bf16[128,2048]{1,0:T(8,128)(2,1)} custom-call(bf16[128,2048]{1,0:T(8,128)(2,1)S(1)} %get-tuple-element.17.q_ref, s32[8,128]{1,0:T(8,128)S(1)} %get-tuple-element.18.limits, bf16[192,256]{1,0:T(8,128)(2,1)S(1)} %collective-permute-done.3.refs_0_, bf16[192,256]{1,0:T(8,128)(2,1)S(1)} %collective-permute-done.7.refs_1_, ...), custom_call_target="tpu_custom_call" | custom-call | flops 402653184 | bytes 524288 | tf_op jit(solution)/shard_map/attend_last/pallas_call | solution.py:323
Async XLA Ops:
  1.1 6.1 %collective-permute-start = (bf16[192,256]{1,0:T(8,128)(2,1)S(1)}, bf16[192,256]{1,0:T(8,128)(2,1)S(1)}, u32[]{:S(2)}, u32[]{:S(2)}) collective-permute-start(bf16[192,256]{1,0:T(8,128)(2,1)S(1)} %get-tuple-element.19.own_keys), channel_id=1, source_target_pairs={{2,6},{6,10},{10,14},{14,12},{12,8},{8,4},{4,0},{0,2},{3,7},{7,11}... | collective-permute-start | bytes 294920 | tf_op jit(solution)/shard_map/ppermute | solution.py:354
  4.1 5.3 %collective-permute-start.4 = (bf16[192,256]{1,0:T(8,128)(2,1)S(1)}, bf16[192,256]{1,0:T(8,128)(2,1)S(1)}, u32[]{:S(2)}, u32[]{:S(2)}) collective-permute-start(bf16[192,256]{1,0:T(8,128)(2,1)S(1)} %get-tuple-element.20.own_values), channel_id=1, source_target_pairs={{6,2},{10,6},{14,10},{12,14},{8,12},{4,8},{0,4},{2,0},{7,3},{11,7}... | collective-permute-start | bytes 294920 | tf_op jit(solution)/shard_map/ppermute | solution.py:355
  4.3 7.2 %collective-permute-start.11 = (bf16[192,256]{1,0:T(8,128)(2,1)S(1)}, bf16[192,256]{1,0:T(8,128)(2,1)S(1)}, u32[]{:S(2)}, u32[]{:S(2)}) collective-permute-start(bf16[192,256]{1,0:T(8,128)(2,1)S(1)} %get-tuple-element.19.own_keys), channel_id=1, source_target_pairs={{6,2},{10,6},{14,10},{12,14},{8,12},{4,8},{0,4},{2,0},{7,3},{11,7}... | collective-permute-start | bytes 294920 | tf_op jit(solution)/shard_map/ppermute | solution.py:358
  6.2 4.8 %collective-permute-start.8 = (bf16[192,256]{1,0:T(8,128)(2,1)S(1)}, bf16[192,256]{1,0:T(8,128)(2,1)S(1)}, u32[]{:S(2)}, u32[]{:S(2)}) collective-permute-start(bf16[192,256]{1,0:T(8,128)(2,1)S(1)} %get-tuple-element.20.own_values), channel_id=1, source_target_pairs={{2,6},{6,10},{10,14},{14,12},{12,8},{8,4},{4,0},{0,2},{3,7},{7,11}... | collective-permute-start | bytes 294920 | tf_op jit(solution)/shard_map/ppermute | solution.py:357
  7.2 5.8 %collective-permute-start.1 = (bf16[192,256]{1,0:T(8,128)(2,1)S(1)}, bf16[192,256]{1,0:T(8,128)(2,1)S(1)}, u32[]{:S(2)}, u32[]{:S(2)}) collective-permute-start(bf16[192,256]{1,0:T(8,128)(2,1)S(1)} %collective-permute-done.refs_0_), channel_id=1, source_target_pairs={{2,6},{6,10},{10,14},{14,12},{12,8},{8,4},{4,0},{0,2},{3,7},{7,11}... | collective-permute-start | bytes 294920 | tf_op jit(solution)/shard_map/ppermute | solution.py:354
  9.4 5.2 %collective-permute-start.5 = (bf16[192,256]{1,0:T(8,128)(2,1)S(1)}, bf16[192,256]{1,0:T(8,128)(2,1)S(1)}, u32[]{:S(2)}, u32[]{:S(2)}) collective-permute-start(bf16[192,256]{1,0:T(8,128)(2,1)S(1)} %collective-permute-done.4.refs_3_), channel_id=1, source_target_pairs={{6,2},{10,6},{14,10},{12,14},{8,12},{4,8},{0,4},{2,0},{7,3},{11,7}... | collective-permute-start | bytes 294920 | tf_op jit(solution)/shard_map/ppermute | solution.py:355
  11.0 4.6 %collective-permute-start.9 = (bf16[192,256]{1,0:T(8,128)(2,1)S(1)}, bf16[192,256]{1,0:T(8,128)(2,1)S(1)}, u32[]{:S(2)}, u32[]{:S(2)}) collective-permute-start(bf16[192,256]{1,0:T(8,128)(2,1)S(1)} %collective-permute-done.8.refs_1_), channel_id=1, source_target_pairs={{2,6},{6,10},{10,14},{14,12},{12,8},{8,4},{4,0},{0,2},{3,7},{7,11}... | collective-permute-start | bytes 294920 | tf_op jit(solution)/shard_map/ppermute | solution.py:357
  11.5 5.3 %collective-permute-start.12 = (bf16[192,256]{1,0:T(8,128)(2,1)S(1)}, bf16[192,256]{1,0:T(8,128)(2,1)S(1)}, u32[]{:S(2)}, u32[]{:S(2)}) collective-permute-start(bf16[192,256]{1,0:T(8,128)(2,1)S(1)} %collective-permute-done.11.refs_2_), channel_id=1, source_target_pairs={{6,2},{10,6},{14,10},{12,14},{8,12},{4,8},{0,4},{2,0},{7,3},{11,7}... | collective-permute-start | bytes 294920 | tf_op jit(solution)/shard_map/ppermute | solution.py:358
  13.0 5.3 %collective-permute-start.2 = (bf16[192,256]{1,0:T(8,128)(2,1)S(1)}, bf16[192,256]{1,0:T(8,128)(2,1)S(1)}, u32[]{:S(2)}, u32[]{:S(2)}) collective-permute-start(bf16[192,256]{1,0:T(8,128)(2,1)S(1)} %collective-permute-done.1.refs_4_), channel_id=1, source_target_pairs={{2,6},{6,10},{10,14},{14,12},{12,8},{8,4},{4,0},{0,2},{3,7},{7,11}... | collective-permute-start | bytes 294920 | tf_op jit(solution)/shard_map/ppermute | solution.py:354
  14.6 5.0 %collective-permute-start.6 = (bf16[192,256]{1,0:T(8,128)(2,1)S(1)}, bf16[192,256]{1,0:T(8,128)(2,1)S(1)}, u32[]{:S(2)}, u32[]{:S(2)}) collective-permute-start(bf16[192,256]{1,0:T(8,128)(2,1)S(1)} %collective-permute-done.5.refs_7_), channel_id=1, source_target_pairs={{6,2},{10,6},{14,10},{12,14},{8,12},{4,8},{0,4},{2,0},{7,3},{11,7}... | collective-permute-start | bytes 294920 | tf_op jit(solution)/shard_map/ppermute | solution.py:355
  15.6 6.2 %collective-permute-start.10 = (bf16[192,256]{1,0:T(8,128)(2,1)S(1)}, bf16[192,256]{1,0:T(8,128)(2,1)S(1)}, u32[]{:S(2)}, u32[]{:S(2)}) collective-permute-start(bf16[192,256]{1,0:T(8,128)(2,1)S(1)} %collective-permute-done.9.refs_5_), channel_id=1, source_target_pairs={{2,6},{6,10},{10,14},{14,12},{12,8},{8,4},{4,0},{0,2},{3,7},{7,11}... | collective-permute-start | bytes 294920 | tf_op jit(solution)/shard_map/ppermute | solution.py:357
  16.8 5.0 %collective-permute-start.13 = (bf16[192,256]{1,0:T(8,128)(2,1)S(1)}, bf16[192,256]{1,0:T(8,128)(2,1)S(1)}, u32[]{:S(2)}, u32[]{:S(2)}) collective-permute-start(bf16[192,256]{1,0:T(8,128)(2,1)S(1)} %collective-permute-done.12.refs_6_), channel_id=1, source_target_pairs={{6,2},{10,6},{14,10},{12,14},{8,12},{4,8},{0,4},{2,0},{7,3},{11,7}... | collective-permute-start | bytes 294920 | tf_op jit(solution)/shard_map/ppermute | solution.py:358
  18.3 4.7 %collective-permute-start.3 = (bf16[192,256]{1,0:T(8,128)(2,1)S(1)}, bf16[192,256]{1,0:T(8,128)(2,1)S(1)}, u32[]{:S(2)}, u32[]{:S(2)}) collective-permute-start(bf16[192,256]{1,0:T(8,128)(2,1)S(1)} %collective-permute-done.2.refs_0_), channel_id=1, source_target_pairs={{2,6},{6,10},{10,14},{14,12},{12,8},{8,4},{4,0},{0,2},{3,7},{7,11}... | collective-permute-start | bytes 294920 | tf_op jit(solution)/shard_map/ppermute | solution.py:354
  19.6 4.6 %collective-permute-start.7 = (bf16[192,256]{1,0:T(8,128)(2,1)S(1)}, bf16[192,256]{1,0:T(8,128)(2,1)S(1)}, u32[]{:S(2)}, u32[]{:S(2)}) collective-permute-start(bf16[192,256]{1,0:T(8,128)(2,1)S(1)} %collective-permute-done.6.refs_3_), channel_id=1, source_target_pairs={{6,2},{10,6},{14,10},{12,14},{8,12},{4,8},{0,4},{2,0},{7,3},{11,7}... | collective-permute-start | bytes 294920 | tf_op jit(solution)/shard_map/ppermute | solution.py:355

commit v13 on v12

--- a/solution.py
+++ b/solution.py
@@ -47,8 +47,12 @@
     return jnp.where(column == 0, rows * (width - 1) + rows - 1 - row, snake)
 
 
+def turn():
+    return 1 - 2 * lax.rem(lax.axis_index("tp"), 2)
+
+
 def load_kernel(count, win_keys, win_values, cache_keys, cache_values, q_hbm, valid_hbm, first_hbm, *refs):
-    keys, values, q_ref, limits, valid_ref, first_ref, sems = refs
+    keys, values, q_ref, limits, acc_out, top_out, key_room, value_room, valid_ref, first_ref, sems = refs
     window_rows = win_keys.shape[0]
     pairs = [
         (valid_hbm, valid_ref),
@@ -68,12 +72,17 @@
     position = position_of(me, count)
     first = first_ref[me]
     for row, offset in enumerate(ring_offsets(count)):
-        place = place_at(lax.rem(position + offset + count, count), count)
+        place = place_at(lax.rem(position + turn() * offset + count, count), count)
         limit = jnp.where((place >= first) & (place <= me), valid_ref[place], 0)
         limits[row : row + 1, :] = jnp.full((1, HD), limit, jnp.int32)
     limits[count - 1 : count, :] = jnp.full((1, HD), valid_ref[me], jnp.int32)
     for copy in copies[2:]:
         copy.wait()
+
+    @pl.when(turn() < 0)
+    def _():
+        sizes = (window_rows, cache_keys.shape[0])
+        take_own(count, sizes, q_ref, limits, keys, values, acc_out, top_out, key_room, value_room)
 
 
 def load(count, win_keys, win_values, cache_keys, cache_values, queries, valid_counts, first_block):
@@ -85,15 +94,17 @@
             jax.ShapeDtypeStruct((rows, width), win_keys.dtype),
             jax.ShapeDtypeStruct(queries.shape, queries.dtype),
             jax.ShapeDtypeStruct((-(-count // 8) * 8, HD), jnp.int32),
+            *state_shapes(queries),
         ],
         in_specs=[pl.BlockSpec(memory_space=pltpu.HBM)] * 7,
-        out_specs=[pl.BlockSpec(memory_space=pltpu.VMEM)] * 4,
+        out_specs=[pl.BlockSpec(memory_space=pltpu.VMEM)] * 6,
         scratch_shapes=[
+            *room(width // HD, -(-rows // HD) * HD),
             pltpu.SMEM(valid_counts.shape, jnp.int32),
             pltpu.SMEM(first_block.shape, jnp.int32),
             pltpu.SemaphoreType.DMA((7,)),
         ],
-        compiler_params=pltpu.CompilerParams(vmem_limit_bytes=4 * 1024 * 1024),
+        compiler_params=pltpu.CompilerParams(vmem_limit_bytes=24 * 1024 * 1024),
         cost_estimate=pl.CostEstimate(flops=0, bytes_accessed=8 * rows * width, transcendentals=0),
         name="load",
     )(win_keys, win_values, cache_keys, cache_values, queries, valid_counts, first_block)
@@ -176,7 +187,7 @@
             yield head, slice(base * rows, (base + size) * rows), query, base
 
 
-def first_kernel(count, sizes, q_ref, limits, own_keys, own_values, acc_out, top_out, keys, values):
+def take_own(count, sizes, q_ref, limits, own_keys, own_values, acc_out, top_out, keys, values):
     window_rows = sizes[0]
     place_window(0, 0, True, sizes, None, own_keys, own_values, keys, values)
     place_cache(0, 1, sizes, own_keys, own_values, keys, values)
@@ -194,6 +205,17 @@
         top_out[at, :] = top
 
 
+def first_kernel(count, sizes, q_ref, limits, own_keys, own_values, acc_in, top_in, acc_out, top_out, keys, values):
+    @pl.when(turn() > 0)
+    def _():
+        take_own(count, sizes, q_ref, limits, own_keys, own_values, acc_out, top_out, keys, values)
+
+    @pl.when(turn() < 0)
+    def _():
+        acc_out[...] = acc_in[...]
+        top_out[...] = top_in[...]
+
+
 def next_kernel(rows_of, last, count, sizes, q_ref, limits, *refs):
     number = len(rows_of)
     key_refs, value_refs = refs[: 2 * number : 2], refs[1 : 2 * number : 2]
@@ -253,7 +275,7 @@
     me = lax.axis_index("ctx")
     position = position_of(me, count)
     offsets = ring_offsets(count)
-    places = [place_at(lax.rem(position + offsets[row] + count, count), count) for row in rows_of]
+    places = [place_at(lax.rem(position + turn() * offsets[row] + count, count), count) for row in rows_of]
     earlier = functools.reduce(jnp.logical_or, [place < me for place in places])
 
     @pl.when(earlier)
@@ -291,7 +313,7 @@
     return [jax.ShapeDtypeStruct((rows, 2 * HD), jnp.float32), jax.ShapeDtypeStruct((rows, HD), jnp.float32)]
 
 
-def attend_first(count, sizes, queries, limits, own_keys, own_values):
+def attend_first(count, sizes, queries, limits, own_keys, own_values, state):
     kv_heads = own_keys.shape[1] // HD
     total_keys = -(-sum(sizes) // HD) * HD
     vmem = pl.BlockSpec(memory_space=pltpu.VMEM)
@@ -299,12 +321,12 @@
         pl.pallas_call(
             functools.partial(first_kernel, count, sizes),
             out_shape=state_shapes(queries),
-            in_specs=[vmem] * 4,
+            in_specs=[vmem] * 6,
             out_specs=[vmem] * 2,
             scratch_shapes=room(kv_heads, total_keys),
             name="attend_first",
             **kernel_options(queries, total_keys, kv_heads),
-        )(queries, limits, own_keys, own_values)
+        )(queries, limits, own_keys, own_values, *state)
     )
 
 
@@ -332,30 +354,38 @@
     return outs[0] if last else tuple(outs)
 
 
-def shards(count, queries, win_keys, win_values, cache_keys, cache_values, valid_counts, first_block):
+def ring_pairs(count, cores, step):
+    ring = [place_at(p, count) for p in range(count)]
+    pairs = []
+    for core in range(cores):
+        way = -step if core % 2 else step
+        pairs += [(ring[p] * cores + core, ring[(p + way) % count] * cores + core) for p in range(count)]
+    return pairs
+
+
+def shards(count, cores, queries, win_keys, win_values, cache_keys, cache_values, valid_counts, first_block):
     sizes = (win_keys.shape[0], cache_keys.shape[0])
     half = count // 2
-    ring = [place_at(p, count) for p in range(count)]
-    onward = [(ring[p], ring[(p + 1) % count]) for p in range(count)]
-    backward = [(b, a) for a, b in onward]
+    onward = functools.partial(lax.ppermute, axis_name=("ctx", "tp"), perm=ring_pairs(count, cores, 1))
+    backward = functools.partial(lax.ppermute, axis_name=("ctx", "tp"), perm=ring_pairs(count, cores, -1))
 
     win_keys, win_values, cache_keys, cache_values, valid_counts, first_block, queries = [
         pltpu.with_memory_space_constraint(x, pltpu.HBM)
         for x in (win_keys, win_values, cache_keys, cache_values, valid_counts, first_block, queries)
     ]
-    own_keys, own_values, near, limits = load(
+    own_keys, own_values, near, limits, *state = load(
         count, win_keys, win_values, cache_keys, cache_values, queries, valid_counts, first_block
     )
     key_on = key_back = own_keys
     value_on = value_back = own_values
-    state = attend_first(count, sizes, near, limits, own_keys, own_values)
+    state = attend_first(count, sizes, near, limits, own_keys, own_values, state)
     arrived = []
     for step in range(1, half + 1):
-        key_on = lax.ppermute(key_on, "ctx", onward)
-        value_back = lax.ppermute(value_back, "ctx", backward)
+        key_on = onward(key_on)
+        value_back = backward(value_back)
         if step < half:
-            value_on = lax.ppermute(value_on, "ctx", onward)
-            key_back = lax.ppermute(key_back, "ctx", backward)
+            value_on = onward(value_on)
+            key_back = backward(key_back)
             row = 2 * (step - 1)
             arrived.append([(row, key_on, value_on), (row + 1, key_back, value_back)])
         else:
@@ -382,7 +412,7 @@
     )
     out_specs = P(("groups", "ctx"), "tp")
     return jax.shard_map(
-        functools.partial(shards, mesh.shape["ctx"]),
+        functools.partial(shards, mesh.shape["ctx"], mesh.shape["tp"]),
         mesh=mesh,
         in_specs=in_specs,
         out_specs=out_specs,

time: 26.2 us -> 26.9 us (1.027)
  waiting for transfers between devices: 3.89 us -> 5.58 us
  starting transfers between devices: 16 us -> 15 us
    ppermute x14, waiting for transfers between devices: 3.89 us -> 5.58 us  [the longest x4 2.94 us: shards(): value_back = backward(value_back)]
    ppermute x14, starting transfers between devices: 16 us -> 15 us  [the longest x4 8.41 us: shards(): key_on = onward(key_on)]
  transfers between devices with their start and end apart: 14 -> 14, of which waited for: 5 -> 8; matrix products, arithmetic and copies ran while one was open for 0% -> 0% of each run, Pallas kernels for 12% -> 12%
where the time goes in v13:
time: 26.9 us; the launch traced here: 26.8 us
  starting transfers between devices  15 us (56%)
  Pallas kernels  5.95 us (22%)
  waiting for transfers between devices  5.58 us (21%)
    ppermute x4, starting transfers between devices, shards(): key_on = onward(key_on)  8.41 us
    pallas_call x3, Pallas kernels, attend_next(): pl.pallas_call(functools.partial(next_kernel, rows_of, last, count, sizes...  3.91 us
    ppermute x3, starting transfers between devices, shards(): key_back = backward(key_back)  3.62 us
    ppermute x4, waiting for transfers between devices, shards(): value_back = backward(value_back)  2.94 us
    ppermute x3, starting transfers between devices, shards(): value_on = onward(value_on)  2.39 us
    ppermute x3, waiting for transfers between devices, shards(): value_on = onward(value_on)  1.71 us
    pallas_call x1, Pallas kernels, load(): pl.pallas_call(functools.partial(load_kernel, count), out_shape=[jax.Shap...  1.11 us
    pallas_call x1, Pallas kernels, attend_first(): pl.pallas_call(functools.partial(first_kernel, count, sizes), out_shape=s...  0.93 us
  transfers between devices with their start and end apart: 14, of which 8 were waited for; matrix products, arithmetic and copies ran while one was open for 0% of the time, Pallas kernels for 12%

profile of v13, /device:TPU:0, one launch (start us, length us, event | category | flops | bytes accessed | tf_op | source)
XLA Modules:
  0.0 26.8 jit_solution(7994775734852975449)
XLA Ops:
  0.0 1.1 %load.1 = (bf16[192,256]{1,0:T(8,128)(2,1)S(1)}, bf16[192,256]{1,0:T(8,128)(2,1)S(1)}, bf16[128,2048]{1,0:T(8,128)(2,1)S(1)}, s32[8,128]{1,0:T(8,128)S(1)}, f32[...) custom-call(bf16[128,256]{1,0:T(8,128)(2,1)} %win_keys.1, bf16[128,256]{1,0:T(8,128)(2,1)} %win_values.1, ...), custom_call_target="tpu_custom_call" | custom-call | bytes 393216 | tf_op jit(solution)/shard_map/load/pallas_call | solution.py:90
  1.1 3.0 %collective-permute-start = (bf16[192,256]{1,0:T(8,128)(2,1)S(1)}, bf16[192,256]{1,0:T(8,128)(2,1)S(1)}, u32[]{:S(2)}, u32[]{:S(2)}) collective-permute-start(bf16[192,256]{1,0:T(8,128)(2,1)S(1)} %get-tuple-element.21.own_keys), channel_id=1, source_target_pairs={{2,6},{6,10},{10,14},{14,12},{12,8},{8,4},{4,0},{0,2},{3,1},{7,3},... | collective-permute-start | bytes 294920 | tf_op jit(solution)/shard_map/ppermute | solution.py:384
  4.1 0.2 collective-permute-start.4
  4.3 2.0 %collective-permute-start.11 = (bf16[192,256]{1,0:T(8,128)(2,1)S(1)}, bf16[192,256]{1,0:T(8,128)(2,1)S(1)}, u32[]{:S(2)}, u32[]{:S(2)}) collective-permute-start(bf16[192,256]{1,0:T(8,128)(2,1)S(1)} %get-tuple-element.21.own_keys), channel_id=1, source_target_pairs={{2,0},{6,2},{10,6},{14,10},{12,14},{8,12},{4,8},{0,4},{3,7},{7,11}... | collective-permute-start | bytes 294920 | tf_op jit(solution)/shard_map/ppermute | solution.py:388
  6.2 0.1 collective-permute-start.8
  6.3 0.9 %attend_first.1 = (f32[2048,256]{1,0:T(8,128)S(1)}, f32[2048,128]{1,0:T(8,128)S(1)}) custom-call(bf16[128,2048]{1,0:T(8,128)(2,1)S(1)} %get-tuple-element.19.q_ref, s32[8,128]{1,0:T(8,128)S(1)} %get-tuple-element.20.limits, bf16[192,256]{1,0:T(8,128)(2,1)S(1)} %get-tuple-element.21.own_keys, bf16[192,256]{1,0:T(8,128)(2,1)S(1)} %get-tuple-element.22.own_values, ...), custom_call_target="tpu_custom_call" | custom-call | flops 402653184 | bytes 524288 | tf_op jit(solution)/shard_map/attend_first/pallas_call | solution.py:321
  7.2 0.1 collective-permute-done.refs_0_
  7.3 2.5 %collective-permute-start.1 = (bf16[192,256]{1,0:T(8,128)(2,1)S(1)}, bf16[192,256]{1,0:T(8,128)(2,1)S(1)}, u32[]{:S(2)}, u32[]{:S(2)}) collective-permute-start(bf16[192,256]{1,0:T(8,128)(2,1)S(1)} %collective-permute-done.refs_0_), channel_id=1, source_target_pairs={{2,6},{6,10},{10,14},{14,12},{12,8},{8,4},{4,0},{0,2},{3,1},{7,3},... | collective-permute-start | bytes 294920 | tf_op jit(solution)/shard_map/ppermute | solution.py:384
  9.8 0.0 collective-permute-done.4.refs_3_
  9.8 0.1 collective-permute-start.5
  9.9 0.9 %collective-permute-done.8.refs_1_ = bf16[192,256]{1,0:T(8,128)(2,1)S(1)} collective-permute-done((bf16[192,256]{1,0:T(8,128)(2,1)S(1)}, bf16[192,256]{1,0:T(8,128)(2,1)S(1)}, u32[]{:S(2)}, u32[]{:S(2)}) %collective-permute-start.8) | collective-permute-done | bytes 98336 | tf_op jit(solution)/shard_map/ppermute | solution.py:387
  10.8 1.0 %collective-permute-start.9 = (bf16[192,256]{1,0:T(8,128)(2,1)S(1)}, bf16[192,256]{1,0:T(8,128)(2,1)S(1)}, u32[]{:S(2)}, u32[]{:S(2)}) collective-permute-start(bf16[192,256]{1,0:T(8,128)(2,1)S(1)} %collective-permute-done.8.refs_1_), channel_id=1, source_target_pairs={{2,6},{6,10},{10,14},{14,12},{12,8},{8,4},{4,0},{0,2},{3,1},{7,3},... | collective-permute-start | bytes 294920 | tf_op jit(solution)/shard_map/ppermute | solution.py:387
  11.8 0.0 collective-permute-done.11.refs_2_
  11.8 1.1 %collective-permute-start.12 = (bf16[192,256]{1,0:T(8,128)(2,1)S(1)}, bf16[192,256]{1,0:T(8,128)(2,1)S(1)}, u32[]{:S(2)}, u32[]{:S(2)}) collective-permute-start(bf16[192,256]{1,0:T(8,128)(2,1)S(1)} %collective-permute-done.11.refs_2_), channel_id=1, source_target_pairs={{2,0},{6,2},{10,6},{14,10},{12,14},{8,12},{4,8},{0,4},{3,7},{7,11}... | collective-permute-start | bytes 294920 | tf_op jit(solution)/shard_map/ppermute | solution.py:388
  12.9 0.0 collective-permute-done.1.refs_4_
  12.9 1.5 %collective-permute-start.2 = (bf16[192,256]{1,0:T(8,128)(2,1)S(1)}, bf16[192,256]{1,0:T(8,128)(2,1)S(1)}, u32[]{:S(2)}, u32[]{:S(2)}) collective-permute-start(bf16[192,256]{1,0:T(8,128)(2,1)S(1)} %collective-permute-done.1.refs_4_), channel_id=1, source_target_pairs={{2,6},{6,10},{10,14},{14,12},{12,8},{8,4},{4,0},{0,2},{3,1},{7,3},... | collective-permute-start | bytes 294920 | tf_op jit(solution)/shard_map/ppermute | solution.py:384
  14.4 0.9 %collective-permute-done.5.refs_7_ = bf16[192,256]{1,0:T(8,128)(2,1)S(1)} collective-permute-done((bf16[192,256]{1,0:T(8,128)(2,1)S(1)}, bf16[192,256]{1,0:T(8,128)(2,1)S(1)}, u32[]{:S(2)}, u32[]{:S(2)}) %collective-permute-start.5) | collective-permute-done | bytes 98336 | tf_op jit(solution)/shard_map/ppermute | solution.py:385
  15.3 0.0 collective-permute-start.6
  15.3 0.8 %collective-permute-done.9.refs_5_ = bf16[192,256]{1,0:T(8,128)(2,1)S(1)} collective-permute-done((bf16[192,256]{1,0:T(8,128)(2,1)S(1)}, bf16[192,256]{1,0:T(8,128)(2,1)S(1)}, u32[]{:S(2)}, u32[]{:S(2)}) %collective-permute-start.9) | collective-permute-done | bytes 98336 | tf_op jit(solution)/shard_map/ppermute | solution.py:387
  16.1 1.3 %collective-permute-start.10 = (bf16[192,256]{1,0:T(8,128)(2,1)S(1)}, bf16[192,256]{1,0:T(8,128)(2,1)S(1)}, u32[]{:S(2)}, u32[]{:S(2)}) collective-permute-start(bf16[192,256]{1,0:T(8,128)(2,1)S(1)} %collective-permute-done.9.refs_5_), channel_id=1, source_target_pairs={{2,6},{6,10},{10,14},{14,12},{12,8},{8,4},{4,0},{0,2},{3,1},{7,3},... | collective-permute-start | bytes 294920 | tf_op jit(solution)/shard_map/ppermute | solution.py:387
  17.5 0.1 collective-permute-done.12.refs_6_
  17.6 0.6 %collective-permute-start.13 = (bf16[192,256]{1,0:T(8,128)(2,1)S(1)}, bf16[192,256]{1,0:T(8,128)(2,1)S(1)}, u32[]{:S(2)}, u32[]{:S(2)}) collective-permute-start(bf16[192,256]{1,0:T(8,128)(2,1)S(1)} %collective-permute-done.12.refs_6_), channel_id=1, source_target_pairs={{2,0},{6,2},{10,6},{14,10},{12,14},{8,12},{4,8},{0,4},{3,7},{7,11}... | collective-permute-start | bytes 294920 | tf_op jit(solution)/shard_map/ppermute | solution.py:388
  18.2 0.0 collective-permute-done.2.refs_0_
  18.2 1.4 %collective-permute-start.3 = (bf16[192,256]{1,0:T(8,128)(2,1)S(1)}, bf16[192,256]{1,0:T(8,128)(2,1)S(1)}, u32[]{:S(2)}, u32[]{:S(2)}) collective-permute-start(bf16[192,256]{1,0:T(8,128)(2,1)S(1)} %collective-permute-done.2.refs_0_), channel_id=1, source_target_pairs={{2,6},{6,10},{10,14},{14,12},{12,8},{8,4},{4,0},{0,2},{3,1},{7,3},... | collective-permute-start | bytes 294920 | tf_op jit(solution)/shard_map/ppermute | solution.py:384
  19.6 0.7 %collective-permute-done.6.refs_3_ = bf16[192,256]{1,0:T(8,128)(2,1)S(1)} collective-permute-done((bf16[192,256]{1,0:T(8,128)(2,1)S(1)}, bf16[192,256]{1,0:T(8,128)(2,1)S(1)}, u32[]{:S(2)}, u32[]{:S(2)}) %collective-permute-start.6) | collective-permute-done | bytes 98336 | tf_op jit(solution)/shard_map/ppermute | solution.py:385
  20.3 0.3 %collective-permute-start.7 = (bf16[192,256]{1,0:T(8,128)(2,1)S(1)}, bf16[192,256]{1,0:T(8,128)(2,1)S(1)}, u32[]{:S(2)}, u32[]{:S(2)}) collective-permute-start(bf16[192,256]{1,0:T(8,128)(2,1)S(1)} %collective-permute-done.6.refs_3_), channel_id=1, source_target_pairs={{2,0},{6,2},{10,6},{14,10},{12,14},{8,12},{4,8},{0,4},{3,7},{7,11}... | collective-permute-start | bytes 294920 | tf_op jit(solution)/shard_map/ppermute | solution.py:385
  20.6 1.0 %attend_next.2 = (f32[2048,256]{1,0:T(8,128)S(1)}, f32[2048,128]{1,0:T(8,128)S(1)}) custom-call(bf16[128,2048]{1,0:T(8,128)(2,1)S(1)} %get-tuple-element.19.q_ref, s32[8,128]{1,0:T(8,128)S(1)} %get-tuple-element.20.limits, bf16[192,256]{1,0:T(8,128)(2,1)S(1)} %collective-permute-done.refs_0_, bf16[192,256]{1,0:T(8,128)(2,1)S(1)} %collective-permute-done.8.refs_1_, ...), custom_call_target="tpu_custom_call" | custom-call | flops 1207959552 | bytes 524288 | tf_op jit(solution)/shard_map/attend_next/pallas_call | solution.py:345
  21.6 0.0 collective-permute-done.10.refs_1_
  21.6 0.8 %collective-permute-done.13.refs_2_ = bf16[192,256]{1,0:T(8,128)(2,1)S(1)} collective-permute-done((bf16[192,256]{1,0:T(8,128)(2,1)S(1)}, bf16[192,256]{1,0:T(8,128)(2,1)S(1)}, u32[]{:S(2)}, u32[]{:S(2)}) %collective-permute-start.13) | collective-permute-done | bytes 98336 | tf_op jit(solution)/shard_map/ppermute | solution.py:388
  22.4 1.2 %attend_next.3 = (f32[2048,256]{1,0:T(8,128)S(1)}, f32[2048,128]{1,0:T(8,128)S(1)}) custom-call(bf16[128,2048]{1,0:T(8,128)(2,1)S(1)} %get-tuple-element.19.q_ref, s32[8,128]{1,0:T(8,128)S(1)} %get-tuple-element.20.limits, bf16[192,256]{1,0:T(8,128)(2,1)S(1)} %collective-permute-done.2.refs_0_, bf16[192,256]{1,0:T(8,128)(2,1)S(1)} %collective-permute-done.10.refs_1_, ...), custom_call_target="tpu_custom_call" | custom-call | flops 603979776 | bytes 524288 | tf_op jit(solution)/shard_map/attend_next/pallas_call | solution.py:345
  23.6 0.0 collective-permute-done.3.refs_0_
  23.6 1.3 %collective-permute-done.7.refs_1_ = bf16[192,256]{1,0:T(8,128)(2,1)S(1)} collective-permute-done((bf16[192,256]{1,0:T(8,128)(2,1)S(1)}, bf16[192,256]{1,0:T(8,128)(2,1)S(1)}, u32[]{:S(2)}, u32[]{:S(2)}) %collective-permute-start.7) | collective-permute-done | bytes 98336 | tf_op jit(solution)/shard_map/ppermute | solution.py:385
  24.9 1.7 %attend_last.1 = bf16[128,2048]{1,0:T(8,128)(2,1)} custom-call(bf16[128,2048]{1,0:T(8,128)(2,1)S(1)} %get-tuple-element.19.q_ref, s32[8,128]{1,0:T(8,128)S(1)} %get-tuple-element.20.limits, bf16[192,256]{1,0:T(8,128)(2,1)S(1)} %collective-permute-done.3.refs_0_, bf16[192,256]{1,0:T(8,128)(2,1)S(1)} %collective-permute-done.7.refs_1_, ...), custom_call_target="tpu_custom_call" | custom-call | flops 402653184 | bytes 524288 | tf_op jit(solution)/shard_map/attend_last/pallas_call | solution.py:345
Async XLA Ops:
  1.1 6.2 %collective-permute-start = (bf16[192,256]{1,0:T(8,128)(2,1)S(1)}, bf16[192,256]{1,0:T(8,128)(2,1)S(1)}, u32[]{:S(2)}, u32[]{:S(2)}) collective-permute-start(bf16[192,256]{1,0:T(8,128)(2,1)S(1)} %get-tuple-element.21.own_keys), channel_id=1, source_target_pairs={{2,6},{6,10},{10,14},{14,12},{12,8},{8,4},{4,0},{0,2},{3,1},{7,3},... | collective-permute-start | bytes 294920 | tf_op jit(solution)/shard_map/ppermute | solution.py:384
  4.1 5.7 %collective-permute-start.4 = (bf16[192,256]{1,0:T(8,128)(2,1)S(1)}, bf16[192,256]{1,0:T(8,128)(2,1)S(1)}, u32[]{:S(2)}, u32[]{:S(2)}) collective-permute-start(bf16[192,256]{1,0:T(8,128)(2,1)S(1)} %get-tuple-element.22.own_values), channel_id=1, source_target_pairs={{2,0},{6,2},{10,6},{14,10},{12,14},{8,12},{4,8},{0,4},{3,7},{7,11}... | collective-permute-start | bytes 294920 | tf_op jit(solution)/shard_map/ppermute | solution.py:385
  4.3 7.6 %collective-permute-start.11 = (bf16[192,256]{1,0:T(8,128)(2,1)S(1)}, bf16[192,256]{1,0:T(8,128)(2,1)S(1)}, u32[]{:S(2)}, u32[]{:S(2)}) collective-permute-start(bf16[192,256]{1,0:T(8,128)(2,1)S(1)} %get-tuple-element.21.own_keys), channel_id=1, source_target_pairs={{2,0},{6,2},{10,6},{14,10},{12,14},{8,12},{4,8},{0,4},{3,7},{7,11}... | collective-permute-start | bytes 294920 | tf_op jit(solution)/shard_map/ppermute | solution.py:388
  6.2 4.6 %collective-permute-start.8 = (bf16[192,256]{1,0:T(8,128)(2,1)S(1)}, bf16[192,256]{1,0:T(8,128)(2,1)S(1)}, u32[]{:S(2)}, u32[]{:S(2)}) collective-permute-start(bf16[192,256]{1,0:T(8,128)(2,1)S(1)} %get-tuple-element.22.own_values), channel_id=1, source_target_pairs={{2,6},{6,10},{10,14},{14,12},{12,8},{8,4},{4,0},{0,2},{3,1},{7,3},... | collective-permute-start | bytes 294920 | tf_op jit(solution)/shard_map/ppermute | solution.py:387
  7.3 5.6 %collective-permute-start.1 = (bf16[192,256]{1,0:T(8,128)(2,1)S(1)}, bf16[192,256]{1,0:T(8,128)(2,1)S(1)}, u32[]{:S(2)}, u32[]{:S(2)}) collective-permute-start(bf16[192,256]{1,0:T(8,128)(2,1)S(1)} %collective-permute-done.refs_0_), channel_id=1, source_target_pairs={{2,6},{6,10},{10,14},{14,12},{12,8},{8,4},{4,0},{0,2},{3,1},{7,3},... | collective-permute-start | bytes 294920 | tf_op jit(solution)/shard_map/ppermute | solution.py:384
  9.8 5.5 %collective-permute-start.5 = (bf16[192,256]{1,0:T(8,128)(2,1)S(1)}, bf16[192,256]{1,0:T(8,128)(2,1)S(1)}, u32[]{:S(2)}, u32[]{:S(2)}) collective-permute-start(bf16[192,256]{1,0:T(8,128)(2,1)S(1)} %collective-permute-done.4.refs_3_), channel_id=1, source_target_pairs={{2,0},{6,2},{10,6},{14,10},{12,14},{8,12},{4,8},{0,4},{3,7},{7,11}... | collective-permute-start | bytes 294920 | tf_op jit(solution)/shard_map/ppermute | solution.py:385
  10.8 5.3 %collective-permute-start.9 = (bf16[192,256]{1,0:T(8,128)(2,1)S(1)}, bf16[192,256]{1,0:T(8,128)(2,1)S(1)}, u32[]{:S(2)}, u32[]{:S(2)}) collective-permute-start(bf16[192,256]{1,0:T(8,128)(2,1)S(1)} %collective-permute-done.8.refs_1_), channel_id=1, source_target_pairs={{2,6},{6,10},{10,14},{14,12},{12,8},{8,4},{4,0},{0,2},{3,1},{7,3},... | collective-permute-start | bytes 294920 | tf_op jit(solution)/shard_map/ppermute | solution.py:387
  11.8 5.7 %collective-permute-start.12 = (bf16[192,256]{1,0:T(8,128)(2,1)S(1)}, bf16[192,256]{1,0:T(8,128)(2,1)S(1)}, u32[]{:S(2)}, u32[]{:S(2)}) collective-permute-start(bf16[192,256]{1,0:T(8,128)(2,1)S(1)} %collective-permute-done.11.refs_2_), channel_id=1, source_target_pairs={{2,0},{6,2},{10,6},{14,10},{12,14},{8,12},{4,8},{0,4},{3,7},{7,11}... | collective-permute-start | bytes 294920 | tf_op jit(solution)/shard_map/ppermute | solution.py:388
  12.9 5.3 %collective-permute-start.2 = (bf16[192,256]{1,0:T(8,128)(2,1)S(1)}, bf16[192,256]{1,0:T(8,128)(2,1)S(1)}, u32[]{:S(2)}, u32[]{:S(2)}) collective-permute-start(bf16[192,256]{1,0:T(8,128)(2,1)S(1)} %collective-permute-done.1.refs_4_), channel_id=1, source_target_pairs={{2,6},{6,10},{10,14},{14,12},{12,8},{8,4},{4,0},{0,2},{3,1},{7,3},... | collective-permute-start | bytes 294920 | tf_op jit(solution)/shard_map/ppermute | solution.py:384
  15.3 4.9 %collective-permute-start.6 = (bf16[192,256]{1,0:T(8,128)(2,1)S(1)}, bf16[192,256]{1,0:T(8,128)(2,1)S(1)}, u32[]{:S(2)}, u32[]{:S(2)}) collective-permute-start(bf16[192,256]{1,0:T(8,128)(2,1)S(1)} %collective-permute-done.5.refs_7_), channel_id=1, source_target_pairs={{2,0},{6,2},{10,6},{14,10},{12,14},{8,12},{4,8},{0,4},{3,7},{7,11}... | collective-permute-start | bytes 294920 | tf_op jit(solution)/shard_map/ppermute | solution.py:385
  16.1 5.5 %collective-permute-start.10 = (bf16[192,256]{1,0:T(8,128)(2,1)S(1)}, bf16[192,256]{1,0:T(8,128)(2,1)S(1)}, u32[]{:S(2)}, u32[]{:S(2)}) collective-permute-start(bf16[192,256]{1,0:T(8,128)(2,1)S(1)} %collective-permute-done.9.refs_5_), channel_id=1, source_target_pairs={{2,6},{6,10},{10,14},{14,12},{12,8},{8,4},{4,0},{0,2},{3,1},{7,3},... | collective-permute-start | bytes 294920 | tf_op jit(solution)/shard_map/ppermute | solution.py:387
  17.6 4.8 %collective-permute-start.13 = (bf16[192,256]{1,0:T(8,128)(2,1)S(1)}, bf16[192,256]{1,0:T(8,128)(2,1)S(1)}, u32[]{:S(2)}, u32[]{:S(2)}) collective-permute-start(bf16[192,256]{1,0:T(8,128)(2,1)S(1)} %collective-permute-done.12.refs_6_), channel_id=1, source_target_pairs={{2,0},{6,2},{10,6},{14,10},{12,14},{8,12},{4,8},{0,4},{3,7},{7,11}... | collective-permute-start | bytes 294920 | tf_op jit(solution)/shard_map/ppermute | solution.py:388
  18.2 5.4 %collective-permute-start.3 = (bf16[192,256]{1,0:T(8,128)(2,1)S(1)}, bf16[192,256]{1,0:T(8,128)(2,1)S(1)}, u32[]{:S(2)}, u32[]{:S(2)}) collective-permute-start(bf16[192,256]{1,0:T(8,128)(2,1)S(1)} %collective-permute-done.2.refs_0_), channel_id=1, source_target_pairs={{2,6},{6,10},{10,14},{14,12},{12,8},{8,4},{4,0},{0,2},{3,1},{7,3},... | collective-permute-start | bytes 294920 | tf_op jit(solution)/shard_map/ppermute | solution.py:384
  20.3 4.6 %collective-permute-start.7 = (bf16[192,256]{1,0:T(8,128)(2,1)S(1)}, bf16[192,256]{1,0:T(8,128)(2,1)S(1)}, u32[]{:S(2)}, u32[]{:S(2)}) collective-permute-start(bf16[192,256]{1,0:T(8,128)(2,1)S(1)} %collective-permute-done.6.refs_3_), channel_id=1, source_target_pairs={{2,0},{6,2},{10,6},{14,10},{12,14},{8,12},{4,8},{0,4},{3,7},{7,11}... | collective-permute-start | bytes 294920 | tf_op jit(solution)/shard_map/ppermute | solution.py:385

commit v14 on v12

--- a/solution.py
+++ b/solution.py
@@ -11,8 +11,8 @@
 HD = 128
 EXP_SCALE = HD**-0.5 * math.log2(math.e)
 HIDDEN = -1.0e30
-CHUNK_HEADS = 8
-LAST_CHUNK_HEADS = 4
+CHUNK_HEADS = 4
+COPY_HEADS = 2
 LARGEST_TOTAL = 2.0**100
 
 
@@ -164,16 +164,17 @@
     return (acc[:, :HD] * (inverse * (2.0 - total * inverse))).astype(jnp.bfloat16)
 
 
-def chunks(q_ref, kv_heads, size):
+def chunks(q_ref, kv_heads, fine_end=False):
     rows = q_ref.shape[0]
     group = q_ref.shape[1] // HD // kv_heads
-    for head in range(kv_heads):
-        for start in range(0, group, size):
-            base = head * group + start
-            query = jnp.concatenate(
-                [q_ref[:, (base + i) * HD : (base + i + 1) * HD] for i in range(size)], axis=0
-            )
-            yield head, slice(base * rows, (base + size) * rows), query, base
+    sizes = [CHUNK_HEADS] * (kv_heads * group // CHUNK_HEADS)
+    if fine_end:
+        sizes[-1:] = [CHUNK_HEADS // 2] * 2
+    base = 0
+    for size in sizes:
+        query = jnp.concatenate([q_ref[:, (base + i) * HD : (base + i + 1) * HD] for i in range(size)], axis=0)
+        yield base // group, slice(base * rows, (base + size) * rows), query, base, size
+        base += size
 
 
 def first_kernel(count, sizes, q_ref, limits, own_keys, own_values, acc_out, top_out, keys, values):
@@ -186,7 +187,7 @@
     query_iota = lax.broadcasted_iota(jnp.int32, (rows, window_rows), 0)
     seen = (key_iota <= query_iota) & (key_iota < limits[count - 1 : count, :])
     bias = jnp.concatenate([jnp.where(seen, 0.0, HIDDEN)] * CHUNK_HEADS, axis=0)
-    for head, at, query, _ in chunks(q_ref, keys.shape[0], CHUNK_HEADS):
+    for head, at, query, _, _ in chunks(q_ref, keys.shape[0]):
         score = scores(query, keys[head])
         score = jnp.concatenate([score[:, :window_rows] + bias, score[:, window_rows:]], axis=1)
         top = wide_top(score)
@@ -203,37 +204,41 @@
         acc_in, top_in, acc_out, top_out, keys, values = refs[2 * number :]
     rows, heads = q_ref.shape[0], q_ref.shape[1] // HD
     kv_heads = keys.shape[0]
-    size = LAST_CHUNK_HEADS if last else CHUNK_HEADS
 
     def sent(base):
-        lanes = slice(base * HD, (base + size) * HD)
-        return pltpu.make_async_copy(result.at[:, lanes], out.at[:, lanes], sems.at[base // size])
-
-    def settle(base, acc):
+        lanes = slice(base * HD, (base + COPY_HEADS) * HD)
+        return pltpu.make_async_copy(result.at[:, lanes], out.at[:, lanes], sems.at[base // COPY_HEADS])
+
+    def settle(base, size, acc):
         done = normalised(acc)
         for i in range(size):
             result[:, (base + i) * HD : (base + i + 1) * HD] = done[i * rows : (i + 1) * rows]
-        sent(base).start()
+        for i in range(0, size, COPY_HEADS):
+            sent(base + i).start()
+
+    def wait_all():
+        for base in range(0, heads, COPY_HEADS):
+            sent(base).wait()
 
     def take_in(begin):
         fine = jnp.ones((8, HD), jnp.float32)
-        for head, at, query, base in chunks(q_ref, kv_heads, size):
+        for head, at, query, base, size in chunks(q_ref, kv_heads, last):
             top = top_in[at, :]
             acc = acc_in[at, :] + weigh(scores(query, keys[head, begin:]), top, values[head, begin:])
             safe = jnp.where(acc[:, HD:] < LARGEST_TOTAL, 1.0, 0.0).reshape(-1, 8, HD)
             fine = jnp.minimum(fine, jnp.min(safe, axis=0))
             if last:
-                settle(base, acc)
+                settle(base, size, acc)
             else:
                 acc_out[at, :] = acc
                 top_out[at, :] = top
+        again = jnp.min(fine) < 0.5
         if last:
-            for base in range(0, heads, size):
-                sent(base).wait()
-
-        @pl.when(jnp.min(fine) < 0.5)
+            wait_all()
+
+        @pl.when(again)
         def _():
-            for head, at, query, base in chunks(q_ref, kv_heads, size):
+            for head, at, query, base, size in chunks(q_ref, kv_heads, last):
                 score = scores(query, keys[head, begin:])
                 before = top_in[at, :]
                 top = jnp.maximum(before, wide_top(score))
@@ -241,15 +246,21 @@
                 acc = acc_in[at, :] * jnp.concatenate([fade, fade], axis=1)
                 acc = acc + weigh(score, top, values[head, begin:])
                 if last:
-                    settle(base, acc)
-                    sent(base).wait()
+                    settle(base, size, acc)
                 else:
                     acc_out[at, :] = acc
                     top_out[at, :] = top
+            if last:
+                wait_all()
 
     for index in range(number):
         place_cache(index, number, sizes, key_refs[index], value_refs[index], keys, values)
     fill_up(number * sum(sizes), keys, values)
+    if number < 4:
+        for index, row in enumerate(rows_of):
+            place_window(index, row, False, sizes, limits, key_refs[index], value_refs[index], keys, values)
+        take_in(0)
+        return
     me = lax.axis_index("ctx")
     position = position_of(me, count)
     offsets = ring_offsets(count)
@@ -318,8 +329,8 @@
     shapes = [jax.ShapeDtypeStruct(queries.shape, queries.dtype)] if last else state_shapes(queries)
     scratch = room(kv_heads, total_keys)
     if last:
-        chunk_count = queries.shape[1] // HD // LAST_CHUNK_HEADS
-        scratch += [pltpu.VMEM(queries.shape, queries.dtype), pltpu.SemaphoreType.DMA((chunk_count,))]
+        copies = queries.shape[1] // HD // COPY_HEADS
+        scratch += [pltpu.VMEM(queries.shape, queries.dtype), pltpu.SemaphoreType.DMA((copies,))]
     outs = pl.pallas_call(
         functools.partial(next_kernel, rows_of, last, count, sizes),
         out_shape=shapes,

time: 26.2 us -> 26 us (level)
  transfers between devices with their start and end apart: 14 -> 14, of which waited for: 5 -> 5; matrix products, arithmetic and copies ran while one was open for 0% -> 0% of each run, Pallas kernels for 12% -> 13%
where the time goes in v14:
time: 26 us; the launch traced here: 25.8 us
  starting transfers between devices  16 us (62%)
  Pallas kernels  6.13 us (24%)
  waiting for transfers between devices  3.66 us (14%)
    ppermute x4, starting transfers between devices, shards(): key_on = lax.ppermute(key_on, 'ctx', onward)  7.72 us
    ppermute x3, starting transfers between devices, shards(): key_back = lax.ppermute(key_back, 'ctx', backward)  4.36 us
    pallas_call x3, Pallas kernels, attend_next(): pl.pallas_call(functools.partial(next_kernel, rows_of, last, count, sizes...  4.09 us
    ppermute x4, starting transfers between devices, shards(): value_back = lax.ppermute(value_back, 'ctx', backward)  2.19 us
    ppermute x3, starting transfers between devices, shards(): value_on = lax.ppermute(value_on, 'ctx', onward)  1.72 us
    ppermute x3, waiting for transfers between devices, shards(): value_on = lax.ppermute(value_on, 'ctx', onward)  1.68 us
    ppermute x4, waiting for transfers between devices, shards(): value_back = lax.ppermute(value_back, 'ctx', backward)  1.3 us
    pallas_call x1, Pallas kernels, load(): pl.pallas_call(functools.partial(load_kernel, count), out_shape=[jax.Shap...  1.11 us
  transfers between devices with their start and end apart: 14, of which 5 were waited for; matrix products, arithmetic and copies ran while one was open for 0% of the time, Pallas kernels for 13%

profile of v14, /device:TPU:0, one launch (start us, length us, event | category | flops | bytes accessed | tf_op | source)
XLA Modules:
  0.0 25.8 jit_solution(8940531224993909759)
XLA Ops:
  0.0 1.1 %load.1 = (bf16[192,256]{1,0:T(8,128)(2,1)S(1)}, bf16[192,256]{1,0:T(8,128)(2,1)S(1)}, bf16[128,2048]{1,0:T(8,128)(2,1)S(1)}, s32[8,128]{1,0:T(8,128)S(1)}) custom-call(bf16[128,256]{1,0:T(8,128)(2,1)} %win_keys.1, bf16[128,256]{1,0:T(8,128)(2,1)} %win_values.1, bf16[64,256]{1,0:T(8,128)(2,1)} %cache_keys.1, bf16[64,256]{1,0:T(8,128)(2,1)} %cache_values.1, ...), custom_call_target="tpu_custom_call" | custom-call | bytes 393216 | tf_op jit(solution)/shard_map/load/pallas_call | solution.py:81
  1.1 3.0 %collective-permute-start = (bf16[192,256]{1,0:T(8,128)(2,1)S(1)}, bf16[192,256]{1,0:T(8,128)(2,1)S(1)}, u32[]{:S(2)}, u32[]{:S(2)}) collective-permute-start(bf16[192,256]{1,0:T(8,128)(2,1)S(1)} %get-tuple-element.19.own_keys), channel_id=1, source_target_pairs={{2,6},{6,10},{10,14},{14,12},{12,8},{8,4},{4,0},{0,2},{3,7},{7,11}... | collective-permute-start | bytes 294920 | tf_op jit(solution)/shard_map/ppermute | solution.py:365
  4.1 0.2 collective-permute-start.4
  4.3 2.0 %collective-permute-start.11 = (bf16[192,256]{1,0:T(8,128)(2,1)S(1)}, bf16[192,256]{1,0:T(8,128)(2,1)S(1)}, u32[]{:S(2)}, u32[]{:S(2)}) collective-permute-start(bf16[192,256]{1,0:T(8,128)(2,1)S(1)} %get-tuple-element.19.own_keys), channel_id=1, source_target_pairs={{6,2},{10,6},{14,10},{12,14},{8,12},{4,8},{0,4},{2,0},{7,3},{11,7}... | collective-permute-start | bytes 294920 | tf_op jit(solution)/shard_map/ppermute | solution.py:369
  6.2 0.1 collective-permute-start.8
  6.3 0.9 %attend_first.1 = (f32[2048,256]{1,0:T(8,128)S(1)}, f32[2048,128]{1,0:T(8,128)S(1)}) custom-call(bf16[128,2048]{1,0:T(8,128)(2,1)S(1)} %get-tuple-element.17.q_ref, s32[8,128]{1,0:T(8,128)S(1)} %get-tuple-element.18.limits, bf16[192,256]{1,0:T(8,128)(2,1)S(1)} %get-tuple-element.19.own_keys, bf16[192,256]{1,0:T(8,128)(2,1)S(1)} %get-tuple-element.20.own_values), custom_call_target="tpu_custom_call" | custom-call | flops 402653184 | bytes 524288 | tf_op jit(solution)/shard_map/attend_first/pallas_call | solution.py:310
  7.2 0.0 collective-permute-done.refs_0_
  7.2 2.1 %collective-permute-start.1 = (bf16[192,256]{1,0:T(8,128)(2,1)S(1)}, bf16[192,256]{1,0:T(8,128)(2,1)S(1)}, u32[]{:S(2)}, u32[]{:S(2)}) collective-permute-start(bf16[192,256]{1,0:T(8,128)(2,1)S(1)} %collective-permute-done.refs_0_), channel_id=1, source_target_pairs={{2,6},{6,10},{10,14},{14,12},{12,8},{8,4},{4,0},{0,2},{3,7},{7,11}... | collective-permute-start | bytes 294920 | tf_op jit(solution)/shard_map/ppermute | solution.py:365
  9.4 0.0 collective-permute-done.4.refs_3_
  9.4 0.2 collective-permute-start.5
  9.7 1.3 %collective-permute-done.8.refs_1_ = bf16[192,256]{1,0:T(8,128)(2,1)S(1)} collective-permute-done((bf16[192,256]{1,0:T(8,128)(2,1)S(1)}, bf16[192,256]{1,0:T(8,128)(2,1)S(1)}, u32[]{:S(2)}, u32[]{:S(2)}) %collective-permute-start.8) | collective-permute-done | bytes 98336 | tf_op jit(solution)/shard_map/ppermute | solution.py:368
  11.0 0.5 %collective-permute-start.9 = (bf16[192,256]{1,0:T(8,128)(2,1)S(1)}, bf16[192,256]{1,0:T(8,128)(2,1)S(1)}, u32[]{:S(2)}, u32[]{:S(2)}) collective-permute-start(bf16[192,256]{1,0:T(8,128)(2,1)S(1)} %collective-permute-done.8.refs_1_), channel_id=1, source_target_pairs={{2,6},{6,10},{10,14},{14,12},{12,8},{8,4},{4,0},{0,2},{3,7},{7,11}... | collective-permute-start | bytes 294920 | tf_op jit(solution)/shard_map/ppermute | solution.py:368
  11.4 0.0 collective-permute-done.11.refs_2_
  11.5 1.6 %collective-permute-start.12 = (bf16[192,256]{1,0:T(8,128)(2,1)S(1)}, bf16[192,256]{1,0:T(8,128)(2,1)S(1)}, u32[]{:S(2)}, u32[]{:S(2)}) collective-permute-start(bf16[192,256]{1,0:T(8,128)(2,1)S(1)} %collective-permute-done.11.refs_2_), channel_id=1, source_target_pairs={{6,2},{10,6},{14,10},{12,14},{8,12},{4,8},{0,4},{2,0},{7,3},{11,7}... | collective-permute-start | bytes 294920 | tf_op jit(solution)/shard_map/ppermute | solution.py:369
  13.0 0.0 collective-permute-done.1.refs_4_
  13.0 1.6 %collective-permute-start.2 = (bf16[192,256]{1,0:T(8,128)(2,1)S(1)}, bf16[192,256]{1,0:T(8,128)(2,1)S(1)}, u32[]{:S(2)}, u32[]{:S(2)}) collective-permute-start(bf16[192,256]{1,0:T(8,128)(2,1)S(1)} %collective-permute-done.1.refs_4_), channel_id=1, source_target_pairs={{2,6},{6,10},{10,14},{14,12},{12,8},{8,4},{4,0},{0,2},{3,7},{7,11}... | collective-permute-start | bytes 294920 | tf_op jit(solution)/shard_map/ppermute | solution.py:365
  14.6 0.0 collective-permute-done.5.refs_7_
  14.6 0.6 %collective-permute-start.6 = (bf16[192,256]{1,0:T(8,128)(2,1)S(1)}, bf16[192,256]{1,0:T(8,128)(2,1)S(1)}, u32[]{:S(2)}, u32[]{:S(2)}) collective-permute-start(bf16[192,256]{1,0:T(8,128)(2,1)S(1)} %collective-permute-done.5.refs_7_), channel_id=1, source_target_pairs={{6,2},{10,6},{14,10},{12,14},{8,12},{4,8},{0,4},{2,0},{7,3},{11,7}... | collective-permute-start | bytes 294920 | tf_op jit(solution)/shard_map/ppermute | solution.py:366
  15.2 0.4 %collective-permute-done.9.refs_5_ = bf16[192,256]{1,0:T(8,128)(2,1)S(1)} collective-permute-done((bf16[192,256]{1,0:T(8,128)(2,1)S(1)}, bf16[192,256]{1,0:T(8,128)(2,1)S(1)}, u32[]{:S(2)}, u32[]{:S(2)}) %collective-permute-start.9) | collective-permute-done | bytes 98336 | tf_op jit(solution)/shard_map/ppermute | solution.py:368
  15.6 1.2 %collective-permute-start.10 = (bf16[192,256]{1,0:T(8,128)(2,1)S(1)}, bf16[192,256]{1,0:T(8,128)(2,1)S(1)}, u32[]{:S(2)}, u32[]{:S(2)}) collective-permute-start(bf16[192,256]{1,0:T(8,128)(2,1)S(1)} %collective-permute-done.9.refs_5_), channel_id=1, source_target_pairs={{2,6},{6,10},{10,14},{14,12},{12,8},{8,4},{4,0},{0,2},{3,7},{7,11}... | collective-permute-start | bytes 294920 | tf_op jit(solution)/shard_map/ppermute | solution.py:368
  16.8 0.0 collective-permute-done.12.refs_6_
  16.8 0.8 %collective-permute-start.13 = (bf16[192,256]{1,0:T(8,128)(2,1)S(1)}, bf16[192,256]{1,0:T(8,128)(2,1)S(1)}, u32[]{:S(2)}, u32[]{:S(2)}) collective-permute-start(bf16[192,256]{1,0:T(8,128)(2,1)S(1)} %collective-permute-done.12.refs_6_), channel_id=1, source_target_pairs={{6,2},{10,6},{14,10},{12,14},{8,12},{4,8},{0,4},{2,0},{7,3},{11,7}... | collective-permute-start | bytes 294920 | tf_op jit(solution)/shard_map/ppermute | solution.py:369
  17.6 0.7 %collective-permute-done.2.refs_0_ = bf16[192,256]{1,0:T(8,128)(2,1)S(1)} collective-permute-done((bf16[192,256]{1,0:T(8,128)(2,1)S(1)}, bf16[192,256]{1,0:T(8,128)(2,1)S(1)}, u32[]{:S(2)}, u32[]{:S(2)}) %collective-permute-start.2) | collective-permute-done | bytes 98336 | tf_op jit(solution)/shard_map/ppermute | solution.py:365
  18.3 1.0 %collective-permute-start.3 = (bf16[192,256]{1,0:T(8,128)(2,1)S(1)}, bf16[192,256]{1,0:T(8,128)(2,1)S(1)}, u32[]{:S(2)}, u32[]{:S(2)}) collective-permute-start(bf16[192,256]{1,0:T(8,128)(2,1)S(1)} %collective-permute-done.2.refs_0_), channel_id=1, source_target_pairs={{2,6},{6,10},{10,14},{14,12},{12,8},{8,4},{4,0},{0,2},{3,7},{7,11}... | collective-permute-start | bytes 294920 | tf_op jit(solution)/shard_map/ppermute | solution.py:365
  19.3 0.3 %collective-permute-done.6.refs_3_ = bf16[192,256]{1,0:T(8,128)(2,1)S(1)} collective-permute-done((bf16[192,256]{1,0:T(8,128)(2,1)S(1)}, bf16[192,256]{1,0:T(8,128)(2,1)S(1)}, u32[]{:S(2)}, u32[]{:S(2)}) %collective-permute-start.6) | collective-permute-done | bytes 98336 | tf_op jit(solution)/shard_map/ppermute | solution.py:366
  19.6 1.2 %collective-permute-start.7 = (bf16[192,256]{1,0:T(8,128)(2,1)S(1)}, bf16[192,256]{1,0:T(8,128)(2,1)S(1)}, u32[]{:S(2)}, u32[]{:S(2)}) collective-permute-start(bf16[192,256]{1,0:T(8,128)(2,1)S(1)} %collective-permute-done.6.refs_3_), channel_id=1, source_target_pairs={{6,2},{10,6},{14,10},{12,14},{8,12},{4,8},{0,4},{2,0},{7,3},{11,7}... | collective-permute-start | bytes 294920 | tf_op jit(solution)/shard_map/ppermute | solution.py:366
  20.7 1.0 %attend_next.2 = (f32[2048,256]{1,0:T(8,128)S(1)}, f32[2048,128]{1,0:T(8,128)S(1)}) custom-call(bf16[128,2048]{1,0:T(8,128)(2,1)S(1)} %get-tuple-element.17.q_ref, s32[8,128]{1,0:T(8,128)S(1)} %get-tuple-element.18.limits, bf16[192,256]{1,0:T(8,128)(2,1)S(1)} %collective-permute-done.refs_0_, bf16[192,256]{1,0:T(8,128)(2,1)S(1)} %collective-permute-done.8.refs_1_, ...), custom_call_target="tpu_custom_call" | custom-call | flops 1207959552 | bytes 524288 | tf_op jit(solution)/shard_map/attend_next/pallas_call | solution.py:334
  21.8 0.0 collective-permute-done.10.refs_1_
  21.8 0.0 collective-permute-done.13.refs_2_
  21.8 1.4 %attend_next.3 = (f32[2048,256]{1,0:T(8,128)S(1)}, f32[2048,128]{1,0:T(8,128)S(1)}) custom-call(bf16[128,2048]{1,0:T(8,128)(2,1)S(1)} %get-tuple-element.17.q_ref, s32[8,128]{1,0:T(8,128)S(1)} %get-tuple-element.18.limits, bf16[192,256]{1,0:T(8,128)(2,1)S(1)} %collective-permute-done.2.refs_0_, bf16[192,256]{1,0:T(8,128)(2,1)S(1)} %collective-permute-done.10.refs_1_, ...), custom_call_target="tpu_custom_call" | custom-call | flops 603979776 | bytes 524288 | tf_op jit(solution)/shard_map/attend_next/pallas_call | solution.py:334
  23.2 0.0 collective-permute-done.3.refs_0_
  23.2 1.0 %collective-permute-done.7.refs_1_ = bf16[192,256]{1,0:T(8,128)(2,1)S(1)} collective-permute-done((bf16[192,256]{1,0:T(8,128)(2,1)S(1)}, bf16[192,256]{1,0:T(8,128)(2,1)S(1)}, u32[]{:S(2)}, u32[]{:S(2)}) %collective-permute-start.7) | collective-permute-done | bytes 98336 | tf_op jit(solution)/shard_map/ppermute | solution.py:366
  24.2 1.6 %attend_last.1 = bf16[128,2048]{1,0:T(8,128)(2,1)} custom-call(bf16[128,2048]{1,0:T(8,128)(2,1)S(1)} %get-tuple-element.17.q_ref, s32[8,128]{1,0:T(8,128)S(1)} %get-tuple-element.18.limits, bf16[192,256]{1,0:T(8,128)(2,1)S(1)} %collective-permute-done.3.refs_0_, bf16[192,256]{1,0:T(8,128)(2,1)S(1)} %collective-permute-done.7.refs_1_, ...), custom_call_target="tpu_custom_call" | custom-call | flops 402653184 | bytes 524288 | tf_op jit(solution)/shard_map/attend_last/pallas_call | solution.py:334
Async XLA Ops:
  1.1 6.1 %collective-permute-start = (bf16[192,256]{1,0:T(8,128)(2,1)S(1)}, bf16[192,256]{1,0:T(8,128)(2,1)S(1)}, u32[]{:S(2)}, u32[]{:S(2)}) collective-permute-start(bf16[192,256]{1,0:T(8,128)(2,1)S(1)} %get-tuple-element.19.own_keys), channel_id=1, source_target_pairs={{2,6},{6,10},{10,14},{14,12},{12,8},{8,4},{4,0},{0,2},{3,7},{7,11}... | collective-permute-start | bytes 294920 | tf_op jit(solution)/shard_map/ppermute | solution.py:365
  4.1 5.3 %collective-permute-start.4 = (bf16[192,256]{1,0:T(8,128)(2,1)S(1)}, bf16[192,256]{1,0:T(8,128)(2,1)S(1)}, u32[]{:S(2)}, u32[]{:S(2)}) collective-permute-start(bf16[192,256]{1,0:T(8,128)(2,1)S(1)} %get-tuple-element.20.own_values), channel_id=1, source_target_pairs={{6,2},{10,6},{14,10},{12,14},{8,12},{4,8},{0,4},{2,0},{7,3},{11,7}... | collective-permute-start | bytes 294920 | tf_op jit(solution)/shard_map/ppermute | solution.py:366
  4.3 7.2 %collective-permute-start.11 = (bf16[192,256]{1,0:T(8,128)(2,1)S(1)}, bf16[192,256]{1,0:T(8,128)(2,1)S(1)}, u32[]{:S(2)}, u32[]{:S(2)}) collective-permute-start(bf16[192,256]{1,0:T(8,128)(2,1)S(1)} %get-tuple-element.19.own_keys), channel_id=1, source_target_pairs={{6,2},{10,6},{14,10},{12,14},{8,12},{4,8},{0,4},{2,0},{7,3},{11,7}... | collective-permute-start | bytes 294920 | tf_op jit(solution)/shard_map/ppermute | solution.py:369
  6.2 4.8 %collective-permute-start.8 = (bf16[192,256]{1,0:T(8,128)(2,1)S(1)}, bf16[192,256]{1,0:T(8,128)(2,1)S(1)}, u32[]{:S(2)}, u32[]{:S(2)}) collective-permute-start(bf16[192,256]{1,0:T(8,128)(2,1)S(1)} %get-tuple-element.20.own_values), channel_id=1, source_target_pairs={{2,6},{6,10},{10,14},{14,12},{12,8},{8,4},{4,0},{0,2},{3,7},{7,11}... | collective-permute-start | bytes 294920 | tf_op jit(solution)/shard_map/ppermute | solution.py:368
  7.2 5.8 %collective-permute-start.1 = (bf16[192,256]{1,0:T(8,128)(2,1)S(1)}, bf16[192,256]{1,0:T(8,128)(2,1)S(1)}, u32[]{:S(2)}, u32[]{:S(2)}) collective-permute-start(bf16[192,256]{1,0:T(8,128)(2,1)S(1)} %collective-permute-done.refs_0_), channel_id=1, source_target_pairs={{2,6},{6,10},{10,14},{14,12},{12,8},{8,4},{4,0},{0,2},{3,7},{7,11}... | collective-permute-start | bytes 294920 | tf_op jit(solution)/shard_map/ppermute | solution.py:365
  9.4 5.2 %collective-permute-start.5 = (bf16[192,256]{1,0:T(8,128)(2,1)S(1)}, bf16[192,256]{1,0:T(8,128)(2,1)S(1)}, u32[]{:S(2)}, u32[]{:S(2)}) collective-permute-start(bf16[192,256]{1,0:T(8,128)(2,1)S(1)} %collective-permute-done.4.refs_3_), channel_id=1, source_target_pairs={{6,2},{10,6},{14,10},{12,14},{8,12},{4,8},{0,4},{2,0},{7,3},{11,7}... | collective-permute-start | bytes 294920 | tf_op jit(solution)/shard_map/ppermute | solution.py:366
  11.0 4.6 %collective-permute-start.9 = (bf16[192,256]{1,0:T(8,128)(2,1)S(1)}, bf16[192,256]{1,0:T(8,128)(2,1)S(1)}, u32[]{:S(2)}, u32[]{:S(2)}) collective-permute-start(bf16[192,256]{1,0:T(8,128)(2,1)S(1)} %collective-permute-done.8.refs_1_), channel_id=1, source_target_pairs={{2,6},{6,10},{10,14},{14,12},{12,8},{8,4},{4,0},{0,2},{3,7},{7,11}... | collective-permute-start | bytes 294920 | tf_op jit(solution)/shard_map/ppermute | solution.py:368
  11.5 5.3 %collective-permute-start.12 = (bf16[192,256]{1,0:T(8,128)(2,1)S(1)}, bf16[192,256]{1,0:T(8,128)(2,1)S(1)}, u32[]{:S(2)}, u32[]{:S(2)}) collective-permute-start(bf16[192,256]{1,0:T(8,128)(2,1)S(1)} %collective-permute-done.11.refs_2_), channel_id=1, source_target_pairs={{6,2},{10,6},{14,10},{12,14},{8,12},{4,8},{0,4},{2,0},{7,3},{11,7}... | collective-permute-start | bytes 294920 | tf_op jit(solution)/shard_map/ppermute | solution.py:369
  13.0 5.3 %collective-permute-start.2 = (bf16[192,256]{1,0:T(8,128)(2,1)S(1)}, bf16[192,256]{1,0:T(8,128)(2,1)S(1)}, u32[]{:S(2)}, u32[]{:S(2)}) collective-permute-start(bf16[192,256]{1,0:T(8,128)(2,1)S(1)} %collective-permute-done.1.refs_4_), channel_id=1, source_target_pairs={{2,6},{6,10},{10,14},{14,12},{12,8},{8,4},{4,0},{0,2},{3,7},{7,11}... | collective-permute-start | bytes 294920 | tf_op jit(solution)/shard_map/ppermute | solution.py:365
  14.6 5.0 %collective-permute-start.6 = (bf16[192,256]{1,0:T(8,128)(2,1)S(1)}, bf16[192,256]{1,0:T(8,128)(2,1)S(1)}, u32[]{:S(2)}, u32[]{:S(2)}) collective-permute-start(bf16[192,256]{1,0:T(8,128)(2,1)S(1)} %collective-permute-done.5.refs_7_), channel_id=1, source_target_pairs={{6,2},{10,6},{14,10},{12,14},{8,12},{4,8},{0,4},{2,0},{7,3},{11,7}... | collective-permute-start | bytes 294920 | tf_op jit(solution)/shard_map/ppermute | solution.py:366
  15.6 6.2 %collective-permute-start.10 = (bf16[192,256]{1,0:T(8,128)(2,1)S(1)}, bf16[192,256]{1,0:T(8,128)(2,1)S(1)}, u32[]{:S(2)}, u32[]{:S(2)}) collective-permute-start(bf16[192,256]{1,0:T(8,128)(2,1)S(1)} %collective-permute-done.9.refs_5_), channel_id=1, source_target_pairs={{2,6},{6,10},{10,14},{14,12},{12,8},{8,4},{4,0},{0,2},{3,7},{7,11}... | collective-permute-start | bytes 294920 | tf_op jit(solution)/shard_map/ppermute | solution.py:368
  16.8 5.0 %collective-permute-start.13 = (bf16[192,256]{1,0:T(8,128)(2,1)S(1)}, bf16[192,256]{1,0:T(8,128)(2,1)S(1)}, u32[]{:S(2)}, u32[]{:S(2)}) collective-permute-start(bf16[192,256]{1,0:T(8,128)(2,1)S(1)} %collective-permute-done.12.refs_6_), channel_id=1, source_target_pairs={{6,2},{10,6},{14,10},{12,14},{8,12},{4,8},{0,4},{2,0},{7,3},{11,7}... | collective-permute-start | bytes 294920 | tf_op jit(solution)/shard_map/ppermute | solution.py:369
  18.3 4.9 %collective-permute-start.3 = (bf16[192,256]{1,0:T(8,128)(2,1)S(1)}, bf16[192,256]{1,0:T(8,128)(2,1)S(1)}, u32[]{:S(2)}, u32[]{:S(2)}) collective-permute-start(bf16[192,256]{1,0:T(8,128)(2,1)S(1)} %collective-permute-done.2.refs_0_), channel_id=1, source_target_pairs={{2,6},{6,10},{10,14},{14,12},{12,8},{8,4},{4,0},{0,2},{3,7},{7,11}... | collective-permute-start | bytes 294920 | tf_op jit(solution)/shard_map/ppermute | solution.py:365
  19.6 4.6 %collective-permute-start.7 = (bf16[192,256]{1,0:T(8,128)(2,1)S(1)}, bf16[192,256]{1,0:T(8,128)(2,1)S(1)}, u32[]{:S(2)}, u32[]{:S(2)}) collective-permute-start(bf16[192,256]{1,0:T(8,128)(2,1)S(1)} %collective-permute-done.6.refs_3_), channel_id=1, source_target_pairs={{6,2},{10,6},{14,10},{12,14},{8,12},{4,8},{0,4},{2,0},{7,3},{11,7}... | collective-permute-start | bytes 294920 | tf_op jit(solution)/shard_map/ppermute | solution.py:366

commit v15 on v14

--- a/solution.py
+++ b/solution.py
@@ -213,8 +213,11 @@
         done = normalised(acc)
         for i in range(size):
             result[:, (base + i) * HD : (base + i + 1) * HD] = done[i * rows : (i + 1) * rows]
-        for i in range(0, size, COPY_HEADS):
-            sent(base + i).start()
+
+    def send(settled):
+        for base, size in settled:
+            for i in range(0, size, COPY_HEADS):
+                sent(base + i).start()
 
     def wait_all():
         for base in range(0, heads, COPY_HEADS):
@@ -222,6 +225,7 @@
 
     def take_in(begin):
         fine = jnp.ones((8, HD), jnp.float32)
+        settled = []
         for head, at, query, base, size in chunks(q_ref, kv_heads, last):
             top = top_in[at, :]
             acc = acc_in[at, :] + weigh(scores(query, keys[head, begin:]), top, values[head, begin:])
@@ -229,9 +233,12 @@
             fine = jnp.minimum(fine, jnp.min(safe, axis=0))
             if last:
                 settle(base, size, acc)
+                send(settled)
+                settled = [(base, size)]
             else:
                 acc_out[at, :] = acc
                 top_out[at, :] = top
+        send(settled)
         again = jnp.min(fine) < 0.5
         if last:
             wait_all()
@@ -247,6 +254,7 @@
                 acc = acc + weigh(score, top, values[head, begin:])
                 if last:
                     settle(base, size, acc)
+                    send([(base, size)])
                 else:
                     acc_out[at, :] = acc
                     top_out[at, :] = top

time: 26 us -> 26 us (level)
  no operation moved by 1% of the time
where the time goes in v15:
time: 26 us; the launch traced here: 25.9 us
  starting transfers between devices  16 us (62%)
  Pallas kernels  6.15 us (24%)
  waiting for transfers between devices  3.66 us (14%)
    ppermute x4, starting transfers between devices, shards(): key_on = lax.ppermute(key_on, 'ctx', onward)  7.72 us
    ppermute x3, starting transfers between devices, shards(): key_back = lax.ppermute(key_back, 'ctx', backward)  4.36 us
    pallas_call x3, Pallas kernels, attend_next(): pl.pallas_call(functools.partial(next_kernel, rows_of, last, count, sizes...  4.11 us
    ppermute x4, starting transfers between devices, shards(): value_back = lax.ppermute(value_back, 'ctx', backward)  2.19 us
    ppermute x3, starting transfers between devices, shards(): value_on = lax.ppermute(value_on, 'ctx', onward)  1.72 us
    ppermute x3, waiting for transfers between devices, shards(): value_on = lax.ppermute(value_on, 'ctx', onward)  1.68 us
    ppermute x4, waiting for transfers between devices, shards(): value_back = lax.ppermute(value_back, 'ctx', backward)  1.3 us
    pallas_call x1, Pallas kernels, load(): pl.pallas_call(functools.partial(load_kernel, count), out_shape=[jax.Shap...  1.11 us
  transfers between devices with their start and end apart: 14, of which 5 were waited for; matrix products, arithmetic and copies ran while one was open for 0% of the time, Pallas kernels for 13%

profile of v15, /device:TPU:0, one launch (start us, length us, event | category | flops | bytes accessed | tf_op | source)
XLA Modules:
  0.0 25.9 jit_solution(17470222704578571524)
XLA Ops:
  0.0 1.1 %load.1 = (bf16[192,256]{1,0:T(8,128)(2,1)S(1)}, bf16[192,256]{1,0:T(8,128)(2,1)S(1)}, bf16[128,2048]{1,0:T(8,128)(2,1)S(1)}, s32[8,128]{1,0:T(8,128)S(1)}) custom-call(bf16[128,256]{1,0:T(8,128)(2,1)} %win_keys.1, bf16[128,256]{1,0:T(8,128)(2,1)} %win_values.1, bf16[64,256]{1,0:T(8,128)(2,1)} %cache_keys.1, bf16[64,256]{1,0:T(8,128)(2,1)} %cache_values.1, ...), custom_call_target="tpu_custom_call" | custom-call | bytes 393216 | tf_op jit(solution)/shard_map/load/pallas_call | solution.py:81
  1.1 3.0 %collective-permute-start = (bf16[192,256]{1,0:T(8,128)(2,1)S(1)}, bf16[192,256]{1,0:T(8,128)(2,1)S(1)}, u32[]{:S(2)}, u32[]{:S(2)}) collective-permute-start(bf16[192,256]{1,0:T(8,128)(2,1)S(1)} %get-tuple-element.19.own_keys), channel_id=1, source_target_pairs={{2,6},{6,10},{10,14},{14,12},{12,8},{8,4},{4,0},{0,2},{3,7},{7,11}... | collective-permute-start | bytes 294920 | tf_op jit(solution)/shard_map/ppermute | solution.py:373
  4.1 0.2 collective-permute-start.4
  4.3 2.0 %collective-permute-start.11 = (bf16[192,256]{1,0:T(8,128)(2,1)S(1)}, bf16[192,256]{1,0:T(8,128)(2,1)S(1)}, u32[]{:S(2)}, u32[]{:S(2)}) collective-permute-start(bf16[192,256]{1,0:T(8,128)(2,1)S(1)} %get-tuple-element.19.own_keys), channel_id=1, source_target_pairs={{6,2},{10,6},{14,10},{12,14},{8,12},{4,8},{0,4},{2,0},{7,3},{11,7}... | collective-permute-start | bytes 294920 | tf_op jit(solution)/shard_map/ppermute | solution.py:377
  6.2 0.1 collective-permute-start.8
  6.3 0.9 %attend_first.1 = (f32[2048,256]{1,0:T(8,128)S(1)}, f32[2048,128]{1,0:T(8,128)S(1)}) custom-call(bf16[128,2048]{1,0:T(8,128)(2,1)S(1)} %get-tuple-element.17.q_ref, s32[8,128]{1,0:T(8,128)S(1)} %get-tuple-element.18.limits, bf16[192,256]{1,0:T(8,128)(2,1)S(1)} %get-tuple-element.19.own_keys, bf16[192,256]{1,0:T(8,128)(2,1)S(1)} %get-tuple-element.20.own_values), custom_call_target="tpu_custom_call" | custom-call | flops 402653184 | bytes 524288 | tf_op jit(solution)/shard_map/attend_first/pallas_call | solution.py:318
  7.2 0.0 collective-permute-done.refs_0_
  7.2 2.1 %collective-permute-start.1 = (bf16[192,256]{1,0:T(8,128)(2,1)S(1)}, bf16[192,256]{1,0:T(8,128)(2,1)S(1)}, u32[]{:S(2)}, u32[]{:S(2)}) collective-permute-start(bf16[192,256]{1,0:T(8,128)(2,1)S(1)} %collective-permute-done.refs_0_), channel_id=1, source_target_pairs={{2,6},{6,10},{10,14},{14,12},{12,8},{8,4},{4,0},{0,2},{3,7},{7,11}... | collective-permute-start | bytes 294920 | tf_op jit(solution)/shard_map/ppermute | solution.py:373
  9.4 0.0 collective-permute-done.4.refs_3_
  9.4 0.2 collective-permute-start.5
  9.7 1.3 %collective-permute-done.8.refs_1_ = bf16[192,256]{1,0:T(8,128)(2,1)S(1)} collective-permute-done((bf16[192,256]{1,0:T(8,128)(2,1)S(1)}, bf16[192,256]{1,0:T(8,128)(2,1)S(1)}, u32[]{:S(2)}, u32[]{:S(2)}) %collective-permute-start.8) | collective-permute-done | bytes 98336 | tf_op jit(solution)/shard_map/ppermute | solution.py:376
  11.0 0.5 %collective-permute-start.9 = (bf16[192,256]{1,0:T(8,128)(2,1)S(1)}, bf16[192,256]{1,0:T(8,128)(2,1)S(1)}, u32[]{:S(2)}, u32[]{:S(2)}) collective-permute-start(bf16[192,256]{1,0:T(8,128)(2,1)S(1)} %collective-permute-done.8.refs_1_), channel_id=1, source_target_pairs={{2,6},{6,10},{10,14},{14,12},{12,8},{8,4},{4,0},{0,2},{3,7},{7,11}... | collective-permute-start | bytes 294920 | tf_op jit(solution)/shard_map/ppermute | solution.py:376
  11.4 0.0 collective-permute-done.11.refs_2_
  11.5 1.6 %collective-permute-start.12 = (bf16[192,256]{1,0:T(8,128)(2,1)S(1)}, bf16[192,256]{1,0:T(8,128)(2,1)S(1)}, u32[]{:S(2)}, u32[]{:S(2)}) collective-permute-start(bf16[192,256]{1,0:T(8,128)(2,1)S(1)} %collective-permute-done.11.refs_2_), channel_id=1, source_target_pairs={{6,2},{10,6},{14,10},{12,14},{8,12},{4,8},{0,4},{2,0},{7,3},{11,7}... | collective-permute-start | bytes 294920 | tf_op jit(solution)/shard_map/ppermute | solution.py:377
  13.0 0.0 collective-permute-done.1.refs_4_
  13.0 1.6 %collective-permute-start.2 = (bf16[192,256]{1,0:T(8,128)(2,1)S(1)}, bf16[192,256]{1,0:T(8,128)(2,1)S(1)}, u32[]{:S(2)}, u32[]{:S(2)}) collective-permute-start(bf16[192,256]{1,0:T(8,128)(2,1)S(1)} %collective-permute-done.1.refs_4_), channel_id=1, source_target_pairs={{2,6},{6,10},{10,14},{14,12},{12,8},{8,4},{4,0},{0,2},{3,7},{7,11}... | collective-permute-start | bytes 294920 | tf_op jit(solution)/shard_map/ppermute | solution.py:373
  14.6 0.0 collective-permute-done.5.refs_7_
  14.6 0.6 %collective-permute-start.6 = (bf16[192,256]{1,0:T(8,128)(2,1)S(1)}, bf16[192,256]{1,0:T(8,128)(2,1)S(1)}, u32[]{:S(2)}, u32[]{:S(2)}) collective-permute-start(bf16[192,256]{1,0:T(8,128)(2,1)S(1)} %collective-permute-done.5.refs_7_), channel_id=1, source_target_pairs={{6,2},{10,6},{14,10},{12,14},{8,12},{4,8},{0,4},{2,0},{7,3},{11,7}... | collective-permute-start | bytes 294920 | tf_op jit(solution)/shard_map/ppermute | solution.py:374
  15.2 0.4 %collective-permute-done.9.refs_5_ = bf16[192,256]{1,0:T(8,128)(2,1)S(1)} collective-permute-done((bf16[192,256]{1,0:T(8,128)(2,1)S(1)}, bf16[192,256]{1,0:T(8,128)(2,1)S(1)}, u32[]{:S(2)}, u32[]{:S(2)}) %collective-permute-start.9) | collective-permute-done | bytes 98336 | tf_op jit(solution)/shard_map/ppermute | solution.py:376
  15.6 1.2 %collective-permute-start.10 = (bf16[192,256]{1,0:T(8,128)(2,1)S(1)}, bf16[192,256]{1,0:T(8,128)(2,1)S(1)}, u32[]{:S(2)}, u32[]{:S(2)}) collective-permute-start(bf16[192,256]{1,0:T(8,128)(2,1)S(1)} %collective-permute-done.9.refs_5_), channel_id=1, source_target_pairs={{2,6},{6,10},{10,14},{14,12},{12,8},{8,4},{4,0},{0,2},{3,7},{7,11}... | collective-permute-start | bytes 294920 | tf_op jit(solution)/shard_map/ppermute | solution.py:376
  16.8 0.0 collective-permute-done.12.refs_6_
  16.8 0.8 %collective-permute-start.13 = (bf16[192,256]{1,0:T(8,128)(2,1)S(1)}, bf16[192,256]{1,0:T(8,128)(2,1)S(1)}, u32[]{:S(2)}, u32[]{:S(2)}) collective-permute-start(bf16[192,256]{1,0:T(8,128)(2,1)S(1)} %collective-permute-done.12.refs_6_), channel_id=1, source_target_pairs={{6,2},{10,6},{14,10},{12,14},{8,12},{4,8},{0,4},{2,0},{7,3},{11,7}... | collective-permute-start | bytes 294920 | tf_op jit(solution)/shard_map/ppermute | solution.py:377
  17.6 0.7 %collective-permute-done.2.refs_0_ = bf16[192,256]{1,0:T(8,128)(2,1)S(1)} collective-permute-done((bf16[192,256]{1,0:T(8,128)(2,1)S(1)}, bf16[192,256]{1,0:T(8,128)(2,1)S(1)}, u32[]{:S(2)}, u32[]{:S(2)}) %collective-permute-start.2) | collective-permute-done | bytes 98336 | tf_op jit(solution)/shard_map/ppermute | solution.py:373
  18.3 1.0 %collective-permute-start.3 = (bf16[192,256]{1,0:T(8,128)(2,1)S(1)}, bf16[192,256]{1,0:T(8,128)(2,1)S(1)}, u32[]{:S(2)}, u32[]{:S(2)}) collective-permute-start(bf16[192,256]{1,0:T(8,128)(2,1)S(1)} %collective-permute-done.2.refs_0_), channel_id=1, source_target_pairs={{2,6},{6,10},{10,14},{14,12},{12,8},{8,4},{4,0},{0,2},{3,7},{7,11}... | collective-permute-start | bytes 294920 | tf_op jit(solution)/shard_map/ppermute | solution.py:373
  19.3 0.3 %collective-permute-done.6.refs_3_ = bf16[192,256]{1,0:T(8,128)(2,1)S(1)} collective-permute-done((bf16[192,256]{1,0:T(8,128)(2,1)S(1)}, bf16[192,256]{1,0:T(8,128)(2,1)S(1)}, u32[]{:S(2)}, u32[]{:S(2)}) %collective-permute-start.6) | collective-permute-done | bytes 98336 | tf_op jit(solution)/shard_map/ppermute | solution.py:374
  19.6 1.2 %collective-permute-start.7 = (bf16[192,256]{1,0:T(8,128)(2,1)S(1)}, bf16[192,256]{1,0:T(8,128)(2,1)S(1)}, u32[]{:S(2)}, u32[]{:S(2)}) collective-permute-start(bf16[192,256]{1,0:T(8,128)(2,1)S(1)} %collective-permute-done.6.refs_3_), channel_id=1, source_target_pairs={{6,2},{10,6},{14,10},{12,14},{8,12},{4,8},{0,4},{2,0},{7,3},{11,7}... | collective-permute-start | bytes 294920 | tf_op jit(solution)/shard_map/ppermute | solution.py:374
  20.7 1.0 %attend_next.2 = (f32[2048,256]{1,0:T(8,128)S(1)}, f32[2048,128]{1,0:T(8,128)S(1)}) custom-call(bf16[128,2048]{1,0:T(8,128)(2,1)S(1)} %get-tuple-element.17.q_ref, s32[8,128]{1,0:T(8,128)S(1)} %get-tuple-element.18.limits, bf16[192,256]{1,0:T(8,128)(2,1)S(1)} %collective-permute-done.refs_0_, bf16[192,256]{1,0:T(8,128)(2,1)S(1)} %collective-permute-done.8.refs_1_, ...), custom_call_target="tpu_custom_call" | custom-call | flops 1207959552 | bytes 524288 | tf_op jit(solution)/shard_map/attend_next/pallas_call | solution.py:342
  21.8 0.0 collective-permute-done.10.refs_1_
  21.8 0.0 collective-permute-done.13.refs_2_
  21.8 1.4 %attend_next.3 = (f32[2048,256]{1,0:T(8,128)S(1)}, f32[2048,128]{1,0:T(8,128)S(1)}) custom-call(bf16[128,2048]{1,0:T(8,128)(2,1)S(1)} %get-tuple-element.17.q_ref, s32[8,128]{1,0:T(8,128)S(1)} %get-tuple-element.18.limits, bf16[192,256]{1,0:T(8,128)(2,1)S(1)} %collective-permute-done.2.refs_0_, bf16[192,256]{1,0:T(8,128)(2,1)S(1)} %collective-permute-done.10.refs_1_, ...), custom_call_target="tpu_custom_call" | custom-call | flops 603979776 | bytes 524288 | tf_op jit(solution)/shard_map/attend_next/pallas_call | solution.py:342
  23.2 0.0 collective-permute-done.3.refs_0_
  23.2 1.0 %collective-permute-done.7.refs_1_ = bf16[192,256]{1,0:T(8,128)(2,1)S(1)} collective-permute-done((bf16[192,256]{1,0:T(8,128)(2,1)S(1)}, bf16[192,256]{1,0:T(8,128)(2,1)S(1)}, u32[]{:S(2)}, u32[]{:S(2)}) %collective-permute-start.7) | collective-permute-done | bytes 98336 | tf_op jit(solution)/shard_map/ppermute | solution.py:374
  24.2 1.7 %attend_last.1 = bf16[128,2048]{1,0:T(8,128)(2,1)} custom-call(bf16[128,2048]{1,0:T(8,128)(2,1)S(1)} %get-tuple-element.17.q_ref, s32[8,128]{1,0:T(8,128)S(1)} %get-tuple-element.18.limits, bf16[192,256]{1,0:T(8,128)(2,1)S(1)} %collective-permute-done.3.refs_0_, bf16[192,256]{1,0:T(8,128)(2,1)S(1)} %collective-permute-done.7.refs_1_, ...), custom_call_target="tpu_custom_call" | custom-call | flops 402653184 | bytes 524288 | tf_op jit(solution)/shard_map/attend_last/pallas_call | solution.py:342
Async XLA Ops:
  1.1 6.1 %collective-permute-start = (bf16[192,256]{1,0:T(8,128)(2,1)S(1)}, bf16[192,256]{1,0:T(8,128)(2,1)S(1)}, u32[]{:S(2)}, u32[]{:S(2)}) collective-permute-start(bf16[192,256]{1,0:T(8,128)(2,1)S(1)} %get-tuple-element.19.own_keys), channel_id=1, source_target_pairs={{2,6},{6,10},{10,14},{14,12},{12,8},{8,4},{4,0},{0,2},{3,7},{7,11}... | collective-permute-start | bytes 294920 | tf_op jit(solution)/shard_map/ppermute | solution.py:373
  4.1 5.3 %collective-permute-start.4 = (bf16[192,256]{1,0:T(8,128)(2,1)S(1)}, bf16[192,256]{1,0:T(8,128)(2,1)S(1)}, u32[]{:S(2)}, u32[]{:S(2)}) collective-permute-start(bf16[192,256]{1,0:T(8,128)(2,1)S(1)} %get-tuple-element.20.own_values), channel_id=1, source_target_pairs={{6,2},{10,6},{14,10},{12,14},{8,12},{4,8},{0,4},{2,0},{7,3},{11,7}... | collective-permute-start | bytes 294920 | tf_op jit(solution)/shard_map/ppermute | solution.py:374
  4.3 7.2 %collective-permute-start.11 = (bf16[192,256]{1,0:T(8,128)(2,1)S(1)}, bf16[192,256]{1,0:T(8,128)(2,1)S(1)}, u32[]{:S(2)}, u32[]{:S(2)}) collective-permute-start(bf16[192,256]{1,0:T(8,128)(2,1)S(1)} %get-tuple-element.19.own_keys), channel_id=1, source_target_pairs={{6,2},{10,6},{14,10},{12,14},{8,12},{4,8},{0,4},{2,0},{7,3},{11,7}... | collective-permute-start | bytes 294920 | tf_op jit(solution)/shard_map/ppermute | solution.py:377
  6.2 4.8 %collective-permute-start.8 = (bf16[192,256]{1,0:T(8,128)(2,1)S(1)}, bf16[192,256]{1,0:T(8,128)(2,1)S(1)}, u32[]{:S(2)}, u32[]{:S(2)}) collective-permute-start(bf16[192,256]{1,0:T(8,128)(2,1)S(1)} %get-tuple-element.20.own_values), channel_id=1, source_target_pairs={{2,6},{6,10},{10,14},{14,12},{12,8},{8,4},{4,0},{0,2},{3,7},{7,11}... | collective-permute-start | bytes 294920 | tf_op jit(solution)/shard_map/ppermute | solution.py:376
  7.2 5.8 %collective-permute-start.1 = (bf16[192,256]{1,0:T(8,128)(2,1)S(1)}, bf16[192,256]{1,0:T(8,128)(2,1)S(1)}, u32[]{:S(2)}, u32[]{:S(2)}) collective-permute-start(bf16[192,256]{1,0:T(8,128)(2,1)S(1)} %collective-permute-done.refs_0_), channel_id=1, source_target_pairs={{2,6},{6,10},{10,14},{14,12},{12,8},{8,4},{4,0},{0,2},{3,7},{7,11}... | collective-permute-start | bytes 294920 | tf_op jit(solution)/shard_map/ppermute | solution.py:373
  9.4 5.2 %collective-permute-start.5 = (bf16[192,256]{1,0:T(8,128)(2,1)S(1)}, bf16[192,256]{1,0:T(8,128)(2,1)S(1)}, u32[]{:S(2)}, u32[]{:S(2)}) collective-permute-start(bf16[192,256]{1,0:T(8,128)(2,1)S(1)} %collective-permute-done.4.refs_3_), channel_id=1, source_target_pairs={{6,2},{10,6},{14,10},{12,14},{8,12},{4,8},{0,4},{2,0},{7,3},{11,7}... | collective-permute-start | bytes 294920 | tf_op jit(solution)/shard_map/ppermute | solution.py:374
  11.0 4.6 %collective-permute-start.9 = (bf16[192,256]{1,0:T(8,128)(2,1)S(1)}, bf16[192,256]{1,0:T(8,128)(2,1)S(1)}, u32[]{:S(2)}, u32[]{:S(2)}) collective-permute-start(bf16[192,256]{1,0:T(8,128)(2,1)S(1)} %collective-permute-done.8.refs_1_), channel_id=1, source_target_pairs={{2,6},{6,10},{10,14},{14,12},{12,8},{8,4},{4,0},{0,2},{3,7},{7,11}... | collective-permute-start | bytes 294920 | tf_op jit(solution)/shard_map/ppermute | solution.py:376
  11.5 5.3 %collective-permute-start.12 = (bf16[192,256]{1,0:T(8,128)(2,1)S(1)}, bf16[192,256]{1,0:T(8,128)(2,1)S(1)}, u32[]{:S(2)}, u32[]{:S(2)}) collective-permute-start(bf16[192,256]{1,0:T(8,128)(2,1)S(1)} %collective-permute-done.11.refs_2_), channel_id=1, source_target_pairs={{6,2},{10,6},{14,10},{12,14},{8,12},{4,8},{0,4},{2,0},{7,3},{11,7}... | collective-permute-start | bytes 294920 | tf_op jit(solution)/shard_map/ppermute | solution.py:377
  13.0 5.3 %collective-permute-start.2 = (bf16[192,256]{1,0:T(8,128)(2,1)S(1)}, bf16[192,256]{1,0:T(8,128)(2,1)S(1)}, u32[]{:S(2)}, u32[]{:S(2)}) collective-permute-start(bf16[192,256]{1,0:T(8,128)(2,1)S(1)} %collective-permute-done.1.refs_4_), channel_id=1, source_target_pairs={{2,6},{6,10},{10,14},{14,12},{12,8},{8,4},{4,0},{0,2},{3,7},{7,11}... | collective-permute-start | bytes 294920 | tf_op jit(solution)/shard_map/ppermute | solution.py:373
  14.6 5.0 %collective-permute-start.6 = (bf16[192,256]{1,0:T(8,128)(2,1)S(1)}, bf16[192,256]{1,0:T(8,128)(2,1)S(1)}, u32[]{:S(2)}, u32[]{:S(2)}) collective-permute-start(bf16[192,256]{1,0:T(8,128)(2,1)S(1)} %collective-permute-done.5.refs_7_), channel_id=1, source_target_pairs={{6,2},{10,6},{14,10},{12,14},{8,12},{4,8},{0,4},{2,0},{7,3},{11,7}... | collective-permute-start | bytes 294920 | tf_op jit(solution)/shard_map/ppermute | solution.py:374
  15.6 6.2 %collective-permute-start.10 = (bf16[192,256]{1,0:T(8,128)(2,1)S(1)}, bf16[192,256]{1,0:T(8,128)(2,1)S(1)}, u32[]{:S(2)}, u32[]{:S(2)}) collective-permute-start(bf16[192,256]{1,0:T(8,128)(2,1)S(1)} %collective-permute-done.9.refs_5_), channel_id=1, source_target_pairs={{2,6},{6,10},{10,14},{14,12},{12,8},{8,4},{4,0},{0,2},{3,7},{7,11}... | collective-permute-start | bytes 294920 | tf_op jit(solution)/shard_map/ppermute | solution.py:376
  16.8 5.0 %collective-permute-start.13 = (bf16[192,256]{1,0:T(8,128)(2,1)S(1)}, bf16[192,256]{1,0:T(8,128)(2,1)S(1)}, u32[]{:S(2)}, u32[]{:S(2)}) collective-permute-start(bf16[192,256]{1,0:T(8,128)(2,1)S(1)} %collective-permute-done.12.refs_6_), channel_id=1, source_target_pairs={{6,2},{10,6},{14,10},{12,14},{8,12},{4,8},{0,4},{2,0},{7,3},{11,7}... | collective-permute-start | bytes 294920 | tf_op jit(solution)/shard_map/ppermute | solution.py:377
  18.3 4.9 %collective-permute-start.3 = (bf16[192,256]{1,0:T(8,128)(2,1)S(1)}, bf16[192,256]{1,0:T(8,128)(2,1)S(1)}, u32[]{:S(2)}, u32[]{:S(2)}) collective-permute-start(bf16[192,256]{1,0:T(8,128)(2,1)S(1)} %collective-permute-done.2.refs_0_), channel_id=1, source_target_pairs={{2,6},{6,10},{10,14},{14,12},{12,8},{8,4},{4,0},{0,2},{3,7},{7,11}... | collective-permute-start | bytes 294920 | tf_op jit(solution)/shard_map/ppermute | solution.py:373
  19.6 4.6 %collective-permute-start.7 = (bf16[192,256]{1,0:T(8,128)(2,1)S(1)}, bf16[192,256]{1,0:T(8,128)(2,1)S(1)}, u32[]{:S(2)}, u32[]{:S(2)}) collective-permute-start(bf16[192,256]{1,0:T(8,128)(2,1)S(1)} %collective-permute-done.6.refs_3_), channel_id=1, source_target_pairs={{6,2},{10,6},{14,10},{12,14},{8,12},{4,8},{0,4},{2,0},{7,3},{11,7}... | collective-permute-start | bytes 294920 | tf_op jit(solution)/shard_map/ppermute | solution.py:374

commit v16 on v14

--- a/solution.py
+++ b/solution.py
@@ -101,7 +101,7 @@
 
 def ring_offsets(count):
     half = count // 2
-    return [sign * step for step in range(1, half) for sign in (-1, 1)] + [half]
+    return [sign * step for step in range(1, half) for sign in (1, -1)] + [half]
 
 
 def place_window(index, limit_row, own, sizes, limits, key, value, keys, values):
@@ -221,18 +221,17 @@
             sent(base).wait()
 
     def take_in(begin):
-        fine = jnp.ones((8, HD), jnp.float32)
+        grand_total = jnp.zeros((8, HD), jnp.float32)
         for head, at, query, base, size in chunks(q_ref, kv_heads, last):
             top = top_in[at, :]
             acc = acc_in[at, :] + weigh(scores(query, keys[head, begin:]), top, values[head, begin:])
-            safe = jnp.where(acc[:, HD:] < LARGEST_TOTAL, 1.0, 0.0).reshape(-1, 8, HD)
-            fine = jnp.minimum(fine, jnp.min(safe, axis=0))
+            grand_total = grand_total + jnp.sum(acc[:, HD:].reshape(-1, 8, HD), axis=0)
             if last:
                 settle(base, size, acc)
             else:
                 acc_out[at, :] = acc
                 top_out[at, :] = top
-        again = jnp.min(fine) < 0.5
+        again = jnp.min(jnp.where(grand_total < LARGEST_TOTAL, 1.0, 0.0)) < 0.5
         if last:
             wait_all()
 
@@ -347,7 +346,7 @@
     sizes = (win_keys.shape[0], cache_keys.shape[0])
     half = count // 2
     ring = [place_at(p, count) for p in range(count)]
-    onward = [(ring[p], ring[(p + 1) % count]) for p in range(count)]
+    onward = [(ring[p], ring[(p - 1) % count]) for p in range(count)]
     backward = [(b, a) for a, b in onward]
 
     win_keys, win_values, cache_keys, cache_values, valid_counts, first_block, queries = [

time: 26 us -> 26 us (level)
  starting transfers between devices: 16 us -> 16.4 us
  waiting for transfers between devices: 3.66 us -> 3.31 us
    ppermute x4, starting transfers between devices: 7.72 us -> 8.66 us  [shards(): key_on = lax.ppermute(key_on, 'ctx', onward)]
    ppermute x4, starting transfers between devices: 2.19 us -> 1.66 us  [shards(): value_back = lax.ppermute(value_back, 'ctx', backward)]
    ppermute x3, starting transfers between devices: 1.72 us -> 2.07 us  [shards(): value_on = lax.ppermute(value_on, 'ctx', onward)]
    ppermute x3, starting transfers between devices: 4.36 us -> 4.04 us  [shards(): key_back = lax.ppermute(key_back, 'ctx', backward)]
where the time goes in v16:
time: 26 us; the launch traced here: 25.9 us
  starting transfers between devices  16.4 us (63%)
  Pallas kernels  6.06 us (23%)
  waiting for transfers between devices  3.31 us (13%)
    ppermute x4, starting transfers between devices, shards(): key_on = lax.ppermute(key_on, 'ctx', onward)  8.66 us
    ppermute x3, starting transfers between devices, shards(): key_back = lax.ppermute(key_back, 'ctx', backward)  4.04 us
    pallas_call x3, Pallas kernels, attend_next(): pl.pallas_call(functools.partial(next_kernel, rows_of, last, count, sizes...  4.02 us
    ppermute x3, starting transfers between devices, shards(): value_on = lax.ppermute(value_on, 'ctx', onward)  2.07 us
    ppermute x4, starting transfers between devices, shards(): value_back = lax.ppermute(value_back, 'ctx', backward)  1.66 us
    ppermute x3, waiting for transfers between devices, shards(): value_on = lax.ppermute(value_on, 'ctx', onward)  1.63 us
    ppermute x4, waiting for transfers between devices, shards(): value_back = lax.ppermute(value_back, 'ctx', backward)  1.14 us
    pallas_call x1, Pallas kernels, load(): pl.pallas_call(functools.partial(load_kernel, count), out_shape=[jax.Shap...  1.11 us
  transfers between devices with their start and end apart: 14, of which 5 were waited for; matrix products, arithmetic and copies ran while one was open for 0% of the time, Pallas kernels for 13%

profile of v16, /device:TPU:0, one launch (start us, length us, event | category | flops | bytes accessed | tf_op | source)
XLA Modules:
  0.0 25.9 jit_solution(18317384889109600508)
XLA Ops:
  0.0 1.1 %load.1 = (bf16[192,256]{1,0:T(8,128)(2,1)S(1)}, bf16[192,256]{1,0:T(8,128)(2,1)S(1)}, bf16[128,2048]{1,0:T(8,128)(2,1)S(1)}, s32[8,128]{1,0:T(8,128)S(1)}) custom-call(bf16[128,256]{1,0:T(8,128)(2,1)} %win_keys.1, bf16[128,256]{1,0:T(8,128)(2,1)} %win_values.1, bf16[64,256]{1,0:T(8,128)(2,1)} %cache_keys.1, bf16[64,256]{1,0:T(8,128)(2,1)} %cache_values.1, ...), custom_call_target="tpu_custom_call" | custom-call | bytes 393216 | tf_op jit(solution)/shard_map/load/pallas_call | solution.py:81
  1.1 3.1 %collective-permute-start = (bf16[192,256]{1,0:T(8,128)(2,1)S(1)}, bf16[192,256]{1,0:T(8,128)(2,1)S(1)}, u32[]{:S(2)}, u32[]{:S(2)}) collective-permute-start(bf16[192,256]{1,0:T(8,128)(2,1)S(1)} %get-tuple-element.19.own_keys), channel_id=1, source_target_pairs={{2,0},{6,2},{10,6},{14,10},{12,14},{8,12},{4,8},{0,4},{3,1},{7,3},... | collective-permute-start | bytes 294920 | tf_op jit(solution)/shard_map/ppermute | solution.py:364
  4.2 0.0 collective-permute-start.4
  4.2 1.9 %collective-permute-start.11 = (bf16[192,256]{1,0:T(8,128)(2,1)S(1)}, bf16[192,256]{1,0:T(8,128)(2,1)S(1)}, u32[]{:S(2)}, u32[]{:S(2)}) collective-permute-start(bf16[192,256]{1,0:T(8,128)(2,1)S(1)} %get-tuple-element.19.own_keys), channel_id=1, source_target_pairs={{0,2},{2,6},{6,10},{10,14},{14,12},{12,8},{8,4},{4,0},{1,3},{3,7},... | collective-permute-start | bytes 294920 | tf_op jit(solution)/shard_map/ppermute | solution.py:368
  6.1 0.1 collective-permute-start.8
  6.3 0.9 %attend_first.1 = (f32[2048,256]{1,0:T(8,128)S(1)}, f32[2048,128]{1,0:T(8,128)S(1)}) custom-call(bf16[128,2048]{1,0:T(8,128)(2,1)S(1)} %get-tuple-element.17.q_ref, s32[8,128]{1,0:T(8,128)S(1)} %get-tuple-element.18.limits, bf16[192,256]{1,0:T(8,128)(2,1)S(1)} %get-tuple-element.19.own_keys, bf16[192,256]{1,0:T(8,128)(2,1)S(1)} %get-tuple-element.20.own_values), custom_call_target="tpu_custom_call" | custom-call | flops 402653184 | bytes 524288 | tf_op jit(solution)/shard_map/attend_first/pallas_call | solution.py:309
  7.2 0.0 collective-permute-done.refs_0_
  7.2 2.4 %collective-permute-start.1 = (bf16[192,256]{1,0:T(8,128)(2,1)S(1)}, bf16[192,256]{1,0:T(8,128)(2,1)S(1)}, u32[]{:S(2)}, u32[]{:S(2)}) collective-permute-start(bf16[192,256]{1,0:T(8,128)(2,1)S(1)} %collective-permute-done.refs_0_), channel_id=1, source_target_pairs={{2,0},{6,2},{10,6},{14,10},{12,14},{8,12},{4,8},{0,4},{3,1},{7,3},... | collective-permute-start | bytes 294920 | tf_op jit(solution)/shard_map/ppermute | solution.py:364
  9.6 0.0 collective-permute-done.4.refs_3_
  9.6 0.0 collective-permute-start.5
  9.6 1.3 %collective-permute-done.8.refs_1_ = bf16[192,256]{1,0:T(8,128)(2,1)S(1)} collective-permute-done((bf16[192,256]{1,0:T(8,128)(2,1)S(1)}, bf16[192,256]{1,0:T(8,128)(2,1)S(1)}, u32[]{:S(2)}, u32[]{:S(2)}) %collective-permute-start.8) | collective-permute-done | bytes 98336 | tf_op jit(solution)/shard_map/ppermute | solution.py:367
  10.9 0.7 %collective-permute-start.9 = (bf16[192,256]{1,0:T(8,128)(2,1)S(1)}, bf16[192,256]{1,0:T(8,128)(2,1)S(1)}, u32[]{:S(2)}, u32[]{:S(2)}) collective-permute-start(bf16[192,256]{1,0:T(8,128)(2,1)S(1)} %collective-permute-done.8.refs_1_), channel_id=1, source_target_pairs={{2,0},{6,2},{10,6},{14,10},{12,14},{8,12},{4,8},{0,4},{3,1},{7,3},... | collective-permute-start | bytes 294920 | tf_op jit(solution)/shard_map/ppermute | solution.py:367
  11.7 0.0 collective-permute-done.11.refs_2_
  11.7 1.3 %collective-permute-start.12 = (bf16[192,256]{1,0:T(8,128)(2,1)S(1)}, bf16[192,256]{1,0:T(8,128)(2,1)S(1)}, u32[]{:S(2)}, u32[]{:S(2)}) collective-permute-start(bf16[192,256]{1,0:T(8,128)(2,1)S(1)} %collective-permute-done.11.refs_2_), channel_id=1, source_target_pairs={{0,2},{2,6},{6,10},{10,14},{14,12},{12,8},{8,4},{4,0},{1,3},{3,7},... | collective-permute-start | bytes 294920 | tf_op jit(solution)/shard_map/ppermute | solution.py:368
  13.0 0.0 collective-permute-done.1.refs_4_
  13.0 1.7 %collective-permute-start.2 = (bf16[192,256]{1,0:T(8,128)(2,1)S(1)}, bf16[192,256]{1,0:T(8,128)(2,1)S(1)}, u32[]{:S(2)}, u32[]{:S(2)}) collective-permute-start(bf16[192,256]{1,0:T(8,128)(2,1)S(1)} %collective-permute-done.1.refs_4_), channel_id=1, source_target_pairs={{2,0},{6,2},{10,6},{14,10},{12,14},{8,12},{4,8},{0,4},{3,1},{7,3},... | collective-permute-start | bytes 294920 | tf_op jit(solution)/shard_map/ppermute | solution.py:364
  14.7 0.0 collective-permute-done.5.refs_7_
  14.7 0.6 %collective-permute-start.6 = (bf16[192,256]{1,0:T(8,128)(2,1)S(1)}, bf16[192,256]{1,0:T(8,128)(2,1)S(1)}, u32[]{:S(2)}, u32[]{:S(2)}) collective-permute-start(bf16[192,256]{1,0:T(8,128)(2,1)S(1)} %collective-permute-done.5.refs_7_), channel_id=1, source_target_pairs={{0,2},{2,6},{6,10},{10,14},{14,12},{12,8},{8,4},{4,0},{1,3},{3,7},... | collective-permute-start | bytes 294920 | tf_op jit(solution)/shard_map/ppermute | solution.py:365
  15.2 0.3 %collective-permute-done.9.refs_5_ = bf16[192,256]{1,0:T(8,128)(2,1)S(1)} collective-permute-done((bf16[192,256]{1,0:T(8,128)(2,1)S(1)}, bf16[192,256]{1,0:T(8,128)(2,1)S(1)}, u32[]{:S(2)}, u32[]{:S(2)}) %collective-permute-start.9) | collective-permute-done | bytes 98336 | tf_op jit(solution)/shard_map/ppermute | solution.py:367
  15.6 1.2 %collective-permute-start.10 = (bf16[192,256]{1,0:T(8,128)(2,1)S(1)}, bf16[192,256]{1,0:T(8,128)(2,1)S(1)}, u32[]{:S(2)}, u32[]{:S(2)}) collective-permute-start(bf16[192,256]{1,0:T(8,128)(2,1)S(1)} %collective-permute-done.9.refs_5_), channel_id=1, source_target_pairs={{2,0},{6,2},{10,6},{14,10},{12,14},{8,12},{4,8},{0,4},{3,1},{7,3},... | collective-permute-start | bytes 294920 | tf_op jit(solution)/shard_map/ppermute | solution.py:367
  16.8 0.0 collective-permute-done.12.refs_6_
  16.8 0.8 %collective-permute-start.13 = (bf16[192,256]{1,0:T(8,128)(2,1)S(1)}, bf16[192,256]{1,0:T(8,128)(2,1)S(1)}, u32[]{:S(2)}, u32[]{:S(2)}) collective-permute-start(bf16[192,256]{1,0:T(8,128)(2,1)S(1)} %collective-permute-done.12.refs_6_), channel_id=1, source_target_pairs={{0,2},{2,6},{6,10},{10,14},{14,12},{12,8},{8,4},{4,0},{1,3},{3,7},... | collective-permute-start | bytes 294920 | tf_op jit(solution)/shard_map/ppermute | solution.py:368
  17.6 0.5 %collective-permute-done.2.refs_0_ = bf16[192,256]{1,0:T(8,128)(2,1)S(1)} collective-permute-done((bf16[192,256]{1,0:T(8,128)(2,1)S(1)}, bf16[192,256]{1,0:T(8,128)(2,1)S(1)}, u32[]{:S(2)}, u32[]{:S(2)}) %collective-permute-start.2) | collective-permute-done | bytes 98336 | tf_op jit(solution)/shard_map/ppermute | solution.py:364
  18.1 1.5 %collective-permute-start.3 = (bf16[192,256]{1,0:T(8,128)(2,1)S(1)}, bf16[192,256]{1,0:T(8,128)(2,1)S(1)}, u32[]{:S(2)}, u32[]{:S(2)}) collective-permute-start(bf16[192,256]{1,0:T(8,128)(2,1)S(1)} %collective-permute-done.2.refs_0_), channel_id=1, source_target_pairs={{2,0},{6,2},{10,6},{14,10},{12,14},{8,12},{4,8},{0,4},{3,1},{7,3},... | collective-permute-start | bytes 294920 | tf_op jit(solution)/shard_map/ppermute | solution.py:364
  19.6 0.1 collective-permute-done.6.refs_3_
  19.7 1.1 %collective-permute-start.7 = (bf16[192,256]{1,0:T(8,128)(2,1)S(1)}, bf16[192,256]{1,0:T(8,128)(2,1)S(1)}, u32[]{:S(2)}, u32[]{:S(2)}) collective-permute-start(bf16[192,256]{1,0:T(8,128)(2,1)S(1)} %collective-permute-done.6.refs_3_), channel_id=1, source_target_pairs={{0,2},{2,6},{6,10},{10,14},{14,12},{12,8},{8,4},{4,0},{1,3},{3,7},... | collective-permute-start | bytes 294920 | tf_op jit(solution)/shard_map/ppermute | solution.py:365
  20.7 1.0 %attend_next.2 = (f32[2048,256]{1,0:T(8,128)S(1)}, f32[2048,128]{1,0:T(8,128)S(1)}) custom-call(bf16[128,2048]{1,0:T(8,128)(2,1)S(1)} %get-tuple-element.17.q_ref, s32[8,128]{1,0:T(8,128)S(1)} %get-tuple-element.18.limits, bf16[192,256]{1,0:T(8,128)(2,1)S(1)} %collective-permute-done.refs_0_, bf16[192,256]{1,0:T(8,128)(2,1)S(1)} %collective-permute-done.8.refs_1_, ...), custom_call_target="tpu_custom_call" | custom-call | flops 1207959552 | bytes 524288 | tf_op jit(solution)/shard_map/attend_next/pallas_call | solution.py:333
  21.8 0.0 collective-permute-done.10.refs_1_
  21.8 0.0 collective-permute-done.13.refs_2_
  21.8 1.4 %attend_next.3 = (f32[2048,256]{1,0:T(8,128)S(1)}, f32[2048,128]{1,0:T(8,128)S(1)}) custom-call(bf16[128,2048]{1,0:T(8,128)(2,1)S(1)} %get-tuple-element.17.q_ref, s32[8,128]{1,0:T(8,128)S(1)} %get-tuple-element.18.limits, bf16[192,256]{1,0:T(8,128)(2,1)S(1)} %collective-permute-done.2.refs_0_, bf16[192,256]{1,0:T(8,128)(2,1)S(1)} %collective-permute-done.10.refs_1_, ...), custom_call_target="tpu_custom_call" | custom-call | flops 603979776 | bytes 524288 | tf_op jit(solution)/shard_map/attend_next/pallas_call | solution.py:333
  23.2 0.0 collective-permute-done.3.refs_0_
  23.2 1.0 %collective-permute-done.7.refs_1_ = bf16[192,256]{1,0:T(8,128)(2,1)S(1)} collective-permute-done((bf16[192,256]{1,0:T(8,128)(2,1)S(1)}, bf16[192,256]{1,0:T(8,128)(2,1)S(1)}, u32[]{:S(2)}, u32[]{:S(2)}) %collective-permute-start.7) | collective-permute-done | bytes 98336 | tf_op jit(solution)/shard_map/ppermute | solution.py:365
  24.3 1.6 %attend_last.1 = bf16[128,2048]{1,0:T(8,128)(2,1)} custom-call(bf16[128,2048]{1,0:T(8,128)(2,1)S(1)} %get-tuple-element.17.q_ref, s32[8,128]{1,0:T(8,128)S(1)} %get-tuple-element.18.limits, bf16[192,256]{1,0:T(8,128)(2,1)S(1)} %collective-permute-done.3.refs_0_, bf16[192,256]{1,0:T(8,128)(2,1)S(1)} %collective-permute-done.7.refs_1_, ...), custom_call_target="tpu_custom_call" | custom-call | flops 402653184 | bytes 524288 | tf_op jit(solution)/shard_map/attend_last/pallas_call | solution.py:333
Async XLA Ops:
  1.1 6.1 %collective-permute-start = (bf16[192,256]{1,0:T(8,128)(2,1)S(1)}, bf16[192,256]{1,0:T(8,128)(2,1)S(1)}, u32[]{:S(2)}, u32[]{:S(2)}) collective-permute-start(bf16[192,256]{1,0:T(8,128)(2,1)S(1)} %get-tuple-element.19.own_keys), channel_id=1, source_target_pairs={{2,0},{6,2},{10,6},{14,10},{12,14},{8,12},{4,8},{0,4},{3,1},{7,3},... | collective-permute-start | bytes 294920 | tf_op jit(solution)/shard_map/ppermute | solution.py:364
  4.2 5.4 %collective-permute-start.4 = (bf16[192,256]{1,0:T(8,128)(2,1)S(1)}, bf16[192,256]{1,0:T(8,128)(2,1)S(1)}, u32[]{:S(2)}, u32[]{:S(2)}) collective-permute-start(bf16[192,256]{1,0:T(8,128)(2,1)S(1)} %get-tuple-element.20.own_values), channel_id=1, source_target_pairs={{0,2},{2,6},{6,10},{10,14},{14,12},{12,8},{8,4},{4,0},{1,3},{3,7},... | collective-permute-start | bytes 294920 | tf_op jit(solution)/shard_map/ppermute | solution.py:365
  4.2 7.5 %collective-permute-start.11 = (bf16[192,256]{1,0:T(8,128)(2,1)S(1)}, bf16[192,256]{1,0:T(8,128)(2,1)S(1)}, u32[]{:S(2)}, u32[]{:S(2)}) collective-permute-start(bf16[192,256]{1,0:T(8,128)(2,1)S(1)} %get-tuple-element.19.own_keys), channel_id=1, source_target_pairs={{0,2},{2,6},{6,10},{10,14},{14,12},{12,8},{8,4},{4,0},{1,3},{3,7},... | collective-permute-start | bytes 294920 | tf_op jit(solution)/shard_map/ppermute | solution.py:368
  6.1 4.8 %collective-permute-start.8 = (bf16[192,256]{1,0:T(8,128)(2,1)S(1)}, bf16[192,256]{1,0:T(8,128)(2,1)S(1)}, u32[]{:S(2)}, u32[]{:S(2)}) collective-permute-start(bf16[192,256]{1,0:T(8,128)(2,1)S(1)} %get-tuple-element.20.own_values), channel_id=1, source_target_pairs={{2,0},{6,2},{10,6},{14,10},{12,14},{8,12},{4,8},{0,4},{3,1},{7,3},... | collective-permute-start | bytes 294920 | tf_op jit(solution)/shard_map/ppermute | solution.py:367
  7.2 5.8 %collective-permute-start.1 = (bf16[192,256]{1,0:T(8,128)(2,1)S(1)}, bf16[192,256]{1,0:T(8,128)(2,1)S(1)}, u32[]{:S(2)}, u32[]{:S(2)}) collective-permute-start(bf16[192,256]{1,0:T(8,128)(2,1)S(1)} %collective-permute-done.refs_0_), channel_id=1, source_target_pairs={{2,0},{6,2},{10,6},{14,10},{12,14},{8,12},{4,8},{0,4},{3,1},{7,3},... | collective-permute-start | bytes 294920 | tf_op jit(solution)/shard_map/ppermute | solution.py:364
  9.6 5.1 %collective-permute-start.5 = (bf16[192,256]{1,0:T(8,128)(2,1)S(1)}, bf16[192,256]{1,0:T(8,128)(2,1)S(1)}, u32[]{:S(2)}, u32[]{:S(2)}) collective-permute-start(bf16[192,256]{1,0:T(8,128)(2,1)S(1)} %collective-permute-done.4.refs_3_), channel_id=1, source_target_pairs={{0,2},{2,6},{6,10},{10,14},{14,12},{12,8},{8,4},{4,0},{1,3},{3,7},... | collective-permute-start | bytes 294920 | tf_op jit(solution)/shard_map/ppermute | solution.py:365
  10.9 4.6 %collective-permute-start.9 = (bf16[192,256]{1,0:T(8,128)(2,1)S(1)}, bf16[192,256]{1,0:T(8,128)(2,1)S(1)}, u32[]{:S(2)}, u32[]{:S(2)}) collective-permute-start(bf16[192,256]{1,0:T(8,128)(2,1)S(1)} %collective-permute-done.8.refs_1_), channel_id=1, source_target_pairs={{2,0},{6,2},{10,6},{14,10},{12,14},{8,12},{4,8},{0,4},{3,1},{7,3},... | collective-permute-start | bytes 294920 | tf_op jit(solution)/shard_map/ppermute | solution.py:367
  11.7 5.1 %collective-permute-start.12 = (bf16[192,256]{1,0:T(8,128)(2,1)S(1)}, bf16[192,256]{1,0:T(8,128)(2,1)S(1)}, u32[]{:S(2)}, u32[]{:S(2)}) collective-permute-start(bf16[192,256]{1,0:T(8,128)(2,1)S(1)} %collective-permute-done.11.refs_2_), channel_id=1, source_target_pairs={{0,2},{2,6},{6,10},{10,14},{14,12},{12,8},{8,4},{4,0},{1,3},{3,7},... | collective-permute-start | bytes 294920 | tf_op jit(solution)/shard_map/ppermute | solution.py:368
  13.0 5.1 %collective-permute-start.2 = (bf16[192,256]{1,0:T(8,128)(2,1)S(1)}, bf16[192,256]{1,0:T(8,128)(2,1)S(1)}, u32[]{:S(2)}, u32[]{:S(2)}) collective-permute-start(bf16[192,256]{1,0:T(8,128)(2,1)S(1)} %collective-permute-done.1.refs_4_), channel_id=1, source_target_pairs={{2,0},{6,2},{10,6},{14,10},{12,14},{8,12},{4,8},{0,4},{3,1},{7,3},... | collective-permute-start | bytes 294920 | tf_op jit(solution)/shard_map/ppermute | solution.py:364
  14.7 5.0 %collective-permute-start.6 = (bf16[192,256]{1,0:T(8,128)(2,1)S(1)}, bf16[192,256]{1,0:T(8,128)(2,1)S(1)}, u32[]{:S(2)}, u32[]{:S(2)}) collective-permute-start(bf16[192,256]{1,0:T(8,128)(2,1)S(1)} %collective-permute-done.5.refs_7_), channel_id=1, source_target_pairs={{0,2},{2,6},{6,10},{10,14},{14,12},{12,8},{8,4},{4,0},{1,3},{3,7},... | collective-permute-start | bytes 294920 | tf_op jit(solution)/shard_map/ppermute | solution.py:365
  15.6 6.2 %collective-permute-start.10 = (bf16[192,256]{1,0:T(8,128)(2,1)S(1)}, bf16[192,256]{1,0:T(8,128)(2,1)S(1)}, u32[]{:S(2)}, u32[]{:S(2)}) collective-permute-start(bf16[192,256]{1,0:T(8,128)(2,1)S(1)} %collective-permute-done.9.refs_5_), channel_id=1, source_target_pairs={{2,0},{6,2},{10,6},{14,10},{12,14},{8,12},{4,8},{0,4},{3,1},{7,3},... | collective-permute-start | bytes 294920 | tf_op jit(solution)/shard_map/ppermute | solution.py:367
  16.8 5.0 %collective-permute-start.13 = (bf16[192,256]{1,0:T(8,128)(2,1)S(1)}, bf16[192,256]{1,0:T(8,128)(2,1)S(1)}, u32[]{:S(2)}, u32[]{:S(2)}) collective-permute-start(bf16[192,256]{1,0:T(8,128)(2,1)S(1)} %collective-permute-done.12.refs_6_), channel_id=1, source_target_pairs={{0,2},{2,6},{6,10},{10,14},{14,12},{12,8},{8,4},{4,0},{1,3},{3,7},... | collective-permute-start | bytes 294920 | tf_op jit(solution)/shard_map/ppermute | solution.py:368
  18.1 5.1 %collective-permute-start.3 = (bf16[192,256]{1,0:T(8,128)(2,1)S(1)}, bf16[192,256]{1,0:T(8,128)(2,1)S(1)}, u32[]{:S(2)}, u32[]{:S(2)}) collective-permute-start(bf16[192,256]{1,0:T(8,128)(2,1)S(1)} %collective-permute-done.2.refs_0_), channel_id=1, source_target_pairs={{2,0},{6,2},{10,6},{14,10},{12,14},{8,12},{4,8},{0,4},{3,1},{7,3},... | collective-permute-start | bytes 294920 | tf_op jit(solution)/shard_map/ppermute | solution.py:364
  19.7 4.6 %collective-permute-start.7 = (bf16[192,256]{1,0:T(8,128)(2,1)S(1)}, bf16[192,256]{1,0:T(8,128)(2,1)S(1)}, u32[]{:S(2)}, u32[]{:S(2)}) collective-permute-start(bf16[192,256]{1,0:T(8,128)(2,1)S(1)} %collective-permute-done.6.refs_3_), channel_id=1, source_target_pairs={{0,2},{2,6},{6,10},{10,14},{14,12},{12,8},{8,4},{4,0},{1,3},{3,7},... | collective-permute-start | bytes 294920 | tf_op jit(solution)/shard_map/ppermute | solution.py:365

commit v17 on v16

--- a/solution.py
+++ b/solution.py
@@ -104,54 +104,65 @@
     return [sign * step for step in range(1, half) for sign in (1, -1)] + [half]
 
 
-def place_window(index, limit_row, own, sizes, limits, key, value, keys, values):
-    window_rows = sizes[0]
+def place_keys(index, number, limit_row, own, sizes, limits, key, keys):
+    window_rows, cache_rows = sizes
+    at = slice(index * window_rows, (index + 1) * window_rows)
+    cache_at = number * window_rows + index * cache_rows
     if not own:
         row_iota = lax.broadcasted_iota(jnp.int32, (window_rows, HD), 0)
         shown = row_iota < limits[limit_row : limit_row + 1, :]
-    at = slice(index * window_rows, (index + 1) * window_rows)
     for head in range(keys.shape[0]):
         lanes = slice(head * HD, (head + 1) * HD)
-        win_key, win_value = key[:window_rows, lanes], value[:window_rows, lanes]
-        if own:
-            keys[head, at, :] = win_key
-            values[head, at, :HD] = win_value
-            values[head, at, HD:] = jnp.ones((window_rows, HD), jnp.bfloat16)
-        else:
+        win_key = key[:window_rows, lanes]
+        if not own:
             fill = key[window_rows : window_rows + 1, lanes].astype(jnp.float32)
-            keys[head, at, :] = jnp.where(shown, win_key.astype(jnp.float32), fill).astype(jnp.bfloat16)
-            values[head, at, :HD] = jnp.where(shown, win_value.astype(jnp.float32), 0.0).astype(jnp.bfloat16)
-            values[head, at, HD:] = jnp.where(shown, 1.0, 0.0).astype(jnp.bfloat16)
-
-
-def place_cache(index, number, sizes, key, value, keys, values):
+            win_key = jnp.where(shown, win_key.astype(jnp.float32), fill).astype(jnp.bfloat16)
+        keys[head, at, :] = win_key
+        keys[head, cache_at : cache_at + cache_rows, :] = key[window_rows:, lanes]
+        spare = keys.shape[1] - number * sum(sizes)
+        if spare and index == 0:
+            row = key[window_rows : window_rows + 1, lanes].astype(jnp.float32)
+            keys[head, keys.shape[1] - spare :, :] = jnp.broadcast_to(row, (spare, HD)).astype(jnp.bfloat16)
+
+
+def place_values(index, number, limit_row, own, sizes, limits, value, values):
     window_rows, cache_rows = sizes
-    start = number * window_rows + index * cache_rows
-    at = slice(start, start + cache_rows)
-    for head in range(keys.shape[0]):
+    at = slice(index * window_rows, (index + 1) * window_rows)
+    cache_at = number * window_rows + index * cache_rows
+    if not own:
+        row_iota = lax.broadcasted_iota(jnp.int32, (window_rows, HD), 0)
+        shown = row_iota < limits[limit_row : limit_row + 1, :]
+    for head in range(values.shape[0]):
         lanes = slice(head * HD, (head + 1) * HD)
-        keys[head, at, :] = key[window_rows:, lanes]
-        values[head, at, :HD] = value[window_rows:, lanes]
-        values[head, at, HD:] = jnp.ones((cache_rows, HD), jnp.bfloat16)
-
-
-def fill_up(filled, keys, values):
-    spare = keys.shape[1] - filled
-    if spare:
-        for head in range(keys.shape[0]):
-            row = keys[head, filled - 1 : filled, :].astype(jnp.float32)
-            keys[head, filled:, :] = jnp.broadcast_to(row, (spare, HD)).astype(jnp.bfloat16)
-            values[head, filled:, :] = jnp.zeros((spare, 2 * HD), jnp.bfloat16)
+        win_value, ones = value[:window_rows, lanes], jnp.ones((window_rows, HD), jnp.bfloat16)
+        if not own:
+            win_value = jnp.where(shown, win_value.astype(jnp.float32), 0.0).astype(jnp.bfloat16)
+            ones = jnp.where(shown, 1.0, 0.0).astype(jnp.bfloat16)
+        values[head, at, :HD] = win_value
+        values[head, at, HD:] = ones
+        values[head, cache_at : cache_at + cache_rows, :HD] = value[window_rows:, lanes]
+        values[head, cache_at : cache_at + cache_rows, HD:] = jnp.ones((cache_rows, HD), jnp.bfloat16)
+        spare = values.shape[1] - number * sum(sizes)
+        if spare and index == 0:
+            values[head, values.shape[1] - spare :, :] = jnp.zeros((spare, 2 * HD), jnp.bfloat16)
+
+
+def place_block(index, number, limit_row, own, sizes, limits, key, value, keys, values):
+    place_keys(index, number, limit_row, own, sizes, limits, key, keys)
+    place_values(index, number, limit_row, own, sizes, limits, value, values)
 
 
 def scores(query, keys):
     return lax.dot_general(query, keys, (((1,), (1,)), ((), ())), preferred_element_type=jnp.float32)
 
 
+def weights(score, top):
+    lanes = score.shape[1] // HD
+    return jnp.exp2(score * EXP_SCALE - jnp.concatenate([top] * lanes, axis=1)).astype(jnp.bfloat16)
+
+
 def weigh(score, top, values):
-    lanes = score.shape[1] // HD
-    weight = jnp.exp2(score * EXP_SCALE - jnp.concatenate([top] * lanes, axis=1)).astype(jnp.bfloat16)
-    return jnp.dot(weight, values, preferred_element_type=jnp.float32)
+    return jnp.dot(weights(score, top), values, preferred_element_type=jnp.float32)
 
 
 def wide_top(score):
@@ -179,9 +190,7 @@
 
 def first_kernel(count, sizes, q_ref, limits, own_keys, own_values, acc_out, top_out, keys, values):
     window_rows = sizes[0]
-    place_window(0, 0, True, sizes, None, own_keys, own_values, keys, values)
-    place_cache(0, 1, sizes, own_keys, own_values, keys, values)
-    fill_up(sum(sizes), keys, values)
+    place_block(0, 1, 0, True, sizes, None, own_keys, own_values, keys, values)
     rows = q_ref.shape[0]
     key_iota = lax.broadcasted_iota(jnp.int32, (rows, window_rows), 1)
     query_iota = lax.broadcasted_iota(jnp.int32, (rows, window_rows), 0)
@@ -195,69 +204,46 @@
         top_out[at, :] = top
 
 
-def next_kernel(rows_of, last, count, sizes, q_ref, limits, *refs):
+def too_large(grand_total):
+    return jnp.min(jnp.where(grand_total < LARGEST_TOTAL, 1.0, 0.0)) < 0.5
+
+
+def sum_totals(acc):
+    return jnp.sum(acc[:, HD:].reshape(-1, 8, HD), axis=0)
+
+
+def anew(score, before, acc, values):
+    top = jnp.maximum(before, wide_top(score))
+    fade = jnp.exp2(before - top)
+    return top, acc * jnp.concatenate([fade, fade], axis=1) + weigh(score, top, values)
+
+
+def next_kernel(rows_of, count, sizes, q_ref, limits, *refs):
     number = len(rows_of)
     key_refs, value_refs = refs[: 2 * number : 2], refs[1 : 2 * number : 2]
-    if last:
-        acc_in, top_in, out, keys, values, result, sems = refs[2 * number :]
-    else:
-        acc_in, top_in, acc_out, top_out, keys, values = refs[2 * number :]
-    rows, heads = q_ref.shape[0], q_ref.shape[1] // HD
+    acc_in, top_in, acc_out, top_out, keys, values = refs[2 * number :]
     kv_heads = keys.shape[0]
-
-    def sent(base):
-        lanes = slice(base * HD, (base + COPY_HEADS) * HD)
-        return pltpu.make_async_copy(result.at[:, lanes], out.at[:, lanes], sems.at[base // COPY_HEADS])
-
-    def settle(base, size, acc):
-        done = normalised(acc)
-        for i in range(size):
-            result[:, (base + i) * HD : (base + i + 1) * HD] = done[i * rows : (i + 1) * rows]
-        for i in range(0, size, COPY_HEADS):
-            sent(base + i).start()
-
-    def wait_all():
-        for base in range(0, heads, COPY_HEADS):
-            sent(base).wait()
+    for index, row in enumerate(rows_of):
+        place_block(index, number, row, False, sizes, limits, key_refs[index], value_refs[index], keys, values)
 
     def take_in(begin):
         grand_total = jnp.zeros((8, HD), jnp.float32)
-        for head, at, query, base, size in chunks(q_ref, kv_heads, last):
+        for head, at, query, _, _ in chunks(q_ref, kv_heads):
             top = top_in[at, :]
             acc = acc_in[at, :] + weigh(scores(query, keys[head, begin:]), top, values[head, begin:])
-            grand_total = grand_total + jnp.sum(acc[:, HD:].reshape(-1, 8, HD), axis=0)
-            if last:
-                settle(base, size, acc)
-            else:
+            grand_total = grand_total + sum_totals(acc)
+            acc_out[at, :] = acc
+            top_out[at, :] = top
+
+        @pl.when(too_large(grand_total))
+        def _():
+            for head, at, query, _, _ in chunks(q_ref, kv_heads):
+                score = scores(query, keys[head, begin:])
+                top, acc = anew(score, top_in[at, :], acc_in[at, :], values[head, begin:])
                 acc_out[at, :] = acc
                 top_out[at, :] = top
-        again = jnp.min(jnp.where(grand_total < LARGEST_TOTAL, 1.0, 0.0)) < 0.5
-        if last:
-            wait_all()
-
-        @pl.when(again)
-        def _():
-            for head, at, query, base, size in chunks(q_ref, kv_heads, last):
-                score = scores(query, keys[head, begin:])
-                before = top_in[at, :]
-                top = jnp.maximum(before, wide_top(score))
-                fade = jnp.exp2(before - top)
-                acc = acc_in[at, :] * jnp.concatenate([fade, fade], axis=1)
-                acc = acc + weigh(score, top, values[head, begin:])
-                if last:
-                    settle(base, size, acc)
-                else:
-                    acc_out[at, :] = acc
-                    top_out[at, :] = top
-            if last:
-                wait_all()
-
-    for index in range(number):
-        place_cache(index, number, sizes, key_refs[index], value_refs[index], keys, values)
-    fill_up(number * sum(sizes), keys, values)
+
     if number < 4:
-        for index, row in enumerate(rows_of):
-            place_window(index, row, False, sizes, limits, key_refs[index], value_refs[index], keys, values)
         take_in(0)
         return
     me = lax.axis_index("ctx")
@@ -268,13 +254,54 @@
 
     @pl.when(earlier)
     def _():
-        for index, row in enumerate(rows_of):
-            place_window(index, row, False, sizes, limits, key_refs[index], value_refs[index], keys, values)
         take_in(0)
 
     @pl.when(jnp.logical_not(earlier))
     def _():
         take_in(number * sizes[0])
+
+
+def weights_kernel(row, sizes, q_ref, limits, key, top_in, weight_out, keys):
+    place_keys(0, 1, row, False, sizes, limits, key, keys)
+    for head, at, query, _, _ in chunks(q_ref, keys.shape[0]):
+        weight_out[at, :] = weights(scores(query, keys[head]), top_in[at, :])
+
+
+def last_kernel(row, sizes, q_ref, limits, key, value, weight_in, acc_in, top_in, out, keys, values, result, sems):
+    rows, heads = q_ref.shape[0], q_ref.shape[1] // HD
+    kv_heads = keys.shape[0]
+    place_values(0, 1, row, False, sizes, limits, value, values)
+
+    def sent(base):
+        lanes = slice(base * HD, (base + COPY_HEADS) * HD)
+        return pltpu.make_async_copy(result.at[:, lanes], out.at[:, lanes], sems.at[base // COPY_HEADS])
+
+    def settle(base, size, acc):
+        done = normalised(acc)
+        for i in range(size):
+            result[:, (base + i) * HD : (base + i + 1) * HD] = done[i * rows : (i + 1) * rows]
+        for i in range(0, size, COPY_HEADS):
+            sent(base + i).start()
+
+    def wait_all():
+        for base in range(0, heads, COPY_HEADS):
+            sent(base).wait()
+
+    grand_total = jnp.zeros((8, HD), jnp.float32)
+    for head, at, _, base, size in chunks(q_ref, kv_heads, True):
+        acc = acc_in[at, :] + jnp.dot(weight_in[at, :], values[head], preferred_element_type=jnp.float32)
+        grand_total = grand_total + sum_totals(acc)
+        settle(base, size, acc)
+    again = too_large(grand_total)
+    wait_all()
+
+    @pl.when(again)
+    def _():
+        place_keys(0, 1, row, False, sizes, limits, key, keys)
+        for head, at, query, base, size in chunks(q_ref, kv_heads, True):
+            _, acc = anew(scores(query, keys[head]), top_in[at, :], acc_in[at, :], values[head])
+            settle(base, size, acc)
+        wait_all()
 
 
 def kernel_options(queries, total_keys, kv_heads):
@@ -318,28 +345,55 @@
     )
 
 
-def attend_next(pieces, state, last, count, sizes, queries, limits):
+def attend_next(pieces, state, count, sizes, queries, limits):
     rows_of = tuple(piece[0] for piece in pieces)
     blocks = [block for piece in pieces for block in piece[1:]]
     kv_heads = blocks[0].shape[1] // HD
     total_keys = -(-len(pieces) * sum(sizes) // HD) * HD
     vmem = pl.BlockSpec(memory_space=pltpu.VMEM)
     operands = [queries, limits, *blocks, *state]
-    shapes = [jax.ShapeDtypeStruct(queries.shape, queries.dtype)] if last else state_shapes(queries)
-    scratch = room(kv_heads, total_keys)
-    if last:
-        copies = queries.shape[1] // HD // COPY_HEADS
-        scratch += [pltpu.VMEM(queries.shape, queries.dtype), pltpu.SemaphoreType.DMA((copies,))]
-    outs = pl.pallas_call(
-        functools.partial(next_kernel, rows_of, last, count, sizes),
-        out_shape=shapes,
-        in_specs=[vmem] * len(operands),
-        out_specs=[pl.BlockSpec(memory_space=pltpu.HBM)] if last else [vmem] * len(shapes),
-        scratch_shapes=scratch,
-        name="attend_last" if last else "attend_next",
-        **kernel_options(queries, total_keys, kv_heads),
-    )(*operands)
-    return outs[0] if last else tuple(outs)
+    return tuple(
+        pl.pallas_call(
+            functools.partial(next_kernel, rows_of, count, sizes),
+            out_shape=state_shapes(queries),
+            in_specs=[vmem] * len(operands),
+            out_specs=[vmem] * 2,
+            scratch_shapes=room(kv_heads, total_keys),
+            name="attend_next",
+            **kernel_options(queries, total_keys, kv_heads),
+        )(*operands)
+    )
+
+
+def attend_last(piece, state, sizes, queries, limits):
+    row, key, value = piece
+    kv_heads = key.shape[1] // HD
+    total_keys = -(-sum(sizes) // HD) * HD
+    copies = queries.shape[1] // HD // COPY_HEADS
+    vmem = pl.BlockSpec(memory_space=pltpu.VMEM)
+    options = kernel_options(queries, total_keys, kv_heads)
+    weight = pl.pallas_call(
+        functools.partial(weights_kernel, row, sizes),
+        out_shape=jax.ShapeDtypeStruct((state[1].shape[0], total_keys), jnp.bfloat16),
+        in_specs=[vmem] * 4,
+        out_specs=vmem,
+        scratch_shapes=room(kv_heads, total_keys)[:1],
+        name="attend_weights",
+        **options,
+    )(queries, limits, key, state[1])
+    return pl.pallas_call(
+        functools.partial(last_kernel, row, sizes),
+        out_shape=jax.ShapeDtypeStruct(queries.shape, queries.dtype),
+        in_specs=[vmem] * 7,
+        out_specs=pl.BlockSpec(memory_space=pltpu.HBM),
+        scratch_shapes=[
+            *room(kv_heads, total_keys),
+            pltpu.VMEM(queries.shape, queries.dtype),
+            pltpu.SemaphoreType.DMA((copies,)),
+        ],
+        name="attend_last",
+        **options,
+    )(queries, limits, key, value, weight, *state)
 
 
 def shards(count, queries, win_keys, win_values, cache_keys, cache_values, valid_counts, first_block):
@@ -375,9 +429,9 @@
             state = (state[0], top)
     for begin in range(0, half - 2, 2):
         pieces = [piece for step in arrived[begin : min(begin + 2, half - 2)] for piece in step]
-        state = attend_next(pieces, state, False, count, sizes, near, limits)
-    state = attend_next(arrived[half - 2], state, False, count, sizes, near, limits)
-    return attend_next(arrived[half - 1], state, True, count, sizes, near, limits)
+        state = attend_next(pieces, state, count, sizes, near, limits)
+    state = attend_next(arrived[half - 2], state, count, sizes, near, limits)
+    return attend_last(arrived[half - 1][0], state, sizes, near, limits)
 
 
 def solution(mesh):

time: 26 us -> 25.7 us (0.988)
  waiting for transfers between devices: 3.31 us -> 2.72 us
  Pallas kernels: 6.06 us -> 6.36 us
    ppermute x4, waiting for transfers between devices: 1.14 us -> 0.57 us  [shards(): value_back = lax.ppermute(value_back, 'ctx', backward)]
    pallas_call x3 -> x4, Pallas kernels: 4.02 us -> 4.32 us  [the longest x2 2.53 us: attend_next(): pl.pallas_call(functools.partial(next_kernel, rows_of, count, sizes), out...]
  transfers between devices with their start and end apart: 14 -> 14, of which waited for: 5 -> 5; matrix products, arithmetic and copies ran while one was open for 0% -> 0% of each run, Pallas kernels for 13% -> 15%
where the time goes in v17:
time: 25.7 us; the launch traced here: 25.6 us
  starting transfers between devices  16.4 us (64%)
  Pallas kernels  6.36 us (25%)
  waiting for transfers between devices  2.72 us (11%)
    ppermute x4, starting transfers between devices, shards(): key_on = lax.ppermute(key_on, 'ctx', onward)  8.67 us
    ppermute x3, starting transfers between devices, shards(): key_back = lax.ppermute(key_back, 'ctx', backward)  4.04 us
    pallas_call x2, Pallas kernels, attend_next(): pl.pallas_call(functools.partial(next_kernel, rows_of, count, sizes), out...  2.53 us
    ppermute x3, starting transfers between devices, shards(): value_on = lax.ppermute(value_on, 'ctx', onward)  2.07 us
    ppermute x4, starting transfers between devices, shards(): value_back = lax.ppermute(value_back, 'ctx', backward)  1.66 us
    ppermute x3, waiting for transfers between devices, shards(): value_on = lax.ppermute(value_on, 'ctx', onward)  1.63 us
    pallas_call x1, Pallas kernels, attend_last(): pl.pallas_call(functools.partial(last_kernel, row, sizes), out_shape=jax....  1.32 us
    pallas_call x1, Pallas kernels, load(): pl.pallas_call(functools.partial(load_kernel, count), out_shape=[jax.Shap...  1.11 us
  transfers between devices with their start and end apart: 14, of which 5 were waited for; matrix products, arithmetic and copies ran while one was open for 0% of the time, Pallas kernels for 15%

profile of v17, /device:TPU:0, one launch (start us, length us, event | category | flops | bytes accessed | tf_op | source)
XLA Modules:
  0.0 25.6 jit_solution(500280628510331877)
XLA Ops:
  0.0 1.1 %load.1 = (bf16[192,256]{1,0:T(8,128)(2,1)S(1)}, bf16[192,256]{1,0:T(8,128)(2,1)S(1)}, bf16[128,2048]{1,0:T(8,128)(2,1)S(1)}, s32[8,128]{1,0:T(8,128)S(1)}) custom-call(bf16[128,256]{1,0:T(8,128)(2,1)} %win_keys.1, bf16[128,256]{1,0:T(8,128)(2,1)} %win_values.1, bf16[64,256]{1,0:T(8,128)(2,1)} %cache_keys.1, bf16[64,256]{1,0:T(8,128)(2,1)} %cache_values.1, ...), custom_call_target="tpu_custom_call" | custom-call | bytes 393216 | tf_op jit(solution)/shard_map/load/pallas_call | solution.py:81
  1.1 3.1 %collective-permute-start = (bf16[192,256]{1,0:T(8,128)(2,1)S(1)}, bf16[192,256]{1,0:T(8,128)(2,1)S(1)}, u32[]{:S(2)}, u32[]{:S(2)}) collective-permute-start(bf16[192,256]{1,0:T(8,128)(2,1)S(1)} %get-tuple-element.19.own_keys), channel_id=1, source_target_pairs={{2,0},{6,2},{10,6},{14,10},{12,14},{8,12},{4,8},{0,4},{3,1},{7,3},... | collective-permute-start | bytes 294920 | tf_op jit(solution)/shard_map/ppermute | solution.py:418
  4.2 0.0 collective-permute-start.4
  4.2 1.9 %collective-permute-start.11 = (bf16[192,256]{1,0:T(8,128)(2,1)S(1)}, bf16[192,256]{1,0:T(8,128)(2,1)S(1)}, u32[]{:S(2)}, u32[]{:S(2)}) collective-permute-start(bf16[192,256]{1,0:T(8,128)(2,1)S(1)} %get-tuple-element.19.own_keys), channel_id=1, source_target_pairs={{0,2},{2,6},{6,10},{10,14},{14,12},{12,8},{8,4},{4,0},{1,3},{3,7},... | collective-permute-start | bytes 294920 | tf_op jit(solution)/shard_map/ppermute | solution.py:422
  6.1 0.1 collective-permute-start.8
  6.3 0.9 %attend_first.1 = (f32[2048,256]{1,0:T(8,128)S(1)}, f32[2048,128]{1,0:T(8,128)S(1)}) custom-call(bf16[128,2048]{1,0:T(8,128)(2,1)S(1)} %get-tuple-element.17.q_ref, s32[8,128]{1,0:T(8,128)S(1)} %get-tuple-element.18.limits, bf16[192,256]{1,0:T(8,128)(2,1)S(1)} %get-tuple-element.19.own_keys, bf16[192,256]{1,0:T(8,128)(2,1)S(1)} %get-tuple-element.20.own_values), custom_call_target="tpu_custom_call" | custom-call | flops 402653184 | bytes 524288 | tf_op jit(solution)/shard_map/attend_first/pallas_call | solution.py:336
  7.2 0.0 collective-permute-done.refs_0_
  7.2 2.4 %collective-permute-start.1 = (bf16[192,256]{1,0:T(8,128)(2,1)S(1)}, bf16[192,256]{1,0:T(8,128)(2,1)S(1)}, u32[]{:S(2)}, u32[]{:S(2)}) collective-permute-start(bf16[192,256]{1,0:T(8,128)(2,1)S(1)} %collective-permute-done.refs_0_), channel_id=1, source_target_pairs={{2,0},{6,2},{10,6},{14,10},{12,14},{8,12},{4,8},{0,4},{3,1},{7,3},... | collective-permute-start | bytes 294920 | tf_op jit(solution)/shard_map/ppermute | solution.py:418
  9.6 0.0 collective-permute-done.4.refs_3_
  9.6 0.0 collective-permute-start.5
  9.6 1.3 %collective-permute-done.8.refs_1_ = bf16[192,256]{1,0:T(8,128)(2,1)S(1)} collective-permute-done((bf16[192,256]{1,0:T(8,128)(2,1)S(1)}, bf16[192,256]{1,0:T(8,128)(2,1)S(1)}, u32[]{:S(2)}, u32[]{:S(2)}) %collective-permute-start.8) | collective-permute-done | bytes 98336 | tf_op jit(solution)/shard_map/ppermute | solution.py:421
  10.9 0.7 %collective-permute-start.9 = (bf16[192,256]{1,0:T(8,128)(2,1)S(1)}, bf16[192,256]{1,0:T(8,128)(2,1)S(1)}, u32[]{:S(2)}, u32[]{:S(2)}) collective-permute-start(bf16[192,256]{1,0:T(8,128)(2,1)S(1)} %collective-permute-done.8.refs_1_), channel_id=1, source_target_pairs={{2,0},{6,2},{10,6},{14,10},{12,14},{8,12},{4,8},{0,4},{3,1},{7,3},... | collective-permute-start | bytes 294920 | tf_op jit(solution)/shard_map/ppermute | solution.py:421
  11.7 0.0 collective-permute-done.11.refs_2_
  11.7 1.3 %collective-permute-start.12 = (bf16[192,256]{1,0:T(8,128)(2,1)S(1)}, bf16[192,256]{1,0:T(8,128)(2,1)S(1)}, u32[]{:S(2)}, u32[]{:S(2)}) collective-permute-start(bf16[192,256]{1,0:T(8,128)(2,1)S(1)} %collective-permute-done.11.refs_2_), channel_id=1, source_target_pairs={{0,2},{2,6},{6,10},{10,14},{14,12},{12,8},{8,4},{4,0},{1,3},{3,7},... | collective-permute-start | bytes 294920 | tf_op jit(solution)/shard_map/ppermute | solution.py:422
  13.0 0.0 collective-permute-done.1.refs_4_
  13.0 1.7 %collective-permute-start.2 = (bf16[192,256]{1,0:T(8,128)(2,1)S(1)}, bf16[192,256]{1,0:T(8,128)(2,1)S(1)}, u32[]{:S(2)}, u32[]{:S(2)}) collective-permute-start(bf16[192,256]{1,0:T(8,128)(2,1)S(1)} %collective-permute-done.1.refs_4_), channel_id=1, source_target_pairs={{2,0},{6,2},{10,6},{14,10},{12,14},{8,12},{4,8},{0,4},{3,1},{7,3},... | collective-permute-start | bytes 294920 | tf_op jit(solution)/shard_map/ppermute | solution.py:418
  14.7 0.0 collective-permute-done.5.refs_7_
  14.7 0.6 %collective-permute-start.6 = (bf16[192,256]{1,0:T(8,128)(2,1)S(1)}, bf16[192,256]{1,0:T(8,128)(2,1)S(1)}, u32[]{:S(2)}, u32[]{:S(2)}) collective-permute-start(bf16[192,256]{1,0:T(8,128)(2,1)S(1)} %collective-permute-done.5.refs_7_), channel_id=1, source_target_pairs={{0,2},{2,6},{6,10},{10,14},{14,12},{12,8},{8,4},{4,0},{1,3},{3,7},... | collective-permute-start | bytes 294920 | tf_op jit(solution)/shard_map/ppermute | solution.py:419
  15.2 0.3 %collective-permute-done.9.refs_5_ = bf16[192,256]{1,0:T(8,128)(2,1)S(1)} collective-permute-done((bf16[192,256]{1,0:T(8,128)(2,1)S(1)}, bf16[192,256]{1,0:T(8,128)(2,1)S(1)}, u32[]{:S(2)}, u32[]{:S(2)}) %collective-permute-start.9) | collective-permute-done | bytes 98336 | tf_op jit(solution)/shard_map/ppermute | solution.py:421
  15.6 1.2 %collective-permute-start.10 = (bf16[192,256]{1,0:T(8,128)(2,1)S(1)}, bf16[192,256]{1,0:T(8,128)(2,1)S(1)}, u32[]{:S(2)}, u32[]{:S(2)}) collective-permute-start(bf16[192,256]{1,0:T(8,128)(2,1)S(1)} %collective-permute-done.9.refs_5_), channel_id=1, source_target_pairs={{2,0},{6,2},{10,6},{14,10},{12,14},{8,12},{4,8},{0,4},{3,1},{7,3},... | collective-permute-start | bytes 294920 | tf_op jit(solution)/shard_map/ppermute | solution.py:421
  16.8 0.0 collective-permute-done.12.refs_6_
  16.8 0.8 %collective-permute-start.13 = (bf16[192,256]{1,0:T(8,128)(2,1)S(1)}, bf16[192,256]{1,0:T(8,128)(2,1)S(1)}, u32[]{:S(2)}, u32[]{:S(2)}) collective-permute-start(bf16[192,256]{1,0:T(8,128)(2,1)S(1)} %collective-permute-done.12.refs_6_), channel_id=1, source_target_pairs={{0,2},{2,6},{6,10},{10,14},{14,12},{12,8},{8,4},{4,0},{1,3},{3,7},... | collective-permute-start | bytes 294920 | tf_op jit(solution)/shard_map/ppermute | solution.py:422
  17.6 0.5 %collective-permute-done.2.refs_0_ = bf16[192,256]{1,0:T(8,128)(2,1)S(1)} collective-permute-done((bf16[192,256]{1,0:T(8,128)(2,1)S(1)}, bf16[192,256]{1,0:T(8,128)(2,1)S(1)}, u32[]{:S(2)}, u32[]{:S(2)}) %collective-permute-start.2) | collective-permute-done | bytes 98336 | tf_op jit(solution)/shard_map/ppermute | solution.py:418
  18.1 1.5 %collective-permute-start.3 = (bf16[192,256]{1,0:T(8,128)(2,1)S(1)}, bf16[192,256]{1,0:T(8,128)(2,1)S(1)}, u32[]{:S(2)}, u32[]{:S(2)}) collective-permute-start(bf16[192,256]{1,0:T(8,128)(2,1)S(1)} %collective-permute-done.2.refs_0_), channel_id=1, source_target_pairs={{2,0},{6,2},{10,6},{14,10},{12,14},{8,12},{4,8},{0,4},{3,1},{7,3},... | collective-permute-start | bytes 294920 | tf_op jit(solution)/shard_map/ppermute | solution.py:418
  19.6 0.1 collective-permute-done.6.refs_3_
  19.7 1.1 %collective-permute-start.7 = (bf16[192,256]{1,0:T(8,128)(2,1)S(1)}, bf16[192,256]{1,0:T(8,128)(2,1)S(1)}, u32[]{:S(2)}, u32[]{:S(2)}) collective-permute-start(bf16[192,256]{1,0:T(8,128)(2,1)S(1)} %collective-permute-done.6.refs_3_), channel_id=1, source_target_pairs={{0,2},{2,6},{6,10},{10,14},{14,12},{12,8},{8,4},{4,0},{1,3},{3,7},... | collective-permute-start | bytes 294920 | tf_op jit(solution)/shard_map/ppermute | solution.py:419
  20.7 1.1 %attend_next.2 = (f32[2048,256]{1,0:T(8,128)S(1)}, f32[2048,128]{1,0:T(8,128)S(1)}) custom-call(bf16[128,2048]{1,0:T(8,128)(2,1)S(1)} %get-tuple-element.17.q_ref, s32[8,128]{1,0:T(8,128)S(1)} %get-tuple-element.18.limits, bf16[192,256]{1,0:T(8,128)(2,1)S(1)} %collective-permute-done.refs_0_, bf16[192,256]{1,0:T(8,128)(2,1)S(1)} %collective-permute-done.8.refs_1_, ...), custom_call_target="tpu_custom_call" | custom-call | flops 1207959552 | bytes 524288 | tf_op jit(solution)/shard_map/attend_next/pallas_call | solution.py:356
  21.9 0.0 collective-permute-done.10.refs_1_
  21.9 0.0 collective-permute-done.13.refs_2_
  21.9 1.4 %attend_next.3 = (f32[2048,256]{1,0:T(8,128)S(1)}, f32[2048,128]{1,0:T(8,128)S(1)}) custom-call(bf16[128,2048]{1,0:T(8,128)(2,1)S(1)} %get-tuple-element.17.q_ref, s32[8,128]{1,0:T(8,128)S(1)} %get-tuple-element.18.limits, bf16[192,256]{1,0:T(8,128)(2,1)S(1)} %collective-permute-done.2.refs_0_, bf16[192,256]{1,0:T(8,128)(2,1)S(1)} %collective-permute-done.10.refs_1_, ...), custom_call_target="tpu_custom_call" | custom-call | flops 603979776 | bytes 524288 | tf_op jit(solution)/shard_map/attend_next/pallas_call | solution.py:356
  23.3 0.0 collective-permute-done.3.key
  23.3 0.5 %attend_weights.1.weight_in = bf16[2048,256]{1,0:T(8,128)(2,1)S(1)} custom-call(bf16[128,2048]{1,0:T(8,128)(2,1)S(1)} %get-tuple-element.17.q_ref, s32[8,128]{1,0:T(8,128)S(1)} %get-tuple-element.18.limits, bf16[192,256]{1,0:T(8,128)(2,1)S(1)} %collective-permute-done.3.key, f32[2048,128]{1,0:T(8,128)S(1)} %get-tuple-element.27.top_in), custom_call_target="tpu_custom_call" | custom-call | flops 402653184 | bytes 524288 | tf_op jit(solution)/shard_map/attend_weights/pallas_call | solution.py:375
  23.8 0.5 %collective-permute-done.7.value = bf16[192,256]{1,0:T(8,128)(2,1)S(1)} collective-permute-done((bf16[192,256]{1,0:T(8,128)(2,1)S(1)}, bf16[192,256]{1,0:T(8,128)(2,1)S(1)}, u32[]{:S(2)}, u32[]{:S(2)}) %collective-permute-start.7) | collective-permute-done | bytes 98336 | tf_op jit(solution)/shard_map/ppermute | solution.py:419
  24.3 1.3 %attend_last.1 = bf16[128,2048]{1,0:T(8,128)(2,1)} custom-call(bf16[128,2048]{1,0:T(8,128)(2,1)S(1)} %get-tuple-element.17.q_ref, s32[8,128]{1,0:T(8,128)S(1)} %get-tuple-element.18.limits, bf16[192,256]{1,0:T(8,128)(2,1)S(1)} %collective-permute-done.3.key, bf16[192,256]{1,0:T(8,128)(2,1)S(1)} %collective-permute-done.7.value, ...), custom_call_target="tpu_custom_call" | custom-call | flops 402653184 | bytes 524288 | tf_op jit(solution)/shard_map/attend_last/pallas_call | solution.py:384
Async XLA Ops:
  1.1 6.1 %collective-permute-start = (bf16[192,256]{1,0:T(8,128)(2,1)S(1)}, bf16[192,256]{1,0:T(8,128)(2,1)S(1)}, u32[]{:S(2)}, u32[]{:S(2)}) collective-permute-start(bf16[192,256]{1,0:T(8,128)(2,1)S(1)} %get-tuple-element.19.own_keys), channel_id=1, source_target_pairs={{2,0},{6,2},{10,6},{14,10},{12,14},{8,12},{4,8},{0,4},{3,1},{7,3},... | collective-permute-start | bytes 294920 | tf_op jit(solution)/shard_map/ppermute | solution.py:418
  4.2 5.4 %collective-permute-start.4 = (bf16[192,256]{1,0:T(8,128)(2,1)S(1)}, bf16[192,256]{1,0:T(8,128)(2,1)S(1)}, u32[]{:S(2)}, u32[]{:S(2)}) collective-permute-start(bf16[192,256]{1,0:T(8,128)(2,1)S(1)} %get-tuple-element.20.own_values), channel_id=1, source_target_pairs={{0,2},{2,6},{6,10},{10,14},{14,12},{12,8},{8,4},{4,0},{1,3},{3,7},... | collective-permute-start | bytes 294920 | tf_op jit(solution)/shard_map/ppermute | solution.py:419
  4.2 7.5 %collective-permute-start.11 = (bf16[192,256]{1,0:T(8,128)(2,1)S(1)}, bf16[192,256]{1,0:T(8,128)(2,1)S(1)}, u32[]{:S(2)}, u32[]{:S(2)}) collective-permute-start(bf16[192,256]{1,0:T(8,128)(2,1)S(1)} %get-tuple-element.19.own_keys), channel_id=1, source_target_pairs={{0,2},{2,6},{6,10},{10,14},{14,12},{12,8},{8,4},{4,0},{1,3},{3,7},... | collective-permute-start | bytes 294920 | tf_op jit(solution)/shard_map/ppermute | solution.py:422
  6.1 4.8 %collective-permute-start.8 = (bf16[192,256]{1,0:T(8,128)(2,1)S(1)}, bf16[192,256]{1,0:T(8,128)(2,1)S(1)}, u32[]{:S(2)}, u32[]{:S(2)}) collective-permute-start(bf16[192,256]{1,0:T(8,128)(2,1)S(1)} %get-tuple-element.20.own_values), channel_id=1, source_target_pairs={{2,0},{6,2},{10,6},{14,10},{12,14},{8,12},{4,8},{0,4},{3,1},{7,3},... | collective-permute-start | bytes 294920 | tf_op jit(solution)/shard_map/ppermute | solution.py:421
  7.2 5.8 %collective-permute-start.1 = (bf16[192,256]{1,0:T(8,128)(2,1)S(1)}, bf16[192,256]{1,0:T(8,128)(2,1)S(1)}, u32[]{:S(2)}, u32[]{:S(2)}) collective-permute-start(bf16[192,256]{1,0:T(8,128)(2,1)S(1)} %collective-permute-done.refs_0_), channel_id=1, source_target_pairs={{2,0},{6,2},{10,6},{14,10},{12,14},{8,12},{4,8},{0,4},{3,1},{7,3},... | collective-permute-start | bytes 294920 | tf_op jit(solution)/shard_map/ppermute | solution.py:418
  9.6 5.1 %collective-permute-start.5 = (bf16[192,256]{1,0:T(8,128)(2,1)S(1)}, bf16[192,256]{1,0:T(8,128)(2,1)S(1)}, u32[]{:S(2)}, u32[]{:S(2)}) collective-permute-start(bf16[192,256]{1,0:T(8,128)(2,1)S(1)} %collective-permute-done.4.refs_3_), channel_id=1, source_target_pairs={{0,2},{2,6},{6,10},{10,14},{14,12},{12,8},{8,4},{4,0},{1,3},{3,7},... | collective-permute-start | bytes 294920 | tf_op jit(solution)/shard_map/ppermute | solution.py:419
  10.9 4.6 %collective-permute-start.9 = (bf16[192,256]{1,0:T(8,128)(2,1)S(1)}, bf16[192,256]{1,0:T(8,128)(2,1)S(1)}, u32[]{:S(2)}, u32[]{:S(2)}) collective-permute-start(bf16[192,256]{1,0:T(8,128)(2,1)S(1)} %collective-permute-done.8.refs_1_), channel_id=1, source_target_pairs={{2,0},{6,2},{10,6},{14,10},{12,14},{8,12},{4,8},{0,4},{3,1},{7,3},... | collective-permute-start | bytes 294920 | tf_op jit(solution)/shard_map/ppermute | solution.py:421
  11.7 5.1 %collective-permute-start.12 = (bf16[192,256]{1,0:T(8,128)(2,1)S(1)}, bf16[192,256]{1,0:T(8,128)(2,1)S(1)}, u32[]{:S(2)}, u32[]{:S(2)}) collective-permute-start(bf16[192,256]{1,0:T(8,128)(2,1)S(1)} %collective-permute-done.11.refs_2_), channel_id=1, source_target_pairs={{0,2},{2,6},{6,10},{10,14},{14,12},{12,8},{8,4},{4,0},{1,3},{3,7},... | collective-permute-start | bytes 294920 | tf_op jit(solution)/shard_map/ppermute | solution.py:422
  13.0 5.1 %collective-permute-start.2 = (bf16[192,256]{1,0:T(8,128)(2,1)S(1)}, bf16[192,256]{1,0:T(8,128)(2,1)S(1)}, u32[]{:S(2)}, u32[]{:S(2)}) collective-permute-start(bf16[192,256]{1,0:T(8,128)(2,1)S(1)} %collective-permute-done.1.refs_4_), channel_id=1, source_target_pairs={{2,0},{6,2},{10,6},{14,10},{12,14},{8,12},{4,8},{0,4},{3,1},{7,3},... | collective-permute-start | bytes 294920 | tf_op jit(solution)/shard_map/ppermute | solution.py:418
  14.7 5.0 %collective-permute-start.6 = (bf16[192,256]{1,0:T(8,128)(2,1)S(1)}, bf16[192,256]{1,0:T(8,128)(2,1)S(1)}, u32[]{:S(2)}, u32[]{:S(2)}) collective-permute-start(bf16[192,256]{1,0:T(8,128)(2,1)S(1)} %collective-permute-done.5.refs_7_), channel_id=1, source_target_pairs={{0,2},{2,6},{6,10},{10,14},{14,12},{12,8},{8,4},{4,0},{1,3},{3,7},... | collective-permute-start | bytes 294920 | tf_op jit(solution)/shard_map/ppermute | solution.py:419
  15.6 6.3 %collective-permute-start.10 = (bf16[192,256]{1,0:T(8,128)(2,1)S(1)}, bf16[192,256]{1,0:T(8,128)(2,1)S(1)}, u32[]{:S(2)}, u32[]{:S(2)}) collective-permute-start(bf16[192,256]{1,0:T(8,128)(2,1)S(1)} %collective-permute-done.9.refs_5_), channel_id=1, source_target_pairs={{2,0},{6,2},{10,6},{14,10},{12,14},{8,12},{4,8},{0,4},{3,1},{7,3},... | collective-permute-start | bytes 294920 | tf_op jit(solution)/shard_map/ppermute | solution.py:421
  16.8 5.1 %collective-permute-start.13 = (bf16[192,256]{1,0:T(8,128)(2,1)S(1)}, bf16[192,256]{1,0:T(8,128)(2,1)S(1)}, u32[]{:S(2)}, u32[]{:S(2)}) collective-permute-start(bf16[192,256]{1,0:T(8,128)(2,1)S(1)} %collective-permute-done.12.refs_6_), channel_id=1, source_target_pairs={{0,2},{2,6},{6,10},{10,14},{14,12},{12,8},{8,4},{4,0},{1,3},{3,7},... | collective-permute-start | bytes 294920 | tf_op jit(solution)/shard_map/ppermute | solution.py:422
  18.1 5.2 %collective-permute-start.3 = (bf16[192,256]{1,0:T(8,128)(2,1)S(1)}, bf16[192,256]{1,0:T(8,128)(2,1)S(1)}, u32[]{:S(2)}, u32[]{:S(2)}) collective-permute-start(bf16[192,256]{1,0:T(8,128)(2,1)S(1)} %collective-permute-done.2.refs_0_), channel_id=1, source_target_pairs={{2,0},{6,2},{10,6},{14,10},{12,14},{8,12},{4,8},{0,4},{3,1},{7,3},... | collective-permute-start | bytes 294920 | tf_op jit(solution)/shard_map/ppermute | solution.py:418
  19.7 4.6 %collective-permute-start.7 = (bf16[192,256]{1,0:T(8,128)(2,1)S(1)}, bf16[192,256]{1,0:T(8,128)(2,1)S(1)}, u32[]{:S(2)}, u32[]{:S(2)}) collective-permute-start(bf16[192,256]{1,0:T(8,128)(2,1)S(1)} %collective-permute-done.6.refs_3_), channel_id=1, source_target_pairs={{0,2},{2,6},{6,10},{10,14},{14,12},{12,8},{8,4},{4,0},{1,3},{3,7},... | collective-permute-start | bytes 294920 | tf_op jit(solution)/shard_map/ppermute | solution.py:419

commit v18 on v17

--- a/solution.py
+++ b/solution.py
@@ -218,7 +218,7 @@
     return top, acc * jnp.concatenate([fade, fade], axis=1) + weigh(score, top, values)
 
 
-def next_kernel(rows_of, count, sizes, q_ref, limits, *refs):
+def next_kernel(rows_of, sizes, q_ref, limits, *refs):
     number = len(rows_of)
     key_refs, value_refs = refs[: 2 * number : 2], refs[1 : 2 * number : 2]
     acc_in, top_in, acc_out, top_out, keys, values = refs[2 * number :]
@@ -226,39 +226,20 @@
     for index, row in enumerate(rows_of):
         place_block(index, number, row, False, sizes, limits, key_refs[index], value_refs[index], keys, values)
 
-    def take_in(begin):
-        grand_total = jnp.zeros((8, HD), jnp.float32)
+    grand_total = jnp.zeros((8, HD), jnp.float32)
+    for head, at, query, _, _ in chunks(q_ref, kv_heads):
+        top = top_in[at, :]
+        acc = acc_in[at, :] + weigh(scores(query, keys[head]), top, values[head])
+        grand_total = grand_total + sum_totals(acc)
+        acc_out[at, :] = acc
+        top_out[at, :] = top
+
+    @pl.when(too_large(grand_total))
+    def _():
         for head, at, query, _, _ in chunks(q_ref, kv_heads):
-            top = top_in[at, :]
-            acc = acc_in[at, :] + weigh(scores(query, keys[head, begin:]), top, values[head, begin:])
-            grand_total = grand_total + sum_totals(acc)
+            top, acc = anew(scores(query, keys[head]), top_in[at, :], acc_in[at, :], values[head])
             acc_out[at, :] = acc
             top_out[at, :] = top
-
-        @pl.when(too_large(grand_total))
-        def _():
-            for head, at, query, _, _ in chunks(q_ref, kv_heads):
-                score = scores(query, keys[head, begin:])
-                top, acc = anew(score, top_in[at, :], acc_in[at, :], values[head, begin:])
-                acc_out[at, :] = acc
-                top_out[at, :] = top
-
-    if number < 4:
-        take_in(0)
-        return
-    me = lax.axis_index("ctx")
-    position = position_of(me, count)
-    offsets = ring_offsets(count)
-    places = [place_at(lax.rem(position + offsets[row] + count, count), count) for row in rows_of]
-    earlier = functools.reduce(jnp.logical_or, [place < me for place in places])
-
-    @pl.when(earlier)
-    def _():
-        take_in(0)
-
-    @pl.when(jnp.logical_not(earlier))
-    def _():
-        take_in(number * sizes[0])
 
 
 def weights_kernel(row, sizes, q_ref, limits, key, top_in, weight_out, keys):
@@ -345,7 +326,7 @@
     )
 
 
-def attend_next(pieces, state, count, sizes, queries, limits):
+def attend_next(pieces, state, sizes, queries, limits):
     rows_of = tuple(piece[0] for piece in pieces)
     blocks = [block for piece in pieces for block in piece[1:]]
     kv_heads = blocks[0].shape[1] // HD
@@ -354,7 +335,7 @@
     operands = [queries, limits, *blocks, *state]
     return tuple(
         pl.pallas_call(
-            functools.partial(next_kernel, rows_of, count, sizes),
+            functools.partial(next_kernel, rows_of, sizes),
             out_shape=state_shapes(queries),
             in_specs=[vmem] * len(operands),
             out_specs=[vmem] * 2,
@@ -418,6 +399,10 @@
         key_on = lax.ppermute(key_on, "ctx", onward)
         value_back = lax.ppermute(value_back, "ctx", backward)
         if step < half:
+            if step > 2:
+                state = attend_next(arrived[step - 3], state, sizes, near, limits)
+                value_on, top = lax.optimization_barrier((value_on, state[1]))
+                state = (state[0], top)
             value_on = lax.ppermute(value_on, "ctx", onward)
             key_back = lax.ppermute(key_back, "ctx", backward)
             row = 2 * (step - 1)
@@ -427,10 +412,8 @@
         if step == 1:
             key_on, top = lax.optimization_barrier((key_on, state[1]))
             state = (state[0], top)
-    for begin in range(0, half - 2, 2):
-        pieces = [piece for step in arrived[begin : min(begin + 2, half - 2)] for piece in step]
-        state = attend_next(pieces, state, count, sizes, near, limits)
-    state = attend_next(arrived[half - 2], state, count, sizes, near, limits)
+    for pieces in arrived[max(half - 3, 0) : half - 1]:
+        state = attend_next(pieces, state, sizes, near, limits)
     return attend_last(arrived[half - 1][0], state, sizes, near, limits)
 
 

time: 25.7 us -> 26.4 us (1.027)
  Pallas kernels: 6.36 us -> 8.03 us
  starting transfers between devices: 16.4 us -> 15.2 us
    ppermute x3, starting transfers between devices: 2.07 us -> 5.85 us  [shards(): value_on = lax.ppermute(value_on, 'ctx', onward)]
    ppermute x3, starting transfers between devices: 4.04 us -> 0.34 us  [shards(): key_back = lax.ppermute(key_back, 'ctx', backward)]
    pallas_call x2 -> x3, Pallas kernels: 2.53 us -> 4.21 us  [attend_next(): pl.pallas_call(functools.partial(next_kernel, rows_of, sizes), out_shape=...]
    ppermute x3, waiting for transfers between devices: 1.63 us -> 0.01 us  [shards(): value_on = lax.ppermute(value_on, 'ctx', onward)]
    ppermute x4, starting transfers between devices: 1.66 us -> 0.53 us  [shards(): value_back = lax.ppermute(value_back, 'ctx', backward)]
    ppermute x4, waiting for transfers between devices: 0.51 us -> 1.47 us  [shards(): key_on = lax.ppermute(key_on, 'ctx', onward)]
    ppermute x3, waiting for transfers between devices: 0.01 us -> 0.85 us  [shards(): key_back = lax.ppermute(key_back, 'ctx', backward)]
  transfers between devices with their start and end apart: 14 -> 14, of which waited for: 5 -> 6; matrix products, arithmetic and copies ran while one was open for 0% -> 0% of each run, Pallas kernels for 15% -> 21%
where the time goes in v18:
time: 26.4 us; the launch traced here: 26.3 us
  starting transfers between devices  15.2 us (58%)
  Pallas kernels  8.03 us (30%)
  waiting for transfers between devices  2.94 us (11%)
    ppermute x4, starting transfers between devices, shards(): key_on = lax.ppermute(key_on, 'ctx', onward)  8.52 us
    ppermute x3, starting transfers between devices, shards(): value_on = lax.ppermute(value_on, 'ctx', onward)  5.85 us
    pallas_call x3, Pallas kernels, attend_next(): pl.pallas_call(functools.partial(next_kernel, rows_of, sizes), out_shape=...  4.21 us
    ppermute x4, waiting for transfers between devices, shards(): key_on = lax.ppermute(key_on, 'ctx', onward)  1.47 us
    pallas_call x1, Pallas kernels, attend_last(): pl.pallas_call(functools.partial(last_kernel, row, sizes), out_shape=jax....  1.32 us
    pallas_call x1, Pallas kernels, load(): pl.pallas_call(functools.partial(load_kernel, count), out_shape=[jax.Shap...  1.11 us
    pallas_call x1, Pallas kernels, attend_first(): pl.pallas_call(functools.partial(first_kernel, count, sizes), out_shape=s...  0.93 us
    ppermute x3, waiting for transfers between devices, shards(): key_back = lax.ppermute(key_back, 'ctx', backward)  0.85 us
  transfers between devices with their start and end apart: 14, of which 6 were waited for; matrix products, arithmetic and copies ran while one was open for 0% of the time, Pallas kernels for 21%

profile of v18, /device:TPU:0, one launch (start us, length us, event | category | flops | bytes accessed | tf_op | source)
XLA Modules:
  0.0 26.3 jit_solution(506287869808004854)
XLA Ops:
  0.0 1.1 %load.1 = (bf16[192,256]{1,0:T(8,128)(2,1)S(1)}, bf16[192,256]{1,0:T(8,128)(2,1)S(1)}, bf16[128,2048]{1,0:T(8,128)(2,1)S(1)}, s32[8,128]{1,0:T(8,128)S(1)}) custom-call(bf16[128,256]{1,0:T(8,128)(2,1)} %win_keys.1, bf16[128,256]{1,0:T(8,128)(2,1)} %win_values.1, bf16[64,256]{1,0:T(8,128)(2,1)} %cache_keys.1, bf16[64,256]{1,0:T(8,128)(2,1)} %cache_values.1, ...), custom_call_target="tpu_custom_call" | custom-call | bytes 393216 | tf_op jit(solution)/shard_map/load/pallas_call | solution.py:81
  1.1 3.1 %collective-permute-start = (bf16[192,256]{1,0:T(8,128)(2,1)S(1)}, bf16[192,256]{1,0:T(8,128)(2,1)S(1)}, u32[]{:S(2)}, u32[]{:S(2)}) collective-permute-start(bf16[192,256]{1,0:T(8,128)(2,1)S(1)} %get-tuple-element.23.own_keys), channel_id=1, source_target_pairs={{2,0},{6,2},{10,6},{14,10},{12,14},{8,12},{4,8},{0,4},{3,1},{7,3},... | collective-permute-start | bytes 294920 | tf_op jit(solution)/shard_map/ppermute | solution.py:399
  4.2 0.0 collective-permute-start.4
  4.2 2.0 %collective-permute-start.8 = (bf16[192,256]{1,0:T(8,128)(2,1)S(1)}, bf16[192,256]{1,0:T(8,128)(2,1)S(1)}, u32[]{:S(2)}, u32[]{:S(2)}) collective-permute-start(bf16[192,256]{1,0:T(8,128)(2,1)S(1)} %get-tuple-element.24.own_values), channel_id=1, source_target_pairs={{2,0},{6,2},{10,6},{14,10},{12,14},{8,12},{4,8},{0,4},{3,1},{7,3},... | collective-permute-start | bytes 294920 | tf_op jit(solution)/shard_map/ppermute | solution.py:406
  6.2 0.0 collective-permute-start.10
  6.2 0.9 %attend_first.1 = (f32[2048,256]{1,0:T(8,128)S(1)}, f32[2048,128]{1,0:T(8,128)S(1)}) custom-call(bf16[128,2048]{1,0:T(8,128)(2,1)S(1)} %get-tuple-element.21.q_ref, s32[8,128]{1,0:T(8,128)S(1)} %get-tuple-element.22.limits, bf16[192,256]{1,0:T(8,128)(2,1)S(1)} %get-tuple-element.23.own_keys, bf16[192,256]{1,0:T(8,128)(2,1)S(1)} %get-tuple-element.24.own_values), custom_call_target="tpu_custom_call" | custom-call | flops 402653184 | bytes 524288 | tf_op jit(solution)/shard_map/attend_first/pallas_call | solution.py:317
  7.2 0.3 %collective-permute-done.refs_0_ = bf16[192,256]{1,0:T(8,128)(2,1)S(1)} collective-permute-done((bf16[192,256]{1,0:T(8,128)(2,1)S(1)}, bf16[192,256]{1,0:T(8,128)(2,1)S(1)}, u32[]{:S(2)}, u32[]{:S(2)}) %collective-permute-start) | collective-permute-done | bytes 98336 | tf_op jit(solution)/shard_map/ppermute | solution.py:399
  7.5 2.0 %collective-permute-start.1 = (bf16[192,256]{1,0:T(8,128)(2,1)S(1)}, bf16[192,256]{1,0:T(8,128)(2,1)S(1)}, u32[]{:S(2)}, u32[]{:S(2)}) collective-permute-start(bf16[192,256]{1,0:T(8,128)(2,1)S(1)} %collective-permute-done.refs_0_), channel_id=1, source_target_pairs={{2,0},{6,2},{10,6},{14,10},{12,14},{8,12},{4,8},{0,4},{3,1},{7,3},... | collective-permute-start | bytes 294920 | tf_op jit(solution)/shard_map/ppermute | solution.py:399
  9.5 0.3 %collective-permute-done.4.refs_3_ = bf16[192,256]{1,0:T(8,128)(2,1)S(1)} collective-permute-done((bf16[192,256]{1,0:T(8,128)(2,1)S(1)}, bf16[192,256]{1,0:T(8,128)(2,1)S(1)}, u32[]{:S(2)}, u32[]{:S(2)}) %collective-permute-start.4) | collective-permute-done | bytes 98336 | tf_op jit(solution)/shard_map/ppermute | solution.py:400
  9.8 0.0 collective-permute-start.5
  9.8 0.0 collective-permute-done.8.refs_1_
  9.8 2.0 %collective-permute-start.9 = (bf16[192,256]{1,0:T(8,128)(2,1)S(1)}, bf16[192,256]{1,0:T(8,128)(2,1)S(1)}, u32[]{:S(2)}, u32[]{:S(2)}) collective-permute-start(bf16[192,256]{1,0:T(8,128)(2,1)S(1)} %collective-permute-done.8.refs_1_), channel_id=1, source_target_pairs={{2,0},{6,2},{10,6},{14,10},{12,14},{8,12},{4,8},{0,4},{3,1},{7,3},... | collective-permute-start | bytes 294920 | tf_op jit(solution)/shard_map/ppermute | solution.py:406
  11.8 0.0 collective-permute-done.10.refs_2_
  11.8 0.0 collective-permute-start.12
  11.9 1.1 %collective-permute-done.1.refs_0_ = bf16[192,256]{1,0:T(8,128)(2,1)S(1)} collective-permute-done((bf16[192,256]{1,0:T(8,128)(2,1)S(1)}, bf16[192,256]{1,0:T(8,128)(2,1)S(1)}, u32[]{:S(2)}, u32[]{:S(2)}) %collective-permute-start.1) | collective-permute-done | bytes 98336 | tf_op jit(solution)/shard_map/ppermute | solution.py:399
  13.0 1.7 %collective-permute-start.2 = (bf16[192,256]{1,0:T(8,128)(2,1)S(1)}, bf16[192,256]{1,0:T(8,128)(2,1)S(1)}, u32[]{:S(2)}, u32[]{:S(2)}) collective-permute-start(bf16[192,256]{1,0:T(8,128)(2,1)S(1)} %collective-permute-done.1.refs_0_), channel_id=1, source_target_pairs={{2,0},{6,2},{10,6},{14,10},{12,14},{8,12},{4,8},{0,4},{3,1},{7,3},... | collective-permute-start | bytes 294920 | tf_op jit(solution)/shard_map/ppermute | solution.py:399
  14.7 0.0 collective-permute-done.5.refs_3_
  14.7 0.3 %collective-permute-start.6 = (bf16[192,256]{1,0:T(8,128)(2,1)S(1)}, bf16[192,256]{1,0:T(8,128)(2,1)S(1)}, u32[]{:S(2)}, u32[]{:S(2)}) collective-permute-start(bf16[192,256]{1,0:T(8,128)(2,1)S(1)} %collective-permute-done.5.refs_3_), channel_id=1, source_target_pairs={{0,2},{2,6},{6,10},{10,14},{14,12},{12,8},{8,4},{4,0},{1,3},{3,7},... | collective-permute-start | bytes 294920 | tf_op jit(solution)/shard_map/ppermute | solution.py:400
  15.0 1.4 %attend_next.3 = (f32[2048,256]{1,0:T(8,128)S(1)}, f32[2048,128]{1,0:T(8,128)S(1)}) custom-call(bf16[128,2048]{1,0:T(8,128)(2,1)S(1)} %get-tuple-element.21.q_ref, s32[8,128]{1,0:T(8,128)S(1)} %get-tuple-element.22.limits, bf16[192,256]{1,0:T(8,128)(2,1)S(1)} %collective-permute-done.refs_0_, bf16[192,256]{1,0:T(8,128)(2,1)S(1)} %collective-permute-done.8.refs_1_, ...), custom_call_target="tpu_custom_call" | custom-call | flops 603979776 | bytes 524288 | tf_op jit(solution)/shard_map/attend_next/pallas_call | solution.py:337
  16.4 0.0 collective-permute-done.9.refs_1_
  16.4 1.8 %collective-permute-start.11 = (bf16[192,256]{1,0:T(8,128)(2,1)S(1)}, bf16[192,256]{1,0:T(8,128)(2,1)S(1)}, u32[]{:S(2)}, u32[]{:S(2)}) collective-permute-start(bf16[192,256]{1,0:T(8,128)(2,1)S(1)} %collective-permute-done.9.refs_1_), channel_id=1, source_target_pairs={{2,0},{6,2},{10,6},{14,10},{12,14},{8,12},{4,8},{0,4},{3,1},{7,3},... | collective-permute-start | bytes 294920 | tf_op jit(solution)/shard_map/ppermute | solution.py:406
  18.2 0.0 collective-permute-done.12.refs_2_
  18.2 0.3 %collective-permute-start.13 = (bf16[192,256]{1,0:T(8,128)(2,1)S(1)}, bf16[192,256]{1,0:T(8,128)(2,1)S(1)}, u32[]{:S(2)}, u32[]{:S(2)}) collective-permute-start(bf16[192,256]{1,0:T(8,128)(2,1)S(1)} %collective-permute-done.12.refs_2_), channel_id=1, source_target_pairs={{0,2},{2,6},{6,10},{10,14},{14,12},{12,8},{8,4},{4,0},{1,3},{3,7},... | collective-permute-start | bytes 294920 | tf_op jit(solution)/shard_map/ppermute | solution.py:407
  18.6 0.0 collective-permute-done.2.refs_0_
  18.6 1.7 %collective-permute-start.3 = (bf16[192,256]{1,0:T(8,128)(2,1)S(1)}, bf16[192,256]{1,0:T(8,128)(2,1)S(1)}, u32[]{:S(2)}, u32[]{:S(2)}) collective-permute-start(bf16[192,256]{1,0:T(8,128)(2,1)S(1)} %collective-permute-done.2.refs_0_), channel_id=1, source_target_pairs={{2,0},{6,2},{10,6},{14,10},{12,14},{8,12},{4,8},{0,4},{3,1},{7,3},... | collective-permute-start | bytes 294920 | tf_op jit(solution)/shard_map/ppermute | solution.py:399
  20.3 0.1 collective-permute-done.6.refs_3_
  20.4 0.2 collective-permute-start.7
  20.6 1.4 %attend_next.4 = (f32[2048,256]{1,0:T(8,128)S(1)}, f32[2048,128]{1,0:T(8,128)S(1)}) custom-call(bf16[128,2048]{1,0:T(8,128)(2,1)S(1)} %get-tuple-element.21.q_ref, s32[8,128]{1,0:T(8,128)S(1)} %get-tuple-element.22.limits, bf16[192,256]{1,0:T(8,128)(2,1)S(1)} %collective-permute-done.1.refs_0_, bf16[192,256]{1,0:T(8,128)(2,1)S(1)} %collective-permute-done.9.refs_1_, ...), custom_call_target="tpu_custom_call" | custom-call | flops 603979776 | bytes 524288 | tf_op jit(solution)/shard_map/attend_next/pallas_call | solution.py:337
  22.0 0.0 collective-permute-done.11.refs_1_
  22.0 0.8 %collective-permute-done.13.refs_2_ = bf16[192,256]{1,0:T(8,128)(2,1)S(1)} collective-permute-done((bf16[192,256]{1,0:T(8,128)(2,1)S(1)}, bf16[192,256]{1,0:T(8,128)(2,1)S(1)}, u32[]{:S(2)}, u32[]{:S(2)}) %collective-permute-start.13) | collective-permute-done | bytes 98336 | tf_op jit(solution)/shard_map/ppermute | solution.py:407
  22.9 1.4 %attend_next.5 = (f32[2048,256]{1,0:T(8,128)S(1)}, f32[2048,128]{1,0:T(8,128)S(1)}) custom-call(bf16[128,2048]{1,0:T(8,128)(2,1)S(1)} %get-tuple-element.21.q_ref, s32[8,128]{1,0:T(8,128)S(1)} %get-tuple-element.22.limits, bf16[192,256]{1,0:T(8,128)(2,1)S(1)} %collective-permute-done.2.refs_0_, bf16[192,256]{1,0:T(8,128)(2,1)S(1)} %collective-permute-done.11.refs_1_, ...), custom_call_target="tpu_custom_call" | custom-call | flops 603979776 | bytes 524288 | tf_op jit(solution)/shard_map/attend_next/pallas_call | solution.py:337
  24.3 0.0 collective-permute-done.3.key
  24.3 0.5 %attend_weights.1.weight_in = bf16[2048,256]{1,0:T(8,128)(2,1)S(1)} custom-call(bf16[128,2048]{1,0:T(8,128)(2,1)S(1)} %get-tuple-element.21.q_ref, s32[8,128]{1,0:T(8,128)S(1)} %get-tuple-element.22.limits, bf16[192,256]{1,0:T(8,128)(2,1)S(1)} %collective-permute-done.3.key, f32[2048,128]{1,0:T(8,128)S(1)} %get-tuple-element.35.top_in), custom_call_target="tpu_custom_call" | custom-call | flops 402653184 | bytes 524288 | tf_op jit(solution)/shard_map/attend_weights/pallas_call | solution.py:356
  24.8 0.2 collective-permute-done.7.value
  25.0 1.3 %attend_last.1 = bf16[128,2048]{1,0:T(8,128)(2,1)} custom-call(bf16[128,2048]{1,0:T(8,128)(2,1)S(1)} %get-tuple-element.21.q_ref, s32[8,128]{1,0:T(8,128)S(1)} %get-tuple-element.22.limits, bf16[192,256]{1,0:T(8,128)(2,1)S(1)} %collective-permute-done.3.key, bf16[192,256]{1,0:T(8,128)(2,1)S(1)} %collective-permute-done.7.value, ...), custom_call_target="tpu_custom_call" | custom-call | flops 402653184 | bytes 524288 | tf_op jit(solution)/shard_map/attend_last/pallas_call | solution.py:365
Async XLA Ops:
  1.1 6.4 %collective-permute-start = (bf16[192,256]{1,0:T(8,128)(2,1)S(1)}, bf16[192,256]{1,0:T(8,128)(2,1)S(1)}, u32[]{:S(2)}, u32[]{:S(2)}) collective-permute-start(bf16[192,256]{1,0:T(8,128)(2,1)S(1)} %get-tuple-element.23.own_keys), channel_id=1, source_target_pairs={{2,0},{6,2},{10,6},{14,10},{12,14},{8,12},{4,8},{0,4},{3,1},{7,3},... | collective-permute-start | bytes 294920 | tf_op jit(solution)/shard_map/ppermute | solution.py:399
  4.2 5.6 %collective-permute-start.4 = (bf16[192,256]{1,0:T(8,128)(2,1)S(1)}, bf16[192,256]{1,0:T(8,128)(2,1)S(1)}, u32[]{:S(2)}, u32[]{:S(2)}) collective-permute-start(bf16[192,256]{1,0:T(8,128)(2,1)S(1)} %get-tuple-element.24.own_values), channel_id=1, source_target_pairs={{0,2},{2,6},{6,10},{10,14},{14,12},{12,8},{8,4},{4,0},{1,3},{3,7},... | collective-permute-start | bytes 294920 | tf_op jit(solution)/shard_map/ppermute | solution.py:400
  4.2 5.6 %collective-permute-start.8 = (bf16[192,256]{1,0:T(8,128)(2,1)S(1)}, bf16[192,256]{1,0:T(8,128)(2,1)S(1)}, u32[]{:S(2)}, u32[]{:S(2)}) collective-permute-start(bf16[192,256]{1,0:T(8,128)(2,1)S(1)} %get-tuple-element.24.own_values), channel_id=1, source_target_pairs={{2,0},{6,2},{10,6},{14,10},{12,14},{8,12},{4,8},{0,4},{3,1},{7,3},... | collective-permute-start | bytes 294920 | tf_op jit(solution)/shard_map/ppermute | solution.py:406
  6.2 5.6 %collective-permute-start.10 = (bf16[192,256]{1,0:T(8,128)(2,1)S(1)}, bf16[192,256]{1,0:T(8,128)(2,1)S(1)}, u32[]{:S(2)}, u32[]{:S(2)}) collective-permute-start(bf16[192,256]{1,0:T(8,128)(2,1)S(1)} %get-tuple-element.23.own_keys), channel_id=1, source_target_pairs={{0,2},{2,6},{6,10},{10,14},{14,12},{12,8},{8,4},{4,0},{1,3},{3,7},... | collective-permute-start | bytes 294920 | tf_op jit(solution)/shard_map/ppermute | solution.py:407
  7.5 5.5 %collective-permute-start.1 = (bf16[192,256]{1,0:T(8,128)(2,1)S(1)}, bf16[192,256]{1,0:T(8,128)(2,1)S(1)}, u32[]{:S(2)}, u32[]{:S(2)}) collective-permute-start(bf16[192,256]{1,0:T(8,128)(2,1)S(1)} %collective-permute-done.refs_0_), channel_id=1, source_target_pairs={{2,0},{6,2},{10,6},{14,10},{12,14},{8,12},{4,8},{0,4},{3,1},{7,3},... | collective-permute-start | bytes 294920 | tf_op jit(solution)/shard_map/ppermute | solution.py:399
  9.8 4.9 %collective-permute-start.5 = (bf16[192,256]{1,0:T(8,128)(2,1)S(1)}, bf16[192,256]{1,0:T(8,128)(2,1)S(1)}, u32[]{:S(2)}, u32[]{:S(2)}) collective-permute-start(bf16[192,256]{1,0:T(8,128)(2,1)S(1)} %collective-permute-done.4.refs_3_), channel_id=1, source_target_pairs={{0,2},{2,6},{6,10},{10,14},{14,12},{12,8},{8,4},{4,0},{1,3},{3,7},... | collective-permute-start | bytes 294920 | tf_op jit(solution)/shard_map/ppermute | solution.py:400
  9.8 6.6 %collective-permute-start.9 = (bf16[192,256]{1,0:T(8,128)(2,1)S(1)}, bf16[192,256]{1,0:T(8,128)(2,1)S(1)}, u32[]{:S(2)}, u32[]{:S(2)}) collective-permute-start(bf16[192,256]{1,0:T(8,128)(2,1)S(1)} %collective-permute-done.8.refs_1_), channel_id=1, source_target_pairs={{2,0},{6,2},{10,6},{14,10},{12,14},{8,12},{4,8},{0,4},{3,1},{7,3},... | collective-permute-start | bytes 294920 | tf_op jit(solution)/shard_map/ppermute | solution.py:406
  11.8 6.4 %collective-permute-start.12 = (bf16[192,256]{1,0:T(8,128)(2,1)S(1)}, bf16[192,256]{1,0:T(8,128)(2,1)S(1)}, u32[]{:S(2)}, u32[]{:S(2)}) collective-permute-start(bf16[192,256]{1,0:T(8,128)(2,1)S(1)} %collective-permute-done.10.refs_2_), channel_id=1, source_target_pairs={{0,2},{2,6},{6,10},{10,14},{14,12},{12,8},{8,4},{4,0},{1,3},{3,7},... | collective-permute-start | bytes 294920 | tf_op jit(solution)/shard_map/ppermute | solution.py:407
  13.0 5.6 %collective-permute-start.2 = (bf16[192,256]{1,0:T(8,128)(2,1)S(1)}, bf16[192,256]{1,0:T(8,128)(2,1)S(1)}, u32[]{:S(2)}, u32[]{:S(2)}) collective-permute-start(bf16[192,256]{1,0:T(8,128)(2,1)S(1)} %collective-permute-done.1.refs_0_), channel_id=1, source_target_pairs={{2,0},{6,2},{10,6},{14,10},{12,14},{8,12},{4,8},{0,4},{3,1},{7,3},... | collective-permute-start | bytes 294920 | tf_op jit(solution)/shard_map/ppermute | solution.py:399
  14.7 5.6 %collective-permute-start.6 = (bf16[192,256]{1,0:T(8,128)(2,1)S(1)}, bf16[192,256]{1,0:T(8,128)(2,1)S(1)}, u32[]{:S(2)}, u32[]{:S(2)}) collective-permute-start(bf16[192,256]{1,0:T(8,128)(2,1)S(1)} %collective-permute-done.5.refs_3_), channel_id=1, source_target_pairs={{0,2},{2,6},{6,10},{10,14},{14,12},{12,8},{8,4},{4,0},{1,3},{3,7},... | collective-permute-start | bytes 294920 | tf_op jit(solution)/shard_map/ppermute | solution.py:400
  16.4 5.6 %collective-permute-start.11 = (bf16[192,256]{1,0:T(8,128)(2,1)S(1)}, bf16[192,256]{1,0:T(8,128)(2,1)S(1)}, u32[]{:S(2)}, u32[]{:S(2)}) collective-permute-start(bf16[192,256]{1,0:T(8,128)(2,1)S(1)} %collective-permute-done.9.refs_1_), channel_id=1, source_target_pairs={{2,0},{6,2},{10,6},{14,10},{12,14},{8,12},{4,8},{0,4},{3,1},{7,3},... | collective-permute-start | bytes 294920 | tf_op jit(solution)/shard_map/ppermute | solution.py:406
  18.2 4.6 %collective-permute-start.13 = (bf16[192,256]{1,0:T(8,128)(2,1)S(1)}, bf16[192,256]{1,0:T(8,128)(2,1)S(1)}, u32[]{:S(2)}, u32[]{:S(2)}) collective-permute-start(bf16[192,256]{1,0:T(8,128)(2,1)S(1)} %collective-permute-done.12.refs_2_), channel_id=1, source_target_pairs={{0,2},{2,6},{6,10},{10,14},{14,12},{12,8},{8,4},{4,0},{1,3},{3,7},... | collective-permute-start | bytes 294920 | tf_op jit(solution)/shard_map/ppermute | solution.py:407
  18.6 5.7 %collective-permute-start.3 = (bf16[192,256]{1,0:T(8,128)(2,1)S(1)}, bf16[192,256]{1,0:T(8,128)(2,1)S(1)}, u32[]{:S(2)}, u32[]{:S(2)}) collective-permute-start(bf16[192,256]{1,0:T(8,128)(2,1)S(1)} %collective-permute-done.2.refs_0_), channel_id=1, source_target_pairs={{2,0},{6,2},{10,6},{14,10},{12,14},{8,12},{4,8},{0,4},{3,1},{7,3},... | collective-permute-start | bytes 294920 | tf_op jit(solution)/shard_map/ppermute | solution.py:399
  20.4 4.6 %collective-permute-start.7 = (bf16[192,256]{1,0:T(8,128)(2,1)S(1)}, bf16[192,256]{1,0:T(8,128)(2,1)S(1)}, u32[]{:S(2)}, u32[]{:S(2)}) collective-permute-start(bf16[192,256]{1,0:T(8,128)(2,1)S(1)} %collective-permute-done.6.refs_3_), channel_id=1, source_target_pairs={{0,2},{2,6},{6,10},{10,14},{14,12},{12,8},{8,4},{4,0},{1,3},{3,7},... | collective-permute-start | bytes 294920 | tf_op jit(solution)/shard_map/ppermute | solution.py:400

commit v19 on v17

--- a/solution.py
+++ b/solution.py
@@ -158,21 +158,20 @@
 
 def weights(score, top):
     lanes = score.shape[1] // HD
-    return jnp.exp2(score * EXP_SCALE - jnp.concatenate([top] * lanes, axis=1)).astype(jnp.bfloat16)
+    return jnp.exp2(score * EXP_SCALE - jnp.concatenate([top] * lanes, axis=1))
 
 
 def weigh(score, top, values):
-    return jnp.dot(weights(score, top), values, preferred_element_type=jnp.float32)
+    return jnp.dot(weights(score, top).astype(jnp.bfloat16), values, preferred_element_type=jnp.float32)
 
 
 def wide_top(score):
     return jnp.broadcast_to(jnp.max(score, axis=1, keepdims=True) * EXP_SCALE, (score.shape[0], HD))
 
 
-def normalised(acc):
-    total = acc[:, HD:]
+def inverse_of(total):
     inverse = pl.reciprocal(total, approx=True)
-    return (acc[:, :HD] * (inverse * (2.0 - total * inverse))).astype(jnp.bfloat16)
+    return inverse * (2.0 - total * inverse)
 
 
 def chunks(q_ref, kv_heads, fine_end=False):
@@ -183,7 +182,9 @@
         sizes[-1:] = [CHUNK_HEADS // 2] * 2
     base = 0
     for size in sizes:
-        query = jnp.concatenate([q_ref[:, (base + i) * HD : (base + i + 1) * HD] for i in range(size)], axis=0)
+        query = None
+        if not fine_end:
+            query = jnp.concatenate([q_ref[:, (base + i) * HD : (base + i + 1) * HD] for i in range(size)], axis=0)
         yield base // group, slice(base * rows, (base + size) * rows), query, base, size
         base += size
 
@@ -261,47 +262,57 @@
         take_in(number * sizes[0])
 
 
-def weights_kernel(row, sizes, q_ref, limits, key, top_in, weight_out, keys):
+def weights_kernel(row, sizes, q_ref, limits, key, acc_in, top_in, weight_out, acc_out, keys, shown):
     place_keys(0, 1, row, False, sizes, limits, key, keys)
+    window_rows, cache_rows = sizes
+    row_iota = lax.broadcasted_iota(jnp.int32, (window_rows, HD), 0)
+    shown[:window_rows, :] = jnp.where(row_iota < limits[row : row + 1, :], 1.0, 0.0).astype(jnp.bfloat16)
+    shown[window_rows : window_rows + cache_rows, :] = jnp.ones((cache_rows, HD), jnp.bfloat16)
+    spare = shown.shape[0] - sum(sizes)
+    if spare:
+        shown[sum(sizes) :, :] = jnp.zeros((spare, HD), jnp.bfloat16)
+
+    def settle(at, score, top, acc):
+        weight = weights(score, top)
+        added = jnp.dot(weight.astype(jnp.bfloat16), shown[...], preferred_element_type=jnp.float32)
+        total = acc[:, HD:] + added
+        inverse = inverse_of(total)
+        acc_out[at, :] = acc[:, :HD] * inverse
+        lanes = score.shape[1] // HD
+        weight_out[at, :] = (weight * jnp.concatenate([inverse] * lanes, axis=1)).astype(jnp.bfloat16)
+        return jnp.sum(total.reshape(-1, 8, HD), axis=0)
+
+    grand_total = jnp.zeros((8, HD), jnp.float32)
     for head, at, query, _, _ in chunks(q_ref, keys.shape[0]):
-        weight_out[at, :] = weights(scores(query, keys[head]), top_in[at, :])
-
-
-def last_kernel(row, sizes, q_ref, limits, key, value, weight_in, acc_in, top_in, out, keys, values, result, sems):
-    rows, heads = q_ref.shape[0], q_ref.shape[1] // HD
-    kv_heads = keys.shape[0]
+        grand_total = grand_total + settle(at, scores(query, keys[head]), top_in[at, :], acc_in[at, :])
+
+    @pl.when(too_large(grand_total))
+    def _():
+        for head, at, query, _, _ in chunks(q_ref, keys.shape[0]):
+            score, before = scores(query, keys[head]), top_in[at, :]
+            top = jnp.maximum(before, wide_top(score))
+            fade = jnp.exp2(before - top)
+            settle(at, score, top, acc_in[at, :] * jnp.concatenate([fade, fade], axis=1))
+
+
+def last_kernel(row, sizes, limits, value, weight_in, acc_in, out, values, result, sems):
+    rows, heads = result.shape[0], result.shape[1] // HD
+    kv_heads = values.shape[0]
     place_values(0, 1, row, False, sizes, limits, value, values)
 
     def sent(base):
         lanes = slice(base * HD, (base + COPY_HEADS) * HD)
         return pltpu.make_async_copy(result.at[:, lanes], out.at[:, lanes], sems.at[base // COPY_HEADS])
 
-    def settle(base, size, acc):
-        done = normalised(acc)
+    for head, at, _, base, size in chunks(result, kv_heads, True):
+        added = jnp.dot(weight_in[at, :], values[head, :, :HD], preferred_element_type=jnp.float32)
+        done = (acc_in[at, :] + added).astype(jnp.bfloat16)
         for i in range(size):
             result[:, (base + i) * HD : (base + i + 1) * HD] = done[i * rows : (i + 1) * rows]
         for i in range(0, size, COPY_HEADS):
             sent(base + i).start()
-
-    def wait_all():
-        for base in range(0, heads, COPY_HEADS):
-            sent(base).wait()
-
-    grand_total = jnp.zeros((8, HD), jnp.float32)
-    for head, at, _, base, size in chunks(q_ref, kv_heads, True):
-        acc = acc_in[at, :] + jnp.dot(weight_in[at, :], values[head], preferred_element_type=jnp.float32)
-        grand_total = grand_total + sum_totals(acc)
-        settle(base, size, acc)
-    again = too_large(grand_total)
-    wait_all()
-
-    @pl.when(again)
-    def _():
-        place_keys(0, 1, row, False, sizes, limits, key, keys)
-        for head, at, query, base, size in chunks(q_ref, kv_heads, True):
-            _, acc = anew(scores(query, keys[head]), top_in[at, :], acc_in[at, :], values[head])
-            settle(base, size, acc)
-        wait_all()
+    for base in range(0, heads, COPY_HEADS):
+        sent(base).wait()
 
 
 def kernel_options(queries, total_keys, kv_heads):
@@ -372,28 +383,32 @@
     copies = queries.shape[1] // HD // COPY_HEADS
     vmem = pl.BlockSpec(memory_space=pltpu.VMEM)
     options = kernel_options(queries, total_keys, kv_heads)
-    weight = pl.pallas_call(
+    acc, top = state
+    weight, acc = pl.pallas_call(
         functools.partial(weights_kernel, row, sizes),
-        out_shape=jax.ShapeDtypeStruct((state[1].shape[0], total_keys), jnp.bfloat16),
-        in_specs=[vmem] * 4,
-        out_specs=vmem,
-        scratch_shapes=room(kv_heads, total_keys)[:1],
+        out_shape=[
+            jax.ShapeDtypeStruct((top.shape[0], total_keys), jnp.bfloat16),
+            jax.ShapeDtypeStruct((top.shape[0], HD), jnp.float32),
+        ],
+        in_specs=[vmem] * 5,
+        out_specs=[vmem] * 2,
+        scratch_shapes=[room(kv_heads, total_keys)[0], pltpu.VMEM((total_keys, HD), jnp.bfloat16)],
         name="attend_weights",
         **options,
-    )(queries, limits, key, state[1])
+    )(queries, limits, key, acc, top)
     return pl.pallas_call(
         functools.partial(last_kernel, row, sizes),
         out_shape=jax.ShapeDtypeStruct(queries.shape, queries.dtype),
-        in_specs=[vmem] * 7,
+        in_specs=[vmem] * 4,
         out_specs=pl.BlockSpec(memory_space=pltpu.HBM),
         scratch_shapes=[
-            *room(kv_heads, total_keys),
+            room(kv_heads, total_keys)[1],
             pltpu.VMEM(queries.shape, queries.dtype),
             pltpu.SemaphoreType.DMA((copies,)),
         ],
         name="attend_last",
         **options,
-    )(queries, limits, key, value, weight, *state)
+    )(limits, value, weight, acc)
 
 
 def shards(count, queries, win_keys, win_values, cache_keys, cache_values, valid_counts, first_block):

time: 25.7 us -> 26.1 us (1.016); the launches traced: 25.6 us -> 25.7 us
  Pallas kernels: 6.36 us -> 6.89 us
  waiting for transfers between devices: 2.72 us -> 2.25 us
    pallas_call x1, Pallas kernels: 0.47 us -> 1.06 us  [attend_last(): pl.pallas_call(functools.partial(weights_kernel, row, sizes), out_shape=[...]
    ppermute x4, waiting for transfers between devices: 0.57 us -> 0.1 us  [shards(): value_back = lax.ppermute(value_back, 'ctx', backward)]
  transfers between devices with their start and end apart: 14 -> 14, of which waited for: 5 -> 4; matrix products, arithmetic and copies ran while one was open for 0% -> 0% of each run, Pallas kernels for 15% -> 18%
where the time goes in v19:
time: 26.1 us; the launch traced here: 25.7 us
  starting transfers between devices  16.4 us (63%)
  Pallas kernels  6.89 us (26%)
  waiting for transfers between devices  2.25 us (9%)
    ppermute x4, starting transfers between devices, shards(): key_on = lax.ppermute(key_on, 'ctx', onward)  8.67 us
    ppermute x3, starting transfers between devices, shards(): key_back = lax.ppermute(key_back, 'ctx', backward)  4.04 us
    pallas_call x2, Pallas kernels, attend_next(): pl.pallas_call(functools.partial(next_kernel, rows_of, count, sizes), out...  2.54 us
    ppermute x3, starting transfers between devices, shards(): value_on = lax.ppermute(value_on, 'ctx', onward)  2.07 us
    ppermute x4, starting transfers between devices, shards(): value_back = lax.ppermute(value_back, 'ctx', backward)  1.66 us
    ppermute x3, waiting for transfers between devices, shards(): value_on = lax.ppermute(value_on, 'ctx', onward)  1.63 us
    pallas_call x1, Pallas kernels, attend_last(): pl.pallas_call(functools.partial(last_kernel, row, sizes), out_shape=jax....  1.25 us
    pallas_call x1, Pallas kernels, load(): pl.pallas_call(functools.partial(load_kernel, count), out_shape=[jax.Shap...  1.11 us
  transfers between devices with their start and end apart: 14, of which 4 were waited for; matrix products, arithmetic and copies ran while one was open for 0% of the time, Pallas kernels for 18%

profile of v19, /device:TPU:0, one launch (start us, length us, event | category | flops | bytes accessed | tf_op | source)
XLA Modules:
  0.0 25.7 jit_solution(4276053885929898250)
XLA Ops:
  0.0 1.1 %load.1 = (bf16[192,256]{1,0:T(8,128)(2,1)S(1)}, bf16[192,256]{1,0:T(8,128)(2,1)S(1)}, bf16[128,2048]{1,0:T(8,128)(2,1)S(1)}, s32[8,128]{1,0:T(8,128)S(1)}) custom-call(bf16[128,256]{1,0:T(8,128)(2,1)} %win_keys.1, bf16[128,256]{1,0:T(8,128)(2,1)} %win_values.1, bf16[64,256]{1,0:T(8,128)(2,1)} %cache_keys.1, bf16[64,256]{1,0:T(8,128)(2,1)} %cache_values.1, ...), custom_call_target="tpu_custom_call" | custom-call | bytes 393216 | tf_op jit(solution)/shard_map/load/pallas_call | solution.py:81
  1.1 3.1 %collective-permute-start.4 = (bf16[192,256]{1,0:T(8,128)(2,1)S(1)}, bf16[192,256]{1,0:T(8,128)(2,1)S(1)}, u32[]{:S(2)}, u32[]{:S(2)}) collective-permute-start(bf16[192,256]{1,0:T(8,128)(2,1)S(1)} %get-tuple-element.22.own_keys), channel_id=1, source_target_pairs={{2,0},{6,2},{10,6},{14,10},{12,14},{8,12},{4,8},{0,4},{3,1},{7,3},... | collective-permute-start | bytes 294920 | tf_op jit(solution)/shard_map/ppermute | solution.py:433
  4.2 0.0 collective-permute-start
  4.2 1.9 %collective-permute-start.11 = (bf16[192,256]{1,0:T(8,128)(2,1)S(1)}, bf16[192,256]{1,0:T(8,128)(2,1)S(1)}, u32[]{:S(2)}, u32[]{:S(2)}) collective-permute-start(bf16[192,256]{1,0:T(8,128)(2,1)S(1)} %get-tuple-element.22.own_keys), channel_id=1, source_target_pairs={{0,2},{2,6},{6,10},{10,14},{14,12},{12,8},{8,4},{4,0},{1,3},{3,7},... | collective-permute-start | bytes 294920 | tf_op jit(solution)/shard_map/ppermute | solution.py:437
  6.1 0.1 collective-permute-start.8
  6.3 0.9 %attend_first.1 = (f32[2048,256]{1,0:T(8,128)S(1)}, f32[2048,128]{1,0:T(8,128)S(1)}) custom-call(bf16[128,2048]{1,0:T(8,128)(2,1)S(1)} %get-tuple-element.21.q_ref, s32[8,128]{1,0:T(8,128)S(1)} %get-tuple-element.19.limits, bf16[192,256]{1,0:T(8,128)(2,1)S(1)} %get-tuple-element.22.own_keys, bf16[192,256]{1,0:T(8,128)(2,1)S(1)} %get-tuple-element.20.own_values), custom_call_target="tpu_custom_call" | custom-call | flops 402653184 | bytes 524288 | tf_op jit(solution)/shard_map/attend_first/pallas_call | solution.py:347
  7.2 0.0 collective-permute-done.4.refs_0_
  7.2 2.4 %collective-permute-start.5 = (bf16[192,256]{1,0:T(8,128)(2,1)S(1)}, bf16[192,256]{1,0:T(8,128)(2,1)S(1)}, u32[]{:S(2)}, u32[]{:S(2)}) collective-permute-start(bf16[192,256]{1,0:T(8,128)(2,1)S(1)} %collective-permute-done.4.refs_0_), channel_id=1, source_target_pairs={{2,0},{6,2},{10,6},{14,10},{12,14},{8,12},{4,8},{0,4},{3,1},{7,3},... | collective-permute-start | bytes 294920 | tf_op jit(solution)/shard_map/ppermute | solution.py:433
  9.6 0.0 collective-permute-done.refs_3_
  9.6 0.0 collective-permute-start.1
  9.6 1.3 %collective-permute-done.8.refs_1_ = bf16[192,256]{1,0:T(8,128)(2,1)S(1)} collective-permute-done((bf16[192,256]{1,0:T(8,128)(2,1)S(1)}, bf16[192,256]{1,0:T(8,128)(2,1)S(1)}, u32[]{:S(2)}, u32[]{:S(2)}) %collective-permute-start.8) | collective-permute-done | bytes 98336 | tf_op jit(solution)/shard_map/ppermute | solution.py:436
  10.9 0.7 %collective-permute-start.9 = (bf16[192,256]{1,0:T(8,128)(2,1)S(1)}, bf16[192,256]{1,0:T(8,128)(2,1)S(1)}, u32[]{:S(2)}, u32[]{:S(2)}) collective-permute-start(bf16[192,256]{1,0:T(8,128)(2,1)S(1)} %collective-permute-done.8.refs_1_), channel_id=1, source_target_pairs={{2,0},{6,2},{10,6},{14,10},{12,14},{8,12},{4,8},{0,4},{3,1},{7,3},... | collective-permute-start | bytes 294920 | tf_op jit(solution)/shard_map/ppermute | solution.py:436
  11.7 0.0 collective-permute-done.11.refs_2_
  11.7 1.3 %collective-permute-start.12 = (bf16[192,256]{1,0:T(8,128)(2,1)S(1)}, bf16[192,256]{1,0:T(8,128)(2,1)S(1)}, u32[]{:S(2)}, u32[]{:S(2)}) collective-permute-start(bf16[192,256]{1,0:T(8,128)(2,1)S(1)} %collective-permute-done.11.refs_2_), channel_id=1, source_target_pairs={{0,2},{2,6},{6,10},{10,14},{14,12},{12,8},{8,4},{4,0},{1,3},{3,7},... | collective-permute-start | bytes 294920 | tf_op jit(solution)/shard_map/ppermute | solution.py:437
  13.0 0.0 collective-permute-done.5.refs_4_
  13.0 1.7 %collective-permute-start.6 = (bf16[192,256]{1,0:T(8,128)(2,1)S(1)}, bf16[192,256]{1,0:T(8,128)(2,1)S(1)}, u32[]{:S(2)}, u32[]{:S(2)}) collective-permute-start(bf16[192,256]{1,0:T(8,128)(2,1)S(1)} %collective-permute-done.5.refs_4_), channel_id=1, source_target_pairs={{2,0},{6,2},{10,6},{14,10},{12,14},{8,12},{4,8},{0,4},{3,1},{7,3},... | collective-permute-start | bytes 294920 | tf_op jit(solution)/shard_map/ppermute | solution.py:433
  14.7 0.0 collective-permute-done.1.refs_7_
  14.7 0.6 %collective-permute-start.2 = (bf16[192,256]{1,0:T(8,128)(2,1)S(1)}, bf16[192,256]{1,0:T(8,128)(2,1)S(1)}, u32[]{:S(2)}, u32[]{:S(2)}) collective-permute-start(bf16[192,256]{1,0:T(8,128)(2,1)S(1)} %collective-permute-done.1.refs_7_), channel_id=1, source_target_pairs={{0,2},{2,6},{6,10},{10,14},{14,12},{12,8},{8,4},{4,0},{1,3},{3,7},... | collective-permute-start | bytes 294920 | tf_op jit(solution)/shard_map/ppermute | solution.py:434
  15.2 0.3 %collective-permute-done.9.refs_5_ = bf16[192,256]{1,0:T(8,128)(2,1)S(1)} collective-permute-done((bf16[192,256]{1,0:T(8,128)(2,1)S(1)}, bf16[192,256]{1,0:T(8,128)(2,1)S(1)}, u32[]{:S(2)}, u32[]{:S(2)}) %collective-permute-start.9) | collective-permute-done | bytes 98336 | tf_op jit(solution)/shard_map/ppermute | solution.py:436
  15.6 1.2 %collective-permute-start.10 = (bf16[192,256]{1,0:T(8,128)(2,1)S(1)}, bf16[192,256]{1,0:T(8,128)(2,1)S(1)}, u32[]{:S(2)}, u32[]{:S(2)}) collective-permute-start(bf16[192,256]{1,0:T(8,128)(2,1)S(1)} %collective-permute-done.9.refs_5_), channel_id=1, source_target_pairs={{2,0},{6,2},{10,6},{14,10},{12,14},{8,12},{4,8},{0,4},{3,1},{7,3},... | collective-permute-start | bytes 294920 | tf_op jit(solution)/shard_map/ppermute | solution.py:436
  16.8 0.0 collective-permute-done.12.refs_6_
  16.8 0.8 %collective-permute-start.13 = (bf16[192,256]{1,0:T(8,128)(2,1)S(1)}, bf16[192,256]{1,0:T(8,128)(2,1)S(1)}, u32[]{:S(2)}, u32[]{:S(2)}) collective-permute-start(bf16[192,256]{1,0:T(8,128)(2,1)S(1)} %collective-permute-done.12.refs_6_), channel_id=1, source_target_pairs={{0,2},{2,6},{6,10},{10,14},{14,12},{12,8},{8,4},{4,0},{1,3},{3,7},... | collective-permute-start | bytes 294920 | tf_op jit(solution)/shard_map/ppermute | solution.py:437
  17.6 0.5 %collective-permute-done.6.refs_0_ = bf16[192,256]{1,0:T(8,128)(2,1)S(1)} collective-permute-done((bf16[192,256]{1,0:T(8,128)(2,1)S(1)}, bf16[192,256]{1,0:T(8,128)(2,1)S(1)}, u32[]{:S(2)}, u32[]{:S(2)}) %collective-permute-start.6) | collective-permute-done | bytes 98336 | tf_op jit(solution)/shard_map/ppermute | solution.py:433
  18.1 1.5 %collective-permute-start.7 = (bf16[192,256]{1,0:T(8,128)(2,1)S(1)}, bf16[192,256]{1,0:T(8,128)(2,1)S(1)}, u32[]{:S(2)}, u32[]{:S(2)}) collective-permute-start(bf16[192,256]{1,0:T(8,128)(2,1)S(1)} %collective-permute-done.6.refs_0_), channel_id=1, source_target_pairs={{2,0},{6,2},{10,6},{14,10},{12,14},{8,12},{4,8},{0,4},{3,1},{7,3},... | collective-permute-start | bytes 294920 | tf_op jit(solution)/shard_map/ppermute | solution.py:433
  19.6 0.1 collective-permute-done.2.refs_3_
  19.7 1.1 %collective-permute-start.3 = (bf16[192,256]{1,0:T(8,128)(2,1)S(1)}, bf16[192,256]{1,0:T(8,128)(2,1)S(1)}, u32[]{:S(2)}, u32[]{:S(2)}) collective-permute-start(bf16[192,256]{1,0:T(8,128)(2,1)S(1)} %collective-permute-done.2.refs_3_), channel_id=1, source_target_pairs={{0,2},{2,6},{6,10},{10,14},{14,12},{12,8},{8,4},{4,0},{1,3},{3,7},... | collective-permute-start | bytes 294920 | tf_op jit(solution)/shard_map/ppermute | solution.py:434
  20.7 1.1 %attend_next.2 = (f32[2048,256]{1,0:T(8,128)S(1)}, f32[2048,128]{1,0:T(8,128)S(1)}) custom-call(bf16[128,2048]{1,0:T(8,128)(2,1)S(1)} %get-tuple-element.21.q_ref, s32[8,128]{1,0:T(8,128)S(1)} %get-tuple-element.19.limits, bf16[192,256]{1,0:T(8,128)(2,1)S(1)} %collective-permute-done.4.refs_0_, bf16[192,256]{1,0:T(8,128)(2,1)S(1)} %collective-permute-done.8.refs_1_, ...), custom_call_target="tpu_custom_call" | custom-call | flops 1207959552 | bytes 524288 | tf_op jit(solution)/shard_map/attend_next/pallas_call | solution.py:367
  21.9 0.0 collective-permute-done.10.refs_1_
  21.9 0.0 collective-permute-done.13.refs_2_
  21.9 1.4 %attend_next.3 = (f32[2048,256]{1,0:T(8,128)S(1)}, f32[2048,128]{1,0:T(8,128)S(1)}) custom-call(bf16[128,2048]{1,0:T(8,128)(2,1)S(1)} %get-tuple-element.21.q_ref, s32[8,128]{1,0:T(8,128)S(1)} %get-tuple-element.19.limits, bf16[192,256]{1,0:T(8,128)(2,1)S(1)} %collective-permute-done.6.refs_0_, bf16[192,256]{1,0:T(8,128)(2,1)S(1)} %collective-permute-done.10.refs_1_, ...), custom_call_target="tpu_custom_call" | custom-call | flops 603979776 | bytes 524288 | tf_op jit(solution)/shard_map/attend_next/pallas_call | solution.py:367
  23.3 0.0 collective-permute-done.7.key
  23.3 1.1 %attend_weights.1 = (bf16[2048,256]{1,0:T(8,128)(2,1)S(1)}, f32[2048,128]{1,0:T(8,128)S(1)}) custom-call(bf16[128,2048]{1,0:T(8,128)(2,1)S(1)} %get-tuple-element.21.q_ref, s32[8,128]{1,0:T(8,128)S(1)} %get-tuple-element.19.limits, bf16[192,256]{1,0:T(8,128)(2,1)S(1)} %collective-permute-done.7.key, f32[2048,256]{1,0:T(8,128)S(1)} %get-tuple-element.29.acc_in, ...), custom_call_target="tpu_custom_call" | custom-call | flops 402653184 | bytes 524288 | tf_op jit(solution)/shard_map/attend_weights/pallas_call | solution.py:387
  24.4 0.0 collective-permute-done.3.value
  24.4 1.3 %attend_last.1 = bf16[128,2048]{1,0:T(8,128)(2,1)} custom-call(s32[8,128]{1,0:T(8,128)S(1)} %get-tuple-element.19.limits, bf16[192,256]{1,0:T(8,128)(2,1)S(1)} %collective-permute-done.3.value, bf16[2048,256]{1,0:T(8,128)(2,1)S(1)} %get-tuple-element.31.weight_in, f32[2048,128]{1,0:T(8,128)S(1)} %get-tuple-element.32.acc_in), custom_call_target="tpu_custom_call" | custom-call | flops 402653184 | bytes 524288 | tf_op jit(solution)/shard_map/attend_last/pallas_call | solution.py:399
Async XLA Ops:
  1.1 6.1 %collective-permute-start.4 = (bf16[192,256]{1,0:T(8,128)(2,1)S(1)}, bf16[192,256]{1,0:T(8,128)(2,1)S(1)}, u32[]{:S(2)}, u32[]{:S(2)}) collective-permute-start(bf16[192,256]{1,0:T(8,128)(2,1)S(1)} %get-tuple-element.22.own_keys), channel_id=1, source_target_pairs={{2,0},{6,2},{10,6},{14,10},{12,14},{8,12},{4,8},{0,4},{3,1},{7,3},... | collective-permute-start | bytes 294920 | tf_op jit(solution)/shard_map/ppermute | solution.py:433
  4.2 5.4 %collective-permute-start = (bf16[192,256]{1,0:T(8,128)(2,1)S(1)}, bf16[192,256]{1,0:T(8,128)(2,1)S(1)}, u32[]{:S(2)}, u32[]{:S(2)}) collective-permute-start(bf16[192,256]{1,0:T(8,128)(2,1)S(1)} %get-tuple-element.20.own_values), channel_id=1, source_target_pairs={{0,2},{2,6},{6,10},{10,14},{14,12},{12,8},{8,4},{4,0},{1,3},{3,7},... | collective-permute-start | bytes 294920 | tf_op jit(solution)/shard_map/ppermute | solution.py:434
  4.2 7.5 %collective-permute-start.11 = (bf16[192,256]{1,0:T(8,128)(2,1)S(1)}, bf16[192,256]{1,0:T(8,128)(2,1)S(1)}, u32[]{:S(2)}, u32[]{:S(2)}) collective-permute-start(bf16[192,256]{1,0:T(8,128)(2,1)S(1)} %get-tuple-element.22.own_keys), channel_id=1, source_target_pairs={{0,2},{2,6},{6,10},{10,14},{14,12},{12,8},{8,4},{4,0},{1,3},{3,7},... | collective-permute-start | bytes 294920 | tf_op jit(solution)/shard_map/ppermute | solution.py:437
  6.1 4.8 %collective-permute-start.8 = (bf16[192,256]{1,0:T(8,128)(2,1)S(1)}, bf16[192,256]{1,0:T(8,128)(2,1)S(1)}, u32[]{:S(2)}, u32[]{:S(2)}) collective-permute-start(bf16[192,256]{1,0:T(8,128)(2,1)S(1)} %get-tuple-element.20.own_values), channel_id=1, source_target_pairs={{2,0},{6,2},{10,6},{14,10},{12,14},{8,12},{4,8},{0,4},{3,1},{7,3},... | collective-permute-start | bytes 294920 | tf_op jit(solution)/shard_map/ppermute | solution.py:436
  7.2 5.8 %collective-permute-start.5 = (bf16[192,256]{1,0:T(8,128)(2,1)S(1)}, bf16[192,256]{1,0:T(8,128)(2,1)S(1)}, u32[]{:S(2)}, u32[]{:S(2)}) collective-permute-start(bf16[192,256]{1,0:T(8,128)(2,1)S(1)} %collective-permute-done.4.refs_0_), channel_id=1, source_target_pairs={{2,0},{6,2},{10,6},{14,10},{12,14},{8,12},{4,8},{0,4},{3,1},{7,3},... | collective-permute-start | bytes 294920 | tf_op jit(solution)/shard_map/ppermute | solution.py:433
  9.6 5.1 %collective-permute-start.1 = (bf16[192,256]{1,0:T(8,128)(2,1)S(1)}, bf16[192,256]{1,0:T(8,128)(2,1)S(1)}, u32[]{:S(2)}, u32[]{:S(2)}) collective-permute-start(bf16[192,256]{1,0:T(8,128)(2,1)S(1)} %collective-permute-done.refs_3_), channel_id=1, source_target_pairs={{0,2},{2,6},{6,10},{10,14},{14,12},{12,8},{8,4},{4,0},{1,3},{3,7},... | collective-permute-start | bytes 294920 | tf_op jit(solution)/shard_map/ppermute | solution.py:434
  10.9 4.6 %collective-permute-start.9 = (bf16[192,256]{1,0:T(8,128)(2,1)S(1)}, bf16[192,256]{1,0:T(8,128)(2,1)S(1)}, u32[]{:S(2)}, u32[]{:S(2)}) collective-permute-start(bf16[192,256]{1,0:T(8,128)(2,1)S(1)} %collective-permute-done.8.refs_1_), channel_id=1, source_target_pairs={{2,0},{6,2},{10,6},{14,10},{12,14},{8,12},{4,8},{0,4},{3,1},{7,3},... | collective-permute-start | bytes 294920 | tf_op jit(solution)/shard_map/ppermute | solution.py:436
  11.7 5.1 %collective-permute-start.12 = (bf16[192,256]{1,0:T(8,128)(2,1)S(1)}, bf16[192,256]{1,0:T(8,128)(2,1)S(1)}, u32[]{:S(2)}, u32[]{:S(2)}) collective-permute-start(bf16[192,256]{1,0:T(8,128)(2,1)S(1)} %collective-permute-done.11.refs_2_), channel_id=1, source_target_pairs={{0,2},{2,6},{6,10},{10,14},{14,12},{12,8},{8,4},{4,0},{1,3},{3,7},... | collective-permute-start | bytes 294920 | tf_op jit(solution)/shard_map/ppermute | solution.py:437
  13.0 5.1 %collective-permute-start.6 = (bf16[192,256]{1,0:T(8,128)(2,1)S(1)}, bf16[192,256]{1,0:T(8,128)(2,1)S(1)}, u32[]{:S(2)}, u32[]{:S(2)}) collective-permute-start(bf16[192,256]{1,0:T(8,128)(2,1)S(1)} %collective-permute-done.5.refs_4_), channel_id=1, source_target_pairs={{2,0},{6,2},{10,6},{14,10},{12,14},{8,12},{4,8},{0,4},{3,1},{7,3},... | collective-permute-start | bytes 294920 | tf_op jit(solution)/shard_map/ppermute | solution.py:433
  14.7 5.0 %collective-permute-start.2 = (bf16[192,256]{1,0:T(8,128)(2,1)S(1)}, bf16[192,256]{1,0:T(8,128)(2,1)S(1)}, u32[]{:S(2)}, u32[]{:S(2)}) collective-permute-start(bf16[192,256]{1,0:T(8,128)(2,1)S(1)} %collective-permute-done.1.refs_7_), channel_id=1, source_target_pairs={{0,2},{2,6},{6,10},{10,14},{14,12},{12,8},{8,4},{4,0},{1,3},{3,7},... | collective-permute-start | bytes 294920 | tf_op jit(solution)/shard_map/ppermute | solution.py:434
  15.6 6.3 %collective-permute-start.10 = (bf16[192,256]{1,0:T(8,128)(2,1)S(1)}, bf16[192,256]{1,0:T(8,128)(2,1)S(1)}, u32[]{:S(2)}, u32[]{:S(2)}) collective-permute-start(bf16[192,256]{1,0:T(8,128)(2,1)S(1)} %collective-permute-done.9.refs_5_), channel_id=1, source_target_pairs={{2,0},{6,2},{10,6},{14,10},{12,14},{8,12},{4,8},{0,4},{3,1},{7,3},... | collective-permute-start | bytes 294920 | tf_op jit(solution)/shard_map/ppermute | solution.py:436
  16.8 5.1 %collective-permute-start.13 = (bf16[192,256]{1,0:T(8,128)(2,1)S(1)}, bf16[192,256]{1,0:T(8,128)(2,1)S(1)}, u32[]{:S(2)}, u32[]{:S(2)}) collective-permute-start(bf16[192,256]{1,0:T(8,128)(2,1)S(1)} %collective-permute-done.12.refs_6_), channel_id=1, source_target_pairs={{0,2},{2,6},{6,10},{10,14},{14,12},{12,8},{8,4},{4,0},{1,3},{3,7},... | collective-permute-start | bytes 294920 | tf_op jit(solution)/shard_map/ppermute | solution.py:437
  18.1 5.2 %collective-permute-start.7 = (bf16[192,256]{1,0:T(8,128)(2,1)S(1)}, bf16[192,256]{1,0:T(8,128)(2,1)S(1)}, u32[]{:S(2)}, u32[]{:S(2)}) collective-permute-start(bf16[192,256]{1,0:T(8,128)(2,1)S(1)} %collective-permute-done.6.refs_0_), channel_id=1, source_target_pairs={{2,0},{6,2},{10,6},{14,10},{12,14},{8,12},{4,8},{0,4},{3,1},{7,3},... | collective-permute-start | bytes 294920 | tf_op jit(solution)/shard_map/ppermute | solution.py:433
  19.7 4.7 %collective-permute-start.3 = (bf16[192,256]{1,0:T(8,128)(2,1)S(1)}, bf16[192,256]{1,0:T(8,128)(2,1)S(1)}, u32[]{:S(2)}, u32[]{:S(2)}) collective-permute-start(bf16[192,256]{1,0:T(8,128)(2,1)S(1)} %collective-permute-done.2.refs_3_), channel_id=1, source_target_pairs={{0,2},{2,6},{6,10},{10,14},{14,12},{12,8},{8,4},{4,0},{1,3},{3,7},... | collective-permute-start | bytes 294920 | tf_op jit(solution)/shard_map/ppermute | solution.py:434

commit v20 on v17

--- a/solution.py
+++ b/solution.py
@@ -12,7 +12,7 @@
 EXP_SCALE = HD**-0.5 * math.log2(math.e)
 HIDDEN = -1.0e30
 CHUNK_HEADS = 4
-COPY_HEADS = 2
+COPY_HEADS = 4
 LARGEST_TOTAL = 2.0**100
 
 
@@ -288,7 +288,7 @@
             sent(base).wait()
 
     grand_total = jnp.zeros((8, HD), jnp.float32)
-    for head, at, _, base, size in chunks(q_ref, kv_heads, True):
+    for head, at, _, base, size in chunks(q_ref, kv_heads):
         acc = acc_in[at, :] + jnp.dot(weight_in[at, :], values[head], preferred_element_type=jnp.float32)
         grand_total = grand_total + sum_totals(acc)
         settle(base, size, acc)
@@ -298,7 +298,7 @@
     @pl.when(again)
     def _():
         place_keys(0, 1, row, False, sizes, limits, key, keys)
-        for head, at, query, base, size in chunks(q_ref, kv_heads, True):
+        for head, at, query, base, size in chunks(q_ref, kv_heads):
             _, acc = anew(scores(query, keys[head]), top_in[at, :], acc_in[at, :], values[head])
             settle(base, size, acc)
         wait_all()

time: 25.7 us -> 25.7 us (level)
  no operation moved by 1% of the time
where the time goes in v20:
time: 25.7 us; the launch traced here: 25.6 us
  starting transfers between devices  16.4 us (64%)
  Pallas kernels  6.32 us (25%)
  waiting for transfers between devices  2.72 us (11%)
    ppermute x4, starting transfers between devices, shards(): key_on = lax.ppermute(key_on, 'ctx', onward)  8.67 us
    ppermute x3, starting transfers between devices, shards(): key_back = lax.ppermute(key_back, 'ctx', backward)  4.04 us
    pallas_call x2, Pallas kernels, attend_next(): pl.pallas_call(functools.partial(next_kernel, rows_of, count, sizes), out...  2.53 us
    ppermute x3, starting transfers between devices, shards(): value_on = lax.ppermute(value_on, 'ctx', onward)  2.07 us
    ppermute x4, starting transfers between devices, shards(): value_back = lax.ppermute(value_back, 'ctx', backward)  1.66 us
    ppermute x3, waiting for transfers between devices, shards(): value_on = lax.ppermute(value_on, 'ctx', onward)  1.63 us
    pallas_call x1, Pallas kernels, attend_last(): pl.pallas_call(functools.partial(last_kernel, row, sizes), out_shape=jax....  1.29 us
    pallas_call x1, Pallas kernels, load(): pl.pallas_call(functools.partial(load_kernel, count), out_shape=[jax.Shap...  1.11 us
  transfers between devices with their start and end apart: 14, of which 5 were waited for; matrix products, arithmetic and copies ran while one was open for 0% of the time, Pallas kernels for 15%

profile of v20, /device:TPU:0, one launch (start us, length us, event | category | flops | bytes accessed | tf_op | source)
XLA Modules:
  0.0 25.6 jit_solution(6061220001857063674)
XLA Ops:
  0.0 1.1 %load.1 = (bf16[192,256]{1,0:T(8,128)(2,1)S(1)}, bf16[192,256]{1,0:T(8,128)(2,1)S(1)}, bf16[128,2048]{1,0:T(8,128)(2,1)S(1)}, s32[8,128]{1,0:T(8,128)S(1)}) custom-call(bf16[128,256]{1,0:T(8,128)(2,1)} %win_keys.1, bf16[128,256]{1,0:T(8,128)(2,1)} %win_values.1, bf16[64,256]{1,0:T(8,128)(2,1)} %cache_keys.1, bf16[64,256]{1,0:T(8,128)(2,1)} %cache_values.1, ...), custom_call_target="tpu_custom_call" | custom-call | bytes 393216 | tf_op jit(solution)/shard_map/load/pallas_call | solution.py:81
  1.1 3.1 %collective-permute-start = (bf16[192,256]{1,0:T(8,128)(2,1)S(1)}, bf16[192,256]{1,0:T(8,128)(2,1)S(1)}, u32[]{:S(2)}, u32[]{:S(2)}) collective-permute-start(bf16[192,256]{1,0:T(8,128)(2,1)S(1)} %get-tuple-element.19.own_keys), channel_id=1, source_target_pairs={{2,0},{6,2},{10,6},{14,10},{12,14},{8,12},{4,8},{0,4},{3,1},{7,3},... | collective-permute-start | bytes 294920 | tf_op jit(solution)/shard_map/ppermute | solution.py:418
  4.2 0.0 collective-permute-start.4
  4.2 1.9 %collective-permute-start.11 = (bf16[192,256]{1,0:T(8,128)(2,1)S(1)}, bf16[192,256]{1,0:T(8,128)(2,1)S(1)}, u32[]{:S(2)}, u32[]{:S(2)}) collective-permute-start(bf16[192,256]{1,0:T(8,128)(2,1)S(1)} %get-tuple-element.19.own_keys), channel_id=1, source_target_pairs={{0,2},{2,6},{6,10},{10,14},{14,12},{12,8},{8,4},{4,0},{1,3},{3,7},... | collective-permute-start | bytes 294920 | tf_op jit(solution)/shard_map/ppermute | solution.py:422
  6.1 0.1 collective-permute-start.8
  6.3 0.9 %attend_first.1 = (f32[2048,256]{1,0:T(8,128)S(1)}, f32[2048,128]{1,0:T(8,128)S(1)}) custom-call(bf16[128,2048]{1,0:T(8,128)(2,1)S(1)} %get-tuple-element.17.q_ref, s32[8,128]{1,0:T(8,128)S(1)} %get-tuple-element.18.limits, bf16[192,256]{1,0:T(8,128)(2,1)S(1)} %get-tuple-element.19.own_keys, bf16[192,256]{1,0:T(8,128)(2,1)S(1)} %get-tuple-element.20.own_values), custom_call_target="tpu_custom_call" | custom-call | flops 402653184 | bytes 524288 | tf_op jit(solution)/shard_map/attend_first/pallas_call | solution.py:336
  7.2 0.0 collective-permute-done.refs_0_
  7.2 2.4 %collective-permute-start.1 = (bf16[192,256]{1,0:T(8,128)(2,1)S(1)}, bf16[192,256]{1,0:T(8,128)(2,1)S(1)}, u32[]{:S(2)}, u32[]{:S(2)}) collective-permute-start(bf16[192,256]{1,0:T(8,128)(2,1)S(1)} %collective-permute-done.refs_0_), channel_id=1, source_target_pairs={{2,0},{6,2},{10,6},{14,10},{12,14},{8,12},{4,8},{0,4},{3,1},{7,3},... | collective-permute-start | bytes 294920 | tf_op jit(solution)/shard_map/ppermute | solution.py:418
  9.6 0.0 collective-permute-done.4.refs_3_
  9.6 0.0 collective-permute-start.5
  9.6 1.3 %collective-permute-done.8.refs_1_ = bf16[192,256]{1,0:T(8,128)(2,1)S(1)} collective-permute-done((bf16[192,256]{1,0:T(8,128)(2,1)S(1)}, bf16[192,256]{1,0:T(8,128)(2,1)S(1)}, u32[]{:S(2)}, u32[]{:S(2)}) %collective-permute-start.8) | collective-permute-done | bytes 98336 | tf_op jit(solution)/shard_map/ppermute | solution.py:421
  10.9 0.7 %collective-permute-start.9 = (bf16[192,256]{1,0:T(8,128)(2,1)S(1)}, bf16[192,256]{1,0:T(8,128)(2,1)S(1)}, u32[]{:S(2)}, u32[]{:S(2)}) collective-permute-start(bf16[192,256]{1,0:T(8,128)(2,1)S(1)} %collective-permute-done.8.refs_1_), channel_id=1, source_target_pairs={{2,0},{6,2},{10,6},{14,10},{12,14},{8,12},{4,8},{0,4},{3,1},{7,3},... | collective-permute-start | bytes 294920 | tf_op jit(solution)/shard_map/ppermute | solution.py:421
  11.7 0.0 collective-permute-done.11.refs_2_
  11.7 1.3 %collective-permute-start.12 = (bf16[192,256]{1,0:T(8,128)(2,1)S(1)}, bf16[192,256]{1,0:T(8,128)(2,1)S(1)}, u32[]{:S(2)}, u32[]{:S(2)}) collective-permute-start(bf16[192,256]{1,0:T(8,128)(2,1)S(1)} %collective-permute-done.11.refs_2_), channel_id=1, source_target_pairs={{0,2},{2,6},{6,10},{10,14},{14,12},{12,8},{8,4},{4,0},{1,3},{3,7},... | collective-permute-start | bytes 294920 | tf_op jit(solution)/shard_map/ppermute | solution.py:422
  13.0 0.0 collective-permute-done.1.refs_4_
  13.0 1.7 %collective-permute-start.2 = (bf16[192,256]{1,0:T(8,128)(2,1)S(1)}, bf16[192,256]{1,0:T(8,128)(2,1)S(1)}, u32[]{:S(2)}, u32[]{:S(2)}) collective-permute-start(bf16[192,256]{1,0:T(8,128)(2,1)S(1)} %collective-permute-done.1.refs_4_), channel_id=1, source_target_pairs={{2,0},{6,2},{10,6},{14,10},{12,14},{8,12},{4,8},{0,4},{3,1},{7,3},... | collective-permute-start | bytes 294920 | tf_op jit(solution)/shard_map/ppermute | solution.py:418
  14.7 0.0 collective-permute-done.5.refs_7_
  14.7 0.6 %collective-permute-start.6 = (bf16[192,256]{1,0:T(8,128)(2,1)S(1)}, bf16[192,256]{1,0:T(8,128)(2,1)S(1)}, u32[]{:S(2)}, u32[]{:S(2)}) collective-permute-start(bf16[192,256]{1,0:T(8,128)(2,1)S(1)} %collective-permute-done.5.refs_7_), channel_id=1, source_target_pairs={{0,2},{2,6},{6,10},{10,14},{14,12},{12,8},{8,4},{4,0},{1,3},{3,7},... | collective-permute-start | bytes 294920 | tf_op jit(solution)/shard_map/ppermute | solution.py:419
  15.2 0.3 %collective-permute-done.9.refs_5_ = bf16[192,256]{1,0:T(8,128)(2,1)S(1)} collective-permute-done((bf16[192,256]{1,0:T(8,128)(2,1)S(1)}, bf16[192,256]{1,0:T(8,128)(2,1)S(1)}, u32[]{:S(2)}, u32[]{:S(2)}) %collective-permute-start.9) | collective-permute-done | bytes 98336 | tf_op jit(solution)/shard_map/ppermute | solution.py:421
  15.6 1.2 %collective-permute-start.10 = (bf16[192,256]{1,0:T(8,128)(2,1)S(1)}, bf16[192,256]{1,0:T(8,128)(2,1)S(1)}, u32[]{:S(2)}, u32[]{:S(2)}) collective-permute-start(bf16[192,256]{1,0:T(8,128)(2,1)S(1)} %collective-permute-done.9.refs_5_), channel_id=1, source_target_pairs={{2,0},{6,2},{10,6},{14,10},{12,14},{8,12},{4,8},{0,4},{3,1},{7,3},... | collective-permute-start | bytes 294920 | tf_op jit(solution)/shard_map/ppermute | solution.py:421
  16.8 0.0 collective-permute-done.12.refs_6_
  16.8 0.8 %collective-permute-start.13 = (bf16[192,256]{1,0:T(8,128)(2,1)S(1)}, bf16[192,256]{1,0:T(8,128)(2,1)S(1)}, u32[]{:S(2)}, u32[]{:S(2)}) collective-permute-start(bf16[192,256]{1,0:T(8,128)(2,1)S(1)} %collective-permute-done.12.refs_6_), channel_id=1, source_target_pairs={{0,2},{2,6},{6,10},{10,14},{14,12},{12,8},{8,4},{4,0},{1,3},{3,7},... | collective-permute-start | bytes 294920 | tf_op jit(solution)/shard_map/ppermute | solution.py:422
  17.6 0.5 %collective-permute-done.2.refs_0_ = bf16[192,256]{1,0:T(8,128)(2,1)S(1)} collective-permute-done((bf16[192,256]{1,0:T(8,128)(2,1)S(1)}, bf16[192,256]{1,0:T(8,128)(2,1)S(1)}, u32[]{:S(2)}, u32[]{:S(2)}) %collective-permute-start.2) | collective-permute-done | bytes 98336 | tf_op jit(solution)/shard_map/ppermute | solution.py:418
  18.1 1.5 %collective-permute-start.3 = (bf16[192,256]{1,0:T(8,128)(2,1)S(1)}, bf16[192,256]{1,0:T(8,128)(2,1)S(1)}, u32[]{:S(2)}, u32[]{:S(2)}) collective-permute-start(bf16[192,256]{1,0:T(8,128)(2,1)S(1)} %collective-permute-done.2.refs_0_), channel_id=1, source_target_pairs={{2,0},{6,2},{10,6},{14,10},{12,14},{8,12},{4,8},{0,4},{3,1},{7,3},... | collective-permute-start | bytes 294920 | tf_op jit(solution)/shard_map/ppermute | solution.py:418
  19.6 0.1 collective-permute-done.6.refs_3_
  19.7 1.1 %collective-permute-start.7 = (bf16[192,256]{1,0:T(8,128)(2,1)S(1)}, bf16[192,256]{1,0:T(8,128)(2,1)S(1)}, u32[]{:S(2)}, u32[]{:S(2)}) collective-permute-start(bf16[192,256]{1,0:T(8,128)(2,1)S(1)} %collective-permute-done.6.refs_3_), channel_id=1, source_target_pairs={{0,2},{2,6},{6,10},{10,14},{14,12},{12,8},{8,4},{4,0},{1,3},{3,7},... | collective-permute-start | bytes 294920 | tf_op jit(solution)/shard_map/ppermute | solution.py:419
  20.7 1.1 %attend_next.2 = (f32[2048,256]{1,0:T(8,128)S(1)}, f32[2048,128]{1,0:T(8,128)S(1)}) custom-call(bf16[128,2048]{1,0:T(8,128)(2,1)S(1)} %get-tuple-element.17.q_ref, s32[8,128]{1,0:T(8,128)S(1)} %get-tuple-element.18.limits, bf16[192,256]{1,0:T(8,128)(2,1)S(1)} %collective-permute-done.refs_0_, bf16[192,256]{1,0:T(8,128)(2,1)S(1)} %collective-permute-done.8.refs_1_, ...), custom_call_target="tpu_custom_call" | custom-call | flops 1207959552 | bytes 524288 | tf_op jit(solution)/shard_map/attend_next/pallas_call | solution.py:356
  21.9 0.0 collective-permute-done.10.refs_1_
  21.9 0.0 collective-permute-done.13.refs_2_
  21.9 1.4 %attend_next.3 = (f32[2048,256]{1,0:T(8,128)S(1)}, f32[2048,128]{1,0:T(8,128)S(1)}) custom-call(bf16[128,2048]{1,0:T(8,128)(2,1)S(1)} %get-tuple-element.17.q_ref, s32[8,128]{1,0:T(8,128)S(1)} %get-tuple-element.18.limits, bf16[192,256]{1,0:T(8,128)(2,1)S(1)} %collective-permute-done.2.refs_0_, bf16[192,256]{1,0:T(8,128)(2,1)S(1)} %collective-permute-done.10.refs_1_, ...), custom_call_target="tpu_custom_call" | custom-call | flops 603979776 | bytes 524288 | tf_op jit(solution)/shard_map/attend_next/pallas_call | solution.py:356
  23.3 0.0 collective-permute-done.3.key
  23.3 0.5 %attend_weights.1.weight_in = bf16[2048,256]{1,0:T(8,128)(2,1)S(1)} custom-call(bf16[128,2048]{1,0:T(8,128)(2,1)S(1)} %get-tuple-element.17.q_ref, s32[8,128]{1,0:T(8,128)S(1)} %get-tuple-element.18.limits, bf16[192,256]{1,0:T(8,128)(2,1)S(1)} %collective-permute-done.3.key, f32[2048,128]{1,0:T(8,128)S(1)} %get-tuple-element.27.top_in), custom_call_target="tpu_custom_call" | custom-call | flops 402653184 | bytes 524288 | tf_op jit(solution)/shard_map/attend_weights/pallas_call | solution.py:375
  23.8 0.5 %collective-permute-done.7.value = bf16[192,256]{1,0:T(8,128)(2,1)S(1)} collective-permute-done((bf16[192,256]{1,0:T(8,128)(2,1)S(1)}, bf16[192,256]{1,0:T(8,128)(2,1)S(1)}, u32[]{:S(2)}, u32[]{:S(2)}) %collective-permute-start.7) | collective-permute-done | bytes 98336 | tf_op jit(solution)/shard_map/ppermute | solution.py:419
  24.3 1.3 %attend_last.1 = bf16[128,2048]{1,0:T(8,128)(2,1)} custom-call(bf16[128,2048]{1,0:T(8,128)(2,1)S(1)} %get-tuple-element.17.q_ref, s32[8,128]{1,0:T(8,128)S(1)} %get-tuple-element.18.limits, bf16[192,256]{1,0:T(8,128)(2,1)S(1)} %collective-permute-done.3.key, bf16[192,256]{1,0:T(8,128)(2,1)S(1)} %collective-permute-done.7.value, ...), custom_call_target="tpu_custom_call" | custom-call | flops 402653184 | bytes 524288 | tf_op jit(solution)/shard_map/attend_last/pallas_call | solution.py:384
Async XLA Ops:
  1.1 6.1 %collective-permute-start = (bf16[192,256]{1,0:T(8,128)(2,1)S(1)}, bf16[192,256]{1,0:T(8,128)(2,1)S(1)}, u32[]{:S(2)}, u32[]{:S(2)}) collective-permute-start(bf16[192,256]{1,0:T(8,128)(2,1)S(1)} %get-tuple-element.19.own_keys), channel_id=1, source_target_pairs={{2,0},{6,2},{10,6},{14,10},{12,14},{8,12},{4,8},{0,4},{3,1},{7,3},... | collective-permute-start | bytes 294920 | tf_op jit(solution)/shard_map/ppermute | solution.py:418
  4.2 5.4 %collective-permute-start.4 = (bf16[192,256]{1,0:T(8,128)(2,1)S(1)}, bf16[192,256]{1,0:T(8,128)(2,1)S(1)}, u32[]{:S(2)}, u32[]{:S(2)}) collective-permute-start(bf16[192,256]{1,0:T(8,128)(2,1)S(1)} %get-tuple-element.20.own_values), channel_id=1, source_target_pairs={{0,2},{2,6},{6,10},{10,14},{14,12},{12,8},{8,4},{4,0},{1,3},{3,7},... | collective-permute-start | bytes 294920 | tf_op jit(solution)/shard_map/ppermute | solution.py:419
  4.2 7.5 %collective-permute-start.11 = (bf16[192,256]{1,0:T(8,128)(2,1)S(1)}, bf16[192,256]{1,0:T(8,128)(2,1)S(1)}, u32[]{:S(2)}, u32[]{:S(2)}) collective-permute-start(bf16[192,256]{1,0:T(8,128)(2,1)S(1)} %get-tuple-element.19.own_keys), channel_id=1, source_target_pairs={{0,2},{2,6},{6,10},{10,14},{14,12},{12,8},{8,4},{4,0},{1,3},{3,7},... | collective-permute-start | bytes 294920 | tf_op jit(solution)/shard_map/ppermute | solution.py:422
  6.1 4.8 %collective-permute-start.8 = (bf16[192,256]{1,0:T(8,128)(2,1)S(1)}, bf16[192,256]{1,0:T(8,128)(2,1)S(1)}, u32[]{:S(2)}, u32[]{:S(2)}) collective-permute-start(bf16[192,256]{1,0:T(8,128)(2,1)S(1)} %get-tuple-element.20.own_values), channel_id=1, source_target_pairs={{2,0},{6,2},{10,6},{14,10},{12,14},{8,12},{4,8},{0,4},{3,1},{7,3},... | collective-permute-start | bytes 294920 | tf_op jit(solution)/shard_map/ppermute | solution.py:421
  7.2 5.8 %collective-permute-start.1 = (bf16[192,256]{1,0:T(8,128)(2,1)S(1)}, bf16[192,256]{1,0:T(8,128)(2,1)S(1)}, u32[]{:S(2)}, u32[]{:S(2)}) collective-permute-start(bf16[192,256]{1,0:T(8,128)(2,1)S(1)} %collective-permute-done.refs_0_), channel_id=1, source_target_pairs={{2,0},{6,2},{10,6},{14,10},{12,14},{8,12},{4,8},{0,4},{3,1},{7,3},... | collective-permute-start | bytes 294920 | tf_op jit(solution)/shard_map/ppermute | solution.py:418
  9.6 5.1 %collective-permute-start.5 = (bf16[192,256]{1,0:T(8,128)(2,1)S(1)}, bf16[192,256]{1,0:T(8,128)(2,1)S(1)}, u32[]{:S(2)}, u32[]{:S(2)}) collective-permute-start(bf16[192,256]{1,0:T(8,128)(2,1)S(1)} %collective-permute-done.4.refs_3_), channel_id=1, source_target_pairs={{0,2},{2,6},{6,10},{10,14},{14,12},{12,8},{8,4},{4,0},{1,3},{3,7},... | collective-permute-start | bytes 294920 | tf_op jit(solution)/shard_map/ppermute | solution.py:419
  10.9 4.6 %collective-permute-start.9 = (bf16[192,256]{1,0:T(8,128)(2,1)S(1)}, bf16[192,256]{1,0:T(8,128)(2,1)S(1)}, u32[]{:S(2)}, u32[]{:S(2)}) collective-permute-start(bf16[192,256]{1,0:T(8,128)(2,1)S(1)} %collective-permute-done.8.refs_1_), channel_id=1, source_target_pairs={{2,0},{6,2},{10,6},{14,10},{12,14},{8,12},{4,8},{0,4},{3,1},{7,3},... | collective-permute-start | bytes 294920 | tf_op jit(solution)/shard_map/ppermute | solution.py:421
  11.7 5.1 %collective-permute-start.12 = (bf16[192,256]{1,0:T(8,128)(2,1)S(1)}, bf16[192,256]{1,0:T(8,128)(2,1)S(1)}, u32[]{:S(2)}, u32[]{:S(2)}) collective-permute-start(bf16[192,256]{1,0:T(8,128)(2,1)S(1)} %collective-permute-done.11.refs_2_), channel_id=1, source_target_pairs={{0,2},{2,6},{6,10},{10,14},{14,12},{12,8},{8,4},{4,0},{1,3},{3,7},... | collective-permute-start | bytes 294920 | tf_op jit(solution)/shard_map/ppermute | solution.py:422
  13.0 5.1 %collective-permute-start.2 = (bf16[192,256]{1,0:T(8,128)(2,1)S(1)}, bf16[192,256]{1,0:T(8,128)(2,1)S(1)}, u32[]{:S(2)}, u32[]{:S(2)}) collective-permute-start(bf16[192,256]{1,0:T(8,128)(2,1)S(1)} %collective-permute-done.1.refs_4_), channel_id=1, source_target_pairs={{2,0},{6,2},{10,6},{14,10},{12,14},{8,12},{4,8},{0,4},{3,1},{7,3},... | collective-permute-start | bytes 294920 | tf_op jit(solution)/shard_map/ppermute | solution.py:418
  14.7 5.0 %collective-permute-start.6 = (bf16[192,256]{1,0:T(8,128)(2,1)S(1)}, bf16[192,256]{1,0:T(8,128)(2,1)S(1)}, u32[]{:S(2)}, u32[]{:S(2)}) collective-permute-start(bf16[192,256]{1,0:T(8,128)(2,1)S(1)} %collective-permute-done.5.refs_7_), channel_id=1, source_target_pairs={{0,2},{2,6},{6,10},{10,14},{14,12},{12,8},{8,4},{4,0},{1,3},{3,7},... | collective-permute-start | bytes 294920 | tf_op jit(solution)/shard_map/ppermute | solution.py:419
  15.6 6.3 %collective-permute-start.10 = (bf16[192,256]{1,0:T(8,128)(2,1)S(1)}, bf16[192,256]{1,0:T(8,128)(2,1)S(1)}, u32[]{:S(2)}, u32[]{:S(2)}) collective-permute-start(bf16[192,256]{1,0:T(8,128)(2,1)S(1)} %collective-permute-done.9.refs_5_), channel_id=1, source_target_pairs={{2,0},{6,2},{10,6},{14,10},{12,14},{8,12},{4,8},{0,4},{3,1},{7,3},... | collective-permute-start | bytes 294920 | tf_op jit(solution)/shard_map/ppermute | solution.py:421
  16.8 5.1 %collective-permute-start.13 = (bf16[192,256]{1,0:T(8,128)(2,1)S(1)}, bf16[192,256]{1,0:T(8,128)(2,1)S(1)}, u32[]{:S(2)}, u32[]{:S(2)}) collective-permute-start(bf16[192,256]{1,0:T(8,128)(2,1)S(1)} %collective-permute-done.12.refs_6_), channel_id=1, source_target_pairs={{0,2},{2,6},{6,10},{10,14},{14,12},{12,8},{8,4},{4,0},{1,3},{3,7},... | collective-permute-start | bytes 294920 | tf_op jit(solution)/shard_map/ppermute | solution.py:422
  18.1 5.2 %collective-permute-start.3 = (bf16[192,256]{1,0:T(8,128)(2,1)S(1)}, bf16[192,256]{1,0:T(8,128)(2,1)S(1)}, u32[]{:S(2)}, u32[]{:S(2)}) collective-permute-start(bf16[192,256]{1,0:T(8,128)(2,1)S(1)} %collective-permute-done.2.refs_0_), channel_id=1, source_target_pairs={{2,0},{6,2},{10,6},{14,10},{12,14},{8,12},{4,8},{0,4},{3,1},{7,3},... | collective-permute-start | bytes 294920 | tf_op jit(solution)/shard_map/ppermute | solution.py:418
  19.7 4.6 %collective-permute-start.7 = (bf16[192,256]{1,0:T(8,128)(2,1)S(1)}, bf16[192,256]{1,0:T(8,128)(2,1)S(1)}, u32[]{:S(2)}, u32[]{:S(2)}) collective-permute-start(bf16[192,256]{1,0:T(8,128)(2,1)S(1)} %collective-permute-done.6.refs_3_), channel_id=1, source_target_pairs={{0,2},{2,6},{6,10},{10,14},{14,12},{12,8},{8,4},{4,0},{1,3},{3,7},... | collective-permute-start | bytes 294920 | tf_op jit(solution)/shard_map/ppermute | solution.py:419

commit v21 on v17

--- a/solution.py
+++ b/solution.py
@@ -243,7 +243,7 @@
                 acc_out[at, :] = acc
                 top_out[at, :] = top
 
-    if number < 4:
+    if number < 3:
         take_in(0)
         return
     me = lax.axis_index("ctx")
@@ -413,11 +413,16 @@
     key_on = key_back = own_keys
     value_on = value_back = own_values
     state = attend_first(count, sizes, near, limits, own_keys, own_values)
-    arrived = []
+    arrived, pending = [], []
     for step in range(1, half + 1):
         key_on = lax.ppermute(key_on, "ctx", onward)
         value_back = lax.ppermute(value_back, "ctx", backward)
         if step < half:
+            if step > 2:
+                pending += arrived[step - 3]
+                state = attend_next([pending.pop(0)], state, count, sizes, near, limits)
+                value_on, top = lax.optimization_barrier((value_on, state[1]))
+                state = (state[0], top)
             value_on = lax.ppermute(value_on, "ctx", onward)
             key_back = lax.ppermute(key_back, "ctx", backward)
             row = 2 * (step - 1)
@@ -427,9 +432,10 @@
         if step == 1:
             key_on, top = lax.optimization_barrier((key_on, state[1]))
             state = (state[0], top)
-    for begin in range(0, half - 2, 2):
-        pieces = [piece for step in arrived[begin : min(begin + 2, half - 2)] for piece in step]
-        state = attend_next(pieces, state, count, sizes, near, limits)
+    if half > 2:
+        pending += arrived[half - 3]
+    for begin in range(0, len(pending), 4):
+        state = attend_next(pending[begin : begin + 4], state, count, sizes, near, limits)
     state = attend_next(arrived[half - 2], state, count, sizes, near, limits)
     return attend_last(arrived[half - 1][0], state, sizes, near, limits)
 

time: 25.7 us -> 26.5 us (1.031)
  Pallas kernels: 6.36 us -> 7.48 us
  starting transfers between devices: 16.4 us -> 15.3 us
  waiting for transfers between devices: 2.72 us -> 3.34 us
    ppermute x3, starting transfers between devices: 2.07 us -> 5.85 us  [shards(): value_on = lax.ppermute(value_on, 'ctx', onward)]
    ppermute x3, starting transfers between devices: 4.04 us -> 0.34 us  [shards(): key_back = lax.ppermute(key_back, 'ctx', backward)]
    ppermute x3, waiting for transfers between devices: 1.63 us -> 0.01 us  [shards(): value_on = lax.ppermute(value_on, 'ctx', onward)]
    ppermute x4, waiting for transfers between devices: 0.51 us -> 1.76 us  [shards(): key_on = lax.ppermute(key_on, 'ctx', onward)]
    ppermute x4, starting transfers between devices: 1.66 us -> 0.48 us  [shards(): value_back = lax.ppermute(value_back, 'ctx', backward)]
    pallas_call x2 -> x3, Pallas kernels: 2.53 us -> 3.66 us  [attend_next(): pl.pallas_call(functools.partial(next_kernel, rows_of, count, sizes), out...]
    ppermute x3, waiting for transfers between devices: 0.01 us -> 0.87 us  [shards(): key_back = lax.ppermute(key_back, 'ctx', backward)]
  transfers between devices with their start and end apart: 14 -> 14, of which waited for: 5 -> 6; matrix products, arithmetic and copies ran while one was open for 0% -> 0% of each run, Pallas kernels for 15% -> 19%
where the time goes in v21:
time: 26.5 us; the launch traced here: 26.4 us
  starting transfers between devices  15.3 us (58%)
  Pallas kernels  7.48 us (28%)
  waiting for transfers between devices  3.34 us (13%)
    ppermute x4, starting transfers between devices, shards(): key_on = lax.ppermute(key_on, 'ctx', onward)  8.64 us
    ppermute x3, starting transfers between devices, shards(): value_on = lax.ppermute(value_on, 'ctx', onward)  5.85 us
    pallas_call x3, Pallas kernels, attend_next(): pl.pallas_call(functools.partial(next_kernel, rows_of, count, sizes), out...  3.66 us
    ppermute x4, waiting for transfers between devices, shards(): key_on = lax.ppermute(key_on, 'ctx', onward)  1.76 us
    pallas_call x1, Pallas kernels, attend_last(): pl.pallas_call(functools.partial(last_kernel, row, sizes), out_shape=jax....  1.32 us
    pallas_call x1, Pallas kernels, load(): pl.pallas_call(functools.partial(load_kernel, count), out_shape=[jax.Shap...  1.11 us
    pallas_call x1, Pallas kernels, attend_first(): pl.pallas_call(functools.partial(first_kernel, count, sizes), out_shape=s...  0.93 us
    ppermute x3, waiting for transfers between devices, shards(): key_back = lax.ppermute(key_back, 'ctx', backward)  0.87 us
  transfers between devices with their start and end apart: 14, of which 6 were waited for; matrix products, arithmetic and copies ran while one was open for 0% of the time, Pallas kernels for 19%

profile of v21, /device:TPU:0, one launch (start us, length us, event | category | flops | bytes accessed | tf_op | source)
XLA Modules:
  0.0 26.4 jit_solution(11755108260904321668)
XLA Ops:
  0.0 1.1 %load.1 = (bf16[192,256]{1,0:T(8,128)(2,1)S(1)}, bf16[192,256]{1,0:T(8,128)(2,1)S(1)}, bf16[128,2048]{1,0:T(8,128)(2,1)S(1)}, s32[8,128]{1,0:T(8,128)S(1)}) custom-call(bf16[128,256]{1,0:T(8,128)(2,1)} %win_keys.1, bf16[128,256]{1,0:T(8,128)(2,1)} %win_values.1, bf16[64,256]{1,0:T(8,128)(2,1)} %cache_keys.1, bf16[64,256]{1,0:T(8,128)(2,1)} %cache_values.1, ...), custom_call_target="tpu_custom_call" | custom-call | bytes 393216 | tf_op jit(solution)/shard_map/load/pallas_call | solution.py:81
  1.1 3.1 %collective-permute-start = (bf16[192,256]{1,0:T(8,128)(2,1)S(1)}, bf16[192,256]{1,0:T(8,128)(2,1)S(1)}, u32[]{:S(2)}, u32[]{:S(2)}) collective-permute-start(bf16[192,256]{1,0:T(8,128)(2,1)S(1)} %get-tuple-element.23.own_keys), channel_id=1, source_target_pairs={{2,0},{6,2},{10,6},{14,10},{12,14},{8,12},{4,8},{0,4},{3,1},{7,3},... | collective-permute-start | bytes 294920 | tf_op jit(solution)/shard_map/ppermute | solution.py:418
  4.2 0.0 collective-permute-start.4
  4.2 2.0 %collective-permute-start.8 = (bf16[192,256]{1,0:T(8,128)(2,1)S(1)}, bf16[192,256]{1,0:T(8,128)(2,1)S(1)}, u32[]{:S(2)}, u32[]{:S(2)}) collective-permute-start(bf16[192,256]{1,0:T(8,128)(2,1)S(1)} %get-tuple-element.24.own_values), channel_id=1, source_target_pairs={{2,0},{6,2},{10,6},{14,10},{12,14},{8,12},{4,8},{0,4},{3,1},{7,3},... | collective-permute-start | bytes 294920 | tf_op jit(solution)/shard_map/ppermute | solution.py:426
  6.2 0.0 collective-permute-start.11
  6.2 0.9 %attend_first.1 = (f32[2048,256]{1,0:T(8,128)S(1)}, f32[2048,128]{1,0:T(8,128)S(1)}) custom-call(bf16[128,2048]{1,0:T(8,128)(2,1)S(1)} %get-tuple-element.21.q_ref, s32[8,128]{1,0:T(8,128)S(1)} %get-tuple-element.22.limits, bf16[192,256]{1,0:T(8,128)(2,1)S(1)} %get-tuple-element.23.own_keys, bf16[192,256]{1,0:T(8,128)(2,1)S(1)} %get-tuple-element.24.own_values), custom_call_target="tpu_custom_call" | custom-call | flops 402653184 | bytes 524288 | tf_op jit(solution)/shard_map/attend_first/pallas_call | solution.py:336
  7.2 0.3 %collective-permute-done.refs_0_ = bf16[192,256]{1,0:T(8,128)(2,1)S(1)} collective-permute-done((bf16[192,256]{1,0:T(8,128)(2,1)S(1)}, bf16[192,256]{1,0:T(8,128)(2,1)S(1)}, u32[]{:S(2)}, u32[]{:S(2)}) %collective-permute-start) | collective-permute-done | bytes 98336 | tf_op jit(solution)/shard_map/ppermute | solution.py:418
  7.5 2.0 %collective-permute-start.1 = (bf16[192,256]{1,0:T(8,128)(2,1)S(1)}, bf16[192,256]{1,0:T(8,128)(2,1)S(1)}, u32[]{:S(2)}, u32[]{:S(2)}) collective-permute-start(bf16[192,256]{1,0:T(8,128)(2,1)S(1)} %collective-permute-done.refs_0_), channel_id=1, source_target_pairs={{2,0},{6,2},{10,6},{14,10},{12,14},{8,12},{4,8},{0,4},{3,1},{7,3},... | collective-permute-start | bytes 294920 | tf_op jit(solution)/shard_map/ppermute | solution.py:418
  9.5 0.3 %collective-permute-done.4.refs_1_ = bf16[192,256]{1,0:T(8,128)(2,1)S(1)} collective-permute-done((bf16[192,256]{1,0:T(8,128)(2,1)S(1)}, bf16[192,256]{1,0:T(8,128)(2,1)S(1)}, u32[]{:S(2)}, u32[]{:S(2)}) %collective-permute-start.4) | collective-permute-done | bytes 98336 | tf_op jit(solution)/shard_map/ppermute | solution.py:419
  9.8 0.0 collective-permute-start.5
  9.8 0.0 collective-permute-done.8.refs_1_
  9.8 2.0 %collective-permute-start.9 = (bf16[192,256]{1,0:T(8,128)(2,1)S(1)}, bf16[192,256]{1,0:T(8,128)(2,1)S(1)}, u32[]{:S(2)}, u32[]{:S(2)}) collective-permute-start(bf16[192,256]{1,0:T(8,128)(2,1)S(1)} %collective-permute-done.8.refs_1_), channel_id=1, source_target_pairs={{2,0},{6,2},{10,6},{14,10},{12,14},{8,12},{4,8},{0,4},{3,1},{7,3},... | collective-permute-start | bytes 294920 | tf_op jit(solution)/shard_map/ppermute | solution.py:426
  11.8 0.0 collective-permute-done.11.refs_0_
  11.8 0.0 collective-permute-start.12
  11.9 1.1 %collective-permute-done.1.refs_2_ = bf16[192,256]{1,0:T(8,128)(2,1)S(1)} collective-permute-done((bf16[192,256]{1,0:T(8,128)(2,1)S(1)}, bf16[192,256]{1,0:T(8,128)(2,1)S(1)}, u32[]{:S(2)}, u32[]{:S(2)}) %collective-permute-start.1) | collective-permute-done | bytes 98336 | tf_op jit(solution)/shard_map/ppermute | solution.py:418
  13.0 1.7 %collective-permute-start.2 = (bf16[192,256]{1,0:T(8,128)(2,1)S(1)}, bf16[192,256]{1,0:T(8,128)(2,1)S(1)}, u32[]{:S(2)}, u32[]{:S(2)}) collective-permute-start(bf16[192,256]{1,0:T(8,128)(2,1)S(1)} %collective-permute-done.1.refs_2_), channel_id=1, source_target_pairs={{2,0},{6,2},{10,6},{14,10},{12,14},{8,12},{4,8},{0,4},{3,1},{7,3},... | collective-permute-start | bytes 294920 | tf_op jit(solution)/shard_map/ppermute | solution.py:418
  14.7 0.0 collective-permute-done.5.refs_5_
  14.7 0.3 %collective-permute-start.6 = (bf16[192,256]{1,0:T(8,128)(2,1)S(1)}, bf16[192,256]{1,0:T(8,128)(2,1)S(1)}, u32[]{:S(2)}, u32[]{:S(2)}) collective-permute-start(bf16[192,256]{1,0:T(8,128)(2,1)S(1)} %collective-permute-done.5.refs_5_), channel_id=1, source_target_pairs={{0,2},{2,6},{6,10},{10,14},{14,12},{12,8},{8,4},{4,0},{1,3},{3,7},... | collective-permute-start | bytes 294920 | tf_op jit(solution)/shard_map/ppermute | solution.py:419
  15.0 1.0 %attend_next.3 = (f32[2048,256]{1,0:T(8,128)S(1)}, f32[2048,128]{1,0:T(8,128)S(1)}) custom-call(bf16[128,2048]{1,0:T(8,128)(2,1)S(1)} %get-tuple-element.21.q_ref, s32[8,128]{1,0:T(8,128)S(1)} %get-tuple-element.22.limits, bf16[192,256]{1,0:T(8,128)(2,1)S(1)} %collective-permute-done.refs_0_, bf16[192,256]{1,0:T(8,128)(2,1)S(1)} %collective-permute-done.8.refs_1_, ...), custom_call_target="tpu_custom_call" | custom-call | flops 402653184 | bytes 524288 | tf_op jit(solution)/shard_map/attend_next/pallas_call | solution.py:356
  16.0 0.0 collective-permute-done.9.refs_3_
  16.0 1.8 %collective-permute-start.10 = (bf16[192,256]{1,0:T(8,128)(2,1)S(1)}, bf16[192,256]{1,0:T(8,128)(2,1)S(1)}, u32[]{:S(2)}, u32[]{:S(2)}) collective-permute-start(bf16[192,256]{1,0:T(8,128)(2,1)S(1)} %collective-permute-done.9.refs_3_), channel_id=1, source_target_pairs={{2,0},{6,2},{10,6},{14,10},{12,14},{8,12},{4,8},{0,4},{3,1},{7,3},... | collective-permute-start | bytes 294920 | tf_op jit(solution)/shard_map/ppermute | solution.py:426
  17.8 0.0 collective-permute-done.12.refs_4_
  17.8 0.3 %collective-permute-start.13 = (bf16[192,256]{1,0:T(8,128)(2,1)S(1)}, bf16[192,256]{1,0:T(8,128)(2,1)S(1)}, u32[]{:S(2)}, u32[]{:S(2)}) collective-permute-start(bf16[192,256]{1,0:T(8,128)(2,1)S(1)} %collective-permute-done.12.refs_4_), channel_id=1, source_target_pairs={{0,2},{2,6},{6,10},{10,14},{14,12},{12,8},{8,4},{4,0},{1,3},{3,7},... | collective-permute-start | bytes 294920 | tf_op jit(solution)/shard_map/ppermute | solution.py:427
  18.1 0.3 %collective-permute-done.2.refs_0_ = bf16[192,256]{1,0:T(8,128)(2,1)S(1)} collective-permute-done((bf16[192,256]{1,0:T(8,128)(2,1)S(1)}, bf16[192,256]{1,0:T(8,128)(2,1)S(1)}, u32[]{:S(2)}, u32[]{:S(2)}) %collective-permute-start.2) | collective-permute-done | bytes 98336 | tf_op jit(solution)/shard_map/ppermute | solution.py:418
  18.4 1.8 %collective-permute-start.3 = (bf16[192,256]{1,0:T(8,128)(2,1)S(1)}, bf16[192,256]{1,0:T(8,128)(2,1)S(1)}, u32[]{:S(2)}, u32[]{:S(2)}) collective-permute-start(bf16[192,256]{1,0:T(8,128)(2,1)S(1)} %collective-permute-done.2.refs_0_), channel_id=1, source_target_pairs={{2,0},{6,2},{10,6},{14,10},{12,14},{8,12},{4,8},{0,4},{3,1},{7,3},... | collective-permute-start | bytes 294920 | tf_op jit(solution)/shard_map/ppermute | solution.py:418
  20.3 0.0 collective-permute-done.6.refs_3_
  20.3 0.2 collective-permute-start.7
  20.5 1.1 %attend_next.4 = (f32[2048,256]{1,0:T(8,128)S(1)}, f32[2048,128]{1,0:T(8,128)S(1)}) custom-call(bf16[128,2048]{1,0:T(8,128)(2,1)S(1)} %get-tuple-element.21.q_ref, s32[8,128]{1,0:T(8,128)S(1)} %get-tuple-element.22.limits, bf16[192,256]{1,0:T(8,128)(2,1)S(1)} %collective-permute-done.11.refs_0_, bf16[192,256]{1,0:T(8,128)(2,1)S(1)} %collective-permute-done.4.refs_1_, ...), custom_call_target="tpu_custom_call" | custom-call | flops 1006632960 | bytes 524288 | tf_op jit(solution)/shard_map/attend_next/pallas_call | solution.py:356
  21.6 0.0 collective-permute-done.10.refs_1_
  21.6 0.9 %collective-permute-done.13.refs_2_ = bf16[192,256]{1,0:T(8,128)(2,1)S(1)} collective-permute-done((bf16[192,256]{1,0:T(8,128)(2,1)S(1)}, bf16[192,256]{1,0:T(8,128)(2,1)S(1)}, u32[]{:S(2)}, u32[]{:S(2)}) %collective-permute-start.13) | collective-permute-done | bytes 98336 | tf_op jit(solution)/shard_map/ppermute | solution.py:427
  22.4 1.6 %attend_next.5 = (f32[2048,256]{1,0:T(8,128)S(1)}, f32[2048,128]{1,0:T(8,128)S(1)}) custom-call(bf16[128,2048]{1,0:T(8,128)(2,1)S(1)} %get-tuple-element.21.q_ref, s32[8,128]{1,0:T(8,128)S(1)} %get-tuple-element.22.limits, bf16[192,256]{1,0:T(8,128)(2,1)S(1)} %collective-permute-done.2.refs_0_, bf16[192,256]{1,0:T(8,128)(2,1)S(1)} %collective-permute-done.10.refs_1_, ...), custom_call_target="tpu_custom_call" | custom-call | flops 603979776 | bytes 524288 | tf_op jit(solution)/shard_map/attend_next/pallas_call | solution.py:356
  24.0 0.0 collective-permute-done.3.key
  24.1 0.5 %attend_weights.1.weight_in = bf16[2048,256]{1,0:T(8,128)(2,1)S(1)} custom-call(bf16[128,2048]{1,0:T(8,128)(2,1)S(1)} %get-tuple-element.21.q_ref, s32[8,128]{1,0:T(8,128)S(1)} %get-tuple-element.22.limits, bf16[192,256]{1,0:T(8,128)(2,1)S(1)} %collective-permute-done.3.key, f32[2048,128]{1,0:T(8,128)S(1)} %get-tuple-element.35.top_in), custom_call_target="tpu_custom_call" | custom-call | flops 402653184 | bytes 524288 | tf_op jit(solution)/shard_map/attend_weights/pallas_call | solution.py:375
  24.5 0.4 %collective-permute-done.7.value = bf16[192,256]{1,0:T(8,128)(2,1)S(1)} collective-permute-done((bf16[192,256]{1,0:T(8,128)(2,1)S(1)}, bf16[192,256]{1,0:T(8,128)(2,1)S(1)}, u32[]{:S(2)}, u32[]{:S(2)}) %collective-permute-start.7) | collective-permute-done | bytes 98336 | tf_op jit(solution)/shard_map/ppermute | solution.py:419
  24.9 1.3 %attend_last.1 = bf16[128,2048]{1,0:T(8,128)(2,1)} custom-call(bf16[128,2048]{1,0:T(8,128)(2,1)S(1)} %get-tuple-element.21.q_ref, s32[8,128]{1,0:T(8,128)S(1)} %get-tuple-element.22.limits, bf16[192,256]{1,0:T(8,128)(2,1)S(1)} %collective-permute-done.3.key, bf16[192,256]{1,0:T(8,128)(2,1)S(1)} %collective-permute-done.7.value, ...), custom_call_target="tpu_custom_call" | custom-call | flops 402653184 | bytes 524288 | tf_op jit(solution)/shard_map/attend_last/pallas_call | solution.py:384
Async XLA Ops:
  1.1 6.4 %collective-permute-start = (bf16[192,256]{1,0:T(8,128)(2,1)S(1)}, bf16[192,256]{1,0:T(8,128)(2,1)S(1)}, u32[]{:S(2)}, u32[]{:S(2)}) collective-permute-start(bf16[192,256]{1,0:T(8,128)(2,1)S(1)} %get-tuple-element.23.own_keys), channel_id=1, source_target_pairs={{2,0},{6,2},{10,6},{14,10},{12,14},{8,12},{4,8},{0,4},{3,1},{7,3},... | collective-permute-start | bytes 294920 | tf_op jit(solution)/shard_map/ppermute | solution.py:418
  4.2 5.6 %collective-permute-start.4 = (bf16[192,256]{1,0:T(8,128)(2,1)S(1)}, bf16[192,256]{1,0:T(8,128)(2,1)S(1)}, u32[]{:S(2)}, u32[]{:S(2)}) collective-permute-start(bf16[192,256]{1,0:T(8,128)(2,1)S(1)} %get-tuple-element.24.own_values), channel_id=1, source_target_pairs={{0,2},{2,6},{6,10},{10,14},{14,12},{12,8},{8,4},{4,0},{1,3},{3,7},... | collective-permute-start | bytes 294920 | tf_op jit(solution)/shard_map/ppermute | solution.py:419
  4.2 5.6 %collective-permute-start.8 = (bf16[192,256]{1,0:T(8,128)(2,1)S(1)}, bf16[192,256]{1,0:T(8,128)(2,1)S(1)}, u32[]{:S(2)}, u32[]{:S(2)}) collective-permute-start(bf16[192,256]{1,0:T(8,128)(2,1)S(1)} %get-tuple-element.24.own_values), channel_id=1, source_target_pairs={{2,0},{6,2},{10,6},{14,10},{12,14},{8,12},{4,8},{0,4},{3,1},{7,3},... | collective-permute-start | bytes 294920 | tf_op jit(solution)/shard_map/ppermute | solution.py:426
  6.2 5.6 %collective-permute-start.11 = (bf16[192,256]{1,0:T(8,128)(2,1)S(1)}, bf16[192,256]{1,0:T(8,128)(2,1)S(1)}, u32[]{:S(2)}, u32[]{:S(2)}) collective-permute-start(bf16[192,256]{1,0:T(8,128)(2,1)S(1)} %get-tuple-element.23.own_keys), channel_id=1, source_target_pairs={{0,2},{2,6},{6,10},{10,14},{14,12},{12,8},{8,4},{4,0},{1,3},{3,7},... | collective-permute-start | bytes 294920 | tf_op jit(solution)/shard_map/ppermute | solution.py:427
  7.5 5.5 %collective-permute-start.1 = (bf16[192,256]{1,0:T(8,128)(2,1)S(1)}, bf16[192,256]{1,0:T(8,128)(2,1)S(1)}, u32[]{:S(2)}, u32[]{:S(2)}) collective-permute-start(bf16[192,256]{1,0:T(8,128)(2,1)S(1)} %collective-permute-done.refs_0_), channel_id=1, source_target_pairs={{2,0},{6,2},{10,6},{14,10},{12,14},{8,12},{4,8},{0,4},{3,1},{7,3},... | collective-permute-start | bytes 294920 | tf_op jit(solution)/shard_map/ppermute | solution.py:418
  9.8 4.9 %collective-permute-start.5 = (bf16[192,256]{1,0:T(8,128)(2,1)S(1)}, bf16[192,256]{1,0:T(8,128)(2,1)S(1)}, u32[]{:S(2)}, u32[]{:S(2)}) collective-permute-start(bf16[192,256]{1,0:T(8,128)(2,1)S(1)} %collective-permute-done.4.refs_1_), channel_id=1, source_target_pairs={{0,2},{2,6},{6,10},{10,14},{14,12},{12,8},{8,4},{4,0},{1,3},{3,7},... | collective-permute-start | bytes 294920 | tf_op jit(solution)/shard_map/ppermute | solution.py:419
  9.8 6.2 %collective-permute-start.9 = (bf16[192,256]{1,0:T(8,128)(2,1)S(1)}, bf16[192,256]{1,0:T(8,128)(2,1)S(1)}, u32[]{:S(2)}, u32[]{:S(2)}) collective-permute-start(bf16[192,256]{1,0:T(8,128)(2,1)S(1)} %collective-permute-done.8.refs_1_), channel_id=1, source_target_pairs={{2,0},{6,2},{10,6},{14,10},{12,14},{8,12},{4,8},{0,4},{3,1},{7,3},... | collective-permute-start | bytes 294920 | tf_op jit(solution)/shard_map/ppermute | solution.py:426
  11.8 6.0 %collective-permute-start.12 = (bf16[192,256]{1,0:T(8,128)(2,1)S(1)}, bf16[192,256]{1,0:T(8,128)(2,1)S(1)}, u32[]{:S(2)}, u32[]{:S(2)}) collective-permute-start(bf16[192,256]{1,0:T(8,128)(2,1)S(1)} %collective-permute-done.11.refs_0_), channel_id=1, source_target_pairs={{0,2},{2,6},{6,10},{10,14},{14,12},{12,8},{8,4},{4,0},{1,3},{3,7},... | collective-permute-start | bytes 294920 | tf_op jit(solution)/shard_map/ppermute | solution.py:427
  13.0 5.5 %collective-permute-start.2 = (bf16[192,256]{1,0:T(8,128)(2,1)S(1)}, bf16[192,256]{1,0:T(8,128)(2,1)S(1)}, u32[]{:S(2)}, u32[]{:S(2)}) collective-permute-start(bf16[192,256]{1,0:T(8,128)(2,1)S(1)} %collective-permute-done.1.refs_2_), channel_id=1, source_target_pairs={{2,0},{6,2},{10,6},{14,10},{12,14},{8,12},{4,8},{0,4},{3,1},{7,3},... | collective-permute-start | bytes 294920 | tf_op jit(solution)/shard_map/ppermute | solution.py:418
  14.7 5.5 %collective-permute-start.6 = (bf16[192,256]{1,0:T(8,128)(2,1)S(1)}, bf16[192,256]{1,0:T(8,128)(2,1)S(1)}, u32[]{:S(2)}, u32[]{:S(2)}) collective-permute-start(bf16[192,256]{1,0:T(8,128)(2,1)S(1)} %collective-permute-done.5.refs_5_), channel_id=1, source_target_pairs={{0,2},{2,6},{6,10},{10,14},{14,12},{12,8},{8,4},{4,0},{1,3},{3,7},... | collective-permute-start | bytes 294920 | tf_op jit(solution)/shard_map/ppermute | solution.py:419
  16.0 5.5 %collective-permute-start.10 = (bf16[192,256]{1,0:T(8,128)(2,1)S(1)}, bf16[192,256]{1,0:T(8,128)(2,1)S(1)}, u32[]{:S(2)}, u32[]{:S(2)}) collective-permute-start(bf16[192,256]{1,0:T(8,128)(2,1)S(1)} %collective-permute-done.9.refs_3_), channel_id=1, source_target_pairs={{2,0},{6,2},{10,6},{14,10},{12,14},{8,12},{4,8},{0,4},{3,1},{7,3},... | collective-permute-start | bytes 294920 | tf_op jit(solution)/shard_map/ppermute | solution.py:426
  17.8 4.6 %collective-permute-start.13 = (bf16[192,256]{1,0:T(8,128)(2,1)S(1)}, bf16[192,256]{1,0:T(8,128)(2,1)S(1)}, u32[]{:S(2)}, u32[]{:S(2)}) collective-permute-start(bf16[192,256]{1,0:T(8,128)(2,1)S(1)} %collective-permute-done.12.refs_4_), channel_id=1, source_target_pairs={{0,2},{2,6},{6,10},{10,14},{14,12},{12,8},{8,4},{4,0},{1,3},{3,7},... | collective-permute-start | bytes 294920 | tf_op jit(solution)/shard_map/ppermute | solution.py:427
  18.4 5.6 %collective-permute-start.3 = (bf16[192,256]{1,0:T(8,128)(2,1)S(1)}, bf16[192,256]{1,0:T(8,128)(2,1)S(1)}, u32[]{:S(2)}, u32[]{:S(2)}) collective-permute-start(bf16[192,256]{1,0:T(8,128)(2,1)S(1)} %collective-permute-done.2.refs_0_), channel_id=1, source_target_pairs={{2,0},{6,2},{10,6},{14,10},{12,14},{8,12},{4,8},{0,4},{3,1},{7,3},... | collective-permute-start | bytes 294920 | tf_op jit(solution)/shard_map/ppermute | solution.py:418
  20.3 4.6 %collective-permute-start.7 = (bf16[192,256]{1,0:T(8,128)(2,1)S(1)}, bf16[192,256]{1,0:T(8,128)(2,1)S(1)}, u32[]{:S(2)}, u32[]{:S(2)}) collective-permute-start(bf16[192,256]{1,0:T(8,128)(2,1)S(1)} %collective-permute-done.6.refs_3_), channel_id=1, source_target_pairs={{0,2},{2,6},{6,10},{10,14},{14,12},{12,8},{8,4},{4,0},{1,3},{3,7},... | collective-permute-start | bytes 294920 | tf_op jit(solution)/shard_map/ppermute | solution.py:419

commit v22 on v17

--- a/solution.py
+++ b/solution.py
@@ -101,7 +101,7 @@
 
 def ring_offsets(count):
     half = count // 2
-    return [sign * step for step in range(1, half) for sign in (1, -1)] + [half]
+    return [sign * step for step in range(1, half) for sign in (-1, 1)] + [half]
 
 
 def place_keys(index, number, limit_row, own, sizes, limits, key, keys):
@@ -400,7 +400,7 @@
     sizes = (win_keys.shape[0], cache_keys.shape[0])
     half = count // 2
     ring = [place_at(p, count) for p in range(count)]
-    onward = [(ring[p], ring[(p - 1) % count]) for p in range(count)]
+    onward = [(ring[p], ring[(p + 1) % count]) for p in range(count)]
     backward = [(b, a) for a, b in onward]
 
     win_keys, win_values, cache_keys, cache_values, valid_counts, first_block, queries = [

time: 25.7 us -> 25.7 us (level)
  starting transfers between devices: 16.4 us -> 16 us
  waiting for transfers between devices: 2.72 us -> 3.08 us
    ppermute x4, starting transfers between devices: 8.67 us -> 7.73 us  [shards(): key_on = lax.ppermute(key_on, 'ctx', onward)]
    ppermute x4, starting transfers between devices: 1.66 us -> 2.19 us  [shards(): value_back = lax.ppermute(value_back, 'ctx', backward)]
    ppermute x3, starting transfers between devices: 2.07 us -> 1.72 us  [shards(): value_on = lax.ppermute(value_on, 'ctx', onward)]
    ppermute x3, starting transfers between devices: 4.04 us -> 4.36 us  [shards(): key_back = lax.ppermute(key_back, 'ctx', backward)]
where the time goes in v22:
time: 25.7 us; the launch traced here: 25.5 us
  starting transfers between devices  16 us (62%)
  Pallas kernels  6.35 us (25%)
  waiting for transfers between devices  3.08 us (12%)
    ppermute x4, starting transfers between devices, shards(): key_on = lax.ppermute(key_on, 'ctx', onward)  7.73 us
    ppermute x3, starting transfers between devices, shards(): key_back = lax.ppermute(key_back, 'ctx', backward)  4.36 us
    pallas_call x2, Pallas kernels, attend_next(): pl.pallas_call(functools.partial(next_kernel, rows_of, count, sizes), out...  2.53 us
    ppermute x4, starting transfers between devices, shards(): value_back = lax.ppermute(value_back, 'ctx', backward)  2.19 us
    ppermute x3, starting transfers between devices, shards(): value_on = lax.ppermute(value_on, 'ctx', onward)  1.72 us
    ppermute x3, waiting for transfers between devices, shards(): value_on = lax.ppermute(value_on, 'ctx', onward)  1.67 us
    pallas_call x1, Pallas kernels, attend_last(): pl.pallas_call(functools.partial(last_kernel, row, sizes), out_shape=jax....  1.32 us
    pallas_call x1, Pallas kernels, load(): pl.pallas_call(functools.partial(load_kernel, count), out_shape=[jax.Shap...  1.11 us
  transfers between devices with their start and end apart: 14, of which 5 were waited for; matrix products, arithmetic and copies ran while one was open for 0% of the time, Pallas kernels for 15%

profile of v22, /device:TPU:0, one launch (start us, length us, event | category | flops | bytes accessed | tf_op | source)
XLA Modules:
  0.0 25.5 jit_solution(4183708249432525336)
XLA Ops:
  0.0 1.1 %load.1 = (bf16[192,256]{1,0:T(8,128)(2,1)S(1)}, bf16[192,256]{1,0:T(8,128)(2,1)S(1)}, bf16[128,2048]{1,0:T(8,128)(2,1)S(1)}, s32[8,128]{1,0:T(8,128)S(1)}) custom-call(bf16[128,256]{1,0:T(8,128)(2,1)} %win_keys.1, bf16[128,256]{1,0:T(8,128)(2,1)} %win_values.1, bf16[64,256]{1,0:T(8,128)(2,1)} %cache_keys.1, bf16[64,256]{1,0:T(8,128)(2,1)} %cache_values.1, ...), custom_call_target="tpu_custom_call" | custom-call | bytes 393216 | tf_op jit(solution)/shard_map/load/pallas_call | solution.py:81
  1.1 3.0 %collective-permute-start = (bf16[192,256]{1,0:T(8,128)(2,1)S(1)}, bf16[192,256]{1,0:T(8,128)(2,1)S(1)}, u32[]{:S(2)}, u32[]{:S(2)}) collective-permute-start(bf16[192,256]{1,0:T(8,128)(2,1)S(1)} %get-tuple-element.19.own_keys), channel_id=1, source_target_pairs={{2,6},{6,10},{10,14},{14,12},{12,8},{8,4},{4,0},{0,2},{3,7},{7,11}... | collective-permute-start | bytes 294920 | tf_op jit(solution)/shard_map/ppermute | solution.py:418
  4.1 0.2 collective-permute-start.4
  4.3 2.0 %collective-permute-start.11 = (bf16[192,256]{1,0:T(8,128)(2,1)S(1)}, bf16[192,256]{1,0:T(8,128)(2,1)S(1)}, u32[]{:S(2)}, u32[]{:S(2)}) collective-permute-start(bf16[192,256]{1,0:T(8,128)(2,1)S(1)} %get-tuple-element.19.own_keys), channel_id=1, source_target_pairs={{6,2},{10,6},{14,10},{12,14},{8,12},{4,8},{0,4},{2,0},{7,3},{11,7}... | collective-permute-start | bytes 294920 | tf_op jit(solution)/shard_map/ppermute | solution.py:422
  6.2 0.1 collective-permute-start.8
  6.3 0.9 %attend_first.1 = (f32[2048,256]{1,0:T(8,128)S(1)}, f32[2048,128]{1,0:T(8,128)S(1)}) custom-call(bf16[128,2048]{1,0:T(8,128)(2,1)S(1)} %get-tuple-element.17.q_ref, s32[8,128]{1,0:T(8,128)S(1)} %get-tuple-element.18.limits, bf16[192,256]{1,0:T(8,128)(2,1)S(1)} %get-tuple-element.19.own_keys, bf16[192,256]{1,0:T(8,128)(2,1)S(1)} %get-tuple-element.20.own_values), custom_call_target="tpu_custom_call" | custom-call | flops 402653184 | bytes 524288 | tf_op jit(solution)/shard_map/attend_first/pallas_call | solution.py:336
  7.2 0.0 collective-permute-done.refs_0_
  7.2 2.1 %collective-permute-start.1 = (bf16[192,256]{1,0:T(8,128)(2,1)S(1)}, bf16[192,256]{1,0:T(8,128)(2,1)S(1)}, u32[]{:S(2)}, u32[]{:S(2)}) collective-permute-start(bf16[192,256]{1,0:T(8,128)(2,1)S(1)} %collective-permute-done.refs_0_), channel_id=1, source_target_pairs={{2,6},{6,10},{10,14},{14,12},{12,8},{8,4},{4,0},{0,2},{3,7},{7,11}... | collective-permute-start | bytes 294920 | tf_op jit(solution)/shard_map/ppermute | solution.py:418
  9.4 0.0 collective-permute-done.4.refs_3_
  9.4 0.2 collective-permute-start.5
  9.7 1.3 %collective-permute-done.8.refs_1_ = bf16[192,256]{1,0:T(8,128)(2,1)S(1)} collective-permute-done((bf16[192,256]{1,0:T(8,128)(2,1)S(1)}, bf16[192,256]{1,0:T(8,128)(2,1)S(1)}, u32[]{:S(2)}, u32[]{:S(2)}) %collective-permute-start.8) | collective-permute-done | bytes 98336 | tf_op jit(solution)/shard_map/ppermute | solution.py:421
  11.0 0.5 %collective-permute-start.9 = (bf16[192,256]{1,0:T(8,128)(2,1)S(1)}, bf16[192,256]{1,0:T(8,128)(2,1)S(1)}, u32[]{:S(2)}, u32[]{:S(2)}) collective-permute-start(bf16[192,256]{1,0:T(8,128)(2,1)S(1)} %collective-permute-done.8.refs_1_), channel_id=1, source_target_pairs={{2,6},{6,10},{10,14},{14,12},{12,8},{8,4},{4,0},{0,2},{3,7},{7,11}... | collective-permute-start | bytes 294920 | tf_op jit(solution)/shard_map/ppermute | solution.py:421
  11.4 0.0 collective-permute-done.11.refs_2_
  11.5 1.6 %collective-permute-start.12 = (bf16[192,256]{1,0:T(8,128)(2,1)S(1)}, bf16[192,256]{1,0:T(8,128)(2,1)S(1)}, u32[]{:S(2)}, u32[]{:S(2)}) collective-permute-start(bf16[192,256]{1,0:T(8,128)(2,1)S(1)} %collective-permute-done.11.refs_2_), channel_id=1, source_target_pairs={{6,2},{10,6},{14,10},{12,14},{8,12},{4,8},{0,4},{2,0},{7,3},{11,7}... | collective-permute-start | bytes 294920 | tf_op jit(solution)/shard_map/ppermute | solution.py:422
  13.0 0.0 collective-permute-done.1.refs_4_
  13.0 1.6 %collective-permute-start.2 = (bf16[192,256]{1,0:T(8,128)(2,1)S(1)}, bf16[192,256]{1,0:T(8,128)(2,1)S(1)}, u32[]{:S(2)}, u32[]{:S(2)}) collective-permute-start(bf16[192,256]{1,0:T(8,128)(2,1)S(1)} %collective-permute-done.1.refs_4_), channel_id=1, source_target_pairs={{2,6},{6,10},{10,14},{14,12},{12,8},{8,4},{4,0},{0,2},{3,7},{7,11}... | collective-permute-start | bytes 294920 | tf_op jit(solution)/shard_map/ppermute | solution.py:418
  14.6 0.0 collective-permute-done.5.refs_7_
  14.6 0.6 %collective-permute-start.6 = (bf16[192,256]{1,0:T(8,128)(2,1)S(1)}, bf16[192,256]{1,0:T(8,128)(2,1)S(1)}, u32[]{:S(2)}, u32[]{:S(2)}) collective-permute-start(bf16[192,256]{1,0:T(8,128)(2,1)S(1)} %collective-permute-done.5.refs_7_), channel_id=1, source_target_pairs={{6,2},{10,6},{14,10},{12,14},{8,12},{4,8},{0,4},{2,0},{7,3},{11,7}... | collective-permute-start | bytes 294920 | tf_op jit(solution)/shard_map/ppermute | solution.py:419
  15.2 0.4 %collective-permute-done.9.refs_5_ = bf16[192,256]{1,0:T(8,128)(2,1)S(1)} collective-permute-done((bf16[192,256]{1,0:T(8,128)(2,1)S(1)}, bf16[192,256]{1,0:T(8,128)(2,1)S(1)}, u32[]{:S(2)}, u32[]{:S(2)}) %collective-permute-start.9) | collective-permute-done | bytes 98336 | tf_op jit(solution)/shard_map/ppermute | solution.py:421
  15.6 1.2 %collective-permute-start.10 = (bf16[192,256]{1,0:T(8,128)(2,1)S(1)}, bf16[192,256]{1,0:T(8,128)(2,1)S(1)}, u32[]{:S(2)}, u32[]{:S(2)}) collective-permute-start(bf16[192,256]{1,0:T(8,128)(2,1)S(1)} %collective-permute-done.9.refs_5_), channel_id=1, source_target_pairs={{2,6},{6,10},{10,14},{14,12},{12,8},{8,4},{4,0},{0,2},{3,7},{7,11}... | collective-permute-start | bytes 294920 | tf_op jit(solution)/shard_map/ppermute | solution.py:421
  16.8 0.0 collective-permute-done.12.refs_6_
  16.8 0.8 %collective-permute-start.13 = (bf16[192,256]{1,0:T(8,128)(2,1)S(1)}, bf16[192,256]{1,0:T(8,128)(2,1)S(1)}, u32[]{:S(2)}, u32[]{:S(2)}) collective-permute-start(bf16[192,256]{1,0:T(8,128)(2,1)S(1)} %collective-permute-done.12.refs_6_), channel_id=1, source_target_pairs={{6,2},{10,6},{14,10},{12,14},{8,12},{4,8},{0,4},{2,0},{7,3},{11,7}... | collective-permute-start | bytes 294920 | tf_op jit(solution)/shard_map/ppermute | solution.py:422
  17.6 0.7 %collective-permute-done.2.refs_0_ = bf16[192,256]{1,0:T(8,128)(2,1)S(1)} collective-permute-done((bf16[192,256]{1,0:T(8,128)(2,1)S(1)}, bf16[192,256]{1,0:T(8,128)(2,1)S(1)}, u32[]{:S(2)}, u32[]{:S(2)}) %collective-permute-start.2) | collective-permute-done | bytes 98336 | tf_op jit(solution)/shard_map/ppermute | solution.py:418
  18.3 1.0 %collective-permute-start.3 = (bf16[192,256]{1,0:T(8,128)(2,1)S(1)}, bf16[192,256]{1,0:T(8,128)(2,1)S(1)}, u32[]{:S(2)}, u32[]{:S(2)}) collective-permute-start(bf16[192,256]{1,0:T(8,128)(2,1)S(1)} %collective-permute-done.2.refs_0_), channel_id=1, source_target_pairs={{2,6},{6,10},{10,14},{14,12},{12,8},{8,4},{4,0},{0,2},{3,7},{7,11}... | collective-permute-start | bytes 294920 | tf_op jit(solution)/shard_map/ppermute | solution.py:418
  19.3 0.3 %collective-permute-done.6.refs_3_ = bf16[192,256]{1,0:T(8,128)(2,1)S(1)} collective-permute-done((bf16[192,256]{1,0:T(8,128)(2,1)S(1)}, bf16[192,256]{1,0:T(8,128)(2,1)S(1)}, u32[]{:S(2)}, u32[]{:S(2)}) %collective-permute-start.6) | collective-permute-done | bytes 98336 | tf_op jit(solution)/shard_map/ppermute | solution.py:419
  19.6 1.2 %collective-permute-start.7 = (bf16[192,256]{1,0:T(8,128)(2,1)S(1)}, bf16[192,256]{1,0:T(8,128)(2,1)S(1)}, u32[]{:S(2)}, u32[]{:S(2)}) collective-permute-start(bf16[192,256]{1,0:T(8,128)(2,1)S(1)} %collective-permute-done.6.refs_3_), channel_id=1, source_target_pairs={{6,2},{10,6},{14,10},{12,14},{8,12},{4,8},{0,4},{2,0},{7,3},{11,7}... | collective-permute-start | bytes 294920 | tf_op jit(solution)/shard_map/ppermute | solution.py:419
  20.7 1.1 %attend_next.2 = (f32[2048,256]{1,0:T(8,128)S(1)}, f32[2048,128]{1,0:T(8,128)S(1)}) custom-call(bf16[128,2048]{1,0:T(8,128)(2,1)S(1)} %get-tuple-element.17.q_ref, s32[8,128]{1,0:T(8,128)S(1)} %get-tuple-element.18.limits, bf16[192,256]{1,0:T(8,128)(2,1)S(1)} %collective-permute-done.refs_0_, bf16[192,256]{1,0:T(8,128)(2,1)S(1)} %collective-permute-done.8.refs_1_, ...), custom_call_target="tpu_custom_call" | custom-call | flops 1207959552 | bytes 524288 | tf_op jit(solution)/shard_map/attend_next/pallas_call | solution.py:356
  21.9 0.0 collective-permute-done.10.refs_1_
  21.9 0.0 collective-permute-done.13.refs_2_
  21.9 1.4 %attend_next.3 = (f32[2048,256]{1,0:T(8,128)S(1)}, f32[2048,128]{1,0:T(8,128)S(1)}) custom-call(bf16[128,2048]{1,0:T(8,128)(2,1)S(1)} %get-tuple-element.17.q_ref, s32[8,128]{1,0:T(8,128)S(1)} %get-tuple-element.18.limits, bf16[192,256]{1,0:T(8,128)(2,1)S(1)} %collective-permute-done.2.refs_0_, bf16[192,256]{1,0:T(8,128)(2,1)S(1)} %collective-permute-done.10.refs_1_, ...), custom_call_target="tpu_custom_call" | custom-call | flops 603979776 | bytes 524288 | tf_op jit(solution)/shard_map/attend_next/pallas_call | solution.py:356
  23.3 0.0 collective-permute-done.3.key
  23.3 0.5 %attend_weights.1.weight_in = bf16[2048,256]{1,0:T(8,128)(2,1)S(1)} custom-call(bf16[128,2048]{1,0:T(8,128)(2,1)S(1)} %get-tuple-element.17.q_ref, s32[8,128]{1,0:T(8,128)S(1)} %get-tuple-element.18.limits, bf16[192,256]{1,0:T(8,128)(2,1)S(1)} %collective-permute-done.3.key, f32[2048,128]{1,0:T(8,128)S(1)} %get-tuple-element.27.top_in), custom_call_target="tpu_custom_call" | custom-call | flops 402653184 | bytes 524288 | tf_op jit(solution)/shard_map/attend_weights/pallas_call | solution.py:375
  23.8 0.4 %collective-permute-done.7.value = bf16[192,256]{1,0:T(8,128)(2,1)S(1)} collective-permute-done((bf16[192,256]{1,0:T(8,128)(2,1)S(1)}, bf16[192,256]{1,0:T(8,128)(2,1)S(1)}, u32[]{:S(2)}, u32[]{:S(2)}) %collective-permute-start.7) | collective-permute-done | bytes 98336 | tf_op jit(solution)/shard_map/ppermute | solution.py:419
  24.2 1.3 %attend_last.1 = bf16[128,2048]{1,0:T(8,128)(2,1)} custom-call(bf16[128,2048]{1,0:T(8,128)(2,1)S(1)} %get-tuple-element.17.q_ref, s32[8,128]{1,0:T(8,128)S(1)} %get-tuple-element.18.limits, bf16[192,256]{1,0:T(8,128)(2,1)S(1)} %collective-permute-done.3.key, bf16[192,256]{1,0:T(8,128)(2,1)S(1)} %collective-permute-done.7.value, ...), custom_call_target="tpu_custom_call" | custom-call | flops 402653184 | bytes 524288 | tf_op jit(solution)/shard_map/attend_last/pallas_call | solution.py:384
Async XLA Ops:
  1.1 6.1 %collective-permute-start = (bf16[192,256]{1,0:T(8,128)(2,1)S(1)}, bf16[192,256]{1,0:T(8,128)(2,1)S(1)}, u32[]{:S(2)}, u32[]{:S(2)}) collective-permute-start(bf16[192,256]{1,0:T(8,128)(2,1)S(1)} %get-tuple-element.19.own_keys), channel_id=1, source_target_pairs={{2,6},{6,10},{10,14},{14,12},{12,8},{8,4},{4,0},{0,2},{3,7},{7,11}... | collective-permute-start | bytes 294920 | tf_op jit(solution)/shard_map/ppermute | solution.py:418
  4.1 5.3 %collective-permute-start.4 = (bf16[192,256]{1,0:T(8,128)(2,1)S(1)}, bf16[192,256]{1,0:T(8,128)(2,1)S(1)}, u32[]{:S(2)}, u32[]{:S(2)}) collective-permute-start(bf16[192,256]{1,0:T(8,128)(2,1)S(1)} %get-tuple-element.20.own_values), channel_id=1, source_target_pairs={{6,2},{10,6},{14,10},{12,14},{8,12},{4,8},{0,4},{2,0},{7,3},{11,7}... | collective-permute-start | bytes 294920 | tf_op jit(solution)/shard_map/ppermute | solution.py:419
  4.3 7.2 %collective-permute-start.11 = (bf16[192,256]{1,0:T(8,128)(2,1)S(1)}, bf16[192,256]{1,0:T(8,128)(2,1)S(1)}, u32[]{:S(2)}, u32[]{:S(2)}) collective-permute-start(bf16[192,256]{1,0:T(8,128)(2,1)S(1)} %get-tuple-element.19.own_keys), channel_id=1, source_target_pairs={{6,2},{10,6},{14,10},{12,14},{8,12},{4,8},{0,4},{2,0},{7,3},{11,7}... | collective-permute-start | bytes 294920 | tf_op jit(solution)/shard_map/ppermute | solution.py:422
  6.2 4.8 %collective-permute-start.8 = (bf16[192,256]{1,0:T(8,128)(2,1)S(1)}, bf16[192,256]{1,0:T(8,128)(2,1)S(1)}, u32[]{:S(2)}, u32[]{:S(2)}) collective-permute-start(bf16[192,256]{1,0:T(8,128)(2,1)S(1)} %get-tuple-element.20.own_values), channel_id=1, source_target_pairs={{2,6},{6,10},{10,14},{14,12},{12,8},{8,4},{4,0},{0,2},{3,7},{7,11}... | collective-permute-start | bytes 294920 | tf_op jit(solution)/shard_map/ppermute | solution.py:421
  7.2 5.8 %collective-permute-start.1 = (bf16[192,256]{1,0:T(8,128)(2,1)S(1)}, bf16[192,256]{1,0:T(8,128)(2,1)S(1)}, u32[]{:S(2)}, u32[]{:S(2)}) collective-permute-start(bf16[192,256]{1,0:T(8,128)(2,1)S(1)} %collective-permute-done.refs_0_), channel_id=1, source_target_pairs={{2,6},{6,10},{10,14},{14,12},{12,8},{8,4},{4,0},{0,2},{3,7},{7,11}... | collective-permute-start | bytes 294920 | tf_op jit(solution)/shard_map/ppermute | solution.py:418
  9.4 5.2 %collective-permute-start.5 = (bf16[192,256]{1,0:T(8,128)(2,1)S(1)}, bf16[192,256]{1,0:T(8,128)(2,1)S(1)}, u32[]{:S(2)}, u32[]{:S(2)}) collective-permute-start(bf16[192,256]{1,0:T(8,128)(2,1)S(1)} %collective-permute-done.4.refs_3_), channel_id=1, source_target_pairs={{6,2},{10,6},{14,10},{12,14},{8,12},{4,8},{0,4},{2,0},{7,3},{11,7}... | collective-permute-start | bytes 294920 | tf_op jit(solution)/shard_map/ppermute | solution.py:419
  11.0 4.6 %collective-permute-start.9 = (bf16[192,256]{1,0:T(8,128)(2,1)S(1)}, bf16[192,256]{1,0:T(8,128)(2,1)S(1)}, u32[]{:S(2)}, u32[]{:S(2)}) collective-permute-start(bf16[192,256]{1,0:T(8,128)(2,1)S(1)} %collective-permute-done.8.refs_1_), channel_id=1, source_target_pairs={{2,6},{6,10},{10,14},{14,12},{12,8},{8,4},{4,0},{0,2},{3,7},{7,11}... | collective-permute-start | bytes 294920 | tf_op jit(solution)/shard_map/ppermute | solution.py:421
  11.5 5.3 %collective-permute-start.12 = (bf16[192,256]{1,0:T(8,128)(2,1)S(1)}, bf16[192,256]{1,0:T(8,128)(2,1)S(1)}, u32[]{:S(2)}, u32[]{:S(2)}) collective-permute-start(bf16[192,256]{1,0:T(8,128)(2,1)S(1)} %collective-permute-done.11.refs_2_), channel_id=1, source_target_pairs={{6,2},{10,6},{14,10},{12,14},{8,12},{4,8},{0,4},{2,0},{7,3},{11,7}... | collective-permute-start | bytes 294920 | tf_op jit(solution)/shard_map/ppermute | solution.py:422
  13.0 5.3 %collective-permute-start.2 = (bf16[192,256]{1,0:T(8,128)(2,1)S(1)}, bf16[192,256]{1,0:T(8,128)(2,1)S(1)}, u32[]{:S(2)}, u32[]{:S(2)}) collective-permute-start(bf16[192,256]{1,0:T(8,128)(2,1)S(1)} %collective-permute-done.1.refs_4_), channel_id=1, source_target_pairs={{2,6},{6,10},{10,14},{14,12},{12,8},{8,4},{4,0},{0,2},{3,7},{7,11}... | collective-permute-start | bytes 294920 | tf_op jit(solution)/shard_map/ppermute | solution.py:418
  14.6 5.0 %collective-permute-start.6 = (bf16[192,256]{1,0:T(8,128)(2,1)S(1)}, bf16[192,256]{1,0:T(8,128)(2,1)S(1)}, u32[]{:S(2)}, u32[]{:S(2)}) collective-permute-start(bf16[192,256]{1,0:T(8,128)(2,1)S(1)} %collective-permute-done.5.refs_7_), channel_id=1, source_target_pairs={{6,2},{10,6},{14,10},{12,14},{8,12},{4,8},{0,4},{2,0},{7,3},{11,7}... | collective-permute-start | bytes 294920 | tf_op jit(solution)/shard_map/ppermute | solution.py:419
  15.6 6.3 %collective-permute-start.10 = (bf16[192,256]{1,0:T(8,128)(2,1)S(1)}, bf16[192,256]{1,0:T(8,128)(2,1)S(1)}, u32[]{:S(2)}, u32[]{:S(2)}) collective-permute-start(bf16[192,256]{1,0:T(8,128)(2,1)S(1)} %collective-permute-done.9.refs_5_), channel_id=1, source_target_pairs={{2,6},{6,10},{10,14},{14,12},{12,8},{8,4},{4,0},{0,2},{3,7},{7,11}... | collective-permute-start | bytes 294920 | tf_op jit(solution)/shard_map/ppermute | solution.py:421
  16.8 5.1 %collective-permute-start.13 = (bf16[192,256]{1,0:T(8,128)(2,1)S(1)}, bf16[192,256]{1,0:T(8,128)(2,1)S(1)}, u32[]{:S(2)}, u32[]{:S(2)}) collective-permute-start(bf16[192,256]{1,0:T(8,128)(2,1)S(1)} %collective-permute-done.12.refs_6_), channel_id=1, source_target_pairs={{6,2},{10,6},{14,10},{12,14},{8,12},{4,8},{0,4},{2,0},{7,3},{11,7}... | collective-permute-start | bytes 294920 | tf_op jit(solution)/shard_map/ppermute | solution.py:422
  18.3 5.0 %collective-permute-start.3 = (bf16[192,256]{1,0:T(8,128)(2,1)S(1)}, bf16[192,256]{1,0:T(8,128)(2,1)S(1)}, u32[]{:S(2)}, u32[]{:S(2)}) collective-permute-start(bf16[192,256]{1,0:T(8,128)(2,1)S(1)} %collective-permute-done.2.refs_0_), channel_id=1, source_target_pairs={{2,6},{6,10},{10,14},{14,12},{12,8},{8,4},{4,0},{0,2},{3,7},{7,11}... | collective-permute-start | bytes 294920 | tf_op jit(solution)/shard_map/ppermute | solution.py:418
  19.6 4.6 %collective-permute-start.7 = (bf16[192,256]{1,0:T(8,128)(2,1)S(1)}, bf16[192,256]{1,0:T(8,128)(2,1)S(1)}, u32[]{:S(2)}, u32[]{:S(2)}) collective-permute-start(bf16[192,256]{1,0:T(8,128)(2,1)S(1)} %collective-permute-done.6.refs_3_), channel_id=1, source_target_pairs={{6,2},{10,6},{14,10},{12,14},{8,12},{4,8},{0,4},{2,0},{7,3},{11,7}... | collective-permute-start | bytes 294920 | tf_op jit(solution)/shard_map/ppermute | solution.py:419
